TPU v7x, 512 devices: a whole 4x8x8 slice. The times are simulated.
512 devices in a mesh: row: 16 (over x_hi, z), col: 32 (over x_lo, y, core).
Axes of the slice: x: 4 (x_hi: 2, x_lo: 2; x = x_hi * 2 + x_lo), y: 8, z: 8, core: 2. Of those that a mesh axis runs over, the one named last changes fastest.
Arguments:
- tokens: bfloat16 [1024, 8192], P('col', 'row'), may hold values from -6 to 6
- grad_out: bfloat16 [1024, 8192], P('col', 'row'), may hold values from -0.59765625 to 0.59765625
- gate_pre: bfloat16 [1024, 14336], P('row', 'col'), may hold values from -8 to 8
- up_pre: bfloat16 [1024, 14336], P('row', 'col'), may hold values from -6 to 6
- gate_latent: bfloat16 [8192, 14336], P('row', 'col'), may hold values from -1 to 1
- up_latent: bfloat16 [8192, 14336], P('row', 'col'), may hold values from -1 to 1
- down_latent: bfloat16 [14336, 8192], P('col', 'row'), may hold values from -1 to 1
Outputs:
- grad_tokens: bfloat16 [1024, 8192], P('col', 'row')
- grad_gate: bfloat16 [8192, 14336], P('row', 'col')
- grad_up: bfloat16 [8192, 14336], P('row', 'col')
- grad_down: bfloat16 [14336, 8192], P('col', 'row')
All inputs are finite; a program needn't handle non-finite values.
Results may differ from a plain program's by a relative error of at most 0.0059.
Values may be sent and summed in bfloat16 or wider, within the bound.
No kernel may reach another device: no remote copies, remote signals or barrier semaphores. Data moves between devices by JAX's collectives and lax.ppermute only.
A program may use at most 64 MiB of HBM per device.

v0:
```python
import jax
import jax.numpy as jnp
from jax import lax
from jax.sharding import PartitionSpec as P

EMBED_SIZE = 8192
GATE_INNER_SIZE = 14336


def contract_last(left, right):
    return lax.dot_general(
        left, right, (((1,), (1,)), ((), ())), preferred_element_type=jnp.float32
    )


def contract_first(left, right):
    return lax.dot_general(
        left, right, (((0,), (0,)), ((), ())), preferred_element_type=jnp.float32
    )


def quantize(values, scale):
    return (scale * jnp.clip(values / scale, -1.0, 1.0)).astype(jnp.bfloat16)


def swiglu_grads(grad_hidden, gate_pre, up_pre):
    gate_f = gate_pre.astype(jnp.float32)
    up_f = up_pre.astype(jnp.float32)
    sigma = jax.nn.sigmoid(gate_f)
    silu_gate = gate_f * sigma
    grad_gpre = (grad_hidden * up_f * sigma * (1.0 + gate_f * (1.0 - sigma))).astype(jnp.bfloat16)
    grad_upre = (grad_hidden * silu_gate).astype(jnp.bfloat16)
    return (grad_gpre, grad_upre)


def hidden_of(gate_pre, up_pre):
    gate_f = gate_pre.astype(jnp.float32)
    return (gate_f * jax.nn.sigmoid(gate_f) * up_pre.astype(jnp.float32)).astype(jnp.bfloat16)


def shards(tokens, grad_out, gate_pre, up_pre, gate_latent, up_latent, down_latent):
    gate_f = gate_latent.astype(jnp.float32)
    up_f = up_latent.astype(jnp.float32)
    down_f = down_latent.astype(jnp.float32)
    sums_gate, sums_up, sums_down = lax.psum(
        (jnp.sum(jnp.abs(gate_f)), jnp.sum(jnp.abs(up_f)), jnp.sum(jnp.abs(down_f))), ("row", "col")
    )
    count = float(EMBED_SIZE * GATE_INNER_SIZE)
    quant_gate = quantize(gate_f, sums_gate / count + 1e-05)
    quant_up = quantize(up_f, sums_up / count + 1e-05)
    quant_down = quantize(down_f, sums_down / count + 1e-05)
    tokens_full, out_full = (
        lax.all_gather(tokens, "col", axis=0, tiled=True),
        lax.all_gather(grad_out, "col", axis=0, tiled=True),
    )
    hidden_full = lax.all_gather(hidden_of(gate_pre, up_pre), "row", axis=0, tiled=True)
    grad_hidden = lax.psum_scatter(
        contract_last(out_full, quant_down), "row", scatter_dimension=0, tiled=True
    )
    grad_gpre, grad_upre = swiglu_grads(grad_hidden, gate_pre, up_pre)
    gpre_full, upre_full = (
        lax.all_gather(grad_gpre, "row", axis=0, tiled=True),
        lax.all_gather(grad_upre, "row", axis=0, tiled=True),
    )
    grad_down = contract_first(hidden_full, out_full).astype(jnp.bfloat16)
    grad_gate = contract_first(tokens_full, gpre_full).astype(jnp.bfloat16)
    grad_up = contract_first(tokens_full, upre_full).astype(jnp.bfloat16)
    grad_tokens = lax.psum_scatter(
        contract_last(gpre_full, quant_gate) + contract_last(upre_full, quant_up),
        "col",
        scatter_dimension=0,
        tiled=True,
    ).astype(jnp.bfloat16)
    return (grad_tokens, grad_gate, grad_up, grad_down)


def solution(mesh):
    in_specs = (
        P("col", "row"),
        P("col", "row"),
        P("row", "col"),
        P("row", "col"),
        P("row", "col"),
        P("row", "col"),
        P("col", "row"),
    )
    out_specs = (P("col", "row"), P("row", "col"), P("row", "col"), P("col", "row"))
    return jax.shard_map(shards, mesh=mesh, in_specs=in_specs, out_specs=out_specs, check_vma=False)
```

profile of v0, /device:TPU:4, one launch (start us, length us, event | category | flops | bytes accessed | tf_op | source)
XLA Modules:
  0.0 542.2 jit_solution(5818952974017263355)
XLA Ops:
  7.2 0.0 all-gather.3.cloned.1.call-start
  7.2 0.7 all-gather.3.cloned.1.call-update
  7.9 0.0 reduce-scatter.7.cloned.1.call-start
  7.9 1.9 fusion.2
  9.8 2.0 fusion.6
  11.8 103.3 %all-reduce = (f32[]{:T(128)}, f32[]{:T(128)}, f32[]{:T(128)}) all-reduce(f32[]{:T(128)} %fusion.2, f32[]{:T(128)} %get-tuple-element.10, f32[]{:T(128)} %get-tuple-element.11), channel_id=1, replica_groups=mesh['row'=16,'col'=32] {'row','col'}, use_global_device_ids=true, to_apply=%region_1.0 | all-reduce | flops 3 | bytes 24 | tf_op jit(solution)/shard_map/psum | solution.py:45
  115.7 0.0 all-gather.3.cloned.1.call-done
  115.8 2.1 convolution_bitcast_fusion
  117.8 0.0 copy-start.2
  117.8 0.0 copy-start.3
  117.8 1.8 copy.20
  119.7 0.0 copy-start
  119.7 0.0 reduce-scatter.7.cloned.1.call-update
  119.7 0.0 all-gather.5.cloned.1.call-start
  119.8 0.7 all-gather.5.cloned.1.call-update
  120.5 0.0 reduce-scatter.5.cloned.1.call-start
  121.8 203.4 %reduce-scatter.7.cloned.1.call-done = f32[64,448]{1,0:T(8,128)} async-done(((f32[1024,448]{1,0:T(8,128)}), f32[64,448]{1,0:T(8,128)}) %reduce-scatter.7.cloned.1.call-update) | async-done | bytes 114704 | tf_op jit(solution)/shard_map/reduce_scatter | solution.py:57
  325.2 0.0 copy-done.2
  325.2 0.0 copy-done.3
  325.2 1.0 multiply_convert_fusion
  326.2 45.2 %all_gather.16 = bf16[1024,448]{1,0:T(8,128)(2,1)S(1)} all-gather(bf16[64,448]{1,0:T(8,128)(2,1)S(1)} %get-tuple-element.8), channel_id=1, replica_groups=mesh['row'=16,'col'=32] {'row'}, dimensions={0}, use_global_device_ids=true | all-gather | bytes 974848 | tf_op jit(solution)/shard_map/all_gather | solution.py:62
  371.4 0.0 copy-done
  371.4 0.0 copy-start.1
  371.4 0.8 fusion.15
  372.2 42.0 %all_gather.17 = bf16[1024,448]{1,0:T(8,128)(2,1)S(1)} all-gather(bf16[64,448]{1,0:T(8,128)(2,1)S(1)} %get-tuple-element.7), channel_id=1, replica_groups=mesh['row'=16,'col'=32] {'row'}, dimensions={0}, use_global_device_ids=true | all-gather | bytes 974848 | tf_op jit(solution)/shard_map/all_gather | solution.py:63
  414.2 0.0 copy-done.1
  414.2 2.1 convolution_add_fusion
  416.3 0.0 reduce-scatter.5.cloned.1.call-update
  416.3 0.0 all-gather.5.cloned.1.call-done
  416.3 0.0 copy-start.5
  416.3 2.8 fusion
  419.1 0.0 copy-done.5
  419.1 0.0 copy-start.4
  419.1 1.4 fusion.1
  420.5 43.1 %all_gather.19 = bf16[1024,448]{1,0:T(8,128)(2,1)S(1)} all-gather(bf16[64,448]{1,0:T(8,128)(2,1)S(1)} %get-tuple-element.9), channel_id=1, replica_groups=mesh['row'=16,'col'=32] {'row'}, dimensions={0}, use_global_device_ids=true | all-gather | bytes 974848 | tf_op jit(solution)/shard_map/all_gather | solution.py:56
  463.6 0.0 copy-done.4
  463.6 1.4 convolution_convert_fusion
  465.1 69.2 %reduce-scatter.5.cloned.1.call-done = f32[32,512]{1,0:T(8,128)} async-done(((f32[1024,512]{1,0:T(8,128)}), f32[32,512]{1,0:T(8,128)}) %reduce-scatter.5.cloned.1.call-update) | async-done | bytes 65552 | tf_op jit(solution)/shard_map/reduce_scatter | solution.py:68
  534.2 1.5 convert_element_type.63
Async XLA Ops:
  7.2 108.6 %all-gather.3.cloned.1.call-start = ((), (), s32[]{:S(2)}) async-start(), calls=%async_computation.2 | async-start | bytes 1081344 | tf_op jit(solution)/shard_map/all_gather | solution.py:54
  7.9 317.3 %reduce-scatter.7.cloned.1.call-start = ((), (), s32[]{:S(2)}) async-start(), calls=%async_computation.5 | async-start | bytes 2228224 | tf_op jit(solution)/shard_map/reduce_scatter | solution.py:57
  117.8 207.4 %copy-start.2 = (bf16[64,448]{1,0:T(8,128)(2,1)S(1)}, bf16[64,448]{1,0:T(8,128)(2,1)}, u32[]{:S(2)}) copy-start(bf16[64,448]{1,0:T(8,128)(2,1)} %param.9) | copy-start | bytes 172036
  117.8 207.4 %copy-start.3 = (bf16[64,448]{1,0:T(8,128)(2,1)S(1)}, bf16[64,448]{1,0:T(8,128)(2,1)}, u32[]{:S(2)}) copy-start(bf16[64,448]{1,0:T(8,128)(2,1)} %param.10) | copy-start | bytes 172036
  119.7 251.7 %copy-start = (bf16[512,448]{0,1:T(8,128)(2,1)S(1)}, bf16[512,448]{0,1:T(8,128)(2,1)}, u32[]{:S(2)}) copy-start(bf16[512,448]{0,1:T(8,128)(2,1)} %param.11) | copy-start | bytes 1376260
  119.7 296.6 %all-gather.5.cloned.1.call-start = ((), (), s32[]{:S(2)}) async-start(), calls=%async_computation.4 | async-start | bytes 1081344 | tf_op jit(solution)/shard_map/all_gather | solution.py:53
  120.5 413.8 %reduce-scatter.5.cloned.1.call-start = ((), (), s32[]{:S(2)}) async-start(), calls=%async_computation.3 | async-start | bytes 2162688 | tf_op jit(solution)/shard_map/reduce_scatter | solution.py:68
  371.4 42.8 %copy-start.1 = (bf16[512,448]{0,1:T(8,128)(2,1)S(1)}, bf16[512,448]{0,1:T(8,128)(2,1)}, u32[]{:S(2)}) copy-start(bf16[512,448]{0,1:T(8,128)(2,1)} %param.12) | copy-start | bytes 1376260
  416.3 2.8 copy-start.5
  419.1 44.5 %copy-start.4 = (bf16[1024,512]{1,0:T(8,128)(2,1)S(1)}, bf16[1024,512]{1,0:T(8,128)(2,1)}, u32[]{:S(2)}) copy-start(bf16[1024,512]{1,0:T(8,128)(2,1)} %all-gather.3.cloned.1.call-done) | copy-start | bytes 3145732
Sparse Core Ops, SparseCore 0:
  10.1 70.4 all-gather.2
  119.8 205.3 reduce-scatter.6
  327.4 64.5 all-gather.4
  416.4 117.7 reduce-scatter.4
where the time goes:
time: 543 us; the launch traced here: 542 us
  waiting for transfers between devices  274 us (50%)
  blocking collectives  234 us (43%)
  between operations  15.8 us (3%)
  matrix products  10.5 us (2%)
  other arithmetic  6.3 us (1%)
    reduce_scatter x1, waiting for transfers between devices, shards(): lax.psum_scatter(contract_last(out_full, quant_down), 'row', scatter_dime...  203 us
    psum x1, blocking collectives, shards(): lax.psum((jnp.sum(jnp.abs(gate_f)), jnp.sum(jnp.abs(up_f)), jnp.sum(jnp.a...  103 us
    reduce_scatter x1, waiting for transfers between devices, shards(): lax.psum_scatter(contract_last(gpre_full, quant_gate) + contract_last(upr...  69.2 us
    all_gather x1, blocking collectives, shards(): lax.all_gather(grad_gpre, 'row', axis=0, tiled=True)  45.2 us
    all_gather x1, blocking collectives, shards(): lax.all_gather(hidden_of(gate_pre, up_pre), 'row', axis=0, tiled=True)  43.1 us
    all_gather x1, blocking collectives, shards(): lax.all_gather(grad_upre, 'row', axis=0, tiled=True)  42 us
  transfers between devices with their start and end apart: 4, of which 2 were waited for; matrix products, arithmetic and copies ran while one was open for 2% of the time, Pallas kernels for 0%

commit v1 on v0

v1 whole, which is shorter than its diff:
```python
import jax
import jax.numpy as jnp
from jax import lax
from jax.sharding import Mesh, PartitionSpec as P

EMBED_SIZE = 8192
GATE_INNER_SIZE = 14336
N_ROW = 16
N_CHIP = 16
ROW = ("xh", "z")
CHIP = ("xl", "y")


def contract_last(left, right):
    return lax.dot_general(
        left, right, (((1,), (1,)), ((), ())), preferred_element_type=jnp.float32
    )


def contract_first(left, right):
    return lax.dot_general(
        left, right, (((0,), (0,)), ((), ())), preferred_element_type=jnp.float32
    )


def quantize(values, scale):
    return (scale * jnp.clip(values.astype(jnp.float32) / scale, -1.0, 1.0)).astype(jnp.bfloat16)


def swiglu_grads(grad_hidden, gate_pre, up_pre):
    gate_f = gate_pre.astype(jnp.float32)
    up_f = up_pre.astype(jnp.float32)
    sigma = jax.nn.sigmoid(gate_f)
    silu_gate = gate_f * sigma
    grad_gpre = (grad_hidden * up_f * sigma * (1.0 + gate_f * (1.0 - sigma))).astype(jnp.bfloat16)
    grad_upre = (grad_hidden * silu_gate).astype(jnp.bfloat16)
    hidden = (silu_gate * up_f).astype(jnp.bfloat16)
    return (grad_gpre, grad_upre, hidden)


def to_all(values, axes, count):
    return lax.all_to_all(jnp.broadcast_to(values, (count,) + values.shape), axes, 0, 0)


def swapped(values):
    return lax.ppermute(values, "core", [(0, 1), (1, 0)])


def in_order(core, mine, other, axis):
    return jnp.where(
        core == 0, jnp.stack([mine, other], axis=axis), jnp.stack([other, mine], axis=axis)
    )


def shards(tokens, grad_out, gate_pre, up_pre, gate_latent, up_latent, down_latent):
    core = lax.axis_index("core")
    width = tokens.shape[1]
    inner = gate_pre.shape[1]
    out_half = to_all(grad_out, CHIP, N_CHIP)
    down_other = swapped(down_latent)
    pre_full = lax.all_gather(
        jnp.concatenate([gate_pre, up_pre], axis=1), ROW, axis=0, tiled=True
    )

    sums = [jnp.sum(jnp.abs(w.astype(jnp.float32))) for w in (gate_latent, up_latent, down_latent)]
    tile = jnp.broadcast_to(jnp.stack(sums + [jnp.float32(0.0)] * 5)[:, None], (8, 128))
    tile = jnp.sum(to_all(tile, ROW + ("core",), 2 * N_ROW), axis=0)
    tile = jnp.sum(to_all(tile, CHIP, N_CHIP), axis=0)
    scales = tile[:, 0] / float(EMBED_SIZE * GATE_INNER_SIZE) + 1e-05

    out_rows = out_half.reshape((-1, width))
    partial = jnp.concatenate(
        [contract_last(out_rows, quantize(down_latent, scales[2])).astype(jnp.bfloat16),
         contract_last(out_rows, quantize(down_other, scales[2])).astype(jnp.bfloat16)],
        axis=1,
    )
    tokens, partial = lax.optimization_barrier((tokens, partial))
    parts = lax.all_to_all(partial.reshape((N_ROW, -1, 2 * inner)), ROW, 0, 0)
    tokens_half = to_all(tokens, CHIP, N_CHIP)
    both_half = jnp.stack([out_half, tokens_half])
    both = in_order(core, both_half, swapped(both_half), 2)
    out_full = both[0].reshape((-1, width))
    tokens_full = both[1].reshape((-1, width))

    summed = jnp.sum(parts.astype(jnp.float32), axis=0).astype(jnp.bfloat16)
    split = in_order(core, summed[:, :inner], summed[:, inner:], 0)
    grad_hidden = lax.all_to_all(
        jnp.broadcast_to(split, (N_ROW,) + split.shape).reshape((2 * N_ROW,) + split.shape[1:]),
        ROW + ("core",), 0, 0,
    ).reshape((-1, inner)).astype(jnp.float32)
    gpre, upre, hidden = swiglu_grads(grad_hidden, pre_full[:, :inner], pre_full[:, inner:])

    partial = contract_last(gpre, quantize(gate_latent, scales[0])) + contract_last(
        upre, quantize(up_latent, scales[1])
    )
    blocks = partial.reshape((N_CHIP, 2, -1, width))
    kept = lax.dynamic_index_in_dim(blocks, core, 1, keepdims=False)
    sent = lax.dynamic_index_in_dim(blocks, 1 - core, 1, keepdims=False).astype(jnp.bfloat16)
    pair = (kept + swapped(sent).astype(jnp.float32)).astype(jnp.bfloat16)
    parts = lax.all_to_all(pair, CHIP, 0, 0)
    grad_down = contract_first(hidden, out_full).astype(jnp.bfloat16)
    grad_gate = contract_first(tokens_full, gpre).astype(jnp.bfloat16)
    grad_up = contract_first(tokens_full, upre).astype(jnp.bfloat16)
    grad_tokens = jnp.sum(parts.astype(jnp.float32), axis=0).astype(jnp.bfloat16)
    return (grad_tokens, grad_gate, grad_up, grad_down)


def solution(mesh):
    fine = Mesh(mesh.devices.reshape((2, 8, 2, 8, 2)), ROW + CHIP + ("core",))
    col = CHIP + ("core",)
    in_specs = (
        P(col, ROW),
        P(col, ROW),
        P(ROW, col),
        P(ROW, col),
        P(ROW, col),
        P(ROW, col),
        P(col, ROW),
    )
    out_specs = (P(col, ROW), P(ROW, col), P(ROW, col), P(col, ROW))
    return jax.shard_map(shards, mesh=fine, in_specs=in_specs, out_specs=out_specs, check_vma=False)
```

time: 543 us -> 228 us (0.42)
  the two profiles are of different devices: /device:TPU:4 before, /device:TPU:8 now
where the time goes in v1:
time: 228 us; the launch traced here: 227 us
  waiting for transfers between devices  100 us (44%)
  blocking collectives  39.9 us (18%)
  starting transfers between devices  33.8 us (15%)
  other arithmetic  15.6 us (7%)
  between operations  14.3 us (6%)
  matrix products  12.4 us (5%)
  local copies, waits for them, and re-layouts  11.4 us (5%)
    all_gather x1, waiting for transfers between devices, shards(): lax.all_gather(jnp.concatenate([gate_pre, up_pre], axis=1), ROW, axis=0,...  45.7 us
    all_to_all x2, blocking collectives, to_all(): lax.all_to_all(jnp.broadcast_to(values, (count,) + values.shape), axes, 0...  39.9 us
    all_to_all x1, waiting for transfers between devices, shards(): parts = lax.all_to_all(partial.reshape((N_ROW, -1, 2 * inner)), ROW, 0, 0)  22.4 us
    all_to_all x2, waiting for transfers between devices, to_all(): lax.all_to_all(jnp.broadcast_to(values, (count,) + values.shape), axes, 0...  22.2 us
    all_to_all x2, starting transfers between devices, to_all(): lax.all_to_all(jnp.broadcast_to(values, (count,) + values.shape), axes, 0...  9.79 us
    all_to_all x1, waiting for transfers between devices, shards(): parts = lax.all_to_all(pair, CHIP, 0, 0)  9.71 us
    all_to_all x1, starting transfers between devices, shards(): lax.all_to_all(jnp.broadcast_to(split, (N_ROW,) + split.shape).reshape((2...  7.61 us
    all_to_all x1, starting transfers between devices, shards(): parts = lax.all_to_all(pair, CHIP, 0, 0)  6.59 us
  transfers between devices with their start and end apart: 9, of which 5 were waited for; matrix products, arithmetic and copies ran while one was open for 10% of the time, Pallas kernels for 0%

profile of v1, /device:TPU:8, one launch (start us, length us, event | category | flops | bytes accessed | tf_op | source)
XLA Modules:
  0.0 227.4 jit_solution(15825816442533456646)
XLA Ops:
  7.2 0.0 copy-start.6
  7.2 0.0 copy-start.10
  7.2 1.9 fusion.22
  9.1 1.9 fusion.18
  11.0 1.9 fusion.14
  12.8 2.0 stack.52
  14.8 0.1 broadcast_in_dim_broadcast_in_dim.2
  14.9 24.9 %all_to_all.35 = f32[32,8,128]{2,1,0:T(8,128)S(1)} all-to-all(f32[32,8,128]{2,1,0:T(8,128)S(1)} %broadcast_in_dim_broadcast_in_dim.2), channel_id=1, replica_groups=mesh['xh'=2,'z'=8,'xl'=2,'y'=8,'core'=2] {'xh','z','core'}, dimensions={0} | all-to-all | bytes 262144 | tf_op jit(solution)/shard_map/all_to_all | solution.py:42
  39.9 15.0 %all_to_all.36 = f32[16,8,128]{2,1,0:T(8,128)S(1)} all-to-all(f32[16,8,128]{2,1,0:T(8,128)S(1)} %broadcast_in_dim.13), channel_id=1, replica_groups=mesh['xh'=2,'z'=8,'xl'=2,'y'=8,'core'=2] {'xl','y'}, dimensions={0} | all-to-all | bytes 131072 | tf_op jit(solution)/shard_map/all_to_all | solution.py:42
  54.9 0.0 copy-done.10
  54.9 0.9 broadcast_in_dim.14
  55.7 4.4 %all-to-all-start.2 = ((bf16[16,32,512]{2,1,0:T(8,128)(2,1)}), bf16[16,32,512]{2,1,0:T(8,128)(2,1)S(1)}, u32[]{:S(2)}, u32[]{:S(2)}) async-start(bf16[16,32,512]{2,1,0:T(8,128)(2,1)} %broadcast_in_dim.14), calls=%async_computation.2 | async-start | bytes 1048576 | tf_op jit(solution)/shard_map/all_to_all | solution.py:42
  60.2 0.0 copy-done.6
  60.2 1.9 collective-permute-start
  62.1 0.5 fusion.54
  62.7 10.6 %all-to-all-done.2 = bf16[16,32,512]{2,1,0:T(8,128)(2,1)S(1)} async-done(((bf16[16,32,512]{2,1,0:T(8,128)(2,1)}), bf16[16,32,512]{2,1,0:T(8,128)(2,1)S(1)}, u32[]{:S(2)}, u32[]{:S(2)}) %all-to-all-start.2) | async-done | bytes 524320 | tf_op jit(solution)/shard_map/all_to_all | solution.py:42
  73.2 1.1 fusion.9
  74.3 0.0 collective-permute-done
  74.3 1.1 fusion.10
  75.4 0.1 pad_maximum_fusion.1
  75.5 0.0 copy-start.8
  75.5 0.0 copy-start.9
  75.5 0.0 copy-start.11
  75.5 1.3 copy.12
  76.8 3.7 %all-to-all-start.3 = ((bf16[16,32,896]{2,1,0:T(8,128)(2,1)}), bf16[16,32,896]{2,1,0:T(8,128)(2,1)S(1)}, u32[]{:S(2)}, u32[]{:S(2)}) async-start(bf16[16,32,896]{2,1,0:T(8,128)(2,1)} %bitcast.7), calls=%async_computation.3 | async-start | bytes 1835008 | tf_op jit(solution)/shard_map/all_to_all | solution.py:78
  80.6 0.0 all-gather.2.cloned.1.call-start
  80.6 0.0 copy-done.8
  80.6 0.0 copy-done.9
  80.6 0.7 pad_maximum_fusion.2
  81.4 0.0 all-gather.2.cloned.1.call-update
  81.4 22.4 %all-to-all-done.3 = bf16[16,32,896]{2,1,0:T(8,128)(2,1)S(1)} async-done(((bf16[16,32,896]{2,1,0:T(8,128)(2,1)}), bf16[16,32,896]{2,1,0:T(8,128)(2,1)S(1)}, u32[]{:S(2)}, u32[]{:S(2)}) %all-to-all-start.3) | async-done | bytes 917536 | tf_op jit(solution)/shard_map/all_to_all | solution.py:78
  103.8 0.0 copy-done.11
  103.8 0.9 broadcast_in_dim.16
  104.7 5.4 %all-to-all-start.6 = ((bf16[16,32,512]{2,1,0:T(8,128)(2,1)}), bf16[16,32,512]{2,1,0:T(8,128)(2,1)S(1)}, u32[]{:S(2)}, u32[]{:S(2)}) async-start(bf16[16,32,512]{2,1,0:T(8,128)(2,1)} %broadcast_in_dim.16), calls=%async_computation.6 | async-start | bytes 1048576 | tf_op jit(solution)/shard_map/all_to_all | solution.py:42
  110.1 0.1 reduce_sum.74
  110.2 0.1 slice_bitcast_fusion.1
  110.3 11.6 %all-to-all-done.6 = bf16[16,32,512]{2,1,0:T(8,128)(2,1)S(1)} async-done(((bf16[16,32,512]{2,1,0:T(8,128)(2,1)}), bf16[16,32,512]{2,1,0:T(8,128)(2,1)S(1)}, u32[]{:S(2)}, u32[]{:S(2)}) %all-to-all-start.6) | async-done | bytes 524320 | tf_op jit(solution)/shard_map/all_to_all | solution.py:42
  121.9 1.1 broadcast_in_dim.15
  123.0 7.6 %all-to-all-start.4 = ((bf16[32,32,448]{2,1,0:T(8,128)(2,1)}), bf16[32,32,448]{2,1,0:T(8,128)(2,1)S(1)}, u32[]{:S(2)}, u32[]{:S(2)}) async-start(bf16[32,32,448]{2,1,0:T(8,128)(2,1)} %bitcast.10), calls=%async_computation.4 | async-start | bytes 2097152 | tf_op jit(solution)/shard_map/all_to_all | solution.py:87
  130.6 1.2 fusion.52
  131.8 2.2 collective-permute-start.2
  134.0 45.7 %all-gather.2.cloned.1.call-done = bf16[1024,896]{1,0:T(8,128)(2,1)} async-done(((bf16[64,896]{1,0:T(8,128)(2,1)}), bf16[1024,896]{1,0:T(8,128)(2,1)}) %all-gather.2.cloned.1.call-update) | async-done | bytes 1835024 | tf_op jit(solution)/shard_map/all_gather | solution.py:61
  179.7 0.0 all-to-all-done.4
  179.7 3.2 %fusion.4 = (bf16[1024,448]{1,0:T(8,128)(2,1)S(1)}, bf16[1024,448]{1,0:T(8,128)(2,1)S(1)}) fusion(bf16[32,32,448]{2,1,0:T(8,128)(2,1)S(1)} %all-to-all-done.4, bf16[1024,896]{1,0:T(8,128)(2,1)} %all-gather.2.cloned.1.call-done), kind=kLoop, calls=%fused_computation.10 | loop fusion | flops 7340032 | bytes 4587520 | tf_op jit(solution)/shard_map/convert_element_type | solution.py:36
  182.9 0.0 copy-start.3
  182.9 0.0 copy-start.7
  182.9 2.5 %fusion.29 = f32[1024,512]{1,0:T(8,128)S(1)} fusion(bf16[1024,448]{1,0:T(8,128)(2,1)S(1)} %get-tuple-element.9, bf16[512,448]{0,1:T(8,128)(2,1)} %param.11, f32[]{:T(128)} %bitcast.12), kind=kOutput, calls=%fused_computation.50 | convolution fusion | flops 470908928 | bytes 3473412 | tf_op jit(solution)/shard_map/dot_general | solution.py:15
  185.4 1.4 convolution_add_fusion
  186.8 0.0 copy-start.1
  186.8 1.3 copy-done.1
  188.2 0.9 fusion.26
  189.0 1.9 collective-permute-start.1
  191.0 0.0 collective-permute-done.2
  191.0 1.9 maximum_select_fusion
  192.9 1.5 fusion.53
  194.4 0.0 collective-permute-done.1
  194.4 0.8 copy-done.2
  195.2 2.0 fusion.12
  197.2 6.6 %all-to-all-start.5 = ((bf16[16,32,512]{2,1,0:T(8,128)(2,1)}), bf16[16,32,512]{2,1,0:T(8,128)(2,1)S(1)}, u32[]{:S(2)}, u32[]{:S(2)}) async-start(bf16[16,32,512]{2,1,0:T(8,128)(2,1)} %fusion.12), calls=%async_computation.5 | async-start | bytes 1048576 | tf_op jit(solution)/shard_map/all_to_all | solution.py:100
  203.9 3.4 %convolution_convert_fusion.2 = bf16[448,512]{1,0:T(8,128)(2,1)} fusion(bf16[1024,512]{1,0:T(8,128)(2,1)} %bitcast.52, bf16[1024,896]{1,0:T(8,128)(2,1)S(1)} %copy-done), kind=kOutput, calls=%fused_computation.19 | convolution fusion | flops 473661440 | bytes 3604480 | tf_op jit(solution)/shard_map/dot_general | solution.py:21
  207.2 1.5 convolution_convert_fusion.3
  208.7 1.5 convolution_convert_fusion.4
  210.2 9.7 %all-to-all-done.5 = bf16[16,32,512]{2,1,0:T(8,128)(2,1)S(1)} async-done(((bf16[16,32,512]{2,1,0:T(8,128)(2,1)}), bf16[16,32,512]{2,1,0:T(8,128)(2,1)S(1)}, u32[]{:S(2)}, u32[]{:S(2)}) %all-to-all-start.5) | async-done | bytes 524320 | tf_op jit(solution)/shard_map/all_to_all | solution.py:100
  219.9 0.7 reduce_sum.75
  (15 shorter events, 0.1 us)
Async XLA Ops:
  7.2 53.0 %copy-start.6 = (bf16[448,512]{1,0:T(8,128)(2,1)S(1)}, bf16[448,512]{1,0:T(8,128)(2,1)}, u32[]{:S(2)}) copy-start(bf16[448,512]{1,0:T(8,128)(2,1)} %param.13) | copy-start | bytes 1376260
  7.2 47.7 %copy-start.10 = (bf16[32,512]{1,0:T(8,128)(2,1)S(1)}, bf16[32,512]{1,0:T(8,128)(2,1)}, u32[]{:S(2)}) copy-start(bf16[32,512]{1,0:T(8,128)(2,1)} %param.8) | copy-start | bytes 98308
  55.7 17.5 %all-to-all-start.2 = ((bf16[16,32,512]{2,1,0:T(8,128)(2,1)}), bf16[16,32,512]{2,1,0:T(8,128)(2,1)S(1)}, u32[]{:S(2)}, u32[]{:S(2)}) async-start(bf16[16,32,512]{2,1,0:T(8,128)(2,1)} %broadcast_in_dim.14), calls=%async_computation.2 | async-start | bytes 1048576 | tf_op jit(solution)/shard_map/all_to_all | solution.py:42
  60.2 14.1 %collective-permute-start = (bf16[448,512]{1,0:T(8,128)(2,1)S(1)}, bf16[448,512]{1,0:T(8,128)(2,1)S(1)}, u32[]{:S(2)}, u32[]{:S(2)}) collective-permute-start(bf16[448,512]{1,0:T(8,128)(2,1)S(1)} %copy-done.6), channel_id=1, source_target_pairs={{0,1},{1,0},{2,3},{3,2},{4,5},{5,4},{6,7},{7,6},{8,9},{9,8},{10,11... | collective-permute-start | bytes 1376264 | tf_op jit(solution)/shard_map/ppermute | solution.py:46
  75.5 5.1 %copy-start.8 = (bf16[64,448]{1,0:T(8,128)(2,1)S(1)}, bf16[64,448]{1,0:T(8,128)(2,1)}, u32[]{:S(2)}) copy-start(bf16[64,448]{1,0:T(8,128)(2,1)} %param.10) | copy-start | bytes 172036
  75.5 5.1 %copy-start.9 = (bf16[64,448]{1,0:T(8,128)(2,1)S(1)}, bf16[64,448]{1,0:T(8,128)(2,1)}, u32[]{:S(2)}) copy-start(bf16[64,448]{1,0:T(8,128)(2,1)} %param.9) | copy-start | bytes 172036
  75.5 28.3 %copy-start.11 = (bf16[32,512]{1,0:T(8,128)(2,1)S(1)}, bf16[32,512]{1,0:T(8,128)(2,1)}, u32[]{:S(2)}) copy-start(bf16[32,512]{1,0:T(8,128)(2,1)} %param.7) | copy-start | bytes 98308
  76.8 27.0 %all-to-all-start.3 = ((bf16[16,32,896]{2,1,0:T(8,128)(2,1)}), bf16[16,32,896]{2,1,0:T(8,128)(2,1)S(1)}, u32[]{:S(2)}, u32[]{:S(2)}) async-start(bf16[16,32,896]{2,1,0:T(8,128)(2,1)} %bitcast.7), calls=%async_computation.3 | async-start | bytes 1835008 | tf_op jit(solution)/shard_map/all_to_all | solution.py:78
  80.6 99.1 %all-gather.2.cloned.1.call-start = ((), (), s32[]{:S(2)}) async-start(), calls=%async_computation.7 | async-start | bytes 1949696 | tf_op jit(solution)/shard_map/all_gather | solution.py:61
  104.7 17.2 %all-to-all-start.6 = ((bf16[16,32,512]{2,1,0:T(8,128)(2,1)}), bf16[16,32,512]{2,1,0:T(8,128)(2,1)S(1)}, u32[]{:S(2)}, u32[]{:S(2)}) async-start(bf16[16,32,512]{2,1,0:T(8,128)(2,1)} %broadcast_in_dim.16), calls=%async_computation.6 | async-start | bytes 1048576 | tf_op jit(solution)/shard_map/all_to_all | solution.py:42
  123.0 56.7 %all-to-all-start.4 = ((bf16[32,32,448]{2,1,0:T(8,128)(2,1)}), bf16[32,32,448]{2,1,0:T(8,128)(2,1)S(1)}, u32[]{:S(2)}, u32[]{:S(2)}) async-start(bf16[32,32,448]{2,1,0:T(8,128)(2,1)} %bitcast.10), calls=%async_computation.4 | async-start | bytes 2097152 | tf_op jit(solution)/shard_map/all_to_all | solution.py:87
  131.8 59.2 %collective-permute-start.2 = (bf16[2,16,32,512]{3,2,1,0:T(8,128)(2,1)}, bf16[2,16,32,512]{3,2,1,0:T(8,128)(2,1)}, u32[]{:S(2)}, u32[]{:S(2)}) collective-permute-start(bf16[2,16,32,512]{3,2,1,0:T(8,128)(2,1)} %get-tuple-element.13), channel_id=1, source_target_pairs={{0,1},{1,0},{2,3},{3,2},{4,5},{5,4},{6,7},{7,6},{8,9},{9,8},{10,11... | collective-permute-start | bytes 3145736 | tf_op jit(solution)/shard_map/ppermute | solution.py:46
  182.9 2.5 %copy-start.3 = (bf16[1024,448]{1,0:T(8,128)(2,1)}, bf16[1024,448]{1,0:T(8,128)(2,1)S(1)}, u32[]{:S(2)}) copy-start(bf16[1024,448]{1,0:T(8,128)(2,1)S(1)} %get-tuple-element.8) | copy-start | bytes 2752516
  182.9 2.5 %copy-start.7 = (bf16[512,448]{0,1:T(8,128)(2,1)S(1)}, bf16[512,448]{0,1:T(8,128)(2,1)}, u32[]{:S(2)}) copy-start(bf16[512,448]{0,1:T(8,128)(2,1)} %param.12) | copy-start | bytes 1376260
  186.8 1.3 copy-start.1
  189.0 5.3 %collective-permute-start.1 = (bf16[16,32,512]{2,1,0:T(8,128)(2,1)}, bf16[16,32,512]{2,1,0:T(8,128)(2,1)}, u32[]{:S(2)}, u32[]{:S(2)}) collective-permute-start(bf16[16,32,512]{2,1,0:T(8,128)(2,1)} %fusion.26), channel_id=1, source_target_pairs={{0,1},{1,0},{2,3},{3,2},{4,5},{5,4},{6,7},{7,6},{8,9},{9,8},{10,11... | collective-permute-start | bytes 1572872 | tf_op jit(solution)/shard_map/ppermute | solution.py:46
  192.9 2.3 %copy-start.2 = (f32[1024,512]{1,0:T(8,128)S(1)}, f32[1024,512]{1,0:T(8,128)}, u32[]{:S(2)}) copy-start(f32[1024,512]{1,0:T(8,128)} %copy-done.1) | copy-start | bytes 6291460
  194.4 9.5 %copy-start = (bf16[1024,896]{1,0:T(8,128)(2,1)S(1)}, bf16[1024,896]{1,0:T(8,128)(2,1)}, u32[]{:S(2)}) copy-start(bf16[1024,896]{1,0:T(8,128)(2,1)} %all-gather.2.cloned.1.call-done) | copy-start | bytes 5505028
  197.2 22.6 %all-to-all-start.5 = ((bf16[16,32,512]{2,1,0:T(8,128)(2,1)}), bf16[16,32,512]{2,1,0:T(8,128)(2,1)S(1)}, u32[]{:S(2)}, u32[]{:S(2)}) async-start(bf16[16,32,512]{2,1,0:T(8,128)(2,1)} %fusion.12), calls=%async_computation.5 | async-start | bytes 1048576 | tf_op jit(solution)/shard_map/all_to_all | solution.py:100
  203.8 3.4 %copy-start.4 = (bf16[1024,448]{1,0:T(8,128)(2,1)S(1)}, bf16[1024,448]{1,0:T(8,128)(2,1)}, u32[]{:S(2)}) copy-start(bf16[1024,448]{1,0:T(8,128)(2,1)} %copy-done.3) | copy-start | bytes 2752516
  203.8 3.4 %copy-start.5 = (bf16[1,16,2,32,512]{4,3,2,1,0:T(8,128)(2,1)S(1)}, bf16[1,16,2,32,512]{4,3,2,1,0:T(8,128)(2,1)}, u32[]{:S(2)}) copy-start(bf16[1,16,2,32,512]{4,3,2,1,0:T(8,128)(2,1)} %get-tuple-element.11) | copy-start | bytes 3145732
Sparse Core Ops, SparseCore 0:
  85.1 94.5 all-gather.1

commit v2 on v1

v2 whole, which is shorter than its diff:
```python
import jax
import jax.numpy as jnp
from jax import lax
from jax.experimental import pallas as pl
from jax.experimental.pallas import tpu as pltpu
from jax.sharding import Mesh, PartitionSpec as P

EMBED_SIZE = 8192
GATE_INNER_SIZE = 14336
N_ROW = 16
N_CHIP = 16
ROW = ("xh", "z")
CHIP = ("xl", "y")
EXTRA = 16
LANES = 128
VMEM = pl.BlockSpec(memory_space=pltpu.VMEM)
PARAMS = pltpu.CompilerParams(vmem_limit_bytes=40 * 1024 * 1024)


def cost(flops, bytes_accessed):
    return pl.CostEstimate(flops=flops, bytes_accessed=bytes_accessed, transcendentals=0)


def contract_last(left, right):
    return lax.dot_general(
        left, right, (((1,), (1,)), ((), ())), preferred_element_type=jnp.float32
    )


def contract_first(left, right):
    return lax.dot_general(
        left, right, (((0,), (0,)), ((), ())), preferred_element_type=jnp.float32
    )


def matmul(left, right):
    return lax.dot_general(
        left, right, (((1,), (0,)), ((), ())), preferred_element_type=jnp.float32
    )


def swiglu_grads(grad_hidden, gate_pre, up_pre):
    gate_f = gate_pre.astype(jnp.float32)
    up_f = up_pre.astype(jnp.float32)
    sigma = jax.nn.sigmoid(gate_f)
    silu_gate = gate_f * sigma
    grad_gpre = (grad_hidden * up_f * sigma * (1.0 + gate_f * (1.0 - sigma))).astype(jnp.bfloat16)
    grad_upre = (grad_hidden * silu_gate).astype(jnp.bfloat16)
    hidden = (silu_gate * up_f).astype(jnp.bfloat16)
    return (grad_gpre, grad_upre, hidden)


def swapped(values):
    return lax.ppermute(values, "core", [(0, 1), (1, 0)])


def payload_kernel(out_ref, tokens_ref, gate_ref, up_ref, down_ref, pre_ref, sent_ref):
    rows, width = out_ref.shape
    pieces = []
    for ref in (gate_ref, up_ref, down_ref):
        total = jnp.sum(jnp.abs(ref[...].astype(jnp.float32)), axis=0, keepdims=True)
        total = jnp.broadcast_to(jnp.sum(total, axis=1, keepdims=True), (1, width))
        for _ in range(3):
            piece = total.astype(jnp.bfloat16).astype(jnp.float32)
            pieces.append(piece)
            total = total - piece
    pieces.append(jnp.zeros((EXTRA - len(pieces), width), jnp.float32))
    extra = jnp.concatenate(pieces, axis=0).astype(jnp.bfloat16)
    out_rows = out_ref[...]
    token_rows = tokens_ref[...]
    for k in range(N_CHIP):
        sent_ref[k, 0:rows, :] = out_rows
        sent_ref[k, rows : 2 * rows, :] = token_rows
        sent_ref[k, 2 * rows :, :] = extra


def payload(grad_out, tokens, gate_t, up_t, down, pre_rows):
    rows, width = grad_out.shape
    return pl.pallas_call(
        payload_kernel,
        out_shape=jax.ShapeDtypeStruct((N_CHIP, 2 * rows + EXTRA, width), jnp.bfloat16),
        in_specs=[VMEM] * 5 + [pl.BlockSpec(memory_space=pl.ANY)],
        out_specs=VMEM,
        compiler_params=PARAMS,
        cost_estimate=cost(1 << 20, 3 << 20),
    )(grad_out, tokens, gate_t, up_t, down, pre_rows)


def tile_kernel(extra_ref, tile_ref):
    total = jnp.sum(extra_ref[...].astype(jnp.float32), axis=0)
    sums = [jnp.sum(total[3 * k : 3 * k + 3], axis=0, keepdims=True) for k in range(3)]
    tile = jnp.concatenate(sums + [jnp.zeros((5, LANES), jnp.float32)], axis=0)
    tile_ref[...] = jnp.broadcast_to(tile[None], tile_ref.shape)


def sums_tile(received):
    rows = received.shape[1] - EXTRA
    return pl.pallas_call(
        tile_kernel,
        grid=(1,),
        out_shape=jax.ShapeDtypeStruct((2 * N_ROW, 8, LANES), jnp.float32),
        in_specs=[pl.BlockSpec((N_CHIP, EXTRA, LANES), lambda i: (0, rows // EXTRA, 0))],
        out_specs=pl.BlockSpec((2 * N_ROW, 8, LANES), lambda i: (0, 0, 0)),
        compiler_params=PARAMS,
        cost_estimate=cost(1 << 16, 1 << 18),
    )(received)


def scale_of(tile_ref, which):
    total = jnp.sum(tile_ref[...], axis=0)[which : which + 1, 0:1]
    return total / float(EMBED_SIZE * GATE_INNER_SIZE) + 1e-05


def clipped(values, scale):
    return jnp.clip(values.astype(jnp.float32), -scale, scale).astype(jnp.bfloat16)


def partial_kernel(tile_ref, received_ref, down_ref, other_ref, partial_ref, halves_ref, quant_ref):
    rows = partial_ref.shape[1]
    inner, width = down_ref.shape

    @pl.when(pl.program_id(0) == 0)
    def _():
        scale = scale_of(tile_ref, 2)
        quant_ref[0:inner, :] = clipped(down_ref[...], scale)
        quant_ref[inner:, :] = clipped(other_ref[...], scale)

    out_rows = received_ref[:, 0:rows, :].reshape((-1, width))
    halves_ref[0] = out_rows
    halves_ref[1] = received_ref[:, rows : 2 * rows, :].reshape((-1, width))
    partial = contract_last(out_rows, quant_ref[...])
    partial_ref[...] = partial.astype(jnp.bfloat16).reshape(partial_ref.shape)


def hidden_partial(tile, received, down, other):
    blocks, steps = 4, N_CHIP // 4
    rows = (received.shape[1] - EXTRA) // 2
    inner, width = down.shape
    whole = pl.BlockSpec((inner, width), lambda i: (0, 0))
    return pl.pallas_call(
        partial_kernel,
        grid=(steps,),
        out_shape=(
            jax.ShapeDtypeStruct((N_ROW, rows, 2 * inner), jnp.bfloat16),
            jax.ShapeDtypeStruct((2, N_CHIP * rows, width), jnp.bfloat16),
        ),
        in_specs=[
            pl.BlockSpec(tile.shape, lambda i: (0, 0, 0)),
            pl.BlockSpec((blocks, 2 * rows + EXTRA, width), lambda i: (i, 0, 0)),
            whole,
            whole,
        ],
        out_specs=(
            pl.BlockSpec((blocks, rows, 2 * inner), lambda i: (i, 0, 0)),
            pl.BlockSpec((2, blocks * rows, width), lambda i: (0, i, 0)),
        ),
        scratch_shapes=[pltpu.VMEM((2 * inner, width), jnp.bfloat16)],
        compiler_params=PARAMS,
        cost_estimate=cost(2 * 512 * 896 * 512, 4 << 20),
    )(tile, received, down, other)


def spread_kernel(parts_ref, sent_ref):
    total = jnp.sum(parts_ref[...].astype(jnp.float32), axis=0).astype(jnp.bfloat16)
    for k in range(N_ROW):
        sent_ref[k] = total


def spread(parts):
    return pl.pallas_call(
        spread_kernel,
        out_shape=jax.ShapeDtypeStruct(parts.shape, jnp.bfloat16),
        in_specs=[VMEM],
        out_specs=VMEM,
        compiler_params=PARAMS,
        cost_estimate=cost(1 << 19, 2 << 20),
    )(parts)


def act_kernel(tile_ref, hid_ref, pre_ref, gate_ref, up_ref, other_ref, partial_ref, own_ref, sent_ref, quant_ref):
    inner, width = gate_ref.shape

    @pl.when(pl.program_id(0) == 0)
    def _():
        for n, ref in enumerate((gate_ref, up_ref)):
            scale = scale_of(tile_ref, n)
            quant_ref[n, 0:inner, :] = clipped(ref[...], scale)
            quant_ref[n, inner:, :] = clipped(other_ref[n], scale)

    grad_hidden = hid_ref[...].reshape((-1, 2 * inner)).astype(jnp.float32)
    acts = swiglu_grads(grad_hidden, pre_ref[:, : 2 * inner], pre_ref[:, 2 * inner :])
    partial = matmul(acts[0], quant_ref[0]) + matmul(acts[1], quant_ref[1])
    partial_ref[...] = partial.astype(jnp.bfloat16).reshape(partial_ref.shape)
    for n, act in enumerate(acts):
        own_ref[n] = act[:, :inner]
        sent_ref[n] = act[:, inner:]


def act_partial(tile, grad_hidden, pre_half, gate_t, up_t, other):
    blocks, steps = 4, N_ROW // 4
    rows = grad_hidden.shape[1]
    inner, width = gate_t.shape
    whole = pl.BlockSpec((inner, width), lambda i: (0, 0))
    halves = jax.ShapeDtypeStruct((3, N_ROW * rows, inner), jnp.bfloat16)
    half = pl.BlockSpec((3, blocks * rows, inner), lambda i: (0, i, 0))
    return pl.pallas_call(
        act_kernel,
        grid=(steps,),
        out_shape=(jax.ShapeDtypeStruct((N_CHIP, rows, width), jnp.bfloat16), halves, halves),
        in_specs=[
            pl.BlockSpec(tile.shape, lambda i: (0, 0, 0)),
            pl.BlockSpec((blocks, rows, 2 * inner), lambda i: (i, 0, 0)),
            pl.BlockSpec((blocks * rows, 4 * inner), lambda i: (i, 0)),
            whole,
            whole,
            pl.BlockSpec(other.shape, lambda i: (0, 0, 0)),
        ],
        out_specs=(pl.BlockSpec((blocks, rows, width), lambda i: (i, 0, 0)), half, half),
        scratch_shapes=[pltpu.VMEM((2, 2 * inner, width), jnp.bfloat16)],
        compiler_params=PARAMS,
        cost_estimate=cost(4 * 512 * 896 * 512, 9 << 20),
    )(tile, grad_hidden, pre_half, gate_t, up_t, other)


def shards(tokens, grad_out, gate_pre, up_pre, gate_latent, up_latent, down_latent):
    core = lax.axis_index("core")
    rows = tokens.shape[0]
    inner = gate_pre.shape[1]

    pre = jnp.concatenate([gate_pre, up_pre], axis=1).reshape((2, rows, 2 * inner))
    pre_own = lax.dynamic_index_in_dim(pre, core, 0, keepdims=False)
    pre_other = swapped(lax.dynamic_index_in_dim(pre, 1 - core, 0, keepdims=False))
    pre_rows = jnp.concatenate(
        [pre_own[:, :inner], pre_other[:, :inner], pre_own[:, inner:], pre_other[:, inner:]], axis=1
    )
    pre_half = lax.all_gather(pre_rows, ROW, axis=0, tiled=True)

    gate_t, up_t = gate_latent.T, up_latent.T
    sent = payload(grad_out, tokens, gate_t, up_t, down_latent, pre_rows)
    received = lax.all_to_all(sent, CHIP, 0, 0)
    down_other = swapped(down_latent)
    tile = lax.all_to_all(sums_tile(received), ROW + ("core",), 0, 0)

    partial, halves = hidden_partial(tile, received, down_latent, down_other)
    parts = lax.all_to_all(partial, ROW, 0, 0)
    gate_s, up_s, halves = lax.optimization_barrier((gate_t, up_t, halves))
    other_halves = swapped(halves)
    other_latents = swapped(jnp.stack([gate_s, up_s]))
    grad_hidden = lax.all_to_all(spread(parts), ROW, 0, 0)

    partial, own, sent = act_partial(tile, grad_hidden, pre_half, gate_t, up_t, other_latents)
    parts = lax.all_to_all(partial, CHIP, 0, 0)
    other = swapped(sent)

    def over_tokens(act, half):
        return (
            contract_first(own[act], halves[half]) + contract_first(other[act], other_halves[half])
        ).astype(jnp.bfloat16)

    grad_gate = over_tokens(0, 1).T
    grad_up = over_tokens(1, 1).T
    grad_down = over_tokens(2, 0)
    grad_tokens = jnp.sum(parts.astype(jnp.float32), axis=0).astype(jnp.bfloat16)
    return (grad_tokens, grad_gate, grad_up, grad_down)


def solution(mesh):
    fine = Mesh(mesh.devices.reshape((2, 8, 2, 8, 2)), ROW + CHIP + ("core",))
    col = CHIP + ("core",)
    in_specs = (
        P(col, ROW),
        P(col, ROW),
        P(ROW, col),
        P(ROW, col),
        P(ROW, col),
        P(ROW, col),
        P(col, ROW),
    )
    out_specs = (P(col, ROW), P(ROW, col), P(ROW, col), P(col, ROW))
    return jax.shard_map(shards, mesh=fine, in_specs=in_specs, out_specs=out_specs, check_vma=False)
```

time: 228 us -> 245 us (1.075)
  the two profiles are of different devices: /device:TPU:8 before, /device:TPU:10 now
where the time goes in v2:
time: 245 us; the launch traced here: 243 us
  waiting for transfers between devices  131 us (53%)
  starting transfers between devices  40.2 us (16%)
  blocking collectives  23.6 us (10%)
  between operations  14.2 us (6%)
  local copies, waits for them, and re-layouts  12.3 us (5%)
  Pallas kernels  9.83 us (4%)
  matrix products  8.39 us (3%)
  other arithmetic  3.83 us (2%)
    all_gather x1, waiting for transfers between devices, shards(): pre_half = lax.all_gather(pre_rows, ROW, axis=0, tiled=True)  63.7 us
    all_to_all x1, waiting for transfers between devices, shards(): received = lax.all_to_all(sent, CHIP, 0, 0)  30.2 us
    all_to_all x1, blocking collectives, shards(): parts = lax.all_to_all(partial, CHIP, 0, 0)  23.6 us
    all_to_all x1, waiting for transfers between devices, shards(): parts = lax.all_to_all(partial, ROW, 0, 0)  23.4 us
    all_to_all x1, waiting for transfers between devices, shards(): tile = lax.all_to_all(sums_tile(received), ROW + ('core',), 0, 0)  11.9 us
    all_to_all x1, starting transfers between devices, shards(): tile = lax.all_to_all(sums_tile(received), ROW + ('core',), 0, 0)  11.4 us
    ppermute x5, starting transfers between devices, swapped(): return lax.ppermute(values, 'core', [(0, 1), (1, 0)])  10.1 us
    all_to_all x1, starting transfers between devices, shards(): received = lax.all_to_all(sent, CHIP, 0, 0)  9.47 us
  transfers between devices with their start and end apart: 10, of which 5 were waited for; matrix products, arithmetic and copies ran while one was open for 1% of the time, Pallas kernels for 1%

profile of v2, /device:TPU:10, one launch (start us, length us, event | category | flops | bytes accessed | tf_op | source)
XLA Modules:
  0.0 243.4 jit_solution(10669492172867815659)
XLA Ops:
  7.2 1.0 pad_maximum_fusion.1
  8.2 1.9 collective-permute-start
  10.1 0.1 fusion.19
  10.2 1.1 collective-permute-done
  11.3 0.1 fusion.18
  11.4 0.1 concatenate.7.pre_ref
  11.5 0.0 copy-start.10
  11.5 0.0 copy-start
  11.5 1.1 copy-done
  12.6 1.0 copy-done.2
  13.6 0.0 copy-start.5
  13.6 1.0 copy-done.5
  14.6 0.0 copy-start.12
  14.6 0.8 copy-done.12
  15.4 0.0 copy-start.13
  15.4 0.8 copy-done.13
  16.1 1.5 shard_map.102
  17.6 0.0 copy-done.10
  17.6 0.0 copy-start.6
  17.6 9.5 %all-to-all-start = ((bf16[16,80,512]{2,1,0:T(8,128)(2,1)}), bf16[16,80,512]{2,1,0:T(8,128)(2,1)S(1)}, u32[]{:S(2)}, u32[]{:S(2)}) async-start(bf16[16,80,512]{2,1,0:T(8,128)(2,1)} %shard_map.102), calls=%async_computation | async-start | bytes 2621440 | tf_op jit(solution)/shard_map/all_to_all | solution.py:240
  27.1 0.0 copy-done.6
  27.1 1.9 collective-permute-start.1
  29.0 30.2 %all-to-all-done.extra_ref.received_ref = bf16[16,80,512]{2,1,0:T(8,128)(2,1)S(1)} async-done(((bf16[16,80,512]{2,1,0:T(8,128)(2,1)}), bf16[16,80,512]{2,1,0:T(8,128)(2,1)S(1)}, u32[]{:S(2)}, u32[]{:S(2)}) %all-to-all-start) | async-done | bytes 1310752 | tf_op jit(solution)/shard_map/all_to_all | solution.py:240
  59.2 0.7 shard_map.103
  59.9 11.4 %all-to-all-start.1 = ((f32[32,8,128]{2,1,0:T(8,128)}), f32[32,8,128]{2,1,0:T(8,128)S(1)}, u32[]{:S(2)}, u32[]{:S(2)}) async-start(f32[32,8,128]{2,1,0:T(8,128)} %shard_map.103), calls=%async_computation.1 | async-start | bytes 262144 | tf_op jit(solution)/shard_map/all_to_all | solution.py:242
  71.3 0.0 collective-permute-done.1.other_ref
  71.3 11.9 %all-to-all-done.1.tile_ref = f32[32,8,128]{2,1,0:T(8,128)S(1)} async-done(((f32[32,8,128]{2,1,0:T(8,128)}), f32[32,8,128]{2,1,0:T(8,128)S(1)}, u32[]{:S(2)}, u32[]{:S(2)}) %all-to-all-start.1) | async-done | bytes 131104 | tf_op jit(solution)/shard_map/all_to_all | solution.py:242
  83.3 2.3 shard_map.104
  85.6 0.0 copy-start.11
  85.6 0.9 copy-done.11
  86.5 3.6 %all-to-all-start.2 = ((bf16[16,32,896]{2,1,0:T(8,128)(2,1)}), bf16[16,32,896]{2,1,0:T(8,128)(2,1)S(1)}, u32[]{:S(2)}, u32[]{:S(2)}) async-start(bf16[16,32,896]{2,1,0:T(8,128)(2,1)} %copy-done.11), calls=%async_computation.2 | async-start | bytes 1835008 | tf_op jit(solution)/shard_map/all_to_all | solution.py:245
  90.2 0.0 all-gather.2.cloned.1.call-start
  90.2 0.7 all-gather.2.cloned.1.call-update
  90.9 23.4 %all-to-all-done.2.parts_ref = bf16[16,32,896]{2,1,0:T(8,128)(2,1)S(1)} async-done(((bf16[16,32,896]{2,1,0:T(8,128)(2,1)}), bf16[16,32,896]{2,1,0:T(8,128)(2,1)S(1)}, u32[]{:S(2)}, u32[]{:S(2)}) %all-to-all-start.2) | async-done | bytes 917536 | tf_op jit(solution)/shard_map/all_to_all | solution.py:245
  114.3 1.1 shard_map.105
  115.4 0.0 copy-start.1
  115.4 0.0 copy-start.3
  115.4 5.6 %all-to-all-start.3 = ((bf16[16,32,896]{2,1,0:T(8,128)(2,1)}), bf16[16,32,896]{2,1,0:T(8,128)(2,1)S(1)}, u32[]{:S(2)}, u32[]{:S(2)}) async-start(bf16[16,32,896]{2,1,0:T(8,128)(2,1)} %shard_map.105), calls=%async_computation.3 | async-start | bytes 1835008 | tf_op jit(solution)/shard_map/all_to_all | solution.py:249
  121.0 0.0 copy-done.1
  121.0 0.0 copy-done.3
  121.0 1.0 pad_maximum_fusion
  122.0 1.9 collective-permute-start.2
  123.9 63.7 %all-gather.2.cloned.1.call-done.pre_ref = bf16[512,1792]{1,0:T(8,128)(2,1)} async-done(((bf16[32,1792]{1,0:T(8,128)(2,1)}), bf16[512,1792]{1,0:T(8,128)(2,1)}) %all-gather.2.cloned.1.call-update) | async-done | bytes 1835024 | tf_op jit(solution)/shard_map/all_gather | solution.py:236
  187.6 0.0 collective-permute-done.2.other_ref
  187.6 0.0 all-to-all-done.3.hid_ref
  187.6 1.5 copy-done.4
  189.1 4.3 %shard_map.106 = (bf16[16,32,512]{2,1,0:T(8,128)(2,1)S(1)}, bf16[3,512,448]{2,1,0:T(8,128)(2,1)S(1)}, bf16[3,512,448]{2,1,0:T(8,128)(2,1)S(1)}) custom-call(f32[32,8,128]{2,1,0:T(8,128)S(1)} %all-to-all-done.1.tile_ref, bf16[16,32,896]{2,1,0:T(8,128)(2,1)S(1)} %all-to-all-done.3.hid_ref, bf16[512,1792]{1,0:T(8,128)(2,1)S(1)} %copy-done.4, ...), custom_call_target="tpu_custom_call" | custom-call | flops 939524096 | bytes 9437184 | tf_op jit(solution)/shard_map/pallas_call | solution.py:206
  193.4 0.0 copy-start.7
  193.4 1.2 copy-done.7
  194.6 1.2 copy-done.9
  195.7 2.6 %copy.11 = bf16[3,512,448]{1,2,0:T(8,128)(2,1)} copy(bf16[3,512,448]{2,1,0:T(8,128)(2,1)} %copy-done.9) | data formatting | bytes 2752512 | tf_op jit(solution)/shard_map/pallas_call | solution.py:206
  198.4 1.9 collective-permute-start.4
  200.3 2.4 collective-permute-start.3
  202.7 23.6 %all_to_all.25 = bf16[16,32,512]{2,1,0:T(8,128)(2,1)} all-to-all(bf16[16,32,512]{2,1,0:T(8,128)(2,1)S(1)} %get-tuple-element.16), channel_id=1, replica_groups=mesh['xh'=2,'z'=8,'xl'=2,'y'=8,'core'=2] {'xl','y'}, dimensions={0} | all-to-all | bytes 1048576 | tf_op jit(solution)/shard_map/all_to_all | solution.py:252
  226.3 1.9 reduce_sum.12
  228.2 0.0 collective-permute-done.3
  228.2 0.0 collective-permute-done.4
  228.2 1.6 fusion.3
  229.8 0.0 copy-done.8
  229.8 1.2 fusion.2
  231.0 1.6 fusion.14
  232.6 1.2 fusion
  233.8 1.6 fusion.15
  235.4 1.2 fusion.1
  (5 shorter events, 0.0 us)
Async XLA Ops:
  8.2 3.1 %collective-permute-start = (bf16[32,896]{1,0:T(8,128)(2,1)S(1)}, bf16[32,896]{1,0:T(8,128)(2,1)S(1)}, u32[]{:S(2)}, u32[]{:S(2)}) collective-permute-start(bf16[32,896]{1,0:T(8,128)(2,1)S(1)} %get-tuple-element.20), channel_id=1, source_target_pairs={{0,1},{1,0},{2,3},{3,2},{4,5},{5,4},{6,7},{7,6},{8,9},{9,8},{10,11... | collective-permute-start | bytes 172040 | tf_op jit(solution)/shard_map/ppermute | solution.py:54
  11.5 6.1 %copy-start.10 = (bf16[32,1792]{1,0:T(8,128)(2,1)}, bf16[32,1792]{1,0:T(8,128)(2,1)S(1)}, u32[]{:S(2)}) copy-start(bf16[32,1792]{1,0:T(8,128)(2,1)S(1)} %concatenate.7.pre_ref) | copy-start | bytes 344068
  11.5 1.1 copy-start
  12.6 1.0 copy-start.2
  13.6 1.0 copy-start.5
  14.6 0.8 copy-start.12
  15.4 0.8 copy-start.13
  17.6 9.5 %copy-start.6 = (bf16[448,512]{1,0:T(8,128)(2,1)S(1)}, bf16[448,512]{1,0:T(8,128)(2,1)}, u32[]{:S(2)}) copy-start(bf16[448,512]{1,0:T(8,128)(2,1)} %down_ref.3) | copy-start | bytes 1376260
  17.6 41.6 %all-to-all-start = ((bf16[16,80,512]{2,1,0:T(8,128)(2,1)}), bf16[16,80,512]{2,1,0:T(8,128)(2,1)S(1)}, u32[]{:S(2)}, u32[]{:S(2)}) async-start(bf16[16,80,512]{2,1,0:T(8,128)(2,1)} %shard_map.102), calls=%async_computation | async-start | bytes 2621440 | tf_op jit(solution)/shard_map/all_to_all | solution.py:240
  27.1 44.2 %collective-permute-start.1 = (bf16[448,512]{1,0:T(8,128)(2,1)S(1)}, bf16[448,512]{1,0:T(8,128)(2,1)S(1)}, u32[]{:S(2)}, u32[]{:S(2)}) collective-permute-start(bf16[448,512]{1,0:T(8,128)(2,1)S(1)} %copy-done.6), channel_id=1, source_target_pairs={{0,1},{1,0},{2,3},{3,2},{4,5},{5,4},{6,7},{7,6},{8,9},{9,8},{10,11... | collective-permute-start | bytes 1376264 | tf_op jit(solution)/shard_map/ppermute | solution.py:54
  59.9 23.4 %all-to-all-start.1 = ((f32[32,8,128]{2,1,0:T(8,128)}), f32[32,8,128]{2,1,0:T(8,128)S(1)}, u32[]{:S(2)}, u32[]{:S(2)}) async-start(f32[32,8,128]{2,1,0:T(8,128)} %shard_map.103), calls=%async_computation.1 | async-start | bytes 262144 | tf_op jit(solution)/shard_map/all_to_all | solution.py:242
  85.6 0.9 copy-start.11
  86.5 27.8 %all-to-all-start.2 = ((bf16[16,32,896]{2,1,0:T(8,128)(2,1)}), bf16[16,32,896]{2,1,0:T(8,128)(2,1)S(1)}, u32[]{:S(2)}, u32[]{:S(2)}) async-start(bf16[16,32,896]{2,1,0:T(8,128)(2,1)} %copy-done.11), calls=%async_computation.2 | async-start | bytes 1835008 | tf_op jit(solution)/shard_map/all_to_all | solution.py:245
  90.2 97.4 %all-gather.2.cloned.1.call-start = ((), (), s32[]{:S(2)}) async-start(), calls=%async_computation.5 | async-start | bytes 1949696 | tf_op jit(solution)/shard_map/all_gather | solution.py:236
  115.4 5.6 %copy-start.1 = (bf16[512,448]{0,1:T(8,128)(2,1)S(1)}, bf16[512,448]{0,1:T(8,128)(2,1)}, u32[]{:S(2)}) copy-start(bf16[512,448]{0,1:T(8,128)(2,1)} %param.11) | copy-start | bytes 1376260
  115.4 5.6 %copy-start.3 = (bf16[512,448]{0,1:T(8,128)(2,1)S(1)}, bf16[512,448]{0,1:T(8,128)(2,1)}, u32[]{:S(2)}) copy-start(bf16[512,448]{0,1:T(8,128)(2,1)} %param.12) | copy-start | bytes 1376260
  115.4 72.2 %all-to-all-start.3 = ((bf16[16,32,896]{2,1,0:T(8,128)(2,1)}), bf16[16,32,896]{2,1,0:T(8,128)(2,1)S(1)}, u32[]{:S(2)}, u32[]{:S(2)}) async-start(bf16[16,32,896]{2,1,0:T(8,128)(2,1)} %shard_map.105), calls=%async_computation.3 | async-start | bytes 1835008 | tf_op jit(solution)/shard_map/all_to_all | solution.py:249
  122.0 65.6 %collective-permute-start.2 = (bf16[2,448,512]{2,1,0:T(8,128)(2,1)}, bf16[2,448,512]{2,1,0:T(8,128)(2,1)}, u32[]{:S(2)}, u32[]{:S(2)}) collective-permute-start(bf16[2,448,512]{2,1,0:T(8,128)(2,1)} %pad_maximum_fusion), channel_id=1, source_target_pairs={{0,1},{1,0},{2,3},{3,2},{4,5},{5,4},{6,7},{7,6},{8,9},{9,8},{10,11... | collective-permute-start | bytes 2752520 | tf_op jit(solution)/shard_map/ppermute | solution.py:54
  187.6 1.5 copy-start.4
  193.4 1.2 copy-start.7
  194.6 1.2 copy-start.9
  198.4 29.8 %collective-permute-start.4 = (bf16[3,512,448]{1,2,0:T(8,128)(2,1)}, bf16[3,512,448]{1,2,0:T(8,128)(2,1)}, u32[]{:S(2)}, u32[]{:S(2)}) collective-permute-start(bf16[3,512,448]{1,2,0:T(8,128)(2,1)} %copy.11), channel_id=1, source_target_pairs={{0,1},{1,0},{2,3},{3,2},{4,5},{5,4},{6,7},{7,6},{8,9},{9,8},{10,11... | collective-permute-start | bytes 4128776 | tf_op jit(solution)/shard_map/ppermute | solution.py:54
  200.3 27.9 %collective-permute-start.3 = (bf16[2,512,512]{2,1,0:T(8,128)(2,1)S(1)}, bf16[2,512,512]{2,1,0:T(8,128)(2,1)}, u32[]{:S(2)}, u32[]{:S(2)}) collective-permute-start(bf16[2,512,512]{2,1,0:T(8,128)(2,1)S(1)} %get-tuple-element.17), channel_id=1, source_target_pairs={{0,1},{1,0},{2,3},{3,2},{4,5},{5,4},{6,7},{7,6},{8,9},{9,8},{10,11... | collective-permute-start | bytes 3145736 | tf_op jit(solution)/shard_map/ppermute | solution.py:54
  226.3 3.5 %copy-start.8 = (bf16[3,512,448]{2,1,0:T(8,128)(2,1)S(1)}, bf16[3,512,448]{2,1,0:T(8,128)(2,1)}, u32[]{:S(2)}) copy-start(bf16[3,512,448]{2,1,0:T(8,128)(2,1)} %copy-done.7) | copy-start | bytes 4128772
Sparse Core Ops, SparseCore 0:
  94.8 92.7 all-gather.1

commit v3 on v2

--- a/solution.py
+++ b/solution.py
@@ -14,6 +14,7 @@
 EXTRA = 16
 LANES = 128
 VMEM = pl.BlockSpec(memory_space=pltpu.VMEM)
+ANY = pl.BlockSpec(memory_space=pl.ANY)
 PARAMS = pltpu.CompilerParams(vmem_limit_bytes=40 * 1024 * 1024)
 
 
@@ -54,7 +55,7 @@
     return lax.ppermute(values, "core", [(0, 1), (1, 0)])
 
 
-def payload_kernel(out_ref, tokens_ref, gate_ref, up_ref, down_ref, pre_ref, sent_ref):
+def payload_kernel(out_ref, tokens_ref, gate_ref, up_ref, down_ref, sent_ref):
     rows, width = out_ref.shape
     pieces = []
     for ref in (gate_ref, up_ref, down_ref):
@@ -74,16 +75,16 @@
         sent_ref[k, 2 * rows :, :] = extra
 
 
-def payload(grad_out, tokens, gate_t, up_t, down, pre_rows):
+def payload(grad_out, tokens, gate_t, up_t, down):
     rows, width = grad_out.shape
     return pl.pallas_call(
         payload_kernel,
         out_shape=jax.ShapeDtypeStruct((N_CHIP, 2 * rows + EXTRA, width), jnp.bfloat16),
-        in_specs=[VMEM] * 5 + [pl.BlockSpec(memory_space=pl.ANY)],
+        in_specs=[VMEM] * 5,
         out_specs=VMEM,
         compiler_params=PARAMS,
         cost_estimate=cost(1 << 20, 3 << 20),
-    )(grad_out, tokens, gate_t, up_t, down, pre_rows)
+    )(grad_out, tokens, gate_t, up_t, down)
 
 
 def tile_kernel(extra_ref, tile_ref):
@@ -192,8 +193,8 @@
     partial = matmul(acts[0], quant_ref[0]) + matmul(acts[1], quant_ref[1])
     partial_ref[...] = partial.astype(jnp.bfloat16).reshape(partial_ref.shape)
     for n, act in enumerate(acts):
-        own_ref[n] = act[:, :inner]
-        sent_ref[n] = act[:, inner:]
+        own_ref[n] = act[:, : own_ref.shape[2]]
+        sent_ref[n] = act[:, 2 * inner - sent_ref.shape[2] :]
 
 
 def act_partial(tile, grad_hidden, pre_half, gate_t, up_t, other):
@@ -201,8 +202,9 @@
     rows = grad_hidden.shape[1]
     inner, width = gate_t.shape
     whole = pl.BlockSpec((inner, width), lambda i: (0, 0))
-    halves = jax.ShapeDtypeStruct((3, N_ROW * rows, inner), jnp.bfloat16)
-    half = pl.BlockSpec((3, blocks * rows, inner), lambda i: (0, i, 0))
+    lanes = -(-inner // LANES) * LANES
+    halves = jax.ShapeDtypeStruct((3, N_ROW * rows, lanes), jnp.bfloat16)
+    half = pl.BlockSpec((3, blocks * rows, lanes), lambda i: (0, i, 0))
     return pl.pallas_call(
         act_kernel,
         grid=(steps,),
@@ -222,9 +224,45 @@
     )(tile, grad_hidden, pre_half, gate_t, up_t, other)
 
 
+def latent_grads_kernel(own_ref, other_ref, halves_ref, other_halves_ref, *grad_refs):
+    for n, grad_ref in enumerate(grad_refs):
+        inner = grad_ref.shape[0]
+        half = 0 if n == 2 else 1
+        own = contract_first(own_ref[n], halves_ref[half])[:inner]
+        other = contract_first(other_ref[n], other_halves_ref[half])[-inner:]
+        grad_ref[...] = (own + other).astype(jnp.bfloat16)
+
+
+def latent_grads(own, other, halves, other_halves, inner):
+    grad = jax.ShapeDtypeStruct((inner, halves.shape[2]), jnp.bfloat16)
+    return pl.pallas_call(
+        latent_grads_kernel,
+        out_shape=(grad, grad, grad),
+        in_specs=[VMEM] * 4,
+        out_specs=(VMEM, VMEM, VMEM),
+        compiler_params=PARAMS,
+        cost_estimate=cost(6 * 1024 * 512 * 512, 6 << 20),
+    )(own, other, halves, other_halves)
+
+
+def total_kernel(parts_ref, after_ref, total_ref):
+    total_ref[...] = jnp.sum(parts_ref[...].astype(jnp.float32), axis=0).astype(jnp.bfloat16)
+
+
+def total(parts, after):
+    return pl.pallas_call(
+        total_kernel,
+        out_shape=jax.ShapeDtypeStruct(parts.shape[1:], jnp.bfloat16),
+        in_specs=[VMEM, ANY],
+        out_specs=VMEM,
+        compiler_params=PARAMS,
+        cost_estimate=cost(1 << 18, 1 << 19),
+    )(parts, after)
+
+
 def shards(tokens, grad_out, gate_pre, up_pre, gate_latent, up_latent, down_latent):
     core = lax.axis_index("core")
-    rows = tokens.shape[0]
+    rows, width = tokens.shape
     inner = gate_pre.shape[1]
 
     pre = jnp.concatenate([gate_pre, up_pre], axis=1).reshape((2, rows, 2 * inner))
@@ -236,32 +274,32 @@
     pre_half = lax.all_gather(pre_rows, ROW, axis=0, tiled=True)
 
     gate_t, up_t = gate_latent.T, up_latent.T
-    sent = payload(grad_out, tokens, gate_t, up_t, down_latent, pre_rows)
-    received = lax.all_to_all(sent, CHIP, 0, 0)
-    down_other = swapped(down_latent)
-    tile = lax.all_to_all(sums_tile(received), ROW + ("core",), 0, 0)
-
-    partial, halves = hidden_partial(tile, received, down_latent, down_other)
-    parts = lax.all_to_all(partial, ROW, 0, 0)
-    gate_s, up_s, halves = lax.optimization_barrier((gate_t, up_t, halves))
-    other_halves = swapped(halves)
-    other_latents = swapped(jnp.stack([gate_s, up_s]))
-    grad_hidden = lax.all_to_all(spread(parts), ROW, 0, 0)
+    sent = payload(grad_out, tokens, gate_t, up_t, down_latent)
+
+    def exchanges(sent, gate_t, up_t, down):
+        received = lax.all_to_all(sent, CHIP, 0, 0)
+        down_other = swapped(down)
+        tile = lax.all_to_all(sums_tile(received), ROW + ("core",), 0, 0)
+        partial, halves = hidden_partial(tile, received, down, down_other)
+        parts = lax.all_to_all(partial, ROW, 0, 0)
+        other_halves = swapped(halves)
+        other_latents = swapped(jnp.stack([gate_t, up_t]))
+        grad_hidden = lax.all_to_all(spread(parts), ROW, 0, 0)
+        return (tile, halves, other_halves, other_latents, grad_hidden)
+
+    def nothing(sent, gate_t, up_t, down):
+        shapes = jax.eval_shape(exchanges, sent, gate_t, up_t, down)
+        return tuple(jnp.zeros(leaf.shape, leaf.dtype) for leaf in shapes)
+
+    tile, halves, other_halves, other_latents, grad_hidden = lax.cond(
+        lax.axis_index("z") < 8, exchanges, nothing, sent, gate_t, up_t, down_latent
+    )
 
     partial, own, sent = act_partial(tile, grad_hidden, pre_half, gate_t, up_t, other_latents)
     parts = lax.all_to_all(partial, CHIP, 0, 0)
-    other = swapped(sent)
-
-    def over_tokens(act, half):
-        return (
-            contract_first(own[act], halves[half]) + contract_first(other[act], other_halves[half])
-        ).astype(jnp.bfloat16)
-
-    grad_gate = over_tokens(0, 1).T
-    grad_up = over_tokens(1, 1).T
-    grad_down = over_tokens(2, 0)
-    grad_tokens = jnp.sum(parts.astype(jnp.float32), axis=0).astype(jnp.bfloat16)
-    return (grad_tokens, grad_gate, grad_up, grad_down)
+    grad_gate, grad_up, grad_down = latent_grads(own, swapped(sent), halves, other_halves, inner)
+    grad_tokens = total(parts, grad_down)
+    return (grad_tokens, grad_gate.T, grad_up.T, grad_down)
 
 
 def solution(mesh):

time: 245 us -> 191 us (0.78)
  waiting for transfers between devices: 131 us -> 74.7 us
  Pallas kernels: 9.83 us -> 19.7 us
  blocking collectives: 23.6 us -> 32.6 us
  matrix products: 8.39 us -> 0 us
  local copies, waits for them, and re-layouts: 12.3 us -> 4.98 us
  other arithmetic: 3.83 us -> 1.1 us
  starting transfers between devices: 40.2 us -> 42.9 us
    all_gather x1, waiting for transfers between devices: 63.7 us -> 0.01 us  [shards(): pre_half = lax.all_gather(pre_rows, ROW, axis=0, tiled=True)]
    all_to_all x1, blocking collectives: 23.6 us -> 32.6 us  [exchanges(): parts = lax.all_to_all(partial, ROW, 0, 0)]
    dot_general x6 -> x0, matrix products: 8.39 us -> none  [contract_first(): lax.dot_general(left, right, (((0,), (0,)), ((), ())), preferred_element_...]
    all_to_all x4, waiting for transfers between devices: 65.6 us -> 71.3 us  [the longest x1 30.2 us: exchanges(): received = lax.all_to_all(sent, CHIP, 0, 0)]
    unnamed x28 -> x14, local copies, waits for them, and re-layouts: 9.39 us -> 4.04 us
    pallas_call x0 -> x2, Pallas kernels: none -> 5.3 us  [the longest x1 4.61 us: latent_grads(): pl.pallas_call(latent_grads_kernel, out_shape=(grad, grad, grad), in_spec...]
    all_to_all x4, starting transfers between devices: 30.1 us -> 32.8 us  [the longest x1 11.5 us: exchanges(): tile = lax.all_to_all(sums_tile(received), ROW + ('core',), 0, 0)]
    pallas_call x1 -> x0, local copies, waits for them, and re-layouts: 2.61 us -> none  [act_partial(): pl.pallas_call(act_kernel, grid=(steps,), out_shape=(jax.ShapeDtypeStruct...]
  transfers between devices with their start and end apart: 10 -> 10, of which waited for: 5 -> 6; matrix products, arithmetic and copies ran while one was open for 1% -> 0% of each run, Pallas kernels for 1% -> 7%
where the time goes in v3:
time: 191 us; the launch traced here: 190 us
  waiting for transfers between devices  74.7 us (39%)
  starting transfers between devices  42.9 us (22%)
  blocking collectives  32.6 us (17%)
  Pallas kernels  19.7 us (10%)
  between operations  14.1 us (7%)
  local copies, waits for them, and re-layouts  4.98 us (3%)
    all_to_all x1, blocking collectives, exchanges(): parts = lax.all_to_all(partial, ROW, 0, 0)  32.6 us
    all_to_all x1, waiting for transfers between devices, exchanges(): received = lax.all_to_all(sent, CHIP, 0, 0)  30.2 us
    all_to_all x1, waiting for transfers between devices, exchanges(): grad_hidden = lax.all_to_all(spread(parts), ROW, 0, 0)  17.7 us
    all_to_all x1, waiting for transfers between devices, exchanges(): tile = lax.all_to_all(sums_tile(received), ROW + ('core',), 0, 0)  11.9 us
    all_to_all x1, starting transfers between devices, exchanges(): tile = lax.all_to_all(sums_tile(received), ROW + ('core',), 0, 0)  11.5 us
    all_to_all x1, waiting for transfers between devices, shards(): parts = lax.all_to_all(partial, CHIP, 0, 0)  11.4 us
    ppermute x5, starting transfers between devices, swapped(): return lax.ppermute(values, 'core', [(0, 1), (1, 0)])  10.1 us
    all_to_all x1, starting transfers between devices, exchanges(): received = lax.all_to_all(sent, CHIP, 0, 0)  9.35 us
  transfers between devices with their start and end apart: 10, of which 6 were waited for; matrix products, arithmetic and copies ran while one was open for 0% of the time, Pallas kernels for 7%

profile of v3, /device:TPU:10, one launch (start us, length us, event | category | flops | bytes accessed | tf_op | source)
XLA Modules:
  0.0 190.2 jit_solution(11989566284596091701)
XLA Ops:
  7.2 0.0 all-gather.2.cloned.1.call-start
  7.2 0.0 copy-start.5
  7.2 1.0 pad_maximum_fusion.1
  8.3 1.9 %collective-permute-start.3 = (bf16[32,896]{1,0:T(8,128)(2,1)S(1)}, bf16[32,896]{1,0:T(8,128)(2,1)S(1)}, u32[]{:S(2)}, u32[]{:S(2)}) collective-permute-start(bf16[32,896]{1,0:T(8,128)(2,1)S(1)} %get-tuple-element.40), channel_id=1, source_target_pairs={{0,1},{1,0},{2,3},{3,2},{4,5},{5,4},{6,7},{7,6},{8,9},{9,8},{10,11... | collective-permute-start | bytes 172040 | tf_op jit(solution)/shard_map/ppermute | solution.py:55
  10.2 0.1 fusion.1
  10.3 1.1 collective-permute-done.3
  11.4 0.0 copy-start.4
  11.4 0.1 fusion
  11.5 0.8 concatenate.7
  12.2 0.0 all-gather.2.cloned.1.call-update
  12.3 0.0 copy-start.2
  12.3 0.7 copy-done.2
  13.0 0.0 copy-start.3
  13.0 0.8 copy-done.3
  13.8 0.0 copy-start.6
  13.8 2.8 %shard_map.102 = bf16[16,80,512]{2,1,0:T(8,128)(2,1)} custom-call(bf16[32,512]{1,0:T(8,128)(2,1)S(1)} %copy-done.2, bf16[32,512]{1,0:T(8,128)(2,1)S(1)} %copy-done.3, bf16[448,512]{1,0:T(8,128)(2,1)} %bitcast.11, bf16[448,512]{1,0:T(8,128)(2,1)} %bitcast.15, bf16[448,512]{1,0:T(8,128)(2,1)} %down_ref.1), custom_call_target="tpu_custom_call" | custom-call | flops 1048576 | bytes 3145728 | tf_op jit(solution)/shard_map/pallas_call | solution.py:80
  16.6 0.0 copy-done.5
  16.6 0.0 copy-done.4
  16.6 0.0 copy-done.6
  16.6 133.3 %conditional.1 = (f32[32,8,128]{2,1,0:T(8,128)}, bf16[2,512,512]{2,1,0:T(8,128)(2,1)}, bf16[2,512,512]{2,1,0:T(8,128)(2,1)}, bf16[2,448,512]{2,1,0:T(8,128)(2,1)}, bf16[16,32,896]{2,1,0:T(8,128)(2,1)}) conditional(s32[]{:T(128)} %convert_element_type.3, () %tuple.16, (bf16[16,80,512]{2,1,0:T(8,128)(2,1)}, bf16[448,512]{1,0:T(8,128)(2,1)S(1)}, ...), branch_computations={%region_0.1_spmd, %region_1.2_spmd} | conditional | flops 470810624 | bytes 27001088 | solution.py:294
  16.6 9.4 %all-to-all-start = ((bf16[16,80,512]{2,1,0:T(8,128)(2,1)}), bf16[16,80,512]{2,1,0:T(8,128)(2,1)S(1)}, u32[]{:S(2)}, u32[]{:S(2)}) async-start(bf16[16,80,512]{2,1,0:T(8,128)(2,1)} %get-tuple-element.8), calls=%async_computation | async-start | bytes 2621440 | tf_op jit(solution)/shard_map/cond/branch_1_fun/all_to_all | solution.py:280
  26.0 1.9 %collective-permute-start = (bf16[448,512]{1,0:T(8,128)(2,1)S(1)}, bf16[448,512]{1,0:T(8,128)(2,1)S(1)}, u32[]{:S(2)}, u32[]{:S(2)}) collective-permute-start(bf16[448,512]{1,0:T(8,128)(2,1)S(1)} %get-tuple-element.9.down_ref), channel_id=1, source_target_pairs={{0,1},{1,0},{2,3},{3,2},{4,5},{5,4},{6,7},{7,6},{8,9},{9,8},{10,11... | collective-permute-start | bytes 1376264 | tf_op jit(solution)/shard_map/cond/branch_1_fun/ppermute | solution.py:55
  27.9 30.2 %all-to-all-done.extra_ref.received_ref = bf16[16,80,512]{2,1,0:T(8,128)(2,1)S(1)} async-done(((bf16[16,80,512]{2,1,0:T(8,128)(2,1)}), bf16[16,80,512]{2,1,0:T(8,128)(2,1)S(1)}, u32[]{:S(2)}, u32[]{:S(2)}) %all-to-all-start) | async-done | bytes 1310752 | tf_op jit(solution)/shard_map/cond/branch_1_fun/all_to_all | solution.py:280
  58.1 0.7 branch_1_fun.3
  58.8 11.5 %all-to-all-start.1 = ((f32[32,8,128]{2,1,0:T(8,128)}), f32[32,8,128]{2,1,0:T(8,128)}, u32[]{:S(2)}, u32[]{:S(2)}) async-start(f32[32,8,128]{2,1,0:T(8,128)} %branch_1_fun.3), calls=%async_computation.1 | async-start | bytes 262144 | tf_op jit(solution)/shard_map/cond/branch_1_fun/all_to_all | solution.py:282
  70.3 0.0 collective-permute-done.other_ref
  70.4 11.9 %all-to-all-done.1.tile_ref = f32[32,8,128]{2,1,0:T(8,128)} async-done(((f32[32,8,128]{2,1,0:T(8,128)}), f32[32,8,128]{2,1,0:T(8,128)}, u32[]{:S(2)}, u32[]{:S(2)}) %all-to-all-start.1) | async-done | bytes 131104 | tf_op jit(solution)/shard_map/cond/branch_1_fun/all_to_all | solution.py:282
  82.3 4.1 %branch_1_fun.4 = (bf16[16,32,896]{2,1,0:T(8,128)(2,1)S(1)}, bf16[2,512,512]{2,1,0:T(8,128)(2,1)}) custom-call(f32[32,8,128]{2,1,0:T(8,128)} %all-to-all-done.1.tile_ref, bf16[16,80,512]{2,1,0:T(8,128)(2,1)S(1)} %all-to-all-done.extra_ref.received_ref, bf16[448,512]{1,0:T(8,128)(2,1)S(1)} %get-tuple-element.9.down_ref, ...), custom_call_target="tpu_custom_call" | custom-call | flops 469762048 | bytes 4194304 | tf_op jit(solution)/shard_map/cond/branch_1_fun/pallas_call | solution.py:141
  86.4 32.6 %all_to_all.21.parts_ref = bf16[16,32,896]{2,1,0:T(8,128)(2,1)S(1)} all-to-all(bf16[16,32,896]{2,1,0:T(8,128)(2,1)S(1)} %get-tuple-element.13), channel_id=1, replica_groups=mesh['xh'=2,'z'=8,'xl'=2,'y'=8,'core'=2] {'xh','z'}, dimensions={0} | all-to-all | bytes 1835008 | tf_op jit(solution)/shard_map/cond/branch_1_fun/all_to_all | solution.py:284
  119.0 1.1 branch_1_fun.5
  120.1 5.4 %all-to-all-start.3 = ((bf16[16,32,896]{2,1,0:T(8,128)(2,1)}), bf16[16,32,896]{2,1,0:T(8,128)(2,1)}, u32[]{:S(2)}, u32[]{:S(2)}) async-start(bf16[16,32,896]{2,1,0:T(8,128)(2,1)} %branch_1_fun.5), calls=%async_computation.3 | async-start | bytes 1835008 | tf_op jit(solution)/shard_map/cond/branch_1_fun/all_to_all | solution.py:287
  125.5 1.9 %collective-permute-start.1 = (bf16[2,512,512]{2,1,0:T(8,128)(2,1)}, bf16[2,512,512]{2,1,0:T(8,128)(2,1)}, u32[]{:S(2)}, u32[]{:S(2)}) collective-permute-start(bf16[2,512,512]{2,1,0:T(8,128)(2,1)} %get-tuple-element.52), channel_id=1, source_target_pairs={{0,1},{1,0},{2,3},{3,2},{4,5},{5,4},{6,7},{7,6},{8,9},{9,8},{10,11... | collective-permute-start | bytes 3145736 | tf_op jit(solution)/shard_map/cond/branch_1_fun/ppermute | solution.py:55
  127.4 0.1 pad_maximum_fusion
  127.5 2.4 %collective-permute-start.2 = (bf16[2,448,512]{2,1,0:T(8,128)(2,1)S(1)}, bf16[2,448,512]{2,1,0:T(8,128)(2,1)}, u32[]{:S(2)}, u32[]{:S(2)}) collective-permute-start(bf16[2,448,512]{2,1,0:T(8,128)(2,1)S(1)} %pad_maximum_fusion), channel_id=1, source_target_pairs={{0,1},{1,0},{2,3},{3,2},{4,5},{5,4},{6,7},{7,6},{8,9},{9,8},{10,11... | collective-permute-start | bytes 2752520 | tf_op jit(solution)/shard_map/cond/branch_1_fun/ppermute | solution.py:55
  129.9 2.2 %collective-permute-done.2 = bf16[2,448,512]{2,1,0:T(8,128)(2,1)} collective-permute-done((bf16[2,448,512]{2,1,0:T(8,128)(2,1)S(1)}, bf16[2,448,512]{2,1,0:T(8,128)(2,1)}, u32[]{:S(2)}, u32[]{:S(2)}) %collective-permute-start.2) | collective-permute-done | bytes 917536 | tf_op jit(solution)/shard_map/cond/branch_1_fun/ppermute | solution.py:55
  132.1 0.0 collective-permute-done.1
  132.1 17.7 %all-to-all-done.3 = bf16[16,32,896]{2,1,0:T(8,128)(2,1)} async-done(((bf16[16,32,896]{2,1,0:T(8,128)(2,1)}), bf16[16,32,896]{2,1,0:T(8,128)(2,1)}, u32[]{:S(2)}, u32[]{:S(2)}) %all-to-all-start.3) | async-done | bytes 917536 | tf_op jit(solution)/shard_map/cond/branch_1_fun/all_to_all | solution.py:287
  149.9 0.0 all-gather.2.cloned.1.call-done.pre_ref
  149.9 0.0 copy-start
  149.9 1.5 copy-done
  151.4 5.8 %shard_map.103 = (bf16[16,32,512]{2,1,0:T(8,128)(2,1)}, bf16[3,512,512]{2,1,0:T(8,128)(2,1)S(1)}, bf16[3,512,512]{2,1,0:T(8,128)(2,1)}) custom-call(f32[32,8,128]{2,1,0:T(8,128)} %get-tuple-element.29.tile_ref, bf16[16,32,896]{2,1,0:T(8,128)(2,1)} %get-tuple-element.30.hid_ref, bf16[512,1792]{1,0:T(8,128)(2,1)S(1)} %copy-done, ...), custom_call_target="tpu_custom_call" | custom-call | flops 939524096 | bytes 9437184 | tf_op jit(solution)/shard_map/pallas_call | solution.py:208
  157.2 1.9 %collective-permute-start.4 = (bf16[3,512,512]{2,1,0:T(8,128)(2,1)}, bf16[3,512,512]{2,1,0:T(8,128)(2,1)}, u32[]{:S(2)}, u32[]{:S(2)}) collective-permute-start(bf16[3,512,512]{2,1,0:T(8,128)(2,1)} %get-tuple-element.34), channel_id=1, source_target_pairs={{0,1},{1,0},{2,3},{3,2},{4,5},{5,4},{6,7},{7,6},{8,9},{9,8},{10,11... | collective-permute-start | bytes 4718600 | tf_op jit(solution)/shard_map/ppermute | solution.py:55
  159.1 6.6 %all-to-all-start.4 = ((bf16[16,32,512]{2,1,0:T(8,128)(2,1)}), bf16[16,32,512]{2,1,0:T(8,128)(2,1)S(1)}, u32[]{:S(2)}, u32[]{:S(2)}) async-start(bf16[16,32,512]{2,1,0:T(8,128)(2,1)} %get-tuple-element.32), calls=%async_computation.4 | async-start | bytes 1048576 | tf_op jit(solution)/shard_map/all_to_all | solution.py:299
  165.6 0.0 collective-permute-done.4.other_ref
  165.6 4.6 %shard_map.104 = (bf16[448,512]{1,0:T(8,128)(2,1)}, bf16[448,512]{1,0:T(8,128)(2,1)}, bf16[448,512]{1,0:T(8,128)(2,1)}) custom-call(bf16[3,512,512]{2,1,0:T(8,128)(2,1)S(1)} %get-tuple-element.33.own_ref, bf16[3,512,512]{2,1,0:T(8,128)(2,1)} %collective-permute-done.4.other_ref, bf16[2,512,512]{2,1,0:T(8,128)(2,1)} %get-tuple-element.35.halves_ref, ...), custom_call_target="tpu_custom_call" | custom-call | flops 1610612736 | bytes 6291456 | tf_op jit(solution)/shard_map/pallas_call | solution.py:238
  170.2 11.4 %all-to-all-done.4.parts_ref = bf16[16,32,512]{2,1,0:T(8,128)(2,1)S(1)} async-done(((bf16[16,32,512]{2,1,0:T(8,128)(2,1)}), bf16[16,32,512]{2,1,0:T(8,128)(2,1)S(1)}, u32[]{:S(2)}, u32[]{:S(2)}) %all-to-all-start.4) | async-done | bytes 524320 | tf_op jit(solution)/shard_map/all_to_all | solution.py:299
  181.7 0.0 copy-start.1
  181.7 1.0 copy-done.1
  182.7 0.7 shard_map.105
  (1 shorter events, 0.0 us)
Async XLA Ops:
  7.2 142.7 %all-gather.2.cloned.1.call-start = ((), (), s32[]{:S(2)}) async-start(), calls=%async_computation.5 | async-start | bytes 1949696 | tf_op jit(solution)/shard_map/all_gather | solution.py:274
  7.2 9.4 %copy-start.5 = (bf16[512,448]{0,1:T(8,128)(2,1)S(1)}, bf16[512,448]{0,1:T(8,128)(2,1)}, u32[]{:S(2)}) copy-start(bf16[512,448]{0,1:T(8,128)(2,1)} %param.14) | copy-start | bytes 1376260
  8.3 3.1 %collective-permute-start.3 = (bf16[32,896]{1,0:T(8,128)(2,1)S(1)}, bf16[32,896]{1,0:T(8,128)(2,1)S(1)}, u32[]{:S(2)}, u32[]{:S(2)}) collective-permute-start(bf16[32,896]{1,0:T(8,128)(2,1)S(1)} %get-tuple-element.40), channel_id=1, source_target_pairs={{0,1},{1,0},{2,3},{3,2},{4,5},{5,4},{6,7},{7,6},{8,9},{9,8},{10,11... | collective-permute-start | bytes 172040 | tf_op jit(solution)/shard_map/ppermute | solution.py:55
  11.4 5.2 %copy-start.4 = (bf16[512,448]{0,1:T(8,128)(2,1)S(1)}, bf16[512,448]{0,1:T(8,128)(2,1)}, u32[]{:S(2)}) copy-start(bf16[512,448]{0,1:T(8,128)(2,1)} %param.13) | copy-start | bytes 1376260
  12.3 0.8 copy-start.2
  13.0 0.8 copy-start.3
  13.8 2.8 %copy-start.6 = (bf16[448,512]{1,0:T(8,128)(2,1)S(1)}, bf16[448,512]{1,0:T(8,128)(2,1)}, u32[]{:S(2)}) copy-start(bf16[448,512]{1,0:T(8,128)(2,1)} %down_ref.1) | copy-start | bytes 1376260
  16.6 41.5 %all-to-all-start = ((bf16[16,80,512]{2,1,0:T(8,128)(2,1)}), bf16[16,80,512]{2,1,0:T(8,128)(2,1)S(1)}, u32[]{:S(2)}, u32[]{:S(2)}) async-start(bf16[16,80,512]{2,1,0:T(8,128)(2,1)} %get-tuple-element.8), calls=%async_computation | async-start | bytes 2621440 | tf_op jit(solution)/shard_map/cond/branch_1_fun/all_to_all | solution.py:280
  26.0 44.4 %collective-permute-start = (bf16[448,512]{1,0:T(8,128)(2,1)S(1)}, bf16[448,512]{1,0:T(8,128)(2,1)S(1)}, u32[]{:S(2)}, u32[]{:S(2)}) collective-permute-start(bf16[448,512]{1,0:T(8,128)(2,1)S(1)} %get-tuple-element.9.down_ref), channel_id=1, source_target_pairs={{0,1},{1,0},{2,3},{3,2},{4,5},{5,4},{6,7},{7,6},{8,9},{9,8},{10,11... | collective-permute-start | bytes 1376264 | tf_op jit(solution)/shard_map/cond/branch_1_fun/ppermute | solution.py:55
  58.8 23.5 %all-to-all-start.1 = ((f32[32,8,128]{2,1,0:T(8,128)}), f32[32,8,128]{2,1,0:T(8,128)}, u32[]{:S(2)}, u32[]{:S(2)}) async-start(f32[32,8,128]{2,1,0:T(8,128)} %branch_1_fun.3), calls=%async_computation.1 | async-start | bytes 262144 | tf_op jit(solution)/shard_map/cond/branch_1_fun/all_to_all | solution.py:282
  120.1 29.8 %all-to-all-start.3 = ((bf16[16,32,896]{2,1,0:T(8,128)(2,1)}), bf16[16,32,896]{2,1,0:T(8,128)(2,1)}, u32[]{:S(2)}, u32[]{:S(2)}) async-start(bf16[16,32,896]{2,1,0:T(8,128)(2,1)} %branch_1_fun.5), calls=%async_computation.3 | async-start | bytes 1835008 | tf_op jit(solution)/shard_map/cond/branch_1_fun/all_to_all | solution.py:287
  125.5 6.7 %collective-permute-start.1 = (bf16[2,512,512]{2,1,0:T(8,128)(2,1)}, bf16[2,512,512]{2,1,0:T(8,128)(2,1)}, u32[]{:S(2)}, u32[]{:S(2)}) collective-permute-start(bf16[2,512,512]{2,1,0:T(8,128)(2,1)} %get-tuple-element.52), channel_id=1, source_target_pairs={{0,1},{1,0},{2,3},{3,2},{4,5},{5,4},{6,7},{7,6},{8,9},{9,8},{10,11... | collective-permute-start | bytes 3145736 | tf_op jit(solution)/shard_map/cond/branch_1_fun/ppermute | solution.py:55
  127.5 4.6 %collective-permute-start.2 = (bf16[2,448,512]{2,1,0:T(8,128)(2,1)S(1)}, bf16[2,448,512]{2,1,0:T(8,128)(2,1)}, u32[]{:S(2)}, u32[]{:S(2)}) collective-permute-start(bf16[2,448,512]{2,1,0:T(8,128)(2,1)S(1)} %pad_maximum_fusion), channel_id=1, source_target_pairs={{0,1},{1,0},{2,3},{3,2},{4,5},{5,4},{6,7},{7,6},{8,9},{9,8},{10,11... | collective-permute-start | bytes 2752520 | tf_op jit(solution)/shard_map/cond/branch_1_fun/ppermute | solution.py:55
  149.9 1.5 copy-start
  157.2 8.5 %collective-permute-start.4 = (bf16[3,512,512]{2,1,0:T(8,128)(2,1)}, bf16[3,512,512]{2,1,0:T(8,128)(2,1)}, u32[]{:S(2)}, u32[]{:S(2)}) collective-permute-start(bf16[3,512,512]{2,1,0:T(8,128)(2,1)} %get-tuple-element.34), channel_id=1, source_target_pairs={{0,1},{1,0},{2,3},{3,2},{4,5},{5,4},{6,7},{7,6},{8,9},{9,8},{10,11... | collective-permute-start | bytes 4718600 | tf_op jit(solution)/shard_map/ppermute | solution.py:55
  159.1 22.6 %all-to-all-start.4 = ((bf16[16,32,512]{2,1,0:T(8,128)(2,1)}), bf16[16,32,512]{2,1,0:T(8,128)(2,1)S(1)}, u32[]{:S(2)}, u32[]{:S(2)}) async-start(bf16[16,32,512]{2,1,0:T(8,128)(2,1)} %get-tuple-element.32), calls=%async_computation.4 | async-start | bytes 1048576 | tf_op jit(solution)/shard_map/all_to_all | solution.py:299
  181.7 1.0 copy-start.1
Sparse Core Ops, SparseCore 0:
  12.4 104.3 all-gather.1

commit v4 on v3

v4 whole, which is shorter than its diff:
```python
import jax
import jax.numpy as jnp
from jax import lax
from jax.experimental import pallas as pl
from jax.experimental.pallas import tpu as pltpu
from jax.sharding import Mesh, PartitionSpec as P

EMBED_SIZE = 8192
GATE_INNER_SIZE = 14336
N_ROW = 16
N_CHIP = 16
ROW = ("xh", "z")
CHIP = ("xl", "y")
EXTRA = 16
N_Y = 8
LANES = 128
VMEM = pl.BlockSpec(memory_space=pltpu.VMEM)
SMEM = pl.BlockSpec(memory_space=pltpu.SMEM)
PARAMS = pltpu.CompilerParams(vmem_limit_bytes=40 * 1024 * 1024)


def cost(flops, bytes_accessed):
    return pl.CostEstimate(flops=flops, bytes_accessed=bytes_accessed, transcendentals=0)


def contract_last(left, right):
    return lax.dot_general(
        left, right, (((1,), (1,)), ((), ())), preferred_element_type=jnp.float32
    )


def contract_first(left, right):
    return lax.dot_general(
        left, right, (((0,), (0,)), ((), ())), preferred_element_type=jnp.float32
    )


def matmul(left, right):
    return lax.dot_general(
        left, right, (((1,), (0,)), ((), ())), preferred_element_type=jnp.float32
    )


def swiglu_grads(grad_hidden, gate_pre, up_pre):
    gate_f = gate_pre.astype(jnp.float32)
    up_f = up_pre.astype(jnp.float32)
    sigma = jax.nn.sigmoid(gate_f)
    silu_gate = gate_f * sigma
    grad_gpre = (grad_hidden * up_f * sigma * (1.0 + gate_f * (1.0 - sigma))).astype(jnp.bfloat16)
    grad_upre = (grad_hidden * silu_gate).astype(jnp.bfloat16)
    hidden = (silu_gate * up_f).astype(jnp.bfloat16)
    return (grad_gpre, grad_upre, hidden)


def swapped(values):
    return lax.ppermute(values, "core", [(0, 1), (1, 0)])


def pieces_of(totals):
    pieces = []
    for total in totals:
        for _ in range(3):
            piece = total.astype(jnp.bfloat16).astype(jnp.float32)
            pieces.append(piece)
            total = total - piece
    pieces.append(jnp.zeros((EXTRA - len(pieces), totals[0].shape[1]), jnp.float32))
    return jnp.concatenate(pieces, axis=0).astype(jnp.bfloat16)


def totals_of(pieces):
    return [jnp.sum(pieces[3 * k : 3 * k + 3], axis=0, keepdims=True) for k in range(3)]


def half_of(ref, core):
    rows = ref.shape[0] // 2
    return ref[pl.ds(pl.multiple_of(core * rows, rows), rows), :]


def first_kernel(core_ref, gate_pre_ref, up_pre_ref, gate_ref, up_ref, down_ref, sent_ref, sums_ref):
    rows, inner = gate_pre_ref.shape[0] // 2, gate_pre_ref.shape[1]
    lanes = sent_ref.shape[1] // 2
    sums = []
    for ref in (gate_ref, up_ref, down_ref):
        total = jnp.sum(jnp.abs(ref[...].astype(jnp.float32)), axis=0, keepdims=True)
        sums.append(jnp.broadcast_to(jnp.sum(total, axis=1, keepdims=True), (1, 2 * lanes)))
    sent_ref[...] = jnp.zeros(sent_ref.shape, sent_ref.dtype)
    sent_ref[0:rows, 0:inner] = half_of(gate_pre_ref, 1 - core_ref[0])
    sent_ref[0:rows, lanes : lanes + inner] = half_of(up_pre_ref, 1 - core_ref[0])
    sent_ref[rows:, :] = pieces_of(sums)
    tile = jnp.concatenate(sums + [jnp.zeros((5, 2 * lanes), jnp.float32)], axis=0)
    sums_ref[...] = tile[:, :LANES]


def first(core, gate_pre, up_pre, gate_t, up_t, down):
    rows, inner = gate_pre.shape
    lanes = -(-inner // LANES) * LANES
    return pl.pallas_call(
        first_kernel,
        out_shape=(
            jax.ShapeDtypeStruct((rows // 2 + EXTRA, 2 * lanes), jnp.bfloat16),
            jax.ShapeDtypeStruct((8, LANES), jnp.float32),
        ),
        in_specs=[SMEM] + [VMEM] * 5,
        out_specs=(VMEM, VMEM),
        compiler_params=PARAMS,
        cost_estimate=cost(1 << 20, 3 << 19),
    )(core, gate_pre, up_pre, gate_t, up_t, down)


def second_kernel(core_ref, gate_pre_ref, up_pre_ref, other_ref, sums_ref, out_ref, pre_ref, sent_ref):
    rows, inner = gate_pre_ref.shape[0] // 2, gate_pre_ref.shape[1]
    lanes = other_ref.shape[1] // 2
    pre_ref[...] = jnp.concatenate(
        [
            half_of(gate_pre_ref, core_ref[0]),
            other_ref[0:rows, 0:inner],
            half_of(up_pre_ref, core_ref[0]),
            other_ref[0:rows, lanes : lanes + inner],
        ],
        axis=1,
    )
    others = totals_of(other_ref[rows:, :LANES].astype(jnp.float32))
    extra = pieces_of([sums_ref[n : n + 1, :] + others[n] for n in range(3)])
    blocks = [out_ref[:, j * LANES : (j + 1) * LANES] for j in range(out_ref.shape[1] // LANES)]
    block = jnp.concatenate(blocks + [extra], axis=0)
    for k in range(N_CHIP):
        sent_ref[k] = block


def second(core, gate_pre, up_pre, other, sums, grad_out):
    rows, width = grad_out.shape
    inner = gate_pre.shape[1]
    return pl.pallas_call(
        second_kernel,
        out_shape=(
            jax.ShapeDtypeStruct((rows, 4 * inner), jnp.bfloat16),
            jax.ShapeDtypeStruct((N_CHIP, rows * width // LANES + EXTRA, LANES), jnp.bfloat16),
        ),
        in_specs=[SMEM] + [VMEM] * 5,
        out_specs=(VMEM, VMEM),
        compiler_params=PARAMS,
        cost_estimate=cost(1 << 16, 1 << 20),
    )(core, gate_pre, up_pre, other, sums, grad_out)


def tile_kernel(extra_ref, tile_ref):
    sums = totals_of(jnp.sum(extra_ref[...].astype(jnp.float32), axis=0))
    tile = jnp.concatenate(sums + [jnp.zeros((5, LANES), jnp.float32)], axis=0)
    tile_ref[...] = jnp.broadcast_to(tile[None], tile_ref.shape)


def sums_tile(received):
    rows = received.shape[1] - EXTRA
    return pl.pallas_call(
        tile_kernel,
        grid=(1,),
        out_shape=jax.ShapeDtypeStruct((N_ROW, 8, LANES), jnp.float32),
        in_specs=[pl.BlockSpec((N_CHIP, EXTRA, LANES), lambda i: (0, rows // EXTRA, 0))],
        out_specs=pl.BlockSpec((N_ROW, 8, LANES), lambda i: (0, 0, 0)),
        compiler_params=PARAMS,
        cost_estimate=cost(1 << 16, 1 << 18),
    )(received)


def scale_of(tile_ref, which):
    total = jnp.sum(tile_ref[...], axis=0)[which : which + 1, 0:1]
    return total / float(EMBED_SIZE * GATE_INNER_SIZE) + 1e-05


def clipped(values, scale):
    return jnp.clip(values.astype(jnp.float32), -scale, scale).astype(jnp.bfloat16)


def partial_kernel(tile_ref, received_ref, down_ref, other_ref, partial_ref, out_ref, quant_ref):
    rows = partial_ref.shape[1]
    inner, width = down_ref.shape

    @pl.when(pl.program_id(0) == 0)
    def _():
        scale = scale_of(tile_ref, 2)
        quant_ref[0:inner, :] = clipped(down_ref[...], scale)
        quant_ref[inner:, :] = clipped(other_ref[...], scale)

    blocks = [received_ref[:, j * rows : (j + 1) * rows, :] for j in range(width // LANES)]
    out_rows = jnp.concatenate([block.reshape((-1, LANES)) for block in blocks], axis=1)
    out_ref[...] = out_rows
    partial = contract_last(out_rows, quant_ref[...])
    partial_ref[...] = partial.astype(jnp.bfloat16).reshape(partial_ref.shape)


def hidden_partial(tile, received, down, other):
    blocks, steps = 4, N_CHIP // 4
    inner, width = down.shape
    rows = (received.shape[1] - EXTRA) * LANES // width
    whole = pl.BlockSpec((inner, width), lambda i: (0, 0))
    return pl.pallas_call(
        partial_kernel,
        grid=(steps,),
        out_shape=(
            jax.ShapeDtypeStruct((N_ROW, rows, 2 * inner), jnp.bfloat16),
            jax.ShapeDtypeStruct((N_CHIP * rows, width), jnp.bfloat16),
        ),
        in_specs=[
            pl.BlockSpec(tile.shape, lambda i: (0, 0, 0)),
            pl.BlockSpec((blocks,) + received.shape[1:], lambda i: (i, 0, 0)),
            whole,
            whole,
        ],
        out_specs=(
            pl.BlockSpec((blocks, rows, 2 * inner), lambda i: (i, 0, 0)),
            pl.BlockSpec((blocks * rows, width), lambda i: (i, 0)),
        ),
        scratch_shapes=[pltpu.VMEM((2 * inner, width), jnp.bfloat16)],
        compiler_params=PARAMS,
        cost_estimate=cost(2 * 512 * 896 * 512, 4 << 20),
    )(tile, received, down, other)


def spread_kernel(parts_ref, sent_ref):
    total = jnp.sum(parts_ref[...].astype(jnp.float32), axis=0).astype(jnp.bfloat16)
    for k in range(N_ROW):
        sent_ref[k] = total


def spread(parts):
    return pl.pallas_call(
        spread_kernel,
        out_shape=jax.ShapeDtypeStruct(parts.shape, jnp.bfloat16),
        in_specs=[VMEM],
        out_specs=VMEM,
        compiler_params=PARAMS,
        cost_estimate=cost(1 << 19, 2 << 20),
    )(parts)


def clip_kernel(tile_ref, gate_ref, up_ref, other_ref, quant_ref):
    inner = gate_ref.shape[0]
    for n, ref in enumerate((gate_ref, up_ref)):
        scale = scale_of(tile_ref, n)
        quant_ref[n, 0:inner, :] = clipped(ref[...], scale)
        quant_ref[n, inner:, :] = clipped(other_ref[n], scale)


def clipped_latents(tile, gate_t, up_t, other):
    inner, width = gate_t.shape
    return pl.pallas_call(
        clip_kernel,
        out_shape=jax.ShapeDtypeStruct((2, 2 * inner, width), jnp.bfloat16),
        in_specs=[VMEM] * 4,
        out_specs=VMEM,
        compiler_params=PARAMS,
        cost_estimate=cost(1 << 20, 4 << 20),
    )(tile, gate_t, up_t, other)


def act_kernel(hid_ref, pre_ref, quant_ref, partial_ref, acts_ref):
    both = hid_ref.shape[2]
    grad_hidden = hid_ref[...].reshape((-1, both)).astype(jnp.float32)
    acts = swiglu_grads(grad_hidden, pre_ref[:, :both], pre_ref[:, both:])
    partial = matmul(acts[0], quant_ref[0]) + matmul(acts[1], quant_ref[1])
    partial_ref[...] = partial.astype(jnp.bfloat16).reshape(partial_ref.shape)
    for n, act in enumerate(acts):
        acts_ref[n] = act


def act_partial(grad_hidden, pre_half, quant):
    blocks, steps = 4, N_ROW // 4
    rows, both = grad_hidden.shape[1:]
    width = quant.shape[2]
    return pl.pallas_call(
        act_kernel,
        grid=(steps,),
        out_shape=(
            jax.ShapeDtypeStruct((N_CHIP, rows, width), jnp.bfloat16),
            jax.ShapeDtypeStruct((3, N_ROW * rows, both), jnp.bfloat16),
        ),
        in_specs=[
            pl.BlockSpec((blocks, rows, both), lambda i: (i, 0, 0)),
            pl.BlockSpec((blocks * rows, 2 * both), lambda i: (i, 0)),
            pl.BlockSpec(quant.shape, lambda i: (0, 0, 0)),
        ],
        out_specs=(
            pl.BlockSpec((blocks, rows, width), lambda i: (i, 0, 0)),
            pl.BlockSpec((3, blocks * rows, both), lambda i: (0, i, 0)),
        ),
        compiler_params=PARAMS,
        cost_estimate=cost(4 * 512 * 896 * 512, 8 << 20),
    )(grad_hidden, pre_half, quant)


def latent_grads_kernel(place_ref, acts_ref, out_ref, *refs):
    token_refs, (own_ref, sent_ref, rows_ref) = refs[:N_Y], refs[N_Y:]
    rows = token_refs[0].shape[1]
    for shift, ref in enumerate(token_refs):
        y = lax.rem(place_ref[1] + shift, N_Y)
        for flip in range(2):
            chip = lax.rem(place_ref[0] + flip, 2) * N_Y + y
            rows_ref[pl.ds(pl.multiple_of(chip * rows, rows), rows), :] = ref[flip]
    inner = own_ref.shape[1]
    for n in range(3):
        half = out_ref[...] if n == 2 else rows_ref[...]
        grad = contract_first(acts_ref[n], half)
        own_ref[n] = grad[:inner]
        sent_ref[n] = grad[inner:].astype(jnp.bfloat16)


def latent_grads(place, acts, out_half, token_blocks):
    inner, width = acts.shape[2] // 2, out_half.shape[1]
    return pl.pallas_call(
        latent_grads_kernel,
        out_shape=(
            jax.ShapeDtypeStruct((3, inner, width), jnp.float32),
            jax.ShapeDtypeStruct((3, inner, width), jnp.bfloat16),
        ),
        in_specs=[SMEM] + [VMEM] * (2 + N_Y),
        out_specs=(VMEM, VMEM),
        scratch_shapes=[pltpu.VMEM(out_half.shape, jnp.bfloat16)],
        compiler_params=PARAMS,
        cost_estimate=cost(6 * 512 * 896 * 512, 8 << 20),
    )(place, acts, out_half, *token_blocks)


def join_kernel(own_ref, other_ref, *refs):
    for n, ref in enumerate(refs[:3]):
        ref[...] = (own_ref[n] + other_ref[n].astype(jnp.float32)).astype(jnp.bfloat16)
    refs[3][...] = jnp.zeros(refs[3].shape, jnp.float32)


def join(own, other):
    grad = jax.ShapeDtypeStruct(own.shape[1:], jnp.bfloat16)
    return pl.pallas_call(
        join_kernel,
        out_shape=(grad, grad, grad, jax.ShapeDtypeStruct((8, LANES), jnp.float32)),
        in_specs=[VMEM] * 2,
        out_specs=(VMEM,) * 4,
        compiler_params=PARAMS,
        cost_estimate=cost(1 << 20, 5 << 20),
    )(own, other)


def total_kernel(parts_ref, after_ref, total_ref):
    total_ref[...] = jnp.sum(parts_ref[...].astype(jnp.float32), axis=0).astype(jnp.bfloat16)


def total(parts, after):
    return pl.pallas_call(
        total_kernel,
        out_shape=jax.ShapeDtypeStruct(parts.shape[1:], jnp.bfloat16),
        in_specs=[VMEM] * 2,
        out_specs=VMEM,
        compiler_params=PARAMS,
        cost_estimate=cost(1 << 18, 1 << 19),
    )(parts, after)


def in_branch(work, *operands):
    def nothing(*operands):
        shapes = jax.eval_shape(work, *operands)
        return tuple(jnp.zeros(leaf.shape, leaf.dtype) for leaf in shapes)

    def always(*operands):
        return tuple(work(*operands))

    return lax.cond(lax.axis_index("z") < 8, always, nothing, *operands)


def shards(tokens, grad_out, gate_pre, up_pre, gate_latent, up_latent, down_latent):
    core = lax.axis_index("core").astype(jnp.int32).reshape((1,))
    place = jnp.stack([lax.axis_index("xl"), lax.axis_index("y")]).astype(jnp.int32)

    gate_t, up_t = gate_latent.T, up_latent.T
    sent, sums = first(core, gate_pre, up_pre, gate_t, up_t, down_latent)
    pre_rows, sent = second(core, gate_pre, up_pre, swapped(sent), sums, grad_out)
    pre_half = lax.all_gather(pre_rows, ROW, axis=0, tiled=True)

    def exchanges(sent, tokens, gate_t, up_t, down):
        received = lax.all_to_all(sent, CHIP, 0, 0)
        down_other = swapped(down)
        tile = lax.all_to_all(sums_tile(received), ROW, 0, 0)
        partial, out_half = hidden_partial(tile, received, down, down_other)
        parts = lax.all_to_all(partial, ROW, 0, 0)
        other_latents = swapped(jnp.stack([gate_t, up_t]))
        quant = clipped_latents(tile, gate_t, up_t, other_latents)
        pair = jnp.stack([tokens, lax.ppermute(tokens, "xl", [(0, 1), (1, 0)])])
        token_blocks = [pair] + [
            lax.ppermute(pair, "y", [((y + shift) % N_Y, y) for y in range(N_Y)])
            for shift in range(1, N_Y)
        ]
        grad_hidden = lax.all_to_all(spread(parts), ROW, 0, 0)
        return (out_half, quant, grad_hidden) + tuple(token_blocks)

    out_half, quant, grad_hidden, *token_blocks = in_branch(
        exchanges, sent, tokens, gate_t, up_t, down_latent
    )

    partial, acts = act_partial(grad_hidden, pre_half, quant)
    parts = lax.all_to_all(partial, CHIP, 0, 0)

    def joined(place, acts, out_half, *token_blocks):
        own, sent = latent_grads(place, acts, out_half, token_blocks)
        return join(own, swapped(sent))

    grad_gate, grad_up, grad_down, done = in_branch(joined, place, acts, out_half, *token_blocks)
    grad_tokens = total(parts, done)
    return (grad_tokens, grad_gate.T, grad_up.T, grad_down)


def solution(mesh):
    fine = Mesh(mesh.devices.reshape((2, 8, 2, 8, 2)), ROW + CHIP + ("core",))
    col = CHIP + ("core",)
    in_specs = (
        P(col, ROW),
        P(col, ROW),
        P(ROW, col),
        P(ROW, col),
        P(ROW, col),
        P(ROW, col),
        P(col, ROW),
    )
    out_specs = (P(col, ROW), P(ROW, col), P(ROW, col), P(col, ROW))
    return jax.shard_map(shards, mesh=fine, in_specs=in_specs, out_specs=out_specs, check_vma=False)
```

time: 191 us -> 176 us (0.921)
  the two profiles are of different devices: /device:TPU:10 before, /device:TPU:14 now
where the time goes in v4:
time: 176 us; the launch traced here: 175 us
  starting transfers between devices  73.1 us (42%)
  waiting for transfers between devices  38.2 us (22%)
  blocking collectives  27.4 us (16%)
  Pallas kernels  17.7 us (10%)
  between operations  14.1 us (8%)
  local copies, waits for them, and re-layouts  3.95 us (2%)
    all_to_all x1, blocking collectives, exchanges(): parts = lax.all_to_all(partial, ROW, 0, 0)  27.4 us
    ppermute x7, starting transfers between devices, exchanges(): lax.ppermute(pair, 'y', [((y + shift) % N_Y, y) for y in range(N_Y)])  27.2 us
    all_to_all x1, waiting for transfers between devices, exchanges(): received = lax.all_to_all(sent, CHIP, 0, 0)  15 us
    all_to_all x1, starting transfers between devices, exchanges(): tile = lax.all_to_all(sums_tile(received), ROW, 0, 0)  13.3 us
    all_to_all x1, starting transfers between devices, exchanges(): received = lax.all_to_all(sent, CHIP, 0, 0)  8.61 us
    ppermute x4, starting transfers between devices, swapped(): return lax.ppermute(values, 'core', [(0, 1), (1, 0)])  7.66 us
    all_to_all x1, starting transfers between devices, exchanges(): grad_hidden = lax.all_to_all(spread(parts), ROW, 0, 0)  7.57 us
    all_to_all x1, waiting for transfers between devices, exchanges(): tile = lax.all_to_all(sums_tile(received), ROW, 0, 0)  7.38 us
  transfers between devices with their start and end apart: 17, of which 8 were waited for; matrix products, arithmetic and copies ran while one was open for 0% of the time, Pallas kernels for 5%

profile of v4, /device:TPU:14, one launch (start us, length us, event | category | flops | bytes accessed | tf_op | source)
XLA Modules:
  0.0 175.4 jit_solution(10850040265645856795)
XLA Ops:
  7.2 0.0 all-gather.2.cloned.1.call-start
  7.2 0.0 copy-start.1
  7.2 0.8 copy-done.1
  8.1 0.8 copy-done.2
  8.9 0.0 copy-start.5
  8.9 0.0 copy-start.7
  8.9 1.8 %shard_map.103 = (bf16[48,1024]{1,0:T(8,128)(2,1)S(1)}, f32[8,128]{1,0:T(8,128)S(1)}) custom-call(s32[1]{0:T(128)} %bitcast.4.core_ref, bf16[64,448]{1,0:T(8,128)(2,1)S(1)} %copy-done.1, bf16[64,448]{1,0:T(8,128)(2,1)S(1)} %copy-done.2, bf16[448,512]{1,0:T(8,128)(2,1)} %bitcast.11, bf16[448,512]{1,0:T(8,128)(2,1)} %bitcast.14, bf16[448,512]{1,0:T(8,128)(2,1)} %down_ref.1), custom_call_target="tpu_custom_call" | custom-call | flops 1048576 | bytes 1572864 | tf_op jit(solution)/shard_map/pallas_call | solution.py:97
  10.7 1.9 %collective-permute-start.11 = (bf16[48,1024]{1,0:T(8,128)(2,1)S(1)}, bf16[48,1024]{1,0:T(8,128)(2,1)S(1)}, u32[]{:S(2)}, u32[]{:S(2)}) collective-permute-start(bf16[48,1024]{1,0:T(8,128)(2,1)S(1)} %get-tuple-element.77), channel_id=1, source_target_pairs={{0,1},{1,0},{2,3},{3,2},{4,5},{5,4},{6,7},{7,6},{8,9},{9,8},{10,11... | collective-permute-start | bytes 294920 | tf_op jit(solution)/shard_map/ppermute | solution.py:56
  12.6 1.3 collective-permute-done.11.other_ref
  13.9 0.0 copy-start.3
  13.9 0.8 copy-done.3
  14.6 0.9 shard_map.104
  15.5 0.0 all-gather.2.cloned.1.call-update
  15.6 0.0 copy-done.4
  15.6 0.0 copy-done.5
  15.6 0.0 copy-done.7
  15.6 125.1 %conditional.2 = (bf16[512,512]{1,0:T(8,128)(2,1)S(1)}, bf16[2,896,512]{2,1,0:T(8,128)(2,1)S(1)}, bf16[16,32,896]{2,1,0:T(8,128)(2,1)}, bf16[2,32,512]{2,1,0:T(8...) conditional(s32[]{:T(128)} %convert_element_type.4, () %tuple.23, ...), branch_computations={%region_0.0_spmd, %region_1.0_spmd} | conditional | flops 471891968 | bytes 28574308 | solution.py:364
  15.6 0.0 copy-start.6
  15.6 8.6 %all-to-all-start = ((bf16[16,144,128]{2,1,0:T(8,128)(2,1)}), bf16[16,144,128]{2,1,0:T(8,128)(2,1)S(1)}, u32[]{:S(2)}, u32[]{:S(2)}) async-start(bf16[16,144,128]{2,1,0:T(8,128)(2,1)} %get-tuple-element.32), calls=%async_computation | async-start | bytes 1179648 | tf_op jit(solution)/shard_map/cond/branch_1_fun/all_to_all | solution.py:377
  24.2 1.9 %collective-permute-start.1 = (bf16[448,512]{1,0:T(8,128)(2,1)}, bf16[448,512]{1,0:T(8,128)(2,1)S(1)}, u32[]{:S(2)}, u32[]{:S(2)}) collective-permute-start(bf16[448,512]{1,0:T(8,128)(2,1)} %get-tuple-element.33.down_ref), channel_id=1, source_target_pairs={{0,1},{1,0},{2,3},{3,2},{4,5},{5,4},{6,7},{7,6},{8,9},{9,8},{10,11... | collective-permute-start | bytes 1376264 | tf_op jit(solution)/shard_map/cond/branch_1_fun/ppermute | solution.py:56
  26.1 15.0 %all-to-all-done.extra_ref.received_ref = bf16[16,144,128]{2,1,0:T(8,128)(2,1)S(1)} async-done(((bf16[16,144,128]{2,1,0:T(8,128)(2,1)}), bf16[16,144,128]{2,1,0:T(8,128)(2,1)S(1)}, u32[]{:S(2)}, u32[]{:S(2)}) %all-to-all-start) | async-done | bytes 589856 | tf_op jit(solution)/shard_map/cond/branch_1_fun/all_to_all | solution.py:377
  41.2 0.7 branch_1_fun.6
  41.9 13.3 %all-to-all-start.1 = ((f32[16,8,128]{2,1,0:T(8,128)}), f32[16,8,128]{2,1,0:T(8,128)S(1)}, u32[]{:S(2)}, u32[]{:S(2)}) async-start(f32[16,8,128]{2,1,0:T(8,128)} %branch_1_fun.6), calls=%async_computation.1 | async-start | bytes 131072 | tf_op jit(solution)/shard_map/cond/branch_1_fun/all_to_all | solution.py:379
  55.1 0.0 collective-permute-done.1.other_ref
  55.2 7.4 %all-to-all-done.1.tile_ref = f32[16,8,128]{2,1,0:T(8,128)S(1)} async-done(((f32[16,8,128]{2,1,0:T(8,128)}), f32[16,8,128]{2,1,0:T(8,128)S(1)}, u32[]{:S(2)}, u32[]{:S(2)}) %all-to-all-start.1) | async-done | bytes 65568 | tf_op jit(solution)/shard_map/cond/branch_1_fun/all_to_all | solution.py:379
  62.5 0.0 copy-done.6
  62.5 2.2 %branch_1_fun.7 = (bf16[16,32,896]{2,1,0:T(8,128)(2,1)S(1)}, bf16[512,512]{1,0:T(8,128)(2,1)S(1)}) custom-call(f32[16,8,128]{2,1,0:T(8,128)S(1)} %all-to-all-done.1.tile_ref, bf16[16,144,128]{2,1,0:T(8,128)(2,1)S(1)} %all-to-all-done.extra_ref.received_ref, bf16[448,512]{1,0:T(8,128)(2,1)S(1)} %copy-done.6, bf16[448,512]{1,0:T(8,128)(2,1)S(1)} %collective-permute-done.1.other_ref), custom_call_target="tpu_custom_call" | custom-call | flops 469762048 | bytes 4194304 | tf_op jit(solution)/shard_map/cond/branch_1_fun/pallas_call | solution.py:196
  64.7 27.4 %all_to_all.21.parts_ref = bf16[16,32,896]{2,1,0:T(8,128)(2,1)S(1)} all-to-all(bf16[16,32,896]{2,1,0:T(8,128)(2,1)S(1)} %get-tuple-element.37), channel_id=1, replica_groups=mesh['xh'=2,'z'=8,'xl'=2,'y'=8,'core'=2] {'xh','z'}, dimensions={0} | all-to-all | bytes 1835008 | tf_op jit(solution)/shard_map/cond/branch_1_fun/all_to_all | solution.py:381
  92.1 1.1 branch_1_fun.9
  93.2 7.6 %all-to-all-start.3 = ((bf16[16,32,896]{2,1,0:T(8,128)(2,1)}), bf16[16,32,896]{2,1,0:T(8,128)(2,1)}, u32[]{:S(2)}, u32[]{:S(2)}) async-start(bf16[16,32,896]{2,1,0:T(8,128)(2,1)} %branch_1_fun.9), calls=%async_computation.3 | async-start | bytes 1835008 | tf_op jit(solution)/shard_map/cond/branch_1_fun/all_to_all | solution.py:389
  100.7 0.1 pad_maximum_fusion
  100.8 1.9 %collective-permute-start.2 = (bf16[2,448,512]{2,1,0:T(8,128)(2,1)S(1)}, bf16[2,448,512]{2,1,0:T(8,128)(2,1)S(1)}, u32[]{:S(2)}, u32[]{:S(2)}) collective-permute-start(bf16[2,448,512]{2,1,0:T(8,128)(2,1)S(1)} %pad_maximum_fusion), channel_id=1, source_target_pairs={{0,1},{1,0},{2,3},{3,2},{4,5},{5,4},{6,7},{7,6},{8,9},{9,8},{10,11... | collective-permute-start | bytes 2752520 | tf_op jit(solution)/shard_map/cond/branch_1_fun/ppermute | solution.py:56
  102.8 2.5 %collective-permute-start.3 = (bf16[32,512]{1,0:T(8,128)(2,1)S(1)}, bf16[32,512]{1,0:T(8,128)(2,1)S(1)}, u32[]{:S(2)}, u32[]{:S(2)}) collective-permute-start(bf16[32,512]{1,0:T(8,128)(2,1)S(1)} %get-tuple-element.99), channel_id=1, source_target_pairs={{0,16},{16,0},{1,17},{17,1},{2,18},{18,2},{3,19},{19,3},{4,20},{20... | collective-permute-start | bytes 98312 | tf_op jit(solution)/shard_map/cond/branch_1_fun/ppermute | solution.py:384
  105.3 3.5 %collective-permute-done.3 = bf16[32,512]{1,0:T(8,128)(2,1)S(1)} collective-permute-done((bf16[32,512]{1,0:T(8,128)(2,1)S(1)}, bf16[32,512]{1,0:T(8,128)(2,1)S(1)}, u32[]{:S(2)}, u32[]{:S(2)}) %collective-permute-start.3) | collective-permute-done | bytes 32800 | tf_op jit(solution)/shard_map/cond/branch_1_fun/ppermute | solution.py:384
  108.7 0.6 pad_maximum_fusion.1
  109.4 1.9 %collective-permute-start.4 = (bf16[2,32,512]{2,1,0:T(8,128)(2,1)}, bf16[2,32,512]{2,1,0:T(8,128)(2,1)}, u32[]{:S(2)}, u32[]{:S(2)}) collective-permute-start(bf16[2,32,512]{2,1,0:T(8,128)(2,1)} %pad_maximum_fusion.1), channel_id=1, source_target_pairs={{2,0},{4,2},{6,4},{8,6},{10,8},{12,10},{14,12},{0,14},{3,1},{5,3},... | collective-permute-start | bytes 196616 | tf_op jit(solution)/shard_map/cond/branch_1_fun/ppermute | solution.py:386
  111.3 5.3 %collective-permute-start.5 = (bf16[2,32,512]{2,1,0:T(8,128)(2,1)}, bf16[2,32,512]{2,1,0:T(8,128)(2,1)}, u32[]{:S(2)}, u32[]{:S(2)}) collective-permute-start(bf16[2,32,512]{2,1,0:T(8,128)(2,1)} %pad_maximum_fusion.1), channel_id=1, source_target_pairs={{4,0},{6,2},{8,4},{10,6},{12,8},{14,10},{0,12},{2,14},{5,1},{7,3},... | collective-permute-start | bytes 196616 | tf_op jit(solution)/shard_map/cond/branch_1_fun/ppermute | solution.py:386
  116.6 4.6 %collective-permute-start.6 = (bf16[2,32,512]{2,1,0:T(8,128)(2,1)}, bf16[2,32,512]{2,1,0:T(8,128)(2,1)}, u32[]{:S(2)}, u32[]{:S(2)}) collective-permute-start(bf16[2,32,512]{2,1,0:T(8,128)(2,1)} %pad_maximum_fusion.1), channel_id=1, source_target_pairs={{6,0},{8,2},{10,4},{12,6},{14,8},{0,10},{2,12},{4,14},{7,1},{9,3},... | collective-permute-start | bytes 196616 | tf_op jit(solution)/shard_map/cond/branch_1_fun/ppermute | solution.py:386
  121.2 3.9 %collective-permute-start.7 = (bf16[2,32,512]{2,1,0:T(8,128)(2,1)}, bf16[2,32,512]{2,1,0:T(8,128)(2,1)}, u32[]{:S(2)}, u32[]{:S(2)}) collective-permute-start(bf16[2,32,512]{2,1,0:T(8,128)(2,1)} %pad_maximum_fusion.1), channel_id=1, source_target_pairs={{8,0},{10,2},{12,4},{14,6},{0,8},{2,10},{4,12},{6,14},{9,1},{11,3}... | collective-permute-start | bytes 196616 | tf_op jit(solution)/shard_map/cond/branch_1_fun/ppermute | solution.py:386
  125.1 0.0 collective-permute-done.4
  125.2 5.8 %collective-permute-start.8 = (bf16[2,32,512]{2,1,0:T(8,128)(2,1)}, bf16[2,32,512]{2,1,0:T(8,128)(2,1)}, u32[]{:S(2)}, u32[]{:S(2)}) collective-permute-start(bf16[2,32,512]{2,1,0:T(8,128)(2,1)} %pad_maximum_fusion.1), channel_id=1, source_target_pairs={{10,0},{12,2},{14,4},{0,6},{2,8},{4,10},{6,12},{8,14},{11,1},{13,3... | collective-permute-start | bytes 196616 | tf_op jit(solution)/shard_map/cond/branch_1_fun/ppermute | solution.py:386
  130.9 0.0 collective-permute-done.5
  131.0 2.8 %collective-permute-start.9 = (bf16[2,32,512]{2,1,0:T(8,128)(2,1)}, bf16[2,32,512]{2,1,0:T(8,128)(2,1)}, u32[]{:S(2)}, u32[]{:S(2)}) collective-permute-start(bf16[2,32,512]{2,1,0:T(8,128)(2,1)} %pad_maximum_fusion.1), channel_id=1, source_target_pairs={{12,0},{14,2},{0,4},{2,6},{4,8},{6,10},{8,12},{10,14},{13,1},{15,3... | collective-permute-start | bytes 196616 | tf_op jit(solution)/shard_map/cond/branch_1_fun/ppermute | solution.py:386
  133.8 0.0 collective-permute-done.2.other_ref
  133.8 2.9 %collective-permute-start.10 = (bf16[2,32,512]{2,1,0:T(8,128)(2,1)}, bf16[2,32,512]{2,1,0:T(8,128)(2,1)}, u32[]{:S(2)}, u32[]{:S(2)}) collective-permute-start(bf16[2,32,512]{2,1,0:T(8,128)(2,1)} %pad_maximum_fusion.1), channel_id=1, source_target_pairs={{14,0},{0,2},{2,4},{4,6},{6,8},{8,10},{10,12},{12,14},{15,1},{1,3}... | collective-permute-start | bytes 196616 | tf_op jit(solution)/shard_map/cond/branch_1_fun/ppermute | solution.py:386
  136.7 0.7 branch_1_fun.8
  137.4 0.0 collective-permute-done.6
  137.4 0.0 collective-permute-done.7
  137.4 0.0 collective-permute-done.8
  137.4 2.7 %collective-permute-done.9 = bf16[2,32,512]{2,1,0:T(8,128)(2,1)} collective-permute-done((bf16[2,32,512]{2,1,0:T(8,128)(2,1)}, bf16[2,32,512]{2,1,0:T(8,128)(2,1)}, u32[]{:S(2)}, u32[]{:S(2)}) %collective-permute-start.9) | collective-permute-done | bytes 65568 | tf_op jit(solution)/shard_map/cond/branch_1_fun/ppermute | solution.py:386
  140.1 0.5 collective-permute-done.10
  140.7 0.0 all-to-all-done.3
  140.7 0.0 all-gather.2.cloned.1.call-done.pre_ref
  140.7 1.5 copy-done
  142.2 4.9 %shard_map.105 = (bf16[16,32,512]{2,1,0:T(8,128)(2,1)}, bf16[3,512,896]{2,1,0:T(8,128)(2,1)}) custom-call(bf16[16,32,896]{2,1,0:T(8,128)(2,1)} %get-tuple-element.80.hid_ref, bf16[512,1792]{1,0:T(8,128)(2,1)S(1)} %copy-done, bf16[2,896,512]{2,1,0:T(8,128)(2,1)S(1)} %get-tuple-element.82.quant_ref), custom_call_target="tpu_custom_call" | custom-call | flops 939524096 | bytes 8388608 | tf_op jit(solution)/shard_map/pallas_call | solution.py:270
  147.1 6.2 %all-to-all-start.4 = ((bf16[16,32,512]{2,1,0:T(8,128)(2,1)}), bf16[16,32,512]{2,1,0:T(8,128)(2,1)S(1)}, u32[]{:S(2)}, u32[]{:S(2)}) async-start(bf16[16,32,512]{2,1,0:T(8,128)(2,1)} %get-tuple-element.83), calls=%async_computation.4 | async-start | bytes 1048576 | tf_op jit(solution)/shard_map/all_to_all | solution.py:397
  153.3 0.1 pad_add_fusion
  153.4 9.9 %conditional.3 = ((bf16[448,512]{1,0:T(8,128)(2,1)}, bf16[448,512]{1,0:T(8,128)(2,1)}, bf16[448,512]{1,0:T(8,128)(2,1)}, f32[8,128]{1,0:T(8,128)S(1)})) conditional(s32[]{:T(128)} %convert_element_type.4, () %tuple.25, (s32[2]{0:T(128)S(1)}, bf16[3,512,896]{2,1,0:T(8,128)(2,1)}, bf16[512,512]{1,0:T(8,128)(2,1)S(1)}, bf16[2,32,512]{2,1,0:T(8,128)(2,1)}, ...), branch_computations={%region_2.0_spmd, %region_3.0_spmd} | conditional | flops 1410334720 | bytes 19136560 | solution.py:364
  153.4 3.6 %branch_1_fun.10 = (f32[3,448,512]{2,1,0:T(8,128)S(1)}, bf16[3,448,512]{2,1,0:T(8,128)(2,1)S(1)}) custom-call(s32[2]{0:T(128)S(1)} %get-tuple-element.39.place_ref, bf16[3,512,896]{2,1,0:T(8,128)(2,1)} %get-tuple-element.40.acts_ref, bf16[512,512]{1,0:T(8,128)(2,1)S(1)} %get-tuple-element.41.out_ref, bf16[2,32,512]{2,1,0:T(8,128)(2,1)} %get-tuple-element.42.refs_0_, ...), custom_call_target="tpu_custom_call" | custom-call | flops 1409286144 | bytes 8388608 | tf_op jit(solution)/shard_map/cond/branch_1_fun/pallas_call | solution.py:309
  157.0 1.9 %collective-permute-start = (bf16[3,448,512]{2,1,0:T(8,128)(2,1)S(1)}, bf16[3,448,512]{2,1,0:T(8,128)(2,1)S(1)}, u32[]{:S(2)}, u32[]{:S(2)}) collective-permute-start(bf16[3,448,512]{2,1,0:T(8,128)(2,1)S(1)} %get-tuple-element.51), channel_id=1, source_target_pairs={{0,1},{1,0},{2,3},{3,2},{4,5},{5,4},{6,7},{7,6},{8,9},{9,8},{10,11... | collective-permute-start | bytes 4128776 | tf_op jit(solution)/shard_map/cond/branch_1_fun/ppermute | solution.py:56
  158.9 3.1 %collective-permute-done.other_ref = bf16[3,448,512]{2,1,0:T(8,128)(2,1)S(1)} collective-permute-done((bf16[3,448,512]{2,1,0:T(8,128)(2,1)S(1)}, bf16[3,448,512]{2,1,0:T(8,128)(2,1)S(1)}, u32[]{:S(2)}, u32[]{:S(2)}) %collective-permute-start) | collective-permute-done | bytes 1376288 | tf_op jit(solution)/shard_map/cond/branch_1_fun/ppermute | solution.py:56
  162.0 1.2 branch_1_fun.11
  163.2 4.6 %all-to-all-done.4.parts_ref = bf16[16,32,512]{2,1,0:T(8,128)(2,1)S(1)} async-done(((bf16[16,32,512]{2,1,0:T(8,128)(2,1)}), bf16[16,32,512]{2,1,0:T(8,128)(2,1)S(1)}, u32[]{:S(2)}, u32[]{:S(2)}) %all-to-all-start.4) | async-done | bytes 524320 | tf_op jit(solution)/shard_map/all_to_all | solution.py:397
  167.8 0.7 shard_map.106
  (3 shorter events, 0.0 us)
Async XLA Ops:
  7.2 133.5 %all-gather.2.cloned.1.call-start = ((), (), s32[]{:S(2)}) async-start(), calls=%async_computation.5 | async-start | bytes 1949696 | tf_op jit(solution)/shard_map/all_gather | solution.py:374
  7.2 0.8 copy-start.1
  8.1 0.8 copy-start.2
  8.9 6.7 %copy-start.4 = (bf16[512,448]{0,1:T(8,128)(2,1)S(1)}, bf16[512,448]{0,1:T(8,128)(2,1)}, u32[]{:S(2)}) copy-start(bf16[512,448]{0,1:T(8,128)(2,1)} %param.15) | copy-start | bytes 1376260
  8.9 6.7 %copy-start.5 = (bf16[512,448]{0,1:T(8,128)(2,1)S(1)}, bf16[512,448]{0,1:T(8,128)(2,1)}, u32[]{:S(2)}) copy-start(bf16[512,448]{0,1:T(8,128)(2,1)} %param.16) | copy-start | bytes 1376260
  8.9 6.7 %copy-start.7 = (bf16[32,512]{1,0:T(8,128)(2,1)S(1)}, bf16[32,512]{1,0:T(8,128)(2,1)}, u32[]{:S(2)}) copy-start(bf16[32,512]{1,0:T(8,128)(2,1)} %param.11) | copy-start | bytes 98308
  10.7 3.2 %collective-permute-start.11 = (bf16[48,1024]{1,0:T(8,128)(2,1)S(1)}, bf16[48,1024]{1,0:T(8,128)(2,1)S(1)}, u32[]{:S(2)}, u32[]{:S(2)}) collective-permute-start(bf16[48,1024]{1,0:T(8,128)(2,1)S(1)} %get-tuple-element.77), channel_id=1, source_target_pairs={{0,1},{1,0},{2,3},{3,2},{4,5},{5,4},{6,7},{7,6},{8,9},{9,8},{10,11... | collective-permute-start | bytes 294920 | tf_op jit(solution)/shard_map/ppermute | solution.py:56
  13.9 0.8 copy-start.3
  15.6 46.9 %copy-start.6 = (bf16[448,512]{1,0:T(8,128)(2,1)S(1)}, bf16[448,512]{1,0:T(8,128)(2,1)}, u32[]{:S(2)}) copy-start(bf16[448,512]{1,0:T(8,128)(2,1)} %get-tuple-element.33.down_ref) | copy-start | bytes 1376260 | tf_op jit(solution)/shard_map/cond
  15.6 25.6 %all-to-all-start = ((bf16[16,144,128]{2,1,0:T(8,128)(2,1)}), bf16[16,144,128]{2,1,0:T(8,128)(2,1)S(1)}, u32[]{:S(2)}, u32[]{:S(2)}) async-start(bf16[16,144,128]{2,1,0:T(8,128)(2,1)} %get-tuple-element.32), calls=%async_computation | async-start | bytes 1179648 | tf_op jit(solution)/shard_map/cond/branch_1_fun/all_to_all | solution.py:377
  24.2 30.9 %collective-permute-start.1 = (bf16[448,512]{1,0:T(8,128)(2,1)}, bf16[448,512]{1,0:T(8,128)(2,1)S(1)}, u32[]{:S(2)}, u32[]{:S(2)}) collective-permute-start(bf16[448,512]{1,0:T(8,128)(2,1)} %get-tuple-element.33.down_ref), channel_id=1, source_target_pairs={{0,1},{1,0},{2,3},{3,2},{4,5},{5,4},{6,7},{7,6},{8,9},{9,8},{10,11... | collective-permute-start | bytes 1376264 | tf_op jit(solution)/shard_map/cond/branch_1_fun/ppermute | solution.py:56
  41.9 20.7 %all-to-all-start.1 = ((f32[16,8,128]{2,1,0:T(8,128)}), f32[16,8,128]{2,1,0:T(8,128)S(1)}, u32[]{:S(2)}, u32[]{:S(2)}) async-start(f32[16,8,128]{2,1,0:T(8,128)} %branch_1_fun.6), calls=%async_computation.1 | async-start | bytes 131072 | tf_op jit(solution)/shard_map/cond/branch_1_fun/all_to_all | solution.py:379
  93.2 47.5 %all-to-all-start.3 = ((bf16[16,32,896]{2,1,0:T(8,128)(2,1)}), bf16[16,32,896]{2,1,0:T(8,128)(2,1)}, u32[]{:S(2)}, u32[]{:S(2)}) async-start(bf16[16,32,896]{2,1,0:T(8,128)(2,1)} %branch_1_fun.9), calls=%async_computation.3 | async-start | bytes 1835008 | tf_op jit(solution)/shard_map/cond/branch_1_fun/all_to_all | solution.py:389
  100.8 32.9 %collective-permute-start.2 = (bf16[2,448,512]{2,1,0:T(8,128)(2,1)S(1)}, bf16[2,448,512]{2,1,0:T(8,128)(2,1)S(1)}, u32[]{:S(2)}, u32[]{:S(2)}) collective-permute-start(bf16[2,448,512]{2,1,0:T(8,128)(2,1)S(1)} %pad_maximum_fusion), channel_id=1, source_target_pairs={{0,1},{1,0},{2,3},{3,2},{4,5},{5,4},{6,7},{7,6},{8,9},{9,8},{10,11... | collective-permute-start | bytes 2752520 | tf_op jit(solution)/shard_map/cond/branch_1_fun/ppermute | solution.py:56
  102.8 6.0 %collective-permute-start.3 = (bf16[32,512]{1,0:T(8,128)(2,1)S(1)}, bf16[32,512]{1,0:T(8,128)(2,1)S(1)}, u32[]{:S(2)}, u32[]{:S(2)}) collective-permute-start(bf16[32,512]{1,0:T(8,128)(2,1)S(1)} %get-tuple-element.99), channel_id=1, source_target_pairs={{0,16},{16,0},{1,17},{17,1},{2,18},{18,2},{3,19},{19,3},{4,20},{20... | collective-permute-start | bytes 98312 | tf_op jit(solution)/shard_map/cond/branch_1_fun/ppermute | solution.py:384
  109.4 15.8 %collective-permute-start.4 = (bf16[2,32,512]{2,1,0:T(8,128)(2,1)}, bf16[2,32,512]{2,1,0:T(8,128)(2,1)}, u32[]{:S(2)}, u32[]{:S(2)}) collective-permute-start(bf16[2,32,512]{2,1,0:T(8,128)(2,1)} %pad_maximum_fusion.1), channel_id=1, source_target_pairs={{2,0},{4,2},{6,4},{8,6},{10,8},{12,10},{14,12},{0,14},{3,1},{5,3},... | collective-permute-start | bytes 196616 | tf_op jit(solution)/shard_map/cond/branch_1_fun/ppermute | solution.py:386
  111.3 19.7 %collective-permute-start.5 = (bf16[2,32,512]{2,1,0:T(8,128)(2,1)}, bf16[2,32,512]{2,1,0:T(8,128)(2,1)}, u32[]{:S(2)}, u32[]{:S(2)}) collective-permute-start(bf16[2,32,512]{2,1,0:T(8,128)(2,1)} %pad_maximum_fusion.1), channel_id=1, source_target_pairs={{4,0},{6,2},{8,4},{10,6},{12,8},{14,10},{0,12},{2,14},{5,1},{7,3},... | collective-permute-start | bytes 196616 | tf_op jit(solution)/shard_map/cond/branch_1_fun/ppermute | solution.py:386
  116.6 20.8 %collective-permute-start.6 = (bf16[2,32,512]{2,1,0:T(8,128)(2,1)}, bf16[2,32,512]{2,1,0:T(8,128)(2,1)}, u32[]{:S(2)}, u32[]{:S(2)}) collective-permute-start(bf16[2,32,512]{2,1,0:T(8,128)(2,1)} %pad_maximum_fusion.1), channel_id=1, source_target_pairs={{6,0},{8,2},{10,4},{12,6},{14,8},{0,10},{2,12},{4,14},{7,1},{9,3},... | collective-permute-start | bytes 196616 | tf_op jit(solution)/shard_map/cond/branch_1_fun/ppermute | solution.py:386
  121.2 16.1 %collective-permute-start.7 = (bf16[2,32,512]{2,1,0:T(8,128)(2,1)}, bf16[2,32,512]{2,1,0:T(8,128)(2,1)}, u32[]{:S(2)}, u32[]{:S(2)}) collective-permute-start(bf16[2,32,512]{2,1,0:T(8,128)(2,1)} %pad_maximum_fusion.1), channel_id=1, source_target_pairs={{8,0},{10,2},{12,4},{14,6},{0,8},{2,10},{4,12},{6,14},{9,1},{11,3}... | collective-permute-start | bytes 196616 | tf_op jit(solution)/shard_map/cond/branch_1_fun/ppermute | solution.py:386
  125.2 12.2 %collective-permute-start.8 = (bf16[2,32,512]{2,1,0:T(8,128)(2,1)}, bf16[2,32,512]{2,1,0:T(8,128)(2,1)}, u32[]{:S(2)}, u32[]{:S(2)}) collective-permute-start(bf16[2,32,512]{2,1,0:T(8,128)(2,1)} %pad_maximum_fusion.1), channel_id=1, source_target_pairs={{10,0},{12,2},{14,4},{0,6},{2,8},{4,10},{6,12},{8,14},{11,1},{13,3... | collective-permute-start | bytes 196616 | tf_op jit(solution)/shard_map/cond/branch_1_fun/ppermute | solution.py:386
  131.0 9.1 %collective-permute-start.9 = (bf16[2,32,512]{2,1,0:T(8,128)(2,1)}, bf16[2,32,512]{2,1,0:T(8,128)(2,1)}, u32[]{:S(2)}, u32[]{:S(2)}) collective-permute-start(bf16[2,32,512]{2,1,0:T(8,128)(2,1)} %pad_maximum_fusion.1), channel_id=1, source_target_pairs={{12,0},{14,2},{0,4},{2,6},{4,8},{6,10},{8,12},{10,14},{13,1},{15,3... | collective-permute-start | bytes 196616 | tf_op jit(solution)/shard_map/cond/branch_1_fun/ppermute | solution.py:386
  133.8 6.9 %collective-permute-start.10 = (bf16[2,32,512]{2,1,0:T(8,128)(2,1)}, bf16[2,32,512]{2,1,0:T(8,128)(2,1)}, u32[]{:S(2)}, u32[]{:S(2)}) collective-permute-start(bf16[2,32,512]{2,1,0:T(8,128)(2,1)} %pad_maximum_fusion.1), channel_id=1, source_target_pairs={{14,0},{0,2},{2,4},{4,6},{6,8},{8,10},{10,12},{12,14},{15,1},{1,3}... | collective-permute-start | bytes 196616 | tf_op jit(solution)/shard_map/cond/branch_1_fun/ppermute | solution.py:386
  140.7 1.5 copy-start
  147.1 20.8 %all-to-all-start.4 = ((bf16[16,32,512]{2,1,0:T(8,128)(2,1)}), bf16[16,32,512]{2,1,0:T(8,128)(2,1)S(1)}, u32[]{:S(2)}, u32[]{:S(2)}) async-start(bf16[16,32,512]{2,1,0:T(8,128)(2,1)} %get-tuple-element.83), calls=%async_computation.4 | async-start | bytes 1048576 | tf_op jit(solution)/shard_map/all_to_all | solution.py:397
  157.0 5.0 %collective-permute-start = (bf16[3,448,512]{2,1,0:T(8,128)(2,1)S(1)}, bf16[3,448,512]{2,1,0:T(8,128)(2,1)S(1)}, u32[]{:S(2)}, u32[]{:S(2)}) collective-permute-start(bf16[3,448,512]{2,1,0:T(8,128)(2,1)S(1)} %get-tuple-element.51), channel_id=1, source_target_pairs={{0,1},{1,0},{2,3},{3,2},{4,5},{5,4},{6,7},{7,6},{8,9},{9,8},{10,11... | collective-permute-start | bytes 4128776 | tf_op jit(solution)/shard_map/cond/branch_1_fun/ppermute | solution.py:56
Sparse Core Ops, SparseCore 0:
  15.7 106.0 all-gather.1

commit v5 on v4

--- a/solution.py
+++ b/solution.py
@@ -16,6 +16,7 @@
 LANES = 128
 VMEM = pl.BlockSpec(memory_space=pltpu.VMEM)
 SMEM = pl.BlockSpec(memory_space=pltpu.SMEM)
+WIDE = pltpu.CompilerParams(vmem_limit_bytes=58 * 1024 * 1024)
 PARAMS = pltpu.CompilerParams(vmem_limit_bytes=40 * 1024 * 1024)
 
 
@@ -102,7 +103,7 @@
         ),
         in_specs=[SMEM] + [VMEM] * 5,
         out_specs=(VMEM, VMEM),
-        compiler_params=PARAMS,
+        compiler_params=WIDE,
         cost_estimate=cost(1 << 20, 3 << 19),
     )(core, gate_pre, up_pre, gate_t, up_t, down)
 
@@ -138,7 +139,7 @@
         ),
         in_specs=[SMEM] + [VMEM] * 5,
         out_specs=(VMEM, VMEM),
-        compiler_params=PARAMS,
+        compiler_params=WIDE,
         cost_estimate=cost(1 << 16, 1 << 20),
     )(core, gate_pre, up_pre, other, sums, grad_out)
 
@@ -171,7 +172,7 @@
     return jnp.clip(values.astype(jnp.float32), -scale, scale).astype(jnp.bfloat16)
 
 
-def partial_kernel(tile_ref, received_ref, down_ref, other_ref, partial_ref, out_ref, quant_ref):
+def partial_kernel(tile_ref, received_ref, down_ref, other_ref, partial_ref, out_ref, done_ref, quant_ref):
     rows = partial_ref.shape[1]
     inner, width = down_ref.shape
 
@@ -184,6 +185,7 @@
     blocks = [received_ref[:, j * rows : (j + 1) * rows, :] for j in range(width // LANES)]
     out_rows = jnp.concatenate([block.reshape((-1, LANES)) for block in blocks], axis=1)
     out_ref[...] = out_rows
+    done_ref[...] = jnp.zeros(done_ref.shape, jnp.float32)
     partial = contract_last(out_rows, quant_ref[...])
     partial_ref[...] = partial.astype(jnp.bfloat16).reshape(partial_ref.shape)
 
@@ -199,6 +201,7 @@
         out_shape=(
             jax.ShapeDtypeStruct((N_ROW, rows, 2 * inner), jnp.bfloat16),
             jax.ShapeDtypeStruct((N_CHIP * rows, width), jnp.bfloat16),
+            jax.ShapeDtypeStruct((8, LANES), jnp.float32),
         ),
         in_specs=[
             pl.BlockSpec(tile.shape, lambda i: (0, 0, 0)),
@@ -209,6 +212,7 @@
         out_specs=(
             pl.BlockSpec((blocks, rows, 2 * inner), lambda i: (i, 0, 0)),
             pl.BlockSpec((blocks * rows, width), lambda i: (i, 0)),
+            pl.BlockSpec((8, LANES), lambda i: (0, 0)),
         ),
         scratch_shapes=[pltpu.VMEM((2 * inner, width), jnp.bfloat16)],
         compiler_params=PARAMS,
@@ -216,21 +220,21 @@
     )(tile, received, down, other)
 
 
-def spread_kernel(parts_ref, sent_ref):
+def spread_kernel(parts_ref, after_ref, sent_ref):
     total = jnp.sum(parts_ref[...].astype(jnp.float32), axis=0).astype(jnp.bfloat16)
     for k in range(N_ROW):
         sent_ref[k] = total
 
 
-def spread(parts):
+def spread(parts, after):
     return pl.pallas_call(
         spread_kernel,
         out_shape=jax.ShapeDtypeStruct(parts.shape, jnp.bfloat16),
-        in_specs=[VMEM],
+        in_specs=[VMEM] * 2,
         out_specs=VMEM,
         compiler_params=PARAMS,
         cost_estimate=cost(1 << 19, 2 << 20),
-    )(parts)
+    )(parts, after)
 
 
 def clip_kernel(tile_ref, gate_ref, up_ref, other_ref, quant_ref):
@@ -283,19 +287,18 @@
             pl.BlockSpec((blocks, rows, width), lambda i: (i, 0, 0)),
             pl.BlockSpec((3, blocks * rows, both), lambda i: (0, i, 0)),
         ),
-        compiler_params=PARAMS,
+        compiler_params=WIDE,
         cost_estimate=cost(4 * 512 * 896 * 512, 8 << 20),
     )(grad_hidden, pre_half, quant)
 
 
-def latent_grads_kernel(place_ref, acts_ref, out_ref, *refs):
-    token_refs, (own_ref, sent_ref, rows_ref) = refs[:N_Y], refs[N_Y:]
-    rows = token_refs[0].shape[1]
-    for shift, ref in enumerate(token_refs):
-        y = lax.rem(place_ref[1] + shift, N_Y)
-        for flip in range(2):
-            chip = lax.rem(place_ref[0] + flip, 2) * N_Y + y
-            rows_ref[pl.ds(pl.multiple_of(chip * rows, rows), rows), :] = ref[flip]
+def latent_grads_kernel(place_ref, acts_ref, out_ref, tokens_ref, own_ref, sent_ref, rows_ref):
+    rows = tokens_ref.shape[1]
+    for block in range(2 * N_Y):
+        flip, bits = block // N_Y, block % N_Y
+        offset = 4 * (bits & 1) + (bits & 2) + bits // 4
+        chip = (place_ref[0] ^ flip) * N_Y + (place_ref[1] ^ offset)
+        rows_ref[pl.ds(pl.multiple_of(chip * rows, rows), rows), :] = tokens_ref[block]
     inner = own_ref.shape[1]
     for n in range(3):
         half = out_ref[...] if n == 2 else rows_ref[...]
@@ -312,12 +315,12 @@
             jax.ShapeDtypeStruct((3, inner, width), jnp.float32),
             jax.ShapeDtypeStruct((3, inner, width), jnp.bfloat16),
         ),
-        in_specs=[SMEM] + [VMEM] * (2 + N_Y),
+        in_specs=[SMEM] + [VMEM] * 3,
         out_specs=(VMEM, VMEM),
         scratch_shapes=[pltpu.VMEM(out_half.shape, jnp.bfloat16)],
         compiler_params=PARAMS,
         cost_estimate=cost(6 * 512 * 896 * 512, 8 << 20),
-    )(place, acts, out_half, *token_blocks)
+    )(place, acts, out_half, token_blocks)
 
 
 def join_kernel(own_ref, other_ref, *refs):
@@ -353,6 +356,33 @@
     )(parts, after)
 
 
+def doubled(blocks, axis, step):
+    count = 2 if axis == "xl" else N_Y
+    other = lax.ppermute(blocks, axis, [(k, k ^ step) for k in range(count)])
+    return jnp.concatenate([blocks, other], axis=0)
+
+
+def copy_kernel(values_ref, after_ref, copy_ref):
+    copy_ref[...] = values_ref[...]
+
+
+def copy_after(values, after):
+    return pl.pallas_call(
+        copy_kernel,
+        out_shape=jax.ShapeDtypeStruct(values.shape, values.dtype),
+        in_specs=[VMEM] * 2,
+        out_specs=VMEM,
+        cost_estimate=cost(1, 1 << 16),
+    )(values, after)
+
+
+def tokens_along_y(tokens, done):
+    blocks = copy_after(tokens, done)[None]
+    for step in (4, 2, 1):
+        blocks = doubled(blocks, "y", step)
+    return blocks, blocks[-1, :EXTRA, :LANES]
+
+
 def in_branch(work, *operands):
     def nothing(*operands):
         shapes = jax.eval_shape(work, *operands)
@@ -377,30 +407,27 @@
         received = lax.all_to_all(sent, CHIP, 0, 0)
         down_other = swapped(down)
         tile = lax.all_to_all(sums_tile(received), ROW, 0, 0)
-        partial, out_half = hidden_partial(tile, received, down, down_other)
+        partial, out_half, done = hidden_partial(tile, received, down, down_other)
         parts = lax.all_to_all(partial, ROW, 0, 0)
+        near_tokens, after = in_branch(tokens_along_y, tokens, done)
         other_latents = swapped(jnp.stack([gate_t, up_t]))
         quant = clipped_latents(tile, gate_t, up_t, other_latents)
-        pair = jnp.stack([tokens, lax.ppermute(tokens, "xl", [(0, 1), (1, 0)])])
-        token_blocks = [pair] + [
-            lax.ppermute(pair, "y", [((y + shift) % N_Y, y) for y in range(N_Y)])
-            for shift in range(1, N_Y)
-        ]
-        grad_hidden = lax.all_to_all(spread(parts), ROW, 0, 0)
-        return (out_half, quant, grad_hidden) + tuple(token_blocks)
-
-    out_half, quant, grad_hidden, *token_blocks = in_branch(
+        token_blocks = doubled(near_tokens, "xl", 1)
+        grad_hidden = lax.all_to_all(spread(parts, after), ROW, 0, 0)
+        return (out_half, quant, grad_hidden, token_blocks)
+
+    out_half, quant, grad_hidden, token_blocks = in_branch(
         exchanges, sent, tokens, gate_t, up_t, down_latent
     )
 
     partial, acts = act_partial(grad_hidden, pre_half, quant)
     parts = lax.all_to_all(partial, CHIP, 0, 0)
 
-    def joined(place, acts, out_half, *token_blocks):
+    def joined(place, acts, out_half, token_blocks):
         own, sent = latent_grads(place, acts, out_half, token_blocks)
         return join(own, swapped(sent))
 
-    grad_gate, grad_up, grad_down, done = in_branch(joined, place, acts, out_half, *token_blocks)
+    grad_gate, grad_up, grad_down, done = in_branch(joined, place, acts, out_half, token_blocks)
     grad_tokens = total(parts, done)
     return (grad_tokens, grad_gate.T, grad_up.T, grad_down)
 

time: 176 us -> 165 us (0.938)
  the two profiles are of different devices: /device:TPU:14 before, /device:TPU:74 now
where the time goes in v5:
time: 165 us; the launch traced here: 164 us
  waiting for transfers between devices  63.2 us (38%)
  starting transfers between devices  61 us (37%)
  Pallas kernels  21.4 us (13%)
  between operations  14.1 us (9%)
  other arithmetic  3.33 us (2%)
    ppermute x4, waiting for transfers between devices, doubled(): other = lax.ppermute(blocks, axis, [(k, k ^ step) for k in range(count)])  27.8 us
    all_to_all x1, waiting for transfers between devices, exchanges(): received = lax.all_to_all(sent, CHIP, 0, 0)  15 us
    ppermute x4, starting transfers between devices, doubled(): other = lax.ppermute(blocks, axis, [(k, k ^ step) for k in range(count)])  12 us
    all_to_all x1, starting transfers between devices, exchanges(): tile = lax.all_to_all(sums_tile(received), ROW, 0, 0)  11.5 us
    all_to_all x1, starting transfers between devices, exchanges(): grad_hidden = lax.all_to_all(spread(parts, after), ROW, 0, 0)  9.7 us
    all_to_all x1, waiting for transfers between devices, exchanges(): tile = lax.all_to_all(sums_tile(received), ROW, 0, 0)  9.14 us
    all_to_all x1, starting transfers between devices, exchanges(): received = lax.all_to_all(sent, CHIP, 0, 0)  8.48 us
    ppermute x4, starting transfers between devices, swapped(): return lax.ppermute(values, 'core', [(0, 1), (1, 0)])  7.66 us
  transfers between devices with their start and end apart: 14, of which 10 were waited for; matrix products, arithmetic and copies ran while one was open for 2% of the time, Pallas kernels for 7%

profile of v5, /device:TPU:74, one launch (start us, length us, event | category | flops | bytes accessed | tf_op | source)
XLA Modules:
  0.0 163.8 jit_solution(6187323208965171361)
XLA Ops:
  7.2 0.0 copy-start
  7.2 0.0 copy-start.1
  7.2 0.0 copy-start.2
  7.2 0.0 copy-start.4
  7.2 0.0 all-gather.2.cloned.1.call-start
  7.3 2.5 %shard_map.103 = (bf16[48,1024]{1,0:T(8,128)(2,1)}, f32[8,128]{1,0:T(8,128)}) custom-call(s32[1]{0:T(128)} %bitcast.4.core_ref, bf16[64,448]{1,0:T(8,128)(2,1)} %gate_pre_ref.3, bf16[64,448]{1,0:T(8,128)(2,1)} %up_pre_ref.3, bf16[448,512]{1,0:T(8,128)(2,1)} %bitcast.12, bf16[448,512]{1,0:T(8,128)(2,1)} %bitcast.15, bf16[448,512]{1,0:T(8,128)(2,1)} %down_ref.1), custom_call_target="tpu_custom_call" | custom-call | flops 1048576 | bytes 1572864 | tf_op jit(solution)/shard_map/pallas_call | solution.py:98
  9.7 1.9 %collective-permute-start.7 = (bf16[48,1024]{1,0:T(8,128)(2,1)}, bf16[48,1024]{1,0:T(8,128)(2,1)S(1)}, u32[]{:S(2)}, u32[]{:S(2)}) collective-permute-start(bf16[48,1024]{1,0:T(8,128)(2,1)} %get-tuple-element.58), channel_id=1, source_target_pairs={{0,1},{1,0},{2,3},{3,2},{4,5},{5,4},{6,7},{7,6},{8,9},{9,8},{10,11... | collective-permute-start | bytes 294920 | tf_op jit(solution)/shard_map/ppermute | solution.py:57
  11.6 1.5 collective-permute-done.7.other_ref
  13.1 0.0 copy-start.3
  13.1 0.6 copy-done.3
  13.8 1.9 %shard_map.104 = (bf16[32,1792]{1,0:T(8,128)(2,1)}, bf16[16,144,128]{2,1,0:T(8,128)(2,1)}) custom-call(s32[1]{0:T(128)} %bitcast.4.core_ref, bf16[64,448]{1,0:T(8,128)(2,1)} %gate_pre_ref.3, bf16[64,448]{1,0:T(8,128)(2,1)} %up_pre_ref.3, bf16[48,1024]{1,0:T(8,128)(2,1)} %copy-done.3, f32[8,128]{1,0:T(8,128)} %get-tuple-element.59.sums_ref, ...), custom_call_target="tpu_custom_call" | custom-call | flops 65536 | bytes 1048576 | tf_op jit(solution)/shard_map/pallas_call | solution.py:134
  15.7 0.0 all-gather.2.cloned.1.call-update
  15.7 0.0 copy-done
  15.7 0.0 copy-done.1
  15.7 0.0 copy-done.2
  15.7 0.0 copy-done.4
  15.7 114.0 %conditional.3 = (bf16[512,512]{1,0:T(8,128)(2,1)}, bf16[2,896,512]{2,1,0:T(8,128)(2,1)S(1)}, bf16[16,32,896]{2,1,0:T(8,128)(2,1)}, bf16[16,32,512]{2,1,0:T(8,128)(2,1)}) conditional(s32[]{:T(128)} %convert_element_type.7, () %tuple.31, (bf16[16,144,128]{2,1,0:T(8,128)(2,1)}, bf16[448,512]{1,0:T(8,128)(2,1)S(1)}, bf16[448,512]{1,0:T(8,128)(2,1)S(1)}, ...), branch_computations={%region_0.0_spmd, %region_1.0_spmd} | conditional | flops 472678400 | bytes 29565404 | solution.py:394
  15.7 8.5 %all-to-all-start = ((bf16[16,144,128]{2,1,0:T(8,128)(2,1)}), bf16[16,144,128]{2,1,0:T(8,128)(2,1)S(1)}, u32[]{:S(2)}, u32[]{:S(2)}) async-start(bf16[16,144,128]{2,1,0:T(8,128)(2,1)} %get-tuple-element.24), calls=%async_computation | async-start | bytes 1179648 | tf_op jit(solution)/shard_map/cond/branch_1_fun/all_to_all | solution.py:407
  24.2 1.9 %collective-permute-start.4 = (bf16[448,512]{1,0:T(8,128)(2,1)S(1)}, bf16[448,512]{1,0:T(8,128)(2,1)S(1)}, u32[]{:S(2)}, u32[]{:S(2)}) collective-permute-start(bf16[448,512]{1,0:T(8,128)(2,1)S(1)} %get-tuple-element.25.down_ref), channel_id=1, source_target_pairs={{0,1},{1,0},{2,3},{3,2},{4,5},{5,4},{6,7},{7,6},{8,9},{9,8},{10,11... | collective-permute-start | bytes 1376264 | tf_op jit(solution)/shard_map/cond/branch_1_fun/ppermute | solution.py:57
  26.1 15.0 %all-to-all-done.extra_ref.received_ref = bf16[16,144,128]{2,1,0:T(8,128)(2,1)S(1)} async-done(((bf16[16,144,128]{2,1,0:T(8,128)(2,1)}), bf16[16,144,128]{2,1,0:T(8,128)(2,1)S(1)}, u32[]{:S(2)}, u32[]{:S(2)}) %all-to-all-start) | async-done | bytes 589856 | tf_op jit(solution)/shard_map/cond/branch_1_fun/all_to_all | solution.py:407
  41.2 0.7 branch_1_fun.8
  41.8 11.5 %all-to-all-start.1 = ((f32[16,8,128]{2,1,0:T(8,128)}), f32[16,8,128]{2,1,0:T(8,128)S(1)}, u32[]{:S(2)}, u32[]{:S(2)}) async-start(f32[16,8,128]{2,1,0:T(8,128)} %branch_1_fun.8), calls=%async_computation.1 | async-start | bytes 131072 | tf_op jit(solution)/shard_map/cond/branch_1_fun/all_to_all | solution.py:409
  53.4 0.0 collective-permute-done.4.other_ref
  53.4 9.1 %all-to-all-done.1.tile_ref = f32[16,8,128]{2,1,0:T(8,128)S(1)} async-done(((f32[16,8,128]{2,1,0:T(8,128)}), f32[16,8,128]{2,1,0:T(8,128)S(1)}, u32[]{:S(2)}, u32[]{:S(2)}) %all-to-all-start.1) | async-done | bytes 65568 | tf_op jit(solution)/shard_map/cond/branch_1_fun/all_to_all | solution.py:409
  62.5 3.1 %branch_1_fun.9 = (bf16[16,32,896]{2,1,0:T(8,128)(2,1)}, bf16[512,512]{1,0:T(8,128)(2,1)}, f32[8,128]{1,0:T(8,128)S(1)}) custom-call(f32[16,8,128]{2,1,0:T(8,128)S(1)} %all-to-all-done.1.tile_ref, bf16[16,144,128]{2,1,0:T(8,128)(2,1)S(1)} %all-to-all-done.extra_ref.received_ref, bf16[448,512]{1,0:T(8,128)(2,1)S(1)} %get-tuple-element.25.down_ref, ...), custom_call_target="tpu_custom_call" | custom-call | flops 469762048 | bytes 4194304 | tf_op jit(solution)/shard_map/cond/branch_1_fun/pallas_call | solution.py:198
  65.6 4.4 %all-to-all-start.2 = ((bf16[16,32,896]{2,1,0:T(8,128)(2,1)}), bf16[16,32,896]{2,1,0:T(8,128)(2,1)S(1)}, u32[]{:S(2)}, u32[]{:S(2)}) async-start(bf16[16,32,896]{2,1,0:T(8,128)(2,1)} %get-tuple-element.29), calls=%async_computation.2 | async-start | bytes 1835008 | tf_op jit(solution)/shard_map/cond/branch_1_fun/all_to_all | solution.py:411
  70.1 26.8 %conditional = (bf16[8,32,512]{2,1,0:T(8,128)(2,1)S(1)}, bf16[16,128]{1,0:T(8,128)(2,1)S(1)}) conditional(s32[]{:T(128)} %convert_element_type.1, () %tuple.21, (bf16[32,512]{1,0:T(8,128)(2,1)S(1)}, f32[8,128]{1,0:T(8,128)S(1)}) %tuple.22), branch_computations={%region_2.0_spmd, %region_3.0_spmd} | conditional | flops 557057 | bytes 1908872 | solution.py:394
  70.1 0.6 branch_1_fun.7
  70.7 3.8 %collective-permute-start.1 = (bf16[1,32,512]{2,1,0:T(8,128)(2,1)}, bf16[1,32,512]{2,1,0:T(8,128)(2,1)S(1)}, u32[]{:S(2)}, u32[]{:S(2)}) collective-permute-start(bf16[1,32,512]{2,1,0:T(8,128)(2,1)} %bitcast.18), channel_id=1, source_target_pairs={{0,8},{2,10},{4,12},{6,14},{8,0},{10,2},{12,4},{14,6},{1,9},{3,11}... | collective-permute-start | bytes 98312 | tf_op jit(solution)/shard_map/cond/branch_1_fun/cond/branch_1_fun/ppermute | solution.py:361
  74.4 6.1 %collective-permute-done.1 = bf16[1,32,512]{2,1,0:T(8,128)(2,1)S(1)} collective-permute-done((bf16[1,32,512]{2,1,0:T(8,128)(2,1)}, bf16[1,32,512]{2,1,0:T(8,128)(2,1)S(1)}, u32[]{:S(2)}, u32[]{:S(2)}) %collective-permute-start.1) | collective-permute-done | bytes 32800 | tf_op jit(solution)/shard_map/cond/branch_1_fun/cond/branch_1_fun/ppermute | solution.py:361
  80.6 0.8 pad_maximum_fusion.2
  81.4 3.2 %collective-permute-start.2 = (bf16[2,32,512]{2,1,0:T(8,128)(2,1)S(1)}, bf16[2,32,512]{2,1,0:T(8,128)(2,1)S(1)}, u32[]{:S(2)}, u32[]{:S(2)}) collective-permute-start(bf16[2,32,512]{2,1,0:T(8,128)(2,1)S(1)} %pad_maximum_fusion.2), channel_id=1, source_target_pairs={{0,4},{2,6},{4,0},{6,2},{8,12},{10,14},{12,8},{14,10},{1,5},{3,7},... | collective-permute-start | bytes 196616 | tf_op jit(solution)/shard_map/cond/branch_1_fun/cond/branch_1_fun/ppermute | solution.py:361
  84.6 3.8 %collective-permute-done.2 = bf16[2,32,512]{2,1,0:T(8,128)(2,1)S(1)} collective-permute-done((bf16[2,32,512]{2,1,0:T(8,128)(2,1)S(1)}, bf16[2,32,512]{2,1,0:T(8,128)(2,1)S(1)}, u32[]{:S(2)}, u32[]{:S(2)}) %collective-permute-start.2) | collective-permute-done | bytes 65568 | tf_op jit(solution)/shard_map/cond/branch_1_fun/cond/branch_1_fun/ppermute | solution.py:361
  88.4 0.8 pad_maximum_fusion.1
  89.2 1.9 %collective-permute-start.3 = (bf16[4,32,512]{2,1,0:T(8,128)(2,1)S(1)}, bf16[4,32,512]{2,1,0:T(8,128)(2,1)S(1)}, u32[]{:S(2)}, u32[]{:S(2)}) collective-permute-start(bf16[4,32,512]{2,1,0:T(8,128)(2,1)S(1)} %pad_maximum_fusion.1), channel_id=1, source_target_pairs={{0,2},{2,0},{4,6},{6,4},{8,10},{10,8},{12,14},{14,12},{1,3},{3,1},... | collective-permute-start | bytes 393224 | tf_op jit(solution)/shard_map/cond/branch_1_fun/cond/branch_1_fun/ppermute | solution.py:361
  91.1 4.9 %collective-permute-done.3 = bf16[4,32,512]{2,1,0:T(8,128)(2,1)S(1)} collective-permute-done((bf16[4,32,512]{2,1,0:T(8,128)(2,1)S(1)}, bf16[4,32,512]{2,1,0:T(8,128)(2,1)S(1)}, u32[]{:S(2)}, u32[]{:S(2)}) %collective-permute-start.3) | collective-permute-done | bytes 131104 | tf_op jit(solution)/shard_map/cond/branch_1_fun/cond/branch_1_fun/ppermute | solution.py:361
  96.0 0.8 pad_maximum_fusion
  96.8 0.0 all-to-all-done.2.parts_ref
  96.9 1.1 branch_1_fun.11
  97.9 9.7 %all-to-all-start.3 = ((bf16[16,32,896]{2,1,0:T(8,128)(2,1)}), bf16[16,32,896]{2,1,0:T(8,128)(2,1)}, u32[]{:S(2)}, u32[]{:S(2)}) async-start(bf16[16,32,896]{2,1,0:T(8,128)(2,1)} %branch_1_fun.11), calls=%async_computation.3 | async-start | bytes 1835008 | tf_op jit(solution)/shard_map/cond/branch_1_fun/all_to_all | solution.py:416
  107.6 0.1 pad_maximum_fusion.3
  107.7 1.9 %collective-permute-start.5 = (bf16[2,448,512]{2,1,0:T(8,128)(2,1)S(1)}, bf16[2,448,512]{2,1,0:T(8,128)(2,1)S(1)}, u32[]{:S(2)}, u32[]{:S(2)}) collective-permute-start(bf16[2,448,512]{2,1,0:T(8,128)(2,1)S(1)} %pad_maximum_fusion.3), channel_id=1, source_target_pairs={{0,1},{1,0},{2,3},{3,2},{4,5},{5,4},{6,7},{7,6},{8,9},{9,8},{10,11... | collective-permute-start | bytes 2752520 | tf_op jit(solution)/shard_map/cond/branch_1_fun/ppermute | solution.py:57
  109.6 3.1 %collective-permute-start.6 = (bf16[8,32,512]{2,1,0:T(8,128)(2,1)S(1)}, bf16[8,32,512]{2,1,0:T(8,128)(2,1)S(1)}, u32[]{:S(2)}, u32[]{:S(2)}) collective-permute-start(bf16[8,32,512]{2,1,0:T(8,128)(2,1)S(1)} %get-tuple-element.33), channel_id=1, source_target_pairs={{0,16},{16,0},{1,17},{17,1},{2,18},{18,2},{3,19},{19,3},{4,20},{20... | collective-permute-start | bytes 786440 | tf_op jit(solution)/shard_map/cond/branch_1_fun/ppermute | solution.py:361
  112.8 0.0 collective-permute-done.5.other_ref
  112.8 0.7 branch_1_fun.10
  113.4 12.9 %collective-permute-done.6 = bf16[8,32,512]{2,1,0:T(8,128)(2,1)S(1)} collective-permute-done((bf16[8,32,512]{2,1,0:T(8,128)(2,1)S(1)}, bf16[8,32,512]{2,1,0:T(8,128)(2,1)S(1)}, u32[]{:S(2)}, u32[]{:S(2)}) %collective-permute-start.6) | collective-permute-done | bytes 262176 | tf_op jit(solution)/shard_map/cond/branch_1_fun/ppermute | solution.py:361
  126.3 0.8 pad_maximum_fusion.4
  127.2 2.5 %all-to-all-done.3 = bf16[16,32,896]{2,1,0:T(8,128)(2,1)} async-done(((bf16[16,32,896]{2,1,0:T(8,128)(2,1)}), bf16[16,32,896]{2,1,0:T(8,128)(2,1)}, u32[]{:S(2)}, u32[]{:S(2)}) %all-to-all-start.3) | async-done | bytes 917536 | tf_op jit(solution)/shard_map/cond/branch_1_fun/all_to_all | solution.py:416
  129.7 0.0 all-gather.2.cloned.1.call-done.pre_ref
  129.7 5.3 %shard_map.105 = (bf16[16,32,512]{2,1,0:T(8,128)(2,1)}, bf16[3,512,896]{2,1,0:T(8,128)(2,1)}) custom-call(bf16[16,32,896]{2,1,0:T(8,128)(2,1)} %get-tuple-element.61.hid_ref, bf16[512,1792]{1,0:T(8,128)(2,1)} %all-gather.2.cloned.1.call-done.pre_ref, bf16[2,896,512]{2,1,0:T(8,128)(2,1)S(1)} %get-tuple-element.63.quant_ref), custom_call_target="tpu_custom_call" | custom-call | flops 939524096 | bytes 8388608 | tf_op jit(solution)/shard_map/pallas_call | solution.py:274
  134.9 7.1 %all-to-all-start.4 = ((bf16[16,32,512]{2,1,0:T(8,128)(2,1)}), bf16[16,32,512]{2,1,0:T(8,128)(2,1)S(1)}, u32[]{:S(2)}, u32[]{:S(2)}) async-start(bf16[16,32,512]{2,1,0:T(8,128)(2,1)} %get-tuple-element.64), calls=%async_computation.4 | async-start | bytes 1048576 | tf_op jit(solution)/shard_map/all_to_all | solution.py:424
  142.1 0.1 pad_add_fusion
  142.1 10.0 %conditional.4 = ((bf16[448,512]{1,0:T(8,128)(2,1)}, bf16[448,512]{1,0:T(8,128)(2,1)}, bf16[448,512]{1,0:T(8,128)(2,1)}, f32[8,128]{1,0:T(8,128)S(1)})) conditional(s32[]{:T(128)} %convert_element_type.7, () %tuple.33, (s32[2]{0:T(128)S(1)}, bf16[3,512,896]{2,1,0:T(8,128)(2,1)}, bf16[512,512]{1,0:T(8,128)(2,1)}, bf16[16,32,512]{2,1,0:T(8,128)(2,1)}) %tuple.34), branch_computations={%region_4.0_spmd, %region_5.0_spmd} | conditional | flops 1410334720 | bytes 19136560 | solution.py:394
  142.1 3.7 %branch_1_fun.12 = (f32[3,448,512]{2,1,0:T(8,128)S(1)}, bf16[3,448,512]{2,1,0:T(8,128)(2,1)S(1)}) custom-call(s32[2]{0:T(128)S(1)} %get-tuple-element.34.place_ref, bf16[3,512,896]{2,1,0:T(8,128)(2,1)} %get-tuple-element.35.acts_ref, bf16[512,512]{1,0:T(8,128)(2,1)} %get-tuple-element.36.out_ref, bf16[16,32,512]{2,1,0:T(8,128)(2,1)} %get-tuple-element.37.tokens_ref), custom_call_target="tpu_custom_call" | custom-call | flops 1409286144 | bytes 8388608 | tf_op jit(solution)/shard_map/cond/branch_1_fun/pallas_call | solution.py:312
  145.8 1.9 %collective-permute-start = (bf16[3,448,512]{2,1,0:T(8,128)(2,1)S(1)}, bf16[3,448,512]{2,1,0:T(8,128)(2,1)S(1)}, u32[]{:S(2)}, u32[]{:S(2)}) collective-permute-start(bf16[3,448,512]{2,1,0:T(8,128)(2,1)S(1)} %get-tuple-element.39), channel_id=1, source_target_pairs={{0,1},{1,0},{2,3},{3,2},{4,5},{5,4},{6,7},{7,6},{8,9},{9,8},{10,11... | collective-permute-start | bytes 4128776 | tf_op jit(solution)/shard_map/cond/branch_1_fun/ppermute | solution.py:57
  147.8 3.1 %collective-permute-done.other_ref = bf16[3,448,512]{2,1,0:T(8,128)(2,1)S(1)} collective-permute-done((bf16[3,448,512]{2,1,0:T(8,128)(2,1)S(1)}, bf16[3,448,512]{2,1,0:T(8,128)(2,1)S(1)}, u32[]{:S(2)}, u32[]{:S(2)}) %collective-permute-start) | collective-permute-done | bytes 1376288 | tf_op jit(solution)/shard_map/cond/branch_1_fun/ppermute | solution.py:57
  150.9 1.2 branch_1_fun.13
  152.1 4.2 %all-to-all-done.4.parts_ref = bf16[16,32,512]{2,1,0:T(8,128)(2,1)S(1)} async-done(((bf16[16,32,512]{2,1,0:T(8,128)(2,1)}), bf16[16,32,512]{2,1,0:T(8,128)(2,1)S(1)}, u32[]{:S(2)}, u32[]{:S(2)}) %all-to-all-start.4) | async-done | bytes 524320 | tf_op jit(solution)/shard_map/all_to_all | solution.py:424
  156.3 0.7 shard_map.106
  (1 shorter events, 0.0 us)
Async XLA Ops:
  7.2 8.5 %copy-start = (bf16[512,448]{0,1:T(8,128)(2,1)S(1)}, bf16[512,448]{0,1:T(8,128)(2,1)}, u32[]{:S(2)}) copy-start(bf16[512,448]{0,1:T(8,128)(2,1)} %param.17) | copy-start | bytes 1376260
  7.2 8.5 %copy-start.1 = (bf16[512,448]{0,1:T(8,128)(2,1)S(1)}, bf16[512,448]{0,1:T(8,128)(2,1)}, u32[]{:S(2)}) copy-start(bf16[512,448]{0,1:T(8,128)(2,1)} %param.18) | copy-start | bytes 1376260
  7.2 8.5 %copy-start.2 = (bf16[448,512]{1,0:T(8,128)(2,1)S(1)}, bf16[448,512]{1,0:T(8,128)(2,1)}, u32[]{:S(2)}) copy-start(bf16[448,512]{1,0:T(8,128)(2,1)} %down_ref.1) | copy-start | bytes 1376260
  7.2 8.5 %copy-start.4 = (bf16[32,512]{1,0:T(8,128)(2,1)S(1)}, bf16[32,512]{1,0:T(8,128)(2,1)}, u32[]{:S(2)}) copy-start(bf16[32,512]{1,0:T(8,128)(2,1)} %param.13) | copy-start | bytes 98308
  7.2 122.5 %all-gather.2.cloned.1.call-start = ((), (), s32[]{:S(2)}) async-start(), calls=%async_computation.5 | async-start | bytes 1949696 | tf_op jit(solution)/shard_map/all_gather | solution.py:404
  9.7 3.4 %collective-permute-start.7 = (bf16[48,1024]{1,0:T(8,128)(2,1)}, bf16[48,1024]{1,0:T(8,128)(2,1)S(1)}, u32[]{:S(2)}, u32[]{:S(2)}) collective-permute-start(bf16[48,1024]{1,0:T(8,128)(2,1)} %get-tuple-element.58), channel_id=1, source_target_pairs={{0,1},{1,0},{2,3},{3,2},{4,5},{5,4},{6,7},{7,6},{8,9},{9,8},{10,11... | collective-permute-start | bytes 294920 | tf_op jit(solution)/shard_map/ppermute | solution.py:57
  13.1 0.6 copy-start.3
  15.7 25.4 %all-to-all-start = ((bf16[16,144,128]{2,1,0:T(8,128)(2,1)}), bf16[16,144,128]{2,1,0:T(8,128)(2,1)S(1)}, u32[]{:S(2)}, u32[]{:S(2)}) async-start(bf16[16,144,128]{2,1,0:T(8,128)(2,1)} %get-tuple-element.24), calls=%async_computation | async-start | bytes 1179648 | tf_op jit(solution)/shard_map/cond/branch_1_fun/all_to_all | solution.py:407
  24.2 29.2 %collective-permute-start.4 = (bf16[448,512]{1,0:T(8,128)(2,1)S(1)}, bf16[448,512]{1,0:T(8,128)(2,1)S(1)}, u32[]{:S(2)}, u32[]{:S(2)}) collective-permute-start(bf16[448,512]{1,0:T(8,128)(2,1)S(1)} %get-tuple-element.25.down_ref), channel_id=1, source_target_pairs={{0,1},{1,0},{2,3},{3,2},{4,5},{5,4},{6,7},{7,6},{8,9},{9,8},{10,11... | collective-permute-start | bytes 1376264 | tf_op jit(solution)/shard_map/cond/branch_1_fun/ppermute | solution.py:57
  41.8 20.7 %all-to-all-start.1 = ((f32[16,8,128]{2,1,0:T(8,128)}), f32[16,8,128]{2,1,0:T(8,128)S(1)}, u32[]{:S(2)}, u32[]{:S(2)}) async-start(f32[16,8,128]{2,1,0:T(8,128)} %branch_1_fun.8), calls=%async_computation.1 | async-start | bytes 131072 | tf_op jit(solution)/shard_map/cond/branch_1_fun/all_to_all | solution.py:409
  65.6 31.2 %all-to-all-start.2 = ((bf16[16,32,896]{2,1,0:T(8,128)(2,1)}), bf16[16,32,896]{2,1,0:T(8,128)(2,1)S(1)}, u32[]{:S(2)}, u32[]{:S(2)}) async-start(bf16[16,32,896]{2,1,0:T(8,128)(2,1)} %get-tuple-element.29), calls=%async_computation.2 | async-start | bytes 1835008 | tf_op jit(solution)/shard_map/cond/branch_1_fun/all_to_all | solution.py:411
  70.7 9.9 %collective-permute-start.1 = (bf16[1,32,512]{2,1,0:T(8,128)(2,1)}, bf16[1,32,512]{2,1,0:T(8,128)(2,1)S(1)}, u32[]{:S(2)}, u32[]{:S(2)}) collective-permute-start(bf16[1,32,512]{2,1,0:T(8,128)(2,1)} %bitcast.18), channel_id=1, source_target_pairs={{0,8},{2,10},{4,12},{6,14},{8,0},{10,2},{12,4},{14,6},{1,9},{3,11}... | collective-permute-start | bytes 98312 | tf_op jit(solution)/shard_map/cond/branch_1_fun/cond/branch_1_fun/ppermute | solution.py:361
  81.4 7.0 %collective-permute-start.2 = (bf16[2,32,512]{2,1,0:T(8,128)(2,1)S(1)}, bf16[2,32,512]{2,1,0:T(8,128)(2,1)S(1)}, u32[]{:S(2)}, u32[]{:S(2)}) collective-permute-start(bf16[2,32,512]{2,1,0:T(8,128)(2,1)S(1)} %pad_maximum_fusion.2), channel_id=1, source_target_pairs={{0,4},{2,6},{4,0},{6,2},{8,12},{10,14},{12,8},{14,10},{1,5},{3,7},... | collective-permute-start | bytes 196616 | tf_op jit(solution)/shard_map/cond/branch_1_fun/cond/branch_1_fun/ppermute | solution.py:361
  89.2 6.9 %collective-permute-start.3 = (bf16[4,32,512]{2,1,0:T(8,128)(2,1)S(1)}, bf16[4,32,512]{2,1,0:T(8,128)(2,1)S(1)}, u32[]{:S(2)}, u32[]{:S(2)}) collective-permute-start(bf16[4,32,512]{2,1,0:T(8,128)(2,1)S(1)} %pad_maximum_fusion.1), channel_id=1, source_target_pairs={{0,2},{2,0},{4,6},{6,4},{8,10},{10,8},{12,14},{14,12},{1,3},{3,1},... | collective-permute-start | bytes 393224 | tf_op jit(solution)/shard_map/cond/branch_1_fun/cond/branch_1_fun/ppermute | solution.py:361
  97.9 31.8 %all-to-all-start.3 = ((bf16[16,32,896]{2,1,0:T(8,128)(2,1)}), bf16[16,32,896]{2,1,0:T(8,128)(2,1)}, u32[]{:S(2)}, u32[]{:S(2)}) async-start(bf16[16,32,896]{2,1,0:T(8,128)(2,1)} %branch_1_fun.11), calls=%async_computation.3 | async-start | bytes 1835008 | tf_op jit(solution)/shard_map/cond/branch_1_fun/all_to_all | solution.py:416
  107.7 5.0 %collective-permute-start.5 = (bf16[2,448,512]{2,1,0:T(8,128)(2,1)S(1)}, bf16[2,448,512]{2,1,0:T(8,128)(2,1)S(1)}, u32[]{:S(2)}, u32[]{:S(2)}) collective-permute-start(bf16[2,448,512]{2,1,0:T(8,128)(2,1)S(1)} %pad_maximum_fusion.3), channel_id=1, source_target_pairs={{0,1},{1,0},{2,3},{3,2},{4,5},{5,4},{6,7},{7,6},{8,9},{9,8},{10,11... | collective-permute-start | bytes 2752520 | tf_op jit(solution)/shard_map/cond/branch_1_fun/ppermute | solution.py:57
  109.6 16.7 %collective-permute-start.6 = (bf16[8,32,512]{2,1,0:T(8,128)(2,1)S(1)}, bf16[8,32,512]{2,1,0:T(8,128)(2,1)S(1)}, u32[]{:S(2)}, u32[]{:S(2)}) collective-permute-start(bf16[8,32,512]{2,1,0:T(8,128)(2,1)S(1)} %get-tuple-element.33), channel_id=1, source_target_pairs={{0,16},{16,0},{1,17},{17,1},{2,18},{18,2},{3,19},{19,3},{4,20},{20... | collective-permute-start | bytes 786440 | tf_op jit(solution)/shard_map/cond/branch_1_fun/ppermute | solution.py:361
  134.9 21.3 %all-to-all-start.4 = ((bf16[16,32,512]{2,1,0:T(8,128)(2,1)}), bf16[16,32,512]{2,1,0:T(8,128)(2,1)S(1)}, u32[]{:S(2)}, u32[]{:S(2)}) async-start(bf16[16,32,512]{2,1,0:T(8,128)(2,1)} %get-tuple-element.64), calls=%async_computation.4 | async-start | bytes 1048576 | tf_op jit(solution)/shard_map/all_to_all | solution.py:424
  145.8 5.0 %collective-permute-start = (bf16[3,448,512]{2,1,0:T(8,128)(2,1)S(1)}, bf16[3,448,512]{2,1,0:T(8,128)(2,1)S(1)}, u32[]{:S(2)}, u32[]{:S(2)}) collective-permute-start(bf16[3,448,512]{2,1,0:T(8,128)(2,1)S(1)} %get-tuple-element.39), channel_id=1, source_target_pairs={{0,1},{1,0},{2,3},{3,2},{4,5},{5,4},{6,7},{7,6},{8,9},{9,8},{10,11... | collective-permute-start | bytes 4128776 | tf_op jit(solution)/shard_map/cond/branch_1_fun/ppermute | solution.py:57
Sparse Core Ops, SparseCore 0:
  15.8 104.0 all-gather.1

commit v6 on v5

--- a/solution.py
+++ b/solution.py
@@ -47,7 +47,8 @@
     up_f = up_pre.astype(jnp.float32)
     sigma = jax.nn.sigmoid(gate_f)
     silu_gate = gate_f * sigma
-    grad_gpre = (grad_hidden * up_f * sigma * (1.0 + gate_f * (1.0 - sigma))).astype(jnp.bfloat16)
+    slope = sigma * (1.0 + gate_f - silu_gate)
+    grad_gpre = (grad_hidden * (up_f * slope)).astype(jnp.bfloat16)
     grad_upre = (grad_hidden * silu_gate).astype(jnp.bfloat16)
     hidden = (silu_gate * up_f).astype(jnp.bfloat16)
     return (grad_gpre, grad_upre, hidden)
@@ -295,7 +296,7 @@
 def latent_grads_kernel(place_ref, acts_ref, out_ref, tokens_ref, own_ref, sent_ref, rows_ref):
     rows = tokens_ref.shape[1]
     for block in range(2 * N_Y):
-        flip, bits = block // N_Y, block % N_Y
+        flip, bits = block & 1, block >> 1
         offset = 4 * (bits & 1) + (bits & 2) + bits // 4
         chip = (place_ref[0] ^ flip) * N_Y + (place_ref[1] ^ offset)
         rows_ref[pl.ds(pl.multiple_of(chip * rows, rows), rows), :] = tokens_ref[block]
@@ -376,9 +377,9 @@
     )(values, after)
 
 
-def tokens_along_y(tokens, done):
-    blocks = copy_after(tokens, done)[None]
-    for step in (4, 2, 1):
+def far_tokens(blocks, done):
+    blocks = copy_after(blocks, done)
+    for step in (4, 2):
         blocks = doubled(blocks, "y", step)
     return blocks, blocks[-1, :EXTRA, :LANES]
 
@@ -406,13 +407,14 @@
     def exchanges(sent, tokens, gate_t, up_t, down):
         received = lax.all_to_all(sent, CHIP, 0, 0)
         down_other = swapped(down)
+        pair = doubled(tokens[None], "xl", 1)
         tile = lax.all_to_all(sums_tile(received), ROW, 0, 0)
         partial, out_half, done = hidden_partial(tile, received, down, down_other)
         parts = lax.all_to_all(partial, ROW, 0, 0)
-        near_tokens, after = in_branch(tokens_along_y, tokens, done)
+        most_tokens, after = in_branch(far_tokens, pair, done)
         other_latents = swapped(jnp.stack([gate_t, up_t]))
         quant = clipped_latents(tile, gate_t, up_t, other_latents)
-        token_blocks = doubled(near_tokens, "xl", 1)
+        token_blocks = doubled(most_tokens, "y", 1)
         grad_hidden = lax.all_to_all(spread(parts, after), ROW, 0, 0)
         return (out_half, quant, grad_hidden, token_blocks)
 

time: 165 us -> 164 us (level)
  starting transfers between devices: 61 us -> 59.3 us
  waiting for transfers between devices: 63.2 us -> 64.9 us
    all_to_all x1, waiting for transfers between devices: 2.51 us -> 5.93 us  [exchanges(): grad_hidden = lax.all_to_all(spread(parts, after), ROW, 0, 0)]
    ppermute x4, starting transfers between devices: 12 us -> 9.01 us  [doubled(): other = lax.ppermute(blocks, axis, [(k, k ^ step) for k in range(count)])]
  transfers between devices with their start and end apart: 14 -> 14, of which waited for: 10 -> 11; matrix products, arithmetic and copies ran while one was open for 2% -> 2% of each run, Pallas kernels for 7% -> 7%
where the time goes in v6:
time: 164 us; the launch traced here: 163 us
  waiting for transfers between devices  64.9 us (40%)
  starting transfers between devices  59.3 us (36%)
  Pallas kernels  21.2 us (13%)
  between operations  14.1 us (9%)
  other arithmetic  2.73 us (2%)
    ppermute x4, waiting for transfers between devices, doubled(): other = lax.ppermute(blocks, axis, [(k, k ^ step) for k in range(count)])  26.7 us
    all_to_all x1, waiting for transfers between devices, exchanges(): received = lax.all_to_all(sent, CHIP, 0, 0)  15 us
    all_to_all x1, starting transfers between devices, exchanges(): tile = lax.all_to_all(sums_tile(received), ROW, 0, 0)  11.5 us
    all_to_all x1, starting transfers between devices, exchanges(): grad_hidden = lax.all_to_all(spread(parts, after), ROW, 0, 0)  10.2 us
    all_to_all x1, waiting for transfers between devices, exchanges(): tile = lax.all_to_all(sums_tile(received), ROW, 0, 0)  9.14 us
    ppermute x4, starting transfers between devices, doubled(): other = lax.ppermute(blocks, axis, [(k, k ^ step) for k in range(count)])  9.01 us
    all_to_all x1, starting transfers between devices, exchanges(): received = lax.all_to_all(sent, CHIP, 0, 0)  8.48 us
    all_to_all x1, starting transfers between devices, shards(): parts = lax.all_to_all(partial, CHIP, 0, 0)  7.95 us
  transfers between devices with their start and end apart: 14, of which 11 were waited for; matrix products, arithmetic and copies ran while one was open for 2% of the time, Pallas kernels for 7%

profile of v6, /device:TPU:74, one launch (start us, length us, event | category | flops | bytes accessed | tf_op | source)
XLA Modules:
  0.0 163.1 jit_solution(9923940293203725381)
XLA Ops:
  7.2 0.0 copy-start
  7.2 0.0 copy-start.1
  7.2 0.0 copy-start.2
  7.2 0.0 copy-start.4
  7.2 0.0 all-gather.2.cloned.1.call-start
  7.3 2.5 %shard_map.103 = (bf16[48,1024]{1,0:T(8,128)(2,1)}, f32[8,128]{1,0:T(8,128)}) custom-call(s32[1]{0:T(128)} %bitcast.4.core_ref, bf16[64,448]{1,0:T(8,128)(2,1)} %gate_pre_ref.3, bf16[64,448]{1,0:T(8,128)(2,1)} %up_pre_ref.3, bf16[448,512]{1,0:T(8,128)(2,1)} %bitcast.12, bf16[448,512]{1,0:T(8,128)(2,1)} %bitcast.15, bf16[448,512]{1,0:T(8,128)(2,1)} %down_ref.1), custom_call_target="tpu_custom_call" | custom-call | flops 1048576 | bytes 1572864 | tf_op jit(solution)/shard_map/pallas_call | solution.py:99
  9.7 1.9 %collective-permute-start.7 = (bf16[48,1024]{1,0:T(8,128)(2,1)}, bf16[48,1024]{1,0:T(8,128)(2,1)S(1)}, u32[]{:S(2)}, u32[]{:S(2)}) collective-permute-start(bf16[48,1024]{1,0:T(8,128)(2,1)} %get-tuple-element.58), channel_id=1, source_target_pairs={{0,1},{1,0},{2,3},{3,2},{4,5},{5,4},{6,7},{7,6},{8,9},{9,8},{10,11... | collective-permute-start | bytes 294920 | tf_op jit(solution)/shard_map/ppermute | solution.py:58
  11.6 1.5 collective-permute-done.7.other_ref
  13.1 0.0 copy-start.3
  13.1 0.6 copy-done.3
  13.8 1.9 %shard_map.104 = (bf16[32,1792]{1,0:T(8,128)(2,1)}, bf16[16,144,128]{2,1,0:T(8,128)(2,1)}) custom-call(s32[1]{0:T(128)} %bitcast.4.core_ref, bf16[64,448]{1,0:T(8,128)(2,1)} %gate_pre_ref.3, bf16[64,448]{1,0:T(8,128)(2,1)} %up_pre_ref.3, bf16[48,1024]{1,0:T(8,128)(2,1)} %copy-done.3, f32[8,128]{1,0:T(8,128)} %get-tuple-element.59.sums_ref, ...), custom_call_target="tpu_custom_call" | custom-call | flops 65536 | bytes 1048576 | tf_op jit(solution)/shard_map/pallas_call | solution.py:135
  15.7 0.0 all-gather.2.cloned.1.call-update
  15.7 0.0 copy-done
  15.7 0.0 copy-done.1
  15.7 0.0 copy-done.2
  15.7 0.0 copy-done.4
  15.7 113.7 %conditional.3 = (bf16[512,512]{1,0:T(8,128)(2,1)}, bf16[2,896,512]{2,1,0:T(8,128)(2,1)S(1)}, bf16[16,32,896]{2,1,0:T(8,128)(2,1)}, bf16[16,32,512]{2,1,0:T(8,128)(2,1)}) conditional(s32[]{:T(128)} %convert_element_type.7, () %tuple.31, (bf16[16,144,128]{2,1,0:T(8,128)(2,1)}, bf16[448,512]{1,0:T(8,128)(2,1)S(1)}, bf16[448,512]{1,0:T(8,128)(2,1)S(1)}, ...), branch_computations={%region_0.0_spmd, %region_1.0_spmd} | conditional | flops 472481792 | bytes 29565404 | solution.py:395
  15.7 8.5 %all-to-all-start = ((bf16[16,144,128]{2,1,0:T(8,128)(2,1)}), bf16[16,144,128]{2,1,0:T(8,128)(2,1)S(1)}, u32[]{:S(2)}, u32[]{:S(2)}) async-start(bf16[16,144,128]{2,1,0:T(8,128)(2,1)} %get-tuple-element.24), calls=%async_computation | async-start | bytes 1179648 | tf_op jit(solution)/shard_map/cond/branch_1_fun/all_to_all | solution.py:408
  24.2 1.9 %collective-permute-start.3 = (bf16[448,512]{1,0:T(8,128)(2,1)S(1)}, bf16[448,512]{1,0:T(8,128)(2,1)S(1)}, u32[]{:S(2)}, u32[]{:S(2)}) collective-permute-start(bf16[448,512]{1,0:T(8,128)(2,1)S(1)} %get-tuple-element.25.down_ref), channel_id=1, source_target_pairs={{0,1},{1,0},{2,3},{3,2},{4,5},{5,4},{6,7},{7,6},{8,9},{9,8},{10,11... | collective-permute-start | bytes 1376264 | tf_op jit(solution)/shard_map/cond/branch_1_fun/ppermute | solution.py:58
  26.1 15.0 %all-to-all-done.extra_ref.received_ref = bf16[16,144,128]{2,1,0:T(8,128)(2,1)S(1)} async-done(((bf16[16,144,128]{2,1,0:T(8,128)(2,1)}), bf16[16,144,128]{2,1,0:T(8,128)(2,1)S(1)}, u32[]{:S(2)}, u32[]{:S(2)}) %all-to-all-start) | async-done | bytes 589856 | tf_op jit(solution)/shard_map/cond/branch_1_fun/all_to_all | solution.py:408
  41.2 0.7 branch_1_fun.8
  41.8 11.5 %all-to-all-start.1 = ((f32[16,8,128]{2,1,0:T(8,128)}), f32[16,8,128]{2,1,0:T(8,128)S(1)}, u32[]{:S(2)}, u32[]{:S(2)}) async-start(f32[16,8,128]{2,1,0:T(8,128)} %branch_1_fun.8), calls=%async_computation.1 | async-start | bytes 131072 | tf_op jit(solution)/shard_map/cond/branch_1_fun/all_to_all | solution.py:411
  53.4 0.0 collective-permute-done.3.other_ref
  53.4 9.1 %all-to-all-done.1.tile_ref = f32[16,8,128]{2,1,0:T(8,128)S(1)} async-done(((f32[16,8,128]{2,1,0:T(8,128)}), f32[16,8,128]{2,1,0:T(8,128)S(1)}, u32[]{:S(2)}, u32[]{:S(2)}) %all-to-all-start.1) | async-done | bytes 65568 | tf_op jit(solution)/shard_map/cond/branch_1_fun/all_to_all | solution.py:411
  62.5 3.1 %branch_1_fun.9 = (bf16[16,32,896]{2,1,0:T(8,128)(2,1)}, bf16[512,512]{1,0:T(8,128)(2,1)}, f32[8,128]{1,0:T(8,128)S(1)}) custom-call(f32[16,8,128]{2,1,0:T(8,128)S(1)} %all-to-all-done.1.tile_ref, bf16[16,144,128]{2,1,0:T(8,128)(2,1)S(1)} %all-to-all-done.extra_ref.received_ref, bf16[448,512]{1,0:T(8,128)(2,1)S(1)} %get-tuple-element.25.down_ref, ...), custom_call_target="tpu_custom_call" | custom-call | flops 469762048 | bytes 4194304 | tf_op jit(solution)/shard_map/cond/branch_1_fun/pallas_call | solution.py:199
  65.6 4.4 %all-to-all-start.2 = ((bf16[16,32,896]{2,1,0:T(8,128)(2,1)}), bf16[16,32,896]{2,1,0:T(8,128)(2,1)S(1)}, u32[]{:S(2)}, u32[]{:S(2)}) async-start(bf16[16,32,896]{2,1,0:T(8,128)(2,1)} %get-tuple-element.29), calls=%async_computation.2 | async-start | bytes 1835008 | tf_op jit(solution)/shard_map/cond/branch_1_fun/all_to_all | solution.py:413
  70.1 3.1 %collective-permute-start.5 = (bf16[1,32,512]{2,1,0:T(8,128)(2,1)S(1)}, bf16[1,32,512]{2,1,0:T(8,128)(2,1)S(1)}, u32[]{:S(2)}, u32[]{:S(2)}) collective-permute-start(bf16[1,32,512]{2,1,0:T(8,128)(2,1)S(1)} %bitcast.20), channel_id=1, source_target_pairs={{0,16},{16,0},{1,17},{17,1},{2,18},{18,2},{3,19},{19,3},{4,20},{20... | collective-permute-start | bytes 98312 | tf_op jit(solution)/shard_map/cond/branch_1_fun/ppermute | solution.py:362
  73.2 5.0 %collective-permute-done.5 = bf16[1,32,512]{2,1,0:T(8,128)(2,1)S(1)} collective-permute-done((bf16[1,32,512]{2,1,0:T(8,128)(2,1)S(1)}, bf16[1,32,512]{2,1,0:T(8,128)(2,1)S(1)}, u32[]{:S(2)}, u32[]{:S(2)}) %collective-permute-start.5) | collective-permute-done | bytes 32800 | tf_op jit(solution)/shard_map/cond/branch_1_fun/ppermute | solution.py:362
  78.2 20.6 %conditional = (bf16[8,32,512]{2,1,0:T(8,128)(2,1)S(1)}, bf16[16,128]{1,0:T(8,128)(2,1)S(1)}) conditional(s32[]{:T(128)} %convert_element_type.1, () %tuple.21, (bf16[2,32,512]{2,1,0:T(8,128)(2,1)S(1)}, f32[8,128]{1,0:T(8,128)S(1)}) %tuple.22), branch_computations={%region_2.0_spmd, %region_3.0_spmd} | conditional | flops 327681 | bytes 1646688 | solution.py:395
  78.2 0.6 branch_1_fun.7
  78.8 2.1 %collective-permute-start.1 = (bf16[2,32,512]{2,1,0:T(8,128)(2,1)}, bf16[2,32,512]{2,1,0:T(8,128)(2,1)S(1)}, u32[]{:S(2)}, u32[]{:S(2)}) collective-permute-start(bf16[2,32,512]{2,1,0:T(8,128)(2,1)} %branch_1_fun.7), channel_id=1, source_target_pairs={{0,8},{2,10},{4,12},{6,14},{8,0},{10,2},{12,4},{14,6},{1,9},{3,11}... | collective-permute-start | bytes 196616 | tf_op jit(solution)/shard_map/cond/branch_1_fun/cond/branch_1_fun/ppermute | solution.py:362
  80.9 8.4 %collective-permute-done.1 = bf16[2,32,512]{2,1,0:T(8,128)(2,1)S(1)} collective-permute-done((bf16[2,32,512]{2,1,0:T(8,128)(2,1)}, bf16[2,32,512]{2,1,0:T(8,128)(2,1)S(1)}, u32[]{:S(2)}, u32[]{:S(2)}) %collective-permute-start.1) | collective-permute-done | bytes 65568 | tf_op jit(solution)/shard_map/cond/branch_1_fun/cond/branch_1_fun/ppermute | solution.py:362
  89.3 0.9 pad_maximum_fusion.1
  90.1 1.9 %collective-permute-start.2 = (bf16[4,32,512]{2,1,0:T(8,128)(2,1)S(1)}, bf16[4,32,512]{2,1,0:T(8,128)(2,1)S(1)}, u32[]{:S(2)}, u32[]{:S(2)}) collective-permute-start(bf16[4,32,512]{2,1,0:T(8,128)(2,1)S(1)} %pad_maximum_fusion.1), channel_id=1, source_target_pairs={{0,4},{2,6},{4,0},{6,2},{8,12},{10,14},{12,8},{14,10},{1,5},{3,7},... | collective-permute-start | bytes 393224 | tf_op jit(solution)/shard_map/cond/branch_1_fun/cond/branch_1_fun/ppermute | solution.py:362
  92.0 5.8 %collective-permute-done.2 = bf16[4,32,512]{2,1,0:T(8,128)(2,1)S(1)} collective-permute-done((bf16[4,32,512]{2,1,0:T(8,128)(2,1)S(1)}, bf16[4,32,512]{2,1,0:T(8,128)(2,1)S(1)}, u32[]{:S(2)}, u32[]{:S(2)}) %collective-permute-start.2) | collective-permute-done | bytes 131104 | tf_op jit(solution)/shard_map/cond/branch_1_fun/cond/branch_1_fun/ppermute | solution.py:362
  97.9 0.9 pad_maximum_fusion
  98.8 0.0 all-to-all-done.2.parts_ref
  98.8 1.1 branch_1_fun.11
  99.8 10.2 %all-to-all-start.3 = ((bf16[16,32,896]{2,1,0:T(8,128)(2,1)}), bf16[16,32,896]{2,1,0:T(8,128)(2,1)}, u32[]{:S(2)}, u32[]{:S(2)}) async-start(bf16[16,32,896]{2,1,0:T(8,128)(2,1)} %branch_1_fun.11), calls=%async_computation.3 | async-start | bytes 1835008 | tf_op jit(solution)/shard_map/cond/branch_1_fun/all_to_all | solution.py:418
  110.1 0.1 pad_maximum_fusion.2
  110.2 1.9 %collective-permute-start.4 = (bf16[2,448,512]{2,1,0:T(8,128)(2,1)S(1)}, bf16[2,448,512]{2,1,0:T(8,128)(2,1)S(1)}, u32[]{:S(2)}, u32[]{:S(2)}) collective-permute-start(bf16[2,448,512]{2,1,0:T(8,128)(2,1)S(1)} %pad_maximum_fusion.2), channel_id=1, source_target_pairs={{0,1},{1,0},{2,3},{3,2},{4,5},{5,4},{6,7},{7,6},{8,9},{9,8},{10,11... | collective-permute-start | bytes 2752520 | tf_op jit(solution)/shard_map/cond/branch_1_fun/ppermute | solution.py:58
  112.1 1.9 %collective-permute-start.6 = (bf16[8,32,512]{2,1,0:T(8,128)(2,1)S(1)}, bf16[8,32,512]{2,1,0:T(8,128)(2,1)S(1)}, u32[]{:S(2)}, u32[]{:S(2)}) collective-permute-start(bf16[8,32,512]{2,1,0:T(8,128)(2,1)S(1)} %get-tuple-element.33), channel_id=1, source_target_pairs={{0,2},{2,0},{4,6},{6,4},{8,10},{10,8},{12,14},{14,12},{1,3},{3,1},... | collective-permute-start | bytes 786440 | tf_op jit(solution)/shard_map/cond/branch_1_fun/ppermute | solution.py:362
  114.0 0.5 collective-permute-done.4.other_ref
  114.5 0.7 branch_1_fun.10
  115.2 7.5 %collective-permute-done.6 = bf16[8,32,512]{2,1,0:T(8,128)(2,1)S(1)} collective-permute-done((bf16[8,32,512]{2,1,0:T(8,128)(2,1)S(1)}, bf16[8,32,512]{2,1,0:T(8,128)(2,1)S(1)}, u32[]{:S(2)}, u32[]{:S(2)}) %collective-permute-start.6) | collective-permute-done | bytes 262176 | tf_op jit(solution)/shard_map/cond/branch_1_fun/ppermute | solution.py:362
  122.7 0.8 pad_maximum_fusion.3
  123.5 5.9 %all-to-all-done.3 = bf16[16,32,896]{2,1,0:T(8,128)(2,1)} async-done(((bf16[16,32,896]{2,1,0:T(8,128)(2,1)}), bf16[16,32,896]{2,1,0:T(8,128)(2,1)}, u32[]{:S(2)}, u32[]{:S(2)}) %all-to-all-start.3) | async-done | bytes 917536 | tf_op jit(solution)/shard_map/cond/branch_1_fun/all_to_all | solution.py:418
  129.5 0.0 all-gather.2.cloned.1.call-done.pre_ref
  129.5 5.1 %shard_map.105 = (bf16[16,32,512]{2,1,0:T(8,128)(2,1)}, bf16[3,512,896]{2,1,0:T(8,128)(2,1)}) custom-call(bf16[16,32,896]{2,1,0:T(8,128)(2,1)} %get-tuple-element.61.hid_ref, bf16[512,1792]{1,0:T(8,128)(2,1)} %all-gather.2.cloned.1.call-done.pre_ref, bf16[2,896,512]{2,1,0:T(8,128)(2,1)S(1)} %get-tuple-element.63.quant_ref), custom_call_target="tpu_custom_call" | custom-call | flops 939524096 | bytes 8388608 | tf_op jit(solution)/shard_map/pallas_call | solution.py:275
  134.6 7.9 %all-to-all-start.4 = ((bf16[16,32,512]{2,1,0:T(8,128)(2,1)}), bf16[16,32,512]{2,1,0:T(8,128)(2,1)S(1)}, u32[]{:S(2)}, u32[]{:S(2)}) async-start(bf16[16,32,512]{2,1,0:T(8,128)(2,1)} %get-tuple-element.64), calls=%async_computation.4 | async-start | bytes 1048576 | tf_op jit(solution)/shard_map/all_to_all | solution.py:426
  142.5 0.1 pad_add_fusion
  142.6 10.0 %conditional.4 = ((bf16[448,512]{1,0:T(8,128)(2,1)}, bf16[448,512]{1,0:T(8,128)(2,1)}, bf16[448,512]{1,0:T(8,128)(2,1)}, f32[8,128]{1,0:T(8,128)S(1)})) conditional(s32[]{:T(128)} %convert_element_type.7, () %tuple.33, (s32[2]{0:T(128)S(1)}, bf16[3,512,896]{2,1,0:T(8,128)(2,1)}, bf16[512,512]{1,0:T(8,128)(2,1)}, bf16[16,32,512]{2,1,0:T(8,128)(2,1)}) %tuple.34), branch_computations={%region_4.0_spmd, %region_5.0_spmd} | conditional | flops 1410334720 | bytes 19136560 | solution.py:395
  142.6 3.7 %branch_1_fun.12 = (f32[3,448,512]{2,1,0:T(8,128)S(1)}, bf16[3,448,512]{2,1,0:T(8,128)(2,1)S(1)}) custom-call(s32[2]{0:T(128)S(1)} %get-tuple-element.34.place_ref, bf16[3,512,896]{2,1,0:T(8,128)(2,1)} %get-tuple-element.35.acts_ref, bf16[512,512]{1,0:T(8,128)(2,1)} %get-tuple-element.36.out_ref, bf16[16,32,512]{2,1,0:T(8,128)(2,1)} %get-tuple-element.37.tokens_ref), custom_call_target="tpu_custom_call" | custom-call | flops 1409286144 | bytes 8388608 | tf_op jit(solution)/shard_map/cond/branch_1_fun/pallas_call | solution.py:313
  146.3 1.9 %collective-permute-start = (bf16[3,448,512]{2,1,0:T(8,128)(2,1)S(1)}, bf16[3,448,512]{2,1,0:T(8,128)(2,1)S(1)}, u32[]{:S(2)}, u32[]{:S(2)}) collective-permute-start(bf16[3,448,512]{2,1,0:T(8,128)(2,1)S(1)} %get-tuple-element.39), channel_id=1, source_target_pairs={{0,1},{1,0},{2,3},{3,2},{4,5},{5,4},{6,7},{7,6},{8,9},{9,8},{10,11... | collective-permute-start | bytes 4128776 | tf_op jit(solution)/shard_map/cond/branch_1_fun/ppermute | solution.py:58
  148.2 3.1 %collective-permute-done.other_ref = bf16[3,448,512]{2,1,0:T(8,128)(2,1)S(1)} collective-permute-done((bf16[3,448,512]{2,1,0:T(8,128)(2,1)S(1)}, bf16[3,448,512]{2,1,0:T(8,128)(2,1)S(1)}, u32[]{:S(2)}, u32[]{:S(2)}) %collective-permute-start) | collective-permute-done | bytes 1376288 | tf_op jit(solution)/shard_map/cond/branch_1_fun/ppermute | solution.py:58
  151.3 1.2 branch_1_fun.13
  152.5 3.0 %all-to-all-done.4.parts_ref = bf16[16,32,512]{2,1,0:T(8,128)(2,1)S(1)} async-done(((bf16[16,32,512]{2,1,0:T(8,128)(2,1)}), bf16[16,32,512]{2,1,0:T(8,128)(2,1)S(1)}, u32[]{:S(2)}, u32[]{:S(2)}) %all-to-all-start.4) | async-done | bytes 524320 | tf_op jit(solution)/shard_map/all_to_all | solution.py:426
  155.5 0.7 shard_map.106
  (2 shorter events, 0.0 us)
Async XLA Ops:
  7.2 8.5 %copy-start = (bf16[512,448]{0,1:T(8,128)(2,1)S(1)}, bf16[512,448]{0,1:T(8,128)(2,1)}, u32[]{:S(2)}) copy-start(bf16[512,448]{0,1:T(8,128)(2,1)} %param.17) | copy-start | bytes 1376260
  7.2 8.5 %copy-start.1 = (bf16[512,448]{0,1:T(8,128)(2,1)S(1)}, bf16[512,448]{0,1:T(8,128)(2,1)}, u32[]{:S(2)}) copy-start(bf16[512,448]{0,1:T(8,128)(2,1)} %param.18) | copy-start | bytes 1376260
  7.2 8.5 %copy-start.2 = (bf16[448,512]{1,0:T(8,128)(2,1)S(1)}, bf16[448,512]{1,0:T(8,128)(2,1)}, u32[]{:S(2)}) copy-start(bf16[448,512]{1,0:T(8,128)(2,1)} %down_ref.1) | copy-start | bytes 1376260
  7.2 8.5 %copy-start.4 = (bf16[32,512]{1,0:T(8,128)(2,1)S(1)}, bf16[32,512]{1,0:T(8,128)(2,1)}, u32[]{:S(2)}) copy-start(bf16[32,512]{1,0:T(8,128)(2,1)} %param.13) | copy-start | bytes 98308
  7.2 122.3 %all-gather.2.cloned.1.call-start = ((), (), s32[]{:S(2)}) async-start(), calls=%async_computation.5 | async-start | bytes 1949696 | tf_op jit(solution)/shard_map/all_gather | solution.py:405
  9.7 3.4 %collective-permute-start.7 = (bf16[48,1024]{1,0:T(8,128)(2,1)}, bf16[48,1024]{1,0:T(8,128)(2,1)S(1)}, u32[]{:S(2)}, u32[]{:S(2)}) collective-permute-start(bf16[48,1024]{1,0:T(8,128)(2,1)} %get-tuple-element.58), channel_id=1, source_target_pairs={{0,1},{1,0},{2,3},{3,2},{4,5},{5,4},{6,7},{7,6},{8,9},{9,8},{10,11... | collective-permute-start | bytes 294920 | tf_op jit(solution)/shard_map/ppermute | solution.py:58
  13.1 0.6 copy-start.3
  15.7 25.4 %all-to-all-start = ((bf16[16,144,128]{2,1,0:T(8,128)(2,1)}), bf16[16,144,128]{2,1,0:T(8,128)(2,1)S(1)}, u32[]{:S(2)}, u32[]{:S(2)}) async-start(bf16[16,144,128]{2,1,0:T(8,128)(2,1)} %get-tuple-element.24), calls=%async_computation | async-start | bytes 1179648 | tf_op jit(solution)/shard_map/cond/branch_1_fun/all_to_all | solution.py:408
  24.2 29.2 %collective-permute-start.3 = (bf16[448,512]{1,0:T(8,128)(2,1)S(1)}, bf16[448,512]{1,0:T(8,128)(2,1)S(1)}, u32[]{:S(2)}, u32[]{:S(2)}) collective-permute-start(bf16[448,512]{1,0:T(8,128)(2,1)S(1)} %get-tuple-element.25.down_ref), channel_id=1, source_target_pairs={{0,1},{1,0},{2,3},{3,2},{4,5},{5,4},{6,7},{7,6},{8,9},{9,8},{10,11... | collective-permute-start | bytes 1376264 | tf_op jit(solution)/shard_map/cond/branch_1_fun/ppermute | solution.py:58
  41.8 20.7 %all-to-all-start.1 = ((f32[16,8,128]{2,1,0:T(8,128)}), f32[16,8,128]{2,1,0:T(8,128)S(1)}, u32[]{:S(2)}, u32[]{:S(2)}) async-start(f32[16,8,128]{2,1,0:T(8,128)} %branch_1_fun.8), calls=%async_computation.1 | async-start | bytes 131072 | tf_op jit(solution)/shard_map/cond/branch_1_fun/all_to_all | solution.py:411
  65.6 33.1 %all-to-all-start.2 = ((bf16[16,32,896]{2,1,0:T(8,128)(2,1)}), bf16[16,32,896]{2,1,0:T(8,128)(2,1)S(1)}, u32[]{:S(2)}, u32[]{:S(2)}) async-start(bf16[16,32,896]{2,1,0:T(8,128)(2,1)} %get-tuple-element.29), calls=%async_computation.2 | async-start | bytes 1835008 | tf_op jit(solution)/shard_map/cond/branch_1_fun/all_to_all | solution.py:413
  70.1 8.1 %collective-permute-start.5 = (bf16[1,32,512]{2,1,0:T(8,128)(2,1)S(1)}, bf16[1,32,512]{2,1,0:T(8,128)(2,1)S(1)}, u32[]{:S(2)}, u32[]{:S(2)}) collective-permute-start(bf16[1,32,512]{2,1,0:T(8,128)(2,1)S(1)} %bitcast.20), channel_id=1, source_target_pairs={{0,16},{16,0},{1,17},{17,1},{2,18},{18,2},{3,19},{19,3},{4,20},{20... | collective-permute-start | bytes 98312 | tf_op jit(solution)/shard_map/cond/branch_1_fun/ppermute | solution.py:362
  78.8 10.5 %collective-permute-start.1 = (bf16[2,32,512]{2,1,0:T(8,128)(2,1)}, bf16[2,32,512]{2,1,0:T(8,128)(2,1)S(1)}, u32[]{:S(2)}, u32[]{:S(2)}) collective-permute-start(bf16[2,32,512]{2,1,0:T(8,128)(2,1)} %branch_1_fun.7), channel_id=1, source_target_pairs={{0,8},{2,10},{4,12},{6,14},{8,0},{10,2},{12,4},{14,6},{1,9},{3,11}... | collective-permute-start | bytes 196616 | tf_op jit(solution)/shard_map/cond/branch_1_fun/cond/branch_1_fun/ppermute | solution.py:362
  90.1 7.8 %collective-permute-start.2 = (bf16[4,32,512]{2,1,0:T(8,128)(2,1)S(1)}, bf16[4,32,512]{2,1,0:T(8,128)(2,1)S(1)}, u32[]{:S(2)}, u32[]{:S(2)}) collective-permute-start(bf16[4,32,512]{2,1,0:T(8,128)(2,1)S(1)} %pad_maximum_fusion.1), channel_id=1, source_target_pairs={{0,4},{2,6},{4,0},{6,2},{8,12},{10,14},{12,8},{14,10},{1,5},{3,7},... | collective-permute-start | bytes 393224 | tf_op jit(solution)/shard_map/cond/branch_1_fun/cond/branch_1_fun/ppermute | solution.py:362
  99.8 29.6 %all-to-all-start.3 = ((bf16[16,32,896]{2,1,0:T(8,128)(2,1)}), bf16[16,32,896]{2,1,0:T(8,128)(2,1)}, u32[]{:S(2)}, u32[]{:S(2)}) async-start(bf16[16,32,896]{2,1,0:T(8,128)(2,1)} %branch_1_fun.11), calls=%async_computation.3 | async-start | bytes 1835008 | tf_op jit(solution)/shard_map/cond/branch_1_fun/all_to_all | solution.py:418
  110.2 4.4 %collective-permute-start.4 = (bf16[2,448,512]{2,1,0:T(8,128)(2,1)S(1)}, bf16[2,448,512]{2,1,0:T(8,128)(2,1)S(1)}, u32[]{:S(2)}, u32[]{:S(2)}) collective-permute-start(bf16[2,448,512]{2,1,0:T(8,128)(2,1)S(1)} %pad_maximum_fusion.2), channel_id=1, source_target_pairs={{0,1},{1,0},{2,3},{3,2},{4,5},{5,4},{6,7},{7,6},{8,9},{9,8},{10,11... | collective-permute-start | bytes 2752520 | tf_op jit(solution)/shard_map/cond/branch_1_fun/ppermute | solution.py:58
  112.1 10.6 %collective-permute-start.6 = (bf16[8,32,512]{2,1,0:T(8,128)(2,1)S(1)}, bf16[8,32,512]{2,1,0:T(8,128)(2,1)S(1)}, u32[]{:S(2)}, u32[]{:S(2)}) collective-permute-start(bf16[8,32,512]{2,1,0:T(8,128)(2,1)S(1)} %get-tuple-element.33), channel_id=1, source_target_pairs={{0,2},{2,0},{4,6},{6,4},{8,10},{10,8},{12,14},{14,12},{1,3},{3,1},... | collective-permute-start | bytes 786440 | tf_op jit(solution)/shard_map/cond/branch_1_fun/ppermute | solution.py:362
  134.6 21.0 %all-to-all-start.4 = ((bf16[16,32,512]{2,1,0:T(8,128)(2,1)}), bf16[16,32,512]{2,1,0:T(8,128)(2,1)S(1)}, u32[]{:S(2)}, u32[]{:S(2)}) async-start(bf16[16,32,512]{2,1,0:T(8,128)(2,1)} %get-tuple-element.64), calls=%async_computation.4 | async-start | bytes 1048576 | tf_op jit(solution)/shard_map/all_to_all | solution.py:426
  146.3 5.0 %collective-permute-start = (bf16[3,448,512]{2,1,0:T(8,128)(2,1)S(1)}, bf16[3,448,512]{2,1,0:T(8,128)(2,1)S(1)}, u32[]{:S(2)}, u32[]{:S(2)}) collective-permute-start(bf16[3,448,512]{2,1,0:T(8,128)(2,1)S(1)} %get-tuple-element.39), channel_id=1, source_target_pairs={{0,1},{1,0},{2,3},{3,2},{4,5},{5,4},{6,7},{7,6},{8,9},{9,8},{10,11... | collective-permute-start | bytes 4128776 | tf_op jit(solution)/shard_map/cond/branch_1_fun/ppermute | solution.py:58
Sparse Core Ops, SparseCore 0:
  15.8 103.5 all-gather.1

commit v7 on v6

--- a/solution.py
+++ b/solution.py
@@ -145,23 +145,26 @@
     )(core, gate_pre, up_pre, other, sums, grad_out)
 
 
-def tile_kernel(extra_ref, tile_ref):
+def tile_kernel(extra_ref, after_ref, tile_ref):
     sums = totals_of(jnp.sum(extra_ref[...].astype(jnp.float32), axis=0))
     tile = jnp.concatenate(sums + [jnp.zeros((5, LANES), jnp.float32)], axis=0)
     tile_ref[...] = jnp.broadcast_to(tile[None], tile_ref.shape)
 
 
-def sums_tile(received):
+def sums_tile(received, after):
     rows = received.shape[1] - EXTRA
     return pl.pallas_call(
         tile_kernel,
         grid=(1,),
         out_shape=jax.ShapeDtypeStruct((N_ROW, 8, LANES), jnp.float32),
-        in_specs=[pl.BlockSpec((N_CHIP, EXTRA, LANES), lambda i: (0, rows // EXTRA, 0))],
+        in_specs=[
+            pl.BlockSpec((N_CHIP, EXTRA, LANES), lambda i: (0, rows // EXTRA, 0)),
+            pl.BlockSpec(after.shape, lambda i: (0, 0)),
+        ],
         out_specs=pl.BlockSpec((N_ROW, 8, LANES), lambda i: (0, 0, 0)),
         compiler_params=PARAMS,
         cost_estimate=cost(1 << 16, 1 << 18),
-    )(received)
+    )(received, after)
 
 
 def scale_of(tile_ref, which):
@@ -297,7 +300,7 @@
     rows = tokens_ref.shape[1]
     for block in range(2 * N_Y):
         flip, bits = block & 1, block >> 1
-        offset = 4 * (bits & 1) + (bits & 2) + bits // 4
+        offset = 2 * (bits & 3) + bits // 4
         chip = (place_ref[0] ^ flip) * N_Y + (place_ref[1] ^ offset)
         rows_ref[pl.ds(pl.multiple_of(chip * rows, rows), rows), :] = tokens_ref[block]
     inner = own_ref.shape[1]
@@ -357,12 +360,6 @@
     )(parts, after)
 
 
-def doubled(blocks, axis, step):
-    count = 2 if axis == "xl" else N_Y
-    other = lax.ppermute(blocks, axis, [(k, k ^ step) for k in range(count)])
-    return jnp.concatenate([blocks, other], axis=0)
-
-
 def copy_kernel(values_ref, after_ref, copy_ref):
     copy_ref[...] = values_ref[...]
 
@@ -377,10 +374,19 @@
     )(values, after)
 
 
+def exchanged(blocks, axis, *steps):
+    count = 2 if axis == "xl" else N_Y
+    others = [lax.ppermute(blocks, axis, [(k, k ^ step) for k in range(count)]) for step in steps]
+    return jnp.concatenate([blocks] + others, axis=0)
+
+
+def token_pair(tokens):
+    blocks = exchanged(tokens[None], "xl", 1)
+    return blocks, blocks[-1, :EXTRA, :LANES]
+
+
 def far_tokens(blocks, done):
-    blocks = copy_after(blocks, done)
-    for step in (4, 2):
-        blocks = doubled(blocks, "y", step)
+    blocks = exchanged(copy_after(blocks, done), "y", 2, 4, 6)
     return blocks, blocks[-1, :EXTRA, :LANES]
 
 
@@ -407,14 +413,14 @@
     def exchanges(sent, tokens, gate_t, up_t, down):
         received = lax.all_to_all(sent, CHIP, 0, 0)
         down_other = swapped(down)
-        pair = doubled(tokens[None], "xl", 1)
-        tile = lax.all_to_all(sums_tile(received), ROW, 0, 0)
+        pair, after = in_branch(token_pair, tokens)
+        tile = lax.all_to_all(sums_tile(received, after), ROW, 0, 0)
         partial, out_half, done = hidden_partial(tile, received, down, down_other)
         parts = lax.all_to_all(partial, ROW, 0, 0)
         most_tokens, after = in_branch(far_tokens, pair, done)
         other_latents = swapped(jnp.stack([gate_t, up_t]))
         quant = clipped_latents(tile, gate_t, up_t, other_latents)
-        token_blocks = doubled(most_tokens, "y", 1)
+        token_blocks = exchanged(most_tokens, "y", 1)
         grad_hidden = lax.all_to_all(spread(parts, after), ROW, 0, 0)
         return (out_half, quant, grad_hidden, token_blocks)
 

time: 164 us -> 165 us (level)
  the two profiles are of different devices: /device:TPU:74 before, /device:TPU:10 now
where the time goes in v7:
time: 165 us; the launch traced here: 164 us
  waiting for transfers between devices  64.8 us (39%)
  starting transfers between devices  61.3 us (37%)
  Pallas kernels  21.2 us (13%)
  between operations  14.1 us (9%)
  other arithmetic  1.88 us (1%)
    ppermute x5, starting transfers between devices, exchanged(): lax.ppermute(blocks, axis, [(k, k ^ step) for k in range(count)])  16.5 us
    ppermute x5, waiting for transfers between devices, exchanged(): lax.ppermute(blocks, axis, [(k, k ^ step) for k in range(count)])  16.4 us
    all_to_all x1, waiting for transfers between devices, exchanges(): grad_hidden = lax.all_to_all(spread(parts, after), ROW, 0, 0)  14.2 us
    all_to_all x1, starting transfers between devices, exchanges(): tile = lax.all_to_all(sums_tile(received, after), ROW, 0, 0)  10.9 us
    all_to_all x1, waiting for transfers between devices, exchanges(): tile = lax.all_to_all(sums_tile(received, after), ROW, 0, 0)  10 us
    all_to_all x1, starting transfers between devices, exchanges(): received = lax.all_to_all(sent, CHIP, 0, 0)  9.23 us
    all_to_all x1, starting transfers between devices, shards(): parts = lax.all_to_all(partial, CHIP, 0, 0)  8.26 us
    all_to_all x1, waiting for transfers between devices, exchanges(): received = lax.all_to_all(sent, CHIP, 0, 0)  7.98 us
  transfers between devices with their start and end apart: 15, of which 12 were waited for; matrix products, arithmetic and copies ran while one was open for 1% of the time, Pallas kernels for 7%

profile of v7, /device:TPU:10, one launch (start us, length us, event | category | flops | bytes accessed | tf_op | source)
XLA Modules:
  0.0 164.1 jit_solution(16236774893107532178)
XLA Ops:
  7.2 0.0 copy-start
  7.2 0.0 copy-start.1
  7.2 0.0 copy-start.2
  7.2 0.0 copy-start.4
  7.2 0.0 all-gather.2.cloned.1.call-start
  7.3 2.5 %shard_map.106 = (bf16[48,1024]{1,0:T(8,128)(2,1)}, f32[8,128]{1,0:T(8,128)}) custom-call(s32[1]{0:T(128)} %bitcast.5.core_ref, bf16[64,448]{1,0:T(8,128)(2,1)} %gate_pre_ref.3, bf16[64,448]{1,0:T(8,128)(2,1)} %up_pre_ref.3, bf16[448,512]{1,0:T(8,128)(2,1)} %bitcast.14, bf16[448,512]{1,0:T(8,128)(2,1)} %bitcast.17, bf16[448,512]{1,0:T(8,128)(2,1)} %down_ref.1), custom_call_target="tpu_custom_call" | custom-call | flops 1048576 | bytes 1572864 | tf_op jit(solution)/shard_map/pallas_call | solution.py:99
  9.7 1.9 %collective-permute-start.8 = (bf16[48,1024]{1,0:T(8,128)(2,1)}, bf16[48,1024]{1,0:T(8,128)(2,1)S(1)}, u32[]{:S(2)}, u32[]{:S(2)}) collective-permute-start(bf16[48,1024]{1,0:T(8,128)(2,1)} %get-tuple-element.61), channel_id=1, source_target_pairs={{0,1},{1,0},{2,3},{3,2},{4,5},{5,4},{6,7},{7,6},{8,9},{9,8},{10,11... | collective-permute-start | bytes 294920 | tf_op jit(solution)/shard_map/ppermute | solution.py:58
  11.6 1.5 collective-permute-done.8.other_ref
  13.1 0.0 copy-start.3
  13.1 0.6 copy-done.3
  13.8 1.9 %shard_map.107 = (bf16[32,1792]{1,0:T(8,128)(2,1)}, bf16[16,144,128]{2,1,0:T(8,128)(2,1)}) custom-call(s32[1]{0:T(128)} %bitcast.5.core_ref, bf16[64,448]{1,0:T(8,128)(2,1)} %gate_pre_ref.3, bf16[64,448]{1,0:T(8,128)(2,1)} %up_pre_ref.3, bf16[48,1024]{1,0:T(8,128)(2,1)} %copy-done.3, f32[8,128]{1,0:T(8,128)} %get-tuple-element.62.sums_ref, ...), custom_call_target="tpu_custom_call" | custom-call | flops 65536 | bytes 1048576 | tf_op jit(solution)/shard_map/pallas_call | solution.py:135
  15.7 0.0 all-gather.2.cloned.1.call-update
  15.7 0.0 copy-done
  15.7 0.0 copy-done.1
  15.7 0.0 copy-done.2
  15.7 0.0 copy-done.4
  15.7 113.4 %conditional.4 = (bf16[512,512]{1,0:T(8,128)(2,1)}, bf16[2,896,512]{2,1,0:T(8,128)(2,1)S(1)}, bf16[16,32,896]{2,1,0:T(8,128)(2,1)}, bf16[16,32,512]{2,1,0:T(8,128)(2,1)}) conditional(s32[]{:T(128)} %convert_element_type.8, () %tuple.39, (bf16[16,144,128]{2,1,0:T(8,128)(2,1)}, bf16[32,512]{1,0:T(8,128)(2,1)S(1)}, bf16[448,512]{1,0:T(8,128)(2,1)S(1)}, ...), branch_computations={%region_0.0_spmd, %region_1.0_spmd} | conditional | flops 472547328 | bytes 29311510 | solution.py:401
  15.7 9.2 %all-to-all-start = ((bf16[16,144,128]{2,1,0:T(8,128)(2,1)}), bf16[16,144,128]{2,1,0:T(8,128)(2,1)S(1)}, u32[]{:S(2)}, u32[]{:S(2)}) async-start(bf16[16,144,128]{2,1,0:T(8,128)(2,1)} %get-tuple-element.25), calls=%async_computation | async-start | bytes 1179648 | tf_op jit(solution)/shard_map/cond/branch_1_fun/all_to_all | solution.py:414
  25.0 1.9 %collective-permute-start.5 = (bf16[448,512]{1,0:T(8,128)(2,1)S(1)}, bf16[448,512]{1,0:T(8,128)(2,1)S(1)}, u32[]{:S(2)}, u32[]{:S(2)}) collective-permute-start(bf16[448,512]{1,0:T(8,128)(2,1)S(1)} %get-tuple-element.28.down_ref), channel_id=1, source_target_pairs={{0,1},{1,0},{2,3},{3,2},{4,5},{5,4},{6,7},{7,6},{8,9},{9,8},{10,11... | collective-permute-start | bytes 1376264 | tf_op jit(solution)/shard_map/cond/branch_1_fun/ppermute | solution.py:58
  26.9 7.4 %conditional = (bf16[2,32,512]{2,1,0:T(8,128)(2,1)S(1)}, bf16[16,128]{1,0:T(8,128)(2,1)S(1)}) conditional(s32[]{:T(128)} %convert_element_type.1, () %tuple.28, bf16[32,512]{1,0:T(8,128)(2,1)S(1)} %get-tuple-element.76), branch_computations={%region_2.0_spmd, %region_3.0_spmd} | conditional | flops 32768 | bytes 270392 | solution.py:401
  26.9 2.4 %collective-permute-start.1 = (bf16[1,32,512]{2,1,0:T(8,128)(2,1)S(1)}, bf16[1,32,512]{2,1,0:T(8,128)(2,1)S(1)}, u32[]{:S(2)}, u32[]{:S(2)}) collective-permute-start(bf16[1,32,512]{2,1,0:T(8,128)(2,1)S(1)} %bitcast.22), channel_id=1, source_target_pairs={{0,16},{16,0},{1,17},{17,1},{2,18},{18,2},{3,19},{19,3},{4,20},{20... | collective-permute-start | bytes 98312 | tf_op jit(solution)/shard_map/cond/branch_1_fun/cond/branch_1_fun/ppermute | solution.py:379
  29.3 5.0 %collective-permute-done.1 = bf16[1,32,512]{2,1,0:T(8,128)(2,1)S(1)} collective-permute-done((bf16[1,32,512]{2,1,0:T(8,128)(2,1)S(1)}, bf16[1,32,512]{2,1,0:T(8,128)(2,1)S(1)}, u32[]{:S(2)}, u32[]{:S(2)}) %collective-permute-start.1) | collective-permute-done | bytes 32800 | tf_op jit(solution)/shard_map/cond/branch_1_fun/cond/branch_1_fun/ppermute | solution.py:379
  34.3 8.0 %all-to-all-done.extra_ref.received_ref = bf16[16,144,128]{2,1,0:T(8,128)(2,1)S(1)} async-done(((bf16[16,144,128]{2,1,0:T(8,128)(2,1)}), bf16[16,144,128]{2,1,0:T(8,128)(2,1)S(1)}, u32[]{:S(2)}, u32[]{:S(2)}) %all-to-all-start) | async-done | bytes 589856 | tf_op jit(solution)/shard_map/cond/branch_1_fun/all_to_all | solution.py:414
  42.3 0.7 branch_1_fun.8
  43.0 10.9 %all-to-all-start.1 = ((f32[16,8,128]{2,1,0:T(8,128)}), f32[16,8,128]{2,1,0:T(8,128)S(1)}, u32[]{:S(2)}, u32[]{:S(2)}) async-start(f32[16,8,128]{2,1,0:T(8,128)} %branch_1_fun.8), calls=%async_computation.1 | async-start | bytes 131072 | tf_op jit(solution)/shard_map/cond/branch_1_fun/all_to_all | solution.py:417
  53.8 0.0 collective-permute-done.5.other_ref
  53.8 10.0 %all-to-all-done.1.tile_ref = f32[16,8,128]{2,1,0:T(8,128)S(1)} async-done(((f32[16,8,128]{2,1,0:T(8,128)}), f32[16,8,128]{2,1,0:T(8,128)S(1)}, u32[]{:S(2)}, u32[]{:S(2)}) %all-to-all-start.1) | async-done | bytes 65568 | tf_op jit(solution)/shard_map/cond/branch_1_fun/all_to_all | solution.py:417
  63.9 3.1 %branch_1_fun.9 = (bf16[16,32,896]{2,1,0:T(8,128)(2,1)}, bf16[512,512]{1,0:T(8,128)(2,1)}, f32[8,128]{1,0:T(8,128)S(1)}) custom-call(f32[16,8,128]{2,1,0:T(8,128)S(1)} %all-to-all-done.1.tile_ref, bf16[16,144,128]{2,1,0:T(8,128)(2,1)S(1)} %all-to-all-done.extra_ref.received_ref, bf16[448,512]{1,0:T(8,128)(2,1)S(1)} %get-tuple-element.28.down_ref, ...), custom_call_target="tpu_custom_call" | custom-call | flops 469762048 | bytes 4194304 | tf_op jit(solution)/shard_map/cond/branch_1_fun/pallas_call | solution.py:202
  67.0 3.6 %all-to-all-start.2 = ((bf16[16,32,896]{2,1,0:T(8,128)(2,1)}), bf16[16,32,896]{2,1,0:T(8,128)(2,1)S(1)}, u32[]{:S(2)}, u32[]{:S(2)}) async-start(bf16[16,32,896]{2,1,0:T(8,128)(2,1)} %get-tuple-element.32), calls=%async_computation.2 | async-start | bytes 1835008 | tf_op jit(solution)/shard_map/cond/branch_1_fun/all_to_all | solution.py:419
  70.6 17.7 %conditional.1 = (bf16[8,32,512]{2,1,0:T(8,128)(2,1)S(1)}, bf16[16,128]{1,0:T(8,128)(2,1)S(1)}) conditional(s32[]{:T(128)} %convert_element_type.1, () %tuple.29, (bf16[2,32,512]{2,1,0:T(8,128)(2,1)S(1)}, f32[8,128]{1,0:T(8,128)S(1)}) %tuple.30), branch_computations={%region_4.0_spmd, %region_5.0_spmd} | conditional | flops 393217 | bytes 1384584 | solution.py:401
  70.6 0.6 branch_1_fun.7
  71.3 3.8 %collective-permute-start.4 = (bf16[2,32,512]{2,1,0:T(8,128)(2,1)}, bf16[2,32,512]{2,1,0:T(8,128)(2,1)S(1)}, u32[]{:S(2)}, u32[]{:S(2)}) collective-permute-start(bf16[2,32,512]{2,1,0:T(8,128)(2,1)} %branch_1_fun.7), channel_id=1, source_target_pairs={{0,12},{2,14},{4,8},{6,10},{8,4},{10,6},{12,0},{14,2},{1,13},{3,15... | collective-permute-start | bytes 196616 | tf_op jit(solution)/shard_map/cond/branch_1_fun/cond/branch_1_fun/ppermute | solution.py:379
  75.1 4.9 %collective-permute-start.3 = (bf16[2,32,512]{2,1,0:T(8,128)(2,1)}, bf16[2,32,512]{2,1,0:T(8,128)(2,1)S(1)}, u32[]{:S(2)}, u32[]{:S(2)}) collective-permute-start(bf16[2,32,512]{2,1,0:T(8,128)(2,1)} %branch_1_fun.7), channel_id=1, source_target_pairs={{0,8},{2,10},{4,12},{6,14},{8,0},{10,2},{12,4},{14,6},{1,9},{3,11}... | collective-permute-start | bytes 196616 | tf_op jit(solution)/shard_map/cond/branch_1_fun/cond/branch_1_fun/ppermute | solution.py:379
  80.0 3.5 %collective-permute-start.2 = (bf16[2,32,512]{2,1,0:T(8,128)(2,1)}, bf16[2,32,512]{2,1,0:T(8,128)(2,1)S(1)}, u32[]{:S(2)}, u32[]{:S(2)}) collective-permute-start(bf16[2,32,512]{2,1,0:T(8,128)(2,1)} %branch_1_fun.7), channel_id=1, source_target_pairs={{0,4},{2,6},{4,0},{6,2},{8,12},{10,14},{12,8},{14,10},{1,5},{3,7},... | collective-permute-start | bytes 196616 | tf_op jit(solution)/shard_map/cond/branch_1_fun/cond/branch_1_fun/ppermute | solution.py:379
  83.5 0.0 collective-permute-done.4
  83.5 3.2 %collective-permute-done.3 = bf16[2,32,512]{2,1,0:T(8,128)(2,1)S(1)} collective-permute-done((bf16[2,32,512]{2,1,0:T(8,128)(2,1)}, bf16[2,32,512]{2,1,0:T(8,128)(2,1)S(1)}, u32[]{:S(2)}, u32[]{:S(2)}) %collective-permute-start.3) | collective-permute-done | bytes 65568 | tf_op jit(solution)/shard_map/cond/branch_1_fun/cond/branch_1_fun/ppermute | solution.py:379
  86.7 0.7 collective-permute-done.2
  87.4 0.9 pad_maximum_fusion.1
  88.3 7.1 %all-to-all-done.2.parts_ref = bf16[16,32,896]{2,1,0:T(8,128)(2,1)S(1)} async-done(((bf16[16,32,896]{2,1,0:T(8,128)(2,1)}), bf16[16,32,896]{2,1,0:T(8,128)(2,1)S(1)}, u32[]{:S(2)}, u32[]{:S(2)}) %all-to-all-start.2) | async-done | bytes 917536 | tf_op jit(solution)/shard_map/cond/branch_1_fun/all_to_all | solution.py:419
  95.4 1.1 branch_1_fun.11
  96.5 5.0 %all-to-all-start.3 = ((bf16[16,32,896]{2,1,0:T(8,128)(2,1)}), bf16[16,32,896]{2,1,0:T(8,128)(2,1)}, u32[]{:S(2)}, u32[]{:S(2)}) async-start(bf16[16,32,896]{2,1,0:T(8,128)(2,1)} %branch_1_fun.11), calls=%async_computation.3 | async-start | bytes 1835008 | tf_op jit(solution)/shard_map/cond/branch_1_fun/all_to_all | solution.py:424
  101.5 0.1 pad_maximum_fusion.2
  101.6 1.9 %collective-permute-start.6 = (bf16[2,448,512]{2,1,0:T(8,128)(2,1)S(1)}, bf16[2,448,512]{2,1,0:T(8,128)(2,1)S(1)}, u32[]{:S(2)}, u32[]{:S(2)}) collective-permute-start(bf16[2,448,512]{2,1,0:T(8,128)(2,1)S(1)} %pad_maximum_fusion.2), channel_id=1, source_target_pairs={{0,1},{1,0},{2,3},{3,2},{4,5},{5,4},{6,7},{7,6},{8,9},{9,8},{10,11... | collective-permute-start | bytes 2752520 | tf_op jit(solution)/shard_map/cond/branch_1_fun/ppermute | solution.py:58
  103.5 1.9 %collective-permute-start.7 = (bf16[8,32,512]{2,1,0:T(8,128)(2,1)S(1)}, bf16[8,32,512]{2,1,0:T(8,128)(2,1)S(1)}, u32[]{:S(2)}, u32[]{:S(2)}) collective-permute-start(bf16[8,32,512]{2,1,0:T(8,128)(2,1)S(1)} %get-tuple-element.36), channel_id=1, source_target_pairs={{0,2},{2,0},{4,6},{6,4},{8,10},{10,8},{12,14},{14,12},{1,3},{3,1},... | collective-permute-start | bytes 786440 | tf_op jit(solution)/shard_map/cond/branch_1_fun/ppermute | solution.py:379
  105.4 0.5 collective-permute-done.6.other_ref
  105.9 0.7 branch_1_fun.10
  106.6 7.5 %collective-permute-done.7 = bf16[8,32,512]{2,1,0:T(8,128)(2,1)S(1)} collective-permute-done((bf16[8,32,512]{2,1,0:T(8,128)(2,1)S(1)}, bf16[8,32,512]{2,1,0:T(8,128)(2,1)S(1)}, u32[]{:S(2)}, u32[]{:S(2)}) %collective-permute-start.7) | collective-permute-done | bytes 262176 | tf_op jit(solution)/shard_map/cond/branch_1_fun/ppermute | solution.py:379
  114.1 0.8 pad_maximum_fusion.3
  114.9 14.2 %all-to-all-done.3 = bf16[16,32,896]{2,1,0:T(8,128)(2,1)} async-done(((bf16[16,32,896]{2,1,0:T(8,128)(2,1)}), bf16[16,32,896]{2,1,0:T(8,128)(2,1)}, u32[]{:S(2)}, u32[]{:S(2)}) %all-to-all-start.3) | async-done | bytes 917536 | tf_op jit(solution)/shard_map/cond/branch_1_fun/all_to_all | solution.py:424
  129.2 0.0 all-gather.2.cloned.1.call-done.pre_ref
  129.2 5.1 %shard_map.108 = (bf16[16,32,512]{2,1,0:T(8,128)(2,1)}, bf16[3,512,896]{2,1,0:T(8,128)(2,1)}) custom-call(bf16[16,32,896]{2,1,0:T(8,128)(2,1)} %get-tuple-element.64.hid_ref, bf16[512,1792]{1,0:T(8,128)(2,1)} %all-gather.2.cloned.1.call-done.pre_ref, bf16[2,896,512]{2,1,0:T(8,128)(2,1)S(1)} %get-tuple-element.66.quant_ref), custom_call_target="tpu_custom_call" | custom-call | flops 939524096 | bytes 8388608 | tf_op jit(solution)/shard_map/pallas_call | solution.py:278
  134.3 8.3 %all-to-all-start.4 = ((bf16[16,32,512]{2,1,0:T(8,128)(2,1)}), bf16[16,32,512]{2,1,0:T(8,128)(2,1)S(1)}, u32[]{:S(2)}, u32[]{:S(2)}) async-start(bf16[16,32,512]{2,1,0:T(8,128)(2,1)} %get-tuple-element.67), calls=%async_computation.4 | async-start | bytes 1048576 | tf_op jit(solution)/shard_map/all_to_all | solution.py:432
  142.5 0.1 pad_add_fusion
  142.6 10.0 %conditional.5 = ((bf16[448,512]{1,0:T(8,128)(2,1)}, bf16[448,512]{1,0:T(8,128)(2,1)}, bf16[448,512]{1,0:T(8,128)(2,1)}, f32[8,128]{1,0:T(8,128)S(1)})) conditional(s32[]{:T(128)} %convert_element_type.8, () %tuple.41, (s32[2]{0:T(128)S(1)}, bf16[3,512,896]{2,1,0:T(8,128)(2,1)}, bf16[512,512]{1,0:T(8,128)(2,1)}, bf16[16,32,512]{2,1,0:T(8,128)(2,1)}) %tuple.42), branch_computations={%region_6.0_spmd, %region_7.0_spmd} | conditional | flops 1410334720 | bytes 19136560 | solution.py:401
  142.6 3.7 %branch_1_fun.12 = (f32[3,448,512]{2,1,0:T(8,128)S(1)}, bf16[3,448,512]{2,1,0:T(8,128)(2,1)S(1)}) custom-call(s32[2]{0:T(128)S(1)} %get-tuple-element.37.place_ref, bf16[3,512,896]{2,1,0:T(8,128)(2,1)} %get-tuple-element.38.acts_ref, bf16[512,512]{1,0:T(8,128)(2,1)} %get-tuple-element.39.out_ref, bf16[16,32,512]{2,1,0:T(8,128)(2,1)} %get-tuple-element.40.tokens_ref), custom_call_target="tpu_custom_call" | custom-call | flops 1409286144 | bytes 8388608 | tf_op jit(solution)/shard_map/cond/branch_1_fun/pallas_call | solution.py:316
  146.3 1.9 %collective-permute-start = (bf16[3,448,512]{2,1,0:T(8,128)(2,1)S(1)}, bf16[3,448,512]{2,1,0:T(8,128)(2,1)S(1)}, u32[]{:S(2)}, u32[]{:S(2)}) collective-permute-start(bf16[3,448,512]{2,1,0:T(8,128)(2,1)S(1)} %get-tuple-element.42), channel_id=1, source_target_pairs={{0,1},{1,0},{2,3},{3,2},{4,5},{5,4},{6,7},{7,6},{8,9},{9,8},{10,11... | collective-permute-start | bytes 4128776 | tf_op jit(solution)/shard_map/cond/branch_1_fun/ppermute | solution.py:58
  148.2 3.1 %collective-permute-done.other_ref = bf16[3,448,512]{2,1,0:T(8,128)(2,1)S(1)} collective-permute-done((bf16[3,448,512]{2,1,0:T(8,128)(2,1)S(1)}, bf16[3,448,512]{2,1,0:T(8,128)(2,1)S(1)}, u32[]{:S(2)}, u32[]{:S(2)}) %collective-permute-start) | collective-permute-done | bytes 1376288 | tf_op jit(solution)/shard_map/cond/branch_1_fun/ppermute | solution.py:58
  151.3 1.2 branch_1_fun.13
  152.6 4.1 %all-to-all-done.4.parts_ref = bf16[16,32,512]{2,1,0:T(8,128)(2,1)S(1)} async-done(((bf16[16,32,512]{2,1,0:T(8,128)(2,1)}), bf16[16,32,512]{2,1,0:T(8,128)(2,1)S(1)}, u32[]{:S(2)}, u32[]{:S(2)}) %all-to-all-start.4) | async-done | bytes 524320 | tf_op jit(solution)/shard_map/all_to_all | solution.py:432
  156.6 0.7 shard_map.109
  (3 shorter events, 0.0 us)
Async XLA Ops:
  7.2 8.5 %copy-start = (bf16[512,448]{0,1:T(8,128)(2,1)S(1)}, bf16[512,448]{0,1:T(8,128)(2,1)}, u32[]{:S(2)}) copy-start(bf16[512,448]{0,1:T(8,128)(2,1)} %param.19) | copy-start | bytes 1376260
  7.2 8.5 %copy-start.1 = (bf16[512,448]{0,1:T(8,128)(2,1)S(1)}, bf16[512,448]{0,1:T(8,128)(2,1)}, u32[]{:S(2)}) copy-start(bf16[512,448]{0,1:T(8,128)(2,1)} %param.20) | copy-start | bytes 1376260
  7.2 8.5 %copy-start.2 = (bf16[448,512]{1,0:T(8,128)(2,1)S(1)}, bf16[448,512]{1,0:T(8,128)(2,1)}, u32[]{:S(2)}) copy-start(bf16[448,512]{1,0:T(8,128)(2,1)} %down_ref.1) | copy-start | bytes 1376260
  7.2 8.5 %copy-start.4 = (bf16[32,512]{1,0:T(8,128)(2,1)S(1)}, bf16[32,512]{1,0:T(8,128)(2,1)}, u32[]{:S(2)}) copy-start(bf16[32,512]{1,0:T(8,128)(2,1)} %param.15) | copy-start | bytes 98308
  7.2 122.0 %all-gather.2.cloned.1.call-start = ((), (), s32[]{:S(2)}) async-start(), calls=%async_computation.5 | async-start | bytes 1949696 | tf_op jit(solution)/shard_map/all_gather | solution.py:411
  9.7 3.4 %collective-permute-start.8 = (bf16[48,1024]{1,0:T(8,128)(2,1)}, bf16[48,1024]{1,0:T(8,128)(2,1)S(1)}, u32[]{:S(2)}, u32[]{:S(2)}) collective-permute-start(bf16[48,1024]{1,0:T(8,128)(2,1)} %get-tuple-element.61), channel_id=1, source_target_pairs={{0,1},{1,0},{2,3},{3,2},{4,5},{5,4},{6,7},{7,6},{8,9},{9,8},{10,11... | collective-permute-start | bytes 294920 | tf_op jit(solution)/shard_map/ppermute | solution.py:58
  13.1 0.6 copy-start.3
  15.7 26.6 %all-to-all-start = ((bf16[16,144,128]{2,1,0:T(8,128)(2,1)}), bf16[16,144,128]{2,1,0:T(8,128)(2,1)S(1)}, u32[]{:S(2)}, u32[]{:S(2)}) async-start(bf16[16,144,128]{2,1,0:T(8,128)(2,1)} %get-tuple-element.25), calls=%async_computation | async-start | bytes 1179648 | tf_op jit(solution)/shard_map/cond/branch_1_fun/all_to_all | solution.py:414
  25.0 28.9 %collective-permute-start.5 = (bf16[448,512]{1,0:T(8,128)(2,1)S(1)}, bf16[448,512]{1,0:T(8,128)(2,1)S(1)}, u32[]{:S(2)}, u32[]{:S(2)}) collective-permute-start(bf16[448,512]{1,0:T(8,128)(2,1)S(1)} %get-tuple-element.28.down_ref), channel_id=1, source_target_pairs={{0,1},{1,0},{2,3},{3,2},{4,5},{5,4},{6,7},{7,6},{8,9},{9,8},{10,11... | collective-permute-start | bytes 1376264 | tf_op jit(solution)/shard_map/cond/branch_1_fun/ppermute | solution.py:58
  26.9 7.4 %collective-permute-start.1 = (bf16[1,32,512]{2,1,0:T(8,128)(2,1)S(1)}, bf16[1,32,512]{2,1,0:T(8,128)(2,1)S(1)}, u32[]{:S(2)}, u32[]{:S(2)}) collective-permute-start(bf16[1,32,512]{2,1,0:T(8,128)(2,1)S(1)} %bitcast.22), channel_id=1, source_target_pairs={{0,16},{16,0},{1,17},{17,1},{2,18},{18,2},{3,19},{19,3},{4,20},{20... | collective-permute-start | bytes 98312 | tf_op jit(solution)/shard_map/cond/branch_1_fun/cond/branch_1_fun/ppermute | solution.py:379
  43.0 20.9 %all-to-all-start.1 = ((f32[16,8,128]{2,1,0:T(8,128)}), f32[16,8,128]{2,1,0:T(8,128)S(1)}, u32[]{:S(2)}, u32[]{:S(2)}) async-start(f32[16,8,128]{2,1,0:T(8,128)} %branch_1_fun.8), calls=%async_computation.1 | async-start | bytes 131072 | tf_op jit(solution)/shard_map/cond/branch_1_fun/all_to_all | solution.py:417
  67.0 28.4 %all-to-all-start.2 = ((bf16[16,32,896]{2,1,0:T(8,128)(2,1)}), bf16[16,32,896]{2,1,0:T(8,128)(2,1)S(1)}, u32[]{:S(2)}, u32[]{:S(2)}) async-start(bf16[16,32,896]{2,1,0:T(8,128)(2,1)} %get-tuple-element.32), calls=%async_computation.2 | async-start | bytes 1835008 | tf_op jit(solution)/shard_map/cond/branch_1_fun/all_to_all | solution.py:419
  71.3 12.2 %collective-permute-start.4 = (bf16[2,32,512]{2,1,0:T(8,128)(2,1)}, bf16[2,32,512]{2,1,0:T(8,128)(2,1)S(1)}, u32[]{:S(2)}, u32[]{:S(2)}) collective-permute-start(bf16[2,32,512]{2,1,0:T(8,128)(2,1)} %branch_1_fun.7), channel_id=1, source_target_pairs={{0,12},{2,14},{4,8},{6,10},{8,4},{10,6},{12,0},{14,2},{1,13},{3,15... | collective-permute-start | bytes 196616 | tf_op jit(solution)/shard_map/cond/branch_1_fun/cond/branch_1_fun/ppermute | solution.py:379
  75.1 11.6 %collective-permute-start.3 = (bf16[2,32,512]{2,1,0:T(8,128)(2,1)}, bf16[2,32,512]{2,1,0:T(8,128)(2,1)S(1)}, u32[]{:S(2)}, u32[]{:S(2)}) collective-permute-start(bf16[2,32,512]{2,1,0:T(8,128)(2,1)} %branch_1_fun.7), channel_id=1, source_target_pairs={{0,8},{2,10},{4,12},{6,14},{8,0},{10,2},{12,4},{14,6},{1,9},{3,11}... | collective-permute-start | bytes 196616 | tf_op jit(solution)/shard_map/cond/branch_1_fun/cond/branch_1_fun/ppermute | solution.py:379
  80.0 7.4 %collective-permute-start.2 = (bf16[2,32,512]{2,1,0:T(8,128)(2,1)}, bf16[2,32,512]{2,1,0:T(8,128)(2,1)S(1)}, u32[]{:S(2)}, u32[]{:S(2)}) collective-permute-start(bf16[2,32,512]{2,1,0:T(8,128)(2,1)} %branch_1_fun.7), channel_id=1, source_target_pairs={{0,4},{2,6},{4,0},{6,2},{8,12},{10,14},{12,8},{14,10},{1,5},{3,7},... | collective-permute-start | bytes 196616 | tf_op jit(solution)/shard_map/cond/branch_1_fun/cond/branch_1_fun/ppermute | solution.py:379
  96.5 32.7 %all-to-all-start.3 = ((bf16[16,32,896]{2,1,0:T(8,128)(2,1)}), bf16[16,32,896]{2,1,0:T(8,128)(2,1)}, u32[]{:S(2)}, u32[]{:S(2)}) async-start(bf16[16,32,896]{2,1,0:T(8,128)(2,1)} %branch_1_fun.11), calls=%async_computation.3 | async-start | bytes 1835008 | tf_op jit(solution)/shard_map/cond/branch_1_fun/all_to_all | solution.py:424
  101.6 4.4 %collective-permute-start.6 = (bf16[2,448,512]{2,1,0:T(8,128)(2,1)S(1)}, bf16[2,448,512]{2,1,0:T(8,128)(2,1)S(1)}, u32[]{:S(2)}, u32[]{:S(2)}) collective-permute-start(bf16[2,448,512]{2,1,0:T(8,128)(2,1)S(1)} %pad_maximum_fusion.2), channel_id=1, source_target_pairs={{0,1},{1,0},{2,3},{3,2},{4,5},{5,4},{6,7},{7,6},{8,9},{9,8},{10,11... | collective-permute-start | bytes 2752520 | tf_op jit(solution)/shard_map/cond/branch_1_fun/ppermute | solution.py:58
  103.5 10.6 %collective-permute-start.7 = (bf16[8,32,512]{2,1,0:T(8,128)(2,1)S(1)}, bf16[8,32,512]{2,1,0:T(8,128)(2,1)S(1)}, u32[]{:S(2)}, u32[]{:S(2)}) collective-permute-start(bf16[8,32,512]{2,1,0:T(8,128)(2,1)S(1)} %get-tuple-element.36), channel_id=1, source_target_pairs={{0,2},{2,0},{4,6},{6,4},{8,10},{10,8},{12,14},{14,12},{1,3},{3,1},... | collective-permute-start | bytes 786440 | tf_op jit(solution)/shard_map/cond/branch_1_fun/ppermute | solution.py:379
  134.3 22.3 %all-to-all-start.4 = ((bf16[16,32,512]{2,1,0:T(8,128)(2,1)}), bf16[16,32,512]{2,1,0:T(8,128)(2,1)S(1)}, u32[]{:S(2)}, u32[]{:S(2)}) async-start(bf16[16,32,512]{2,1,0:T(8,128)(2,1)} %get-tuple-element.67), calls=%async_computation.4 | async-start | bytes 1048576 | tf_op jit(solution)/shard_map/all_to_all | solution.py:432
  146.3 5.0 %collective-permute-start = (bf16[3,448,512]{2,1,0:T(8,128)(2,1)S(1)}, bf16[3,448,512]{2,1,0:T(8,128)(2,1)S(1)}, u32[]{:S(2)}, u32[]{:S(2)}) collective-permute-start(bf16[3,448,512]{2,1,0:T(8,128)(2,1)S(1)} %get-tuple-element.42), channel_id=1, source_target_pairs={{0,1},{1,0},{2,3},{3,2},{4,5},{5,4},{6,7},{7,6},{8,9},{9,8},{10,11... | collective-permute-start | bytes 4128776 | tf_op jit(solution)/shard_map/cond/branch_1_fun/ppermute | solution.py:58
Sparse Core Ops, SparseCore 0:
  15.8 109.9 all-gather.1

commit v8 on v7

--- a/solution.py
+++ b/solution.py
@@ -109,17 +109,15 @@
     )(core, gate_pre, up_pre, gate_t, up_t, down)
 
 
-def second_kernel(core_ref, gate_pre_ref, up_pre_ref, other_ref, sums_ref, out_ref, pre_ref, sent_ref):
+def second_kernel(core_ref, gate_pre_ref, up_pre_ref, other_ref, sums_ref, out_ref, gate_rows_ref, up_rows_ref, sent_ref):
     rows, inner = gate_pre_ref.shape[0] // 2, gate_pre_ref.shape[1]
     lanes = other_ref.shape[1] // 2
-    pre_ref[...] = jnp.concatenate(
-        [
-            half_of(gate_pre_ref, core_ref[0]),
-            other_ref[0:rows, 0:inner],
-            half_of(up_pre_ref, core_ref[0]),
-            other_ref[0:rows, lanes : lanes + inner],
-        ],
-        axis=1,
+    pad = jnp.zeros((rows, gate_rows_ref.shape[1] - 2 * inner), jnp.bfloat16)
+    gate_rows_ref[...] = jnp.concatenate(
+        [half_of(gate_pre_ref, core_ref[0]), other_ref[0:rows, 0:inner], pad], axis=1
+    )
+    up_rows_ref[...] = jnp.concatenate(
+        [half_of(up_pre_ref, core_ref[0]), other_ref[0:rows, lanes : lanes + inner], pad], axis=1
     )
     others = totals_of(other_ref[rows:, :LANES].astype(jnp.float32))
     extra = pieces_of([sums_ref[n : n + 1, :] + others[n] for n in range(3)])
@@ -135,11 +133,12 @@
     return pl.pallas_call(
         second_kernel,
         out_shape=(
-            jax.ShapeDtypeStruct((rows, 4 * inner), jnp.bfloat16),
+            jax.ShapeDtypeStruct((rows, other.shape[1]), jnp.bfloat16),
+            jax.ShapeDtypeStruct((rows, other.shape[1]), jnp.bfloat16),
             jax.ShapeDtypeStruct((N_CHIP, rows * width // LANES + EXTRA, LANES), jnp.bfloat16),
         ),
         in_specs=[SMEM] + [VMEM] * 5,
-        out_specs=(VMEM, VMEM),
+        out_specs=(VMEM, VMEM, VMEM),
         compiler_params=WIDE,
         cost_estimate=cost(1 << 16, 1 << 20),
     )(core, gate_pre, up_pre, other, sums, grad_out)
@@ -176,7 +175,7 @@
     return jnp.clip(values.astype(jnp.float32), -scale, scale).astype(jnp.bfloat16)
 
 
-def partial_kernel(tile_ref, received_ref, down_ref, other_ref, partial_ref, out_ref, done_ref, quant_ref):
+def partial_kernel(tile_ref, received_ref, down_ref, other_ref, partial_ref, out_ref, quant_ref):
     rows = partial_ref.shape[1]
     inner, width = down_ref.shape
 
@@ -189,7 +188,6 @@
     blocks = [received_ref[:, j * rows : (j + 1) * rows, :] for j in range(width // LANES)]
     out_rows = jnp.concatenate([block.reshape((-1, LANES)) for block in blocks], axis=1)
     out_ref[...] = out_rows
-    done_ref[...] = jnp.zeros(done_ref.shape, jnp.float32)
     partial = contract_last(out_rows, quant_ref[...])
     partial_ref[...] = partial.astype(jnp.bfloat16).reshape(partial_ref.shape)
 
@@ -205,7 +203,6 @@
         out_shape=(
             jax.ShapeDtypeStruct((N_ROW, rows, 2 * inner), jnp.bfloat16),
             jax.ShapeDtypeStruct((N_CHIP * rows, width), jnp.bfloat16),
-            jax.ShapeDtypeStruct((8, LANES), jnp.float32),
         ),
         in_specs=[
             pl.BlockSpec(tile.shape, lambda i: (0, 0, 0)),
@@ -216,7 +213,6 @@
         out_specs=(
             pl.BlockSpec((blocks, rows, 2 * inner), lambda i: (i, 0, 0)),
             pl.BlockSpec((blocks * rows, width), lambda i: (i, 0)),
-            pl.BlockSpec((8, LANES), lambda i: (0, 0)),
         ),
         scratch_shapes=[pltpu.VMEM((2 * inner, width), jnp.bfloat16)],
         compiler_params=PARAMS,
@@ -261,20 +257,22 @@
     )(tile, gate_t, up_t, other)
 
 
-def act_kernel(hid_ref, pre_ref, quant_ref, partial_ref, acts_ref):
+def act_kernel(hid_ref, gate_ref, up_ref, quant_ref, partial_ref, acts_ref):
     both = hid_ref.shape[2]
     grad_hidden = hid_ref[...].reshape((-1, both)).astype(jnp.float32)
-    acts = swiglu_grads(grad_hidden, pre_ref[:, :both], pre_ref[:, both:])
+    up_pre = up_ref[...].reshape((-1, up_ref.shape[3]))[:, :both]
+    acts = swiglu_grads(grad_hidden, gate_ref[:, :both], up_pre)
     partial = matmul(acts[0], quant_ref[0]) + matmul(acts[1], quant_ref[1])
     partial_ref[...] = partial.astype(jnp.bfloat16).reshape(partial_ref.shape)
     for n, act in enumerate(acts):
         acts_ref[n] = act
 
 
-def act_partial(grad_hidden, pre_half, quant):
+def act_partial(grad_hidden, gate_half, up_half, quant):
     blocks, steps = 4, N_ROW // 4
     rows, both = grad_hidden.shape[1:]
-    width = quant.shape[2]
+    width, lanes = quant.shape[2], gate_half.shape[1]
+    up_half = up_half.reshape((N_ROW // 2, 2, rows, lanes))
     return pl.pallas_call(
         act_kernel,
         grid=(steps,),
@@ -284,7 +282,8 @@
         ),
         in_specs=[
             pl.BlockSpec((blocks, rows, both), lambda i: (i, 0, 0)),
-            pl.BlockSpec((blocks * rows, 2 * both), lambda i: (i, 0)),
+            pl.BlockSpec((blocks * rows, lanes), lambda i: (i, 0)),
+            pl.BlockSpec((blocks, 1, rows, lanes), lambda i: (i % 2, i // 2, 0, 0)),
             pl.BlockSpec(quant.shape, lambda i: (0, 0, 0)),
         ],
         out_specs=(
@@ -293,7 +292,7 @@
         ),
         compiler_params=WIDE,
         cost_estimate=cost(4 * 512 * 896 * 512, 8 << 20),
-    )(grad_hidden, pre_half, quant)
+    )(grad_hidden, gate_half, up_half, quant)
 
 
 def latent_grads_kernel(place_ref, acts_ref, out_ref, tokens_ref, own_ref, sent_ref, rows_ref):
@@ -407,17 +406,18 @@
 
     gate_t, up_t = gate_latent.T, up_latent.T
     sent, sums = first(core, gate_pre, up_pre, gate_t, up_t, down_latent)
-    pre_rows, sent = second(core, gate_pre, up_pre, swapped(sent), sums, grad_out)
-    pre_half = lax.all_gather(pre_rows, ROW, axis=0, tiled=True)
+    gate_rows, up_rows, sent = second(core, gate_pre, up_pre, swapped(sent), sums, grad_out)
+    gate_half = lax.all_gather(gate_rows, ROW, axis=0, tiled=True)
+    up_half = lax.all_gather(up_rows, ROW[::-1], axis=0, tiled=True)
 
     def exchanges(sent, tokens, gate_t, up_t, down):
         received = lax.all_to_all(sent, CHIP, 0, 0)
         down_other = swapped(down)
         pair, after = in_branch(token_pair, tokens)
         tile = lax.all_to_all(sums_tile(received, after), ROW, 0, 0)
-        partial, out_half, done = hidden_partial(tile, received, down, down_other)
+        partial, out_half = hidden_partial(tile, received, down, down_other)
         parts = lax.all_to_all(partial, ROW, 0, 0)
-        most_tokens, after = in_branch(far_tokens, pair, done)
+        most_tokens, after = in_branch(far_tokens, pair, out_half[:EXTRA, :LANES])
         other_latents = swapped(jnp.stack([gate_t, up_t]))
         quant = clipped_latents(tile, gate_t, up_t, other_latents)
         token_blocks = exchanged(most_tokens, "y", 1)
@@ -428,7 +428,7 @@
         exchanges, sent, tokens, gate_t, up_t, down_latent
     )
 
-    partial, acts = act_partial(grad_hidden, pre_half, quant)
+    partial, acts = act_partial(grad_hidden, gate_half, up_half, quant)
     parts = lax.all_to_all(partial, CHIP, 0, 0)
 
     def joined(place, acts, out_half, token_blocks):

time: 165 us -> 234 us (1.42)
  waiting for transfers between devices: 64.8 us -> 131 us
    all_gather x1 -> x2, waiting for transfers between devices: 0.01 us -> 74.6 us  [the longest x1 74.6 us: shards(): up_half = lax.all_gather(up_rows, ROW[::-1], axis=0, tiled=True)]
    all_to_all x1, waiting for transfers between devices: 14.2 us -> 10.4 us  [exchanges(): grad_hidden = lax.all_to_all(spread(parts, after), ROW, 0, 0)]
    all_to_all x1, waiting for transfers between devices: 7.09 us -> 4.32 us  [exchanges(): parts = lax.all_to_all(partial, ROW, 0, 0)]
    all_to_all x1, waiting for transfers between devices: 4.05 us -> 1.64 us  [shards(): parts = lax.all_to_all(partial, CHIP, 0, 0)]
  transfers between devices with their start and end apart: 15 -> 16, of which waited for: 12 -> 13; matrix products, arithmetic and copies ran while one was open for 1% -> 1% of each run, Pallas kernels for 7% -> 5%
where the time goes in v8:
time: 234 us; the launch traced here: 233 us
  waiting for transfers between devices  131 us (56%)
  starting transfers between devices  61.7 us (26%)
  Pallas kernels  22.1 us (9%)
  between operations  14.1 us (6%)
    all_gather x1, waiting for transfers between devices, shards(): up_half = lax.all_gather(up_rows, ROW[::-1], axis=0, tiled=True)  74.6 us
    ppermute x5, starting transfers between devices, exchanged(): lax.ppermute(blocks, axis, [(k, k ^ step) for k in range(count)])  16.5 us
    ppermute x5, waiting for transfers between devices, exchanged(): lax.ppermute(blocks, axis, [(k, k ^ step) for k in range(count)])  16.3 us
    all_to_all x1, starting transfers between devices, exchanges(): tile = lax.all_to_all(sums_tile(received, after), ROW, 0, 0)  10.9 us
    all_to_all x1, waiting for transfers between devices, exchanges(): grad_hidden = lax.all_to_all(spread(parts, after), ROW, 0, 0)  10.4 us
    all_to_all x1, waiting for transfers between devices, exchanges(): tile = lax.all_to_all(sums_tile(received, after), ROW, 0, 0)  10 us
    all_to_all x1, starting transfers between devices, exchanges(): received = lax.all_to_all(sent, CHIP, 0, 0)  9.23 us
    all_to_all x1, starting transfers between devices, shards(): parts = lax.all_to_all(partial, CHIP, 0, 0)  8.19 us
  transfers between devices with their start and end apart: 16, of which 13 were waited for; matrix products, arithmetic and copies ran while one was open for 1% of the time, Pallas kernels for 5%

profile of v8, /device:TPU:10, one launch (start us, length us, event | category | flops | bytes accessed | tf_op | source)
XLA Modules:
  0.0 233.0 jit_solution(17185239430690628184)
XLA Ops:
  7.2 0.0 copy-start
  7.2 0.0 copy-start.1
  7.2 0.0 copy-start.2
  7.2 0.0 copy-start.4
  7.2 0.0 all-gather.3.cloned.1.call-start
  7.3 2.5 %shard_map.106 = (bf16[48,1024]{1,0:T(8,128)(2,1)}, f32[8,128]{1,0:T(8,128)}) custom-call(s32[1]{0:T(128)} %bitcast.5.core_ref, bf16[64,448]{1,0:T(8,128)(2,1)} %gate_pre_ref.3, bf16[64,448]{1,0:T(8,128)(2,1)} %up_pre_ref.3, bf16[448,512]{1,0:T(8,128)(2,1)} %bitcast.15, bf16[448,512]{1,0:T(8,128)(2,1)} %bitcast.18, bf16[448,512]{1,0:T(8,128)(2,1)} %down_ref.1), custom_call_target="tpu_custom_call" | custom-call | flops 1048576 | bytes 1572864 | tf_op jit(solution)/shard_map/pallas_call | solution.py:99
  9.7 1.9 collective-permute-start.8
  11.6 1.5 collective-permute-done.8.other_ref
  13.1 0.0 copy-start.3
  13.1 0.6 copy-done.3
  13.8 1.9 shard_map.107
  15.7 0.0 all-gather.3.cloned.1.call-update
  15.7 0.0 all-gather.5.cloned.1.call-start
  15.8 0.7 all-gather.5.cloned.1.call-update
  16.5 0.0 copy-done
  16.5 0.0 copy-done.1
  16.5 0.0 copy-done.2
  16.5 0.0 copy-done.4
  16.5 109.3 %conditional.4 = (bf16[512,512]{1,0:T(8,128)(2,1)}, bf16[2,896,512]{2,1,0:T(8,128)(2,1)S(1)}, bf16[16,32,896]{2,1,0:T(8,128)(2,1)}, bf16[16,32,512]{2,1,0:T(8,128)(2,1)}) conditional(s32[]{:T(128)} %convert_element_type.8, () %tuple.39, (bf16[16,144,128]{2,1,0:T(8,128)(2,1)}, bf16[32,512]{1,0:T(8,128)(2,1)S(1)}, bf16[448,512]{1,0:T(8,128)(2,1)S(1)}, ...), branch_computations={%region_0.0_spmd, %region_1.0_spmd} | conditional | flops 472547328 | bytes 29319702 | solution.py:400
  16.5 9.2 %all-to-all-start = ((bf16[16,144,128]{2,1,0:T(8,128)(2,1)}), bf16[16,144,128]{2,1,0:T(8,128)(2,1)S(1)}, u32[]{:S(2)}, u32[]{:S(2)}) async-start(bf16[16,144,128]{2,1,0:T(8,128)(2,1)} %get-tuple-element.26), calls=%async_computation | async-start | bytes 1179648 | tf_op jit(solution)/shard_map/cond/branch_1_fun/all_to_all | solution.py:414
  25.7 1.9 collective-permute-start.5
  27.7 7.4 %conditional = (bf16[2,32,512]{2,1,0:T(8,128)(2,1)S(1)}, bf16[16,128]{1,0:T(8,128)(2,1)S(1)}) conditional(s32[]{:T(128)} %convert_element_type.1, () %tuple.28, bf16[32,512]{1,0:T(8,128)(2,1)S(1)} %get-tuple-element.78), branch_computations={%region_2.0_spmd, %region_3.0_spmd} | conditional | flops 32768 | bytes 270392 | solution.py:400
  27.7 2.4 %collective-permute-start.1 = (bf16[1,32,512]{2,1,0:T(8,128)(2,1)S(1)}, bf16[1,32,512]{2,1,0:T(8,128)(2,1)S(1)}, u32[]{:S(2)}, u32[]{:S(2)}) collective-permute-start(bf16[1,32,512]{2,1,0:T(8,128)(2,1)S(1)} %bitcast.24), channel_id=1, source_target_pairs={{0,16},{16,0},{1,17},{17,1},{2,18},{18,2},{3,19},{19,3},{4,20},{20... | collective-permute-start | bytes 98312 | tf_op jit(solution)/shard_map/cond/branch_1_fun/cond/branch_1_fun/ppermute | solution.py:378
  30.1 5.0 %collective-permute-done.1 = bf16[1,32,512]{2,1,0:T(8,128)(2,1)S(1)} collective-permute-done((bf16[1,32,512]{2,1,0:T(8,128)(2,1)S(1)}, bf16[1,32,512]{2,1,0:T(8,128)(2,1)S(1)}, u32[]{:S(2)}, u32[]{:S(2)}) %collective-permute-start.1) | collective-permute-done | bytes 32800 | tf_op jit(solution)/shard_map/cond/branch_1_fun/cond/branch_1_fun/ppermute | solution.py:378
  35.1 8.0 %all-to-all-done.extra_ref.received_ref = bf16[16,144,128]{2,1,0:T(8,128)(2,1)S(1)} async-done(((bf16[16,144,128]{2,1,0:T(8,128)(2,1)}), bf16[16,144,128]{2,1,0:T(8,128)(2,1)S(1)}, u32[]{:S(2)}, u32[]{:S(2)}) %all-to-all-start) | async-done | bytes 589856 | tf_op jit(solution)/shard_map/cond/branch_1_fun/all_to_all | solution.py:414
  43.1 0.7 branch_1_fun.8
  43.7 10.9 %all-to-all-start.1 = ((f32[16,8,128]{2,1,0:T(8,128)}), f32[16,8,128]{2,1,0:T(8,128)S(1)}, u32[]{:S(2)}, u32[]{:S(2)}) async-start(f32[16,8,128]{2,1,0:T(8,128)} %branch_1_fun.8), calls=%async_computation.1 | async-start | bytes 131072 | tf_op jit(solution)/shard_map/cond/branch_1_fun/all_to_all | solution.py:417
  54.6 0.0 collective-permute-done.5.other_ref
  54.6 10.0 %all-to-all-done.1.tile_ref = f32[16,8,128]{2,1,0:T(8,128)S(1)} async-done(((f32[16,8,128]{2,1,0:T(8,128)}), f32[16,8,128]{2,1,0:T(8,128)S(1)}, u32[]{:S(2)}, u32[]{:S(2)}) %all-to-all-start.1) | async-done | bytes 65568 | tf_op jit(solution)/shard_map/cond/branch_1_fun/all_to_all | solution.py:417
  64.6 3.1 %branch_1_fun.9 = (bf16[16,32,896]{2,1,0:T(8,128)(2,1)}, bf16[512,512]{1,0:T(8,128)(2,1)}) custom-call(f32[16,8,128]{2,1,0:T(8,128)S(1)} %all-to-all-done.1.tile_ref, bf16[16,144,128]{2,1,0:T(8,128)(2,1)S(1)} %all-to-all-done.extra_ref.received_ref, bf16[448,512]{1,0:T(8,128)(2,1)S(1)} %get-tuple-element.29.down_ref, ...), custom_call_target="tpu_custom_call" | custom-call | flops 469762048 | bytes 4194304 | tf_op jit(solution)/shard_map/cond/branch_1_fun/pallas_call | solution.py:200
  67.8 3.6 %all-to-all-start.2 = ((bf16[16,32,896]{2,1,0:T(8,128)(2,1)}), bf16[16,32,896]{2,1,0:T(8,128)(2,1)S(1)}, u32[]{:S(2)}, u32[]{:S(2)}) async-start(bf16[16,32,896]{2,1,0:T(8,128)(2,1)} %get-tuple-element.33), calls=%async_computation.2 | async-start | bytes 1835008 | tf_op jit(solution)/shard_map/cond/branch_1_fun/all_to_all | solution.py:419
  71.4 19.6 %conditional.1 = (bf16[8,32,512]{2,1,0:T(8,128)(2,1)S(1)}, bf16[16,128]{1,0:T(8,128)(2,1)S(1)}) conditional(s32[]{:T(128)} %convert_element_type.1, () %tuple.29, (bf16[512,512]{1,0:T(8,128)(2,1)}, bf16[2,32,512]{2,1,0:T(8,128)(2,1)S(1)}) %tuple.30), branch_computations={%region_4.0_spmd, %region_5.0_spmd} | conditional | flops 393217 | bytes 1392776 | solution.py:400
  71.4 1.3 slice.8.after_ref
  72.7 1.3 branch_1_fun.7
  74.0 3.9 %collective-permute-start.4 = (bf16[2,32,512]{2,1,0:T(8,128)(2,1)}, bf16[2,32,512]{2,1,0:T(8,128)(2,1)S(1)}, u32[]{:S(2)}, u32[]{:S(2)}) collective-permute-start(bf16[2,32,512]{2,1,0:T(8,128)(2,1)} %branch_1_fun.7), channel_id=1, source_target_pairs={{0,12},{2,14},{4,8},{6,10},{8,4},{10,6},{12,0},{14,2},{1,13},{3,15... | collective-permute-start | bytes 196616 | tf_op jit(solution)/shard_map/cond/branch_1_fun/cond/branch_1_fun/ppermute | solution.py:378
  77.9 4.9 %collective-permute-start.3 = (bf16[2,32,512]{2,1,0:T(8,128)(2,1)}, bf16[2,32,512]{2,1,0:T(8,128)(2,1)S(1)}, u32[]{:S(2)}, u32[]{:S(2)}) collective-permute-start(bf16[2,32,512]{2,1,0:T(8,128)(2,1)} %branch_1_fun.7), channel_id=1, source_target_pairs={{0,8},{2,10},{4,12},{6,14},{8,0},{10,2},{12,4},{14,6},{1,9},{3,11}... | collective-permute-start | bytes 196616 | tf_op jit(solution)/shard_map/cond/branch_1_fun/cond/branch_1_fun/ppermute | solution.py:378
  82.8 3.4 %collective-permute-start.2 = (bf16[2,32,512]{2,1,0:T(8,128)(2,1)}, bf16[2,32,512]{2,1,0:T(8,128)(2,1)S(1)}, u32[]{:S(2)}, u32[]{:S(2)}) collective-permute-start(bf16[2,32,512]{2,1,0:T(8,128)(2,1)} %branch_1_fun.7), channel_id=1, source_target_pairs={{0,4},{2,6},{4,0},{6,2},{8,12},{10,14},{12,8},{14,10},{1,5},{3,7},... | collective-permute-start | bytes 196616 | tf_op jit(solution)/shard_map/cond/branch_1_fun/cond/branch_1_fun/ppermute | solution.py:378
  86.2 0.0 collective-permute-done.4
  86.3 3.2 %collective-permute-done.3 = bf16[2,32,512]{2,1,0:T(8,128)(2,1)S(1)} collective-permute-done((bf16[2,32,512]{2,1,0:T(8,128)(2,1)}, bf16[2,32,512]{2,1,0:T(8,128)(2,1)S(1)}, u32[]{:S(2)}, u32[]{:S(2)}) %collective-permute-start.3) | collective-permute-done | bytes 65568 | tf_op jit(solution)/shard_map/cond/branch_1_fun/cond/branch_1_fun/ppermute | solution.py:378
  89.4 0.7 collective-permute-done.2
  90.1 0.9 pad_maximum_fusion.1
  91.0 4.3 %all-to-all-done.2.parts_ref = bf16[16,32,896]{2,1,0:T(8,128)(2,1)S(1)} async-done(((bf16[16,32,896]{2,1,0:T(8,128)(2,1)}), bf16[16,32,896]{2,1,0:T(8,128)(2,1)S(1)}, u32[]{:S(2)}, u32[]{:S(2)}) %all-to-all-start.2) | async-done | bytes 917536 | tf_op jit(solution)/shard_map/cond/branch_1_fun/all_to_all | solution.py:419
  95.3 1.1 branch_1_fun.11
  96.4 5.5 %all-to-all-start.3 = ((bf16[16,32,896]{2,1,0:T(8,128)(2,1)}), bf16[16,32,896]{2,1,0:T(8,128)(2,1)}, u32[]{:S(2)}, u32[]{:S(2)}) async-start(bf16[16,32,896]{2,1,0:T(8,128)(2,1)} %branch_1_fun.11), calls=%async_computation.3 | async-start | bytes 1835008 | tf_op jit(solution)/shard_map/cond/branch_1_fun/all_to_all | solution.py:424
  101.9 0.1 pad_maximum_fusion.2
  102.0 1.9 collective-permute-start.6
  104.0 1.9 collective-permute-start.7
  105.9 0.5 collective-permute-done.6.other_ref
  106.4 0.7 branch_1_fun.10
  107.1 7.5 %collective-permute-done.7 = bf16[8,32,512]{2,1,0:T(8,128)(2,1)S(1)} collective-permute-done((bf16[8,32,512]{2,1,0:T(8,128)(2,1)S(1)}, bf16[8,32,512]{2,1,0:T(8,128)(2,1)S(1)}, u32[]{:S(2)}, u32[]{:S(2)}) %collective-permute-start.7) | collective-permute-done | bytes 262176 | tf_op jit(solution)/shard_map/cond/branch_1_fun/ppermute | solution.py:378
  114.6 0.8 pad_maximum_fusion.3
  115.4 10.4 %all-to-all-done.3 = bf16[16,32,896]{2,1,0:T(8,128)(2,1)} async-done(((bf16[16,32,896]{2,1,0:T(8,128)(2,1)}), bf16[16,32,896]{2,1,0:T(8,128)(2,1)}, u32[]{:S(2)}, u32[]{:S(2)}) %all-to-all-start.3) | async-done | bytes 917536 | tf_op jit(solution)/shard_map/cond/branch_1_fun/all_to_all | solution.py:424
  125.8 0.0 all-gather.3.cloned.1.call-done.gate_ref
  125.8 74.6 %all-gather.5.cloned.1.call-done = bf16[512,1024]{1,0:T(8,128)(2,1)} async-done(((bf16[32,1024]{1,0:T(8,128)(2,1)}), bf16[512,1024]{1,0:T(8,128)(2,1)}) %all-gather.5.cloned.1.call-update) | async-done | bytes 1048592 | tf_op jit(solution)/shard_map/all_gather | solution.py:411
  200.4 5.2 %shard_map.108 = (bf16[16,32,512]{2,1,0:T(8,128)(2,1)}, bf16[3,512,896]{2,1,0:T(8,128)(2,1)}) custom-call(bf16[16,32,896]{2,1,0:T(8,128)(2,1)} %get-tuple-element.65.hid_ref, bf16[512,1024]{1,0:T(8,128)(2,1)} %all-gather.3.cloned.1.call-done.gate_ref, bf16[8,2,32,1024]{3,2,1,0:T(8,128)(2,1)} %bitcast.21, bf16[2,896,512]{2,1,0:T(8,128)(2,1)S(1)} %get-tuple-element.68.quant_ref), custom_call_target="tpu_custom_call" | custom-call | flops 939524096 | bytes 8388608 | tf_op jit(solution)/shard_map/pallas_call | solution.py:276
  205.5 8.2 %all-to-all-start.4 = ((bf16[16,32,512]{2,1,0:T(8,128)(2,1)}), bf16[16,32,512]{2,1,0:T(8,128)(2,1)S(1)}, u32[]{:S(2)}, u32[]{:S(2)}) async-start(bf16[16,32,512]{2,1,0:T(8,128)(2,1)} %get-tuple-element.69), calls=%async_computation.4 | async-start | bytes 1048576 | tf_op jit(solution)/shard_map/all_to_all | solution.py:432
  213.7 0.1 pad_add_fusion
  213.8 10.1 %conditional.5 = ((bf16[448,512]{1,0:T(8,128)(2,1)}, bf16[448,512]{1,0:T(8,128)(2,1)}, bf16[448,512]{1,0:T(8,128)(2,1)}, f32[8,128]{1,0:T(8,128)S(1)})) conditional(s32[]{:T(128)} %convert_element_type.8, () %tuple.41, (s32[2]{0:T(128)S(1)}, bf16[3,512,896]{2,1,0:T(8,128)(2,1)}, bf16[512,512]{1,0:T(8,128)(2,1)}, bf16[16,32,512]{2,1,0:T(8,128)(2,1)}) %tuple.42), branch_computations={%region_6.0_spmd, %region_7.0_spmd} | conditional | flops 1410334720 | bytes 19136560 | solution.py:400
  213.8 3.7 %branch_1_fun.12 = (f32[3,448,512]{2,1,0:T(8,128)S(1)}, bf16[3,448,512]{2,1,0:T(8,128)(2,1)S(1)}) custom-call(s32[2]{0:T(128)S(1)} %get-tuple-element.37.place_ref, bf16[3,512,896]{2,1,0:T(8,128)(2,1)} %get-tuple-element.38.acts_ref, bf16[512,512]{1,0:T(8,128)(2,1)} %get-tuple-element.39.out_ref, bf16[16,32,512]{2,1,0:T(8,128)(2,1)} %get-tuple-element.40.tokens_ref), custom_call_target="tpu_custom_call" | custom-call | flops 1409286144 | bytes 8388608 | tf_op jit(solution)/shard_map/cond/branch_1_fun/pallas_call | solution.py:315
  217.5 1.9 collective-permute-start
  219.4 3.1 %collective-permute-done.other_ref = bf16[3,448,512]{2,1,0:T(8,128)(2,1)S(1)} collective-permute-done((bf16[3,448,512]{2,1,0:T(8,128)(2,1)S(1)}, bf16[3,448,512]{2,1,0:T(8,128)(2,1)S(1)}, u32[]{:S(2)}, u32[]{:S(2)}) %collective-permute-start) | collective-permute-done | bytes 1376288 | tf_op jit(solution)/shard_map/cond/branch_1_fun/ppermute | solution.py:58
  222.5 1.4 branch_1_fun.13
  223.9 1.6 all-to-all-done.4.parts_ref
  225.5 0.7 shard_map.109
  (3 shorter events, 0.0 us)
Async XLA Ops:
  7.2 9.3 %copy-start = (bf16[512,448]{0,1:T(8,128)(2,1)S(1)}, bf16[512,448]{0,1:T(8,128)(2,1)}, u32[]{:S(2)}) copy-start(bf16[512,448]{0,1:T(8,128)(2,1)} %param.19) | copy-start | bytes 1376260
  7.2 9.3 %copy-start.1 = (bf16[512,448]{0,1:T(8,128)(2,1)S(1)}, bf16[512,448]{0,1:T(8,128)(2,1)}, u32[]{:S(2)}) copy-start(bf16[512,448]{0,1:T(8,128)(2,1)} %param.20) | copy-start | bytes 1376260
  7.2 9.3 %copy-start.2 = (bf16[448,512]{1,0:T(8,128)(2,1)S(1)}, bf16[448,512]{1,0:T(8,128)(2,1)}, u32[]{:S(2)}) copy-start(bf16[448,512]{1,0:T(8,128)(2,1)} %down_ref.1) | copy-start | bytes 1376260
  7.2 9.3 %copy-start.4 = (bf16[32,512]{1,0:T(8,128)(2,1)S(1)}, bf16[32,512]{1,0:T(8,128)(2,1)}, u32[]{:S(2)}) copy-start(bf16[32,512]{1,0:T(8,128)(2,1)} %param.15) | copy-start | bytes 98308
  7.2 118.6 %all-gather.3.cloned.1.call-start = ((), (), s32[]{:S(2)}) async-start(), calls=%async_computation.5 | async-start | bytes 1114112 | tf_op jit(solution)/shard_map/all_gather | solution.py:410
  9.7 3.4 %collective-permute-start.8 = (bf16[48,1024]{1,0:T(8,128)(2,1)}, bf16[48,1024]{1,0:T(8,128)(2,1)S(1)}, u32[]{:S(2)}, u32[]{:S(2)}) collective-permute-start(bf16[48,1024]{1,0:T(8,128)(2,1)} %get-tuple-element.62), channel_id=1, source_target_pairs={{0,1},{1,0},{2,3},{3,2},{4,5},{5,4},{6,7},{7,6},{8,9},{9,8},{10,11... | collective-permute-start | bytes 294920 | tf_op jit(solution)/shard_map/ppermute | solution.py:58
  13.1 0.6 copy-start.3
  15.7 184.7 %all-gather.5.cloned.1.call-start = ((), (), s32[]{:S(2)}) async-start(), calls=%async_computation.6 | async-start | bytes 1114112 | tf_op jit(solution)/shard_map/all_gather | solution.py:411
  16.5 26.6 %all-to-all-start = ((bf16[16,144,128]{2,1,0:T(8,128)(2,1)}), bf16[16,144,128]{2,1,0:T(8,128)(2,1)S(1)}, u32[]{:S(2)}, u32[]{:S(2)}) async-start(bf16[16,144,128]{2,1,0:T(8,128)(2,1)} %get-tuple-element.26), calls=%async_computation | async-start | bytes 1179648 | tf_op jit(solution)/shard_map/cond/branch_1_fun/all_to_all | solution.py:414
  25.7 28.9 %collective-permute-start.5 = (bf16[448,512]{1,0:T(8,128)(2,1)S(1)}, bf16[448,512]{1,0:T(8,128)(2,1)S(1)}, u32[]{:S(2)}, u32[]{:S(2)}) collective-permute-start(bf16[448,512]{1,0:T(8,128)(2,1)S(1)} %get-tuple-element.29.down_ref), channel_id=1, source_target_pairs={{0,1},{1,0},{2,3},{3,2},{4,5},{5,4},{6,7},{7,6},{8,9},{9,8},{10,11... | collective-permute-start | bytes 1376264 | tf_op jit(solution)/shard_map/cond/branch_1_fun/ppermute | solution.py:58
  27.7 7.4 %collective-permute-start.1 = (bf16[1,32,512]{2,1,0:T(8,128)(2,1)S(1)}, bf16[1,32,512]{2,1,0:T(8,128)(2,1)S(1)}, u32[]{:S(2)}, u32[]{:S(2)}) collective-permute-start(bf16[1,32,512]{2,1,0:T(8,128)(2,1)S(1)} %bitcast.24), channel_id=1, source_target_pairs={{0,16},{16,0},{1,17},{17,1},{2,18},{18,2},{3,19},{19,3},{4,20},{20... | collective-permute-start | bytes 98312 | tf_op jit(solution)/shard_map/cond/branch_1_fun/cond/branch_1_fun/ppermute | solution.py:378
  43.7 20.9 %all-to-all-start.1 = ((f32[16,8,128]{2,1,0:T(8,128)}), f32[16,8,128]{2,1,0:T(8,128)S(1)}, u32[]{:S(2)}, u32[]{:S(2)}) async-start(f32[16,8,128]{2,1,0:T(8,128)} %branch_1_fun.8), calls=%async_computation.1 | async-start | bytes 131072 | tf_op jit(solution)/shard_map/cond/branch_1_fun/all_to_all | solution.py:417
  67.8 27.6 %all-to-all-start.2 = ((bf16[16,32,896]{2,1,0:T(8,128)(2,1)}), bf16[16,32,896]{2,1,0:T(8,128)(2,1)S(1)}, u32[]{:S(2)}, u32[]{:S(2)}) async-start(bf16[16,32,896]{2,1,0:T(8,128)(2,1)} %get-tuple-element.33), calls=%async_computation.2 | async-start | bytes 1835008 | tf_op jit(solution)/shard_map/cond/branch_1_fun/all_to_all | solution.py:419
  74.0 12.2 %collective-permute-start.4 = (bf16[2,32,512]{2,1,0:T(8,128)(2,1)}, bf16[2,32,512]{2,1,0:T(8,128)(2,1)S(1)}, u32[]{:S(2)}, u32[]{:S(2)}) collective-permute-start(bf16[2,32,512]{2,1,0:T(8,128)(2,1)} %branch_1_fun.7), channel_id=1, source_target_pairs={{0,12},{2,14},{4,8},{6,10},{8,4},{10,6},{12,0},{14,2},{1,13},{3,15... | collective-permute-start | bytes 196616 | tf_op jit(solution)/shard_map/cond/branch_1_fun/cond/branch_1_fun/ppermute | solution.py:378
  77.9 11.6 %collective-permute-start.3 = (bf16[2,32,512]{2,1,0:T(8,128)(2,1)}, bf16[2,32,512]{2,1,0:T(8,128)(2,1)S(1)}, u32[]{:S(2)}, u32[]{:S(2)}) collective-permute-start(bf16[2,32,512]{2,1,0:T(8,128)(2,1)} %branch_1_fun.7), channel_id=1, source_target_pairs={{0,8},{2,10},{4,12},{6,14},{8,0},{10,2},{12,4},{14,6},{1,9},{3,11}... | collective-permute-start | bytes 196616 | tf_op jit(solution)/shard_map/cond/branch_1_fun/cond/branch_1_fun/ppermute | solution.py:378
  82.8 7.4 %collective-permute-start.2 = (bf16[2,32,512]{2,1,0:T(8,128)(2,1)}, bf16[2,32,512]{2,1,0:T(8,128)(2,1)S(1)}, u32[]{:S(2)}, u32[]{:S(2)}) collective-permute-start(bf16[2,32,512]{2,1,0:T(8,128)(2,1)} %branch_1_fun.7), channel_id=1, source_target_pairs={{0,4},{2,6},{4,0},{6,2},{8,12},{10,14},{12,8},{14,10},{1,5},{3,7},... | collective-permute-start | bytes 196616 | tf_op jit(solution)/shard_map/cond/branch_1_fun/cond/branch_1_fun/ppermute | solution.py:378
  96.4 29.4 %all-to-all-start.3 = ((bf16[16,32,896]{2,1,0:T(8,128)(2,1)}), bf16[16,32,896]{2,1,0:T(8,128)(2,1)}, u32[]{:S(2)}, u32[]{:S(2)}) async-start(bf16[16,32,896]{2,1,0:T(8,128)(2,1)} %branch_1_fun.11), calls=%async_computation.3 | async-start | bytes 1835008 | tf_op jit(solution)/shard_map/cond/branch_1_fun/all_to_all | solution.py:424
  102.0 4.4 %collective-permute-start.6 = (bf16[2,448,512]{2,1,0:T(8,128)(2,1)S(1)}, bf16[2,448,512]{2,1,0:T(8,128)(2,1)S(1)}, u32[]{:S(2)}, u32[]{:S(2)}) collective-permute-start(bf16[2,448,512]{2,1,0:T(8,128)(2,1)S(1)} %pad_maximum_fusion.2), channel_id=1, source_target_pairs={{0,1},{1,0},{2,3},{3,2},{4,5},{5,4},{6,7},{7,6},{8,9},{9,8},{10,11... | collective-permute-start | bytes 2752520 | tf_op jit(solution)/shard_map/cond/branch_1_fun/ppermute | solution.py:58
  104.0 10.6 %collective-permute-start.7 = (bf16[8,32,512]{2,1,0:T(8,128)(2,1)S(1)}, bf16[8,32,512]{2,1,0:T(8,128)(2,1)S(1)}, u32[]{:S(2)}, u32[]{:S(2)}) collective-permute-start(bf16[8,32,512]{2,1,0:T(8,128)(2,1)S(1)} %get-tuple-element.36), channel_id=1, source_target_pairs={{0,2},{2,0},{4,6},{6,4},{8,10},{10,8},{12,14},{14,12},{1,3},{3,1},... | collective-permute-start | bytes 786440 | tf_op jit(solution)/shard_map/cond/branch_1_fun/ppermute | solution.py:378
  205.5 20.0 %all-to-all-start.4 = ((bf16[16,32,512]{2,1,0:T(8,128)(2,1)}), bf16[16,32,512]{2,1,0:T(8,128)(2,1)S(1)}, u32[]{:S(2)}, u32[]{:S(2)}) async-start(bf16[16,32,512]{2,1,0:T(8,128)(2,1)} %get-tuple-element.69), calls=%async_computation.4 | async-start | bytes 1048576 | tf_op jit(solution)/shard_map/all_to_all | solution.py:432
  217.5 5.0 %collective-permute-start = (bf16[3,448,512]{2,1,0:T(8,128)(2,1)S(1)}, bf16[3,448,512]{2,1,0:T(8,128)(2,1)S(1)}, u32[]{:S(2)}, u32[]{:S(2)}) collective-permute-start(bf16[3,448,512]{2,1,0:T(8,128)(2,1)S(1)} %get-tuple-element.42), channel_id=1, source_target_pairs={{0,1},{1,0},{2,3},{3,2},{4,5},{5,4},{6,7},{7,6},{8,9},{9,8},{10,11... | collective-permute-start | bytes 4128776 | tf_op jit(solution)/shard_map/cond/branch_1_fun/ppermute | solution.py:58
Sparse Core Ops, SparseCore 0:
  15.8 96.4 all-gather.2
  116.1 84.2 all-gather.4

commit v9 on v7

--- a/solution.py
+++ b/solution.py
@@ -73,76 +73,27 @@
     return [jnp.sum(pieces[3 * k : 3 * k + 3], axis=0, keepdims=True) for k in range(3)]
 
 
-def half_of(ref, core):
-    rows = ref.shape[0] // 2
-    return ref[pl.ds(pl.multiple_of(core * rows, rows), rows), :]
-
-
-def first_kernel(core_ref, gate_pre_ref, up_pre_ref, gate_ref, up_ref, down_ref, sent_ref, sums_ref):
-    rows, inner = gate_pre_ref.shape[0] // 2, gate_pre_ref.shape[1]
-    lanes = sent_ref.shape[1] // 2
+def first_kernel(out_ref, gate_ref, up_ref, down_ref, sent_ref):
     sums = []
     for ref in (gate_ref, up_ref, down_ref):
         total = jnp.sum(jnp.abs(ref[...].astype(jnp.float32)), axis=0, keepdims=True)
-        sums.append(jnp.broadcast_to(jnp.sum(total, axis=1, keepdims=True), (1, 2 * lanes)))
-    sent_ref[...] = jnp.zeros(sent_ref.shape, sent_ref.dtype)
-    sent_ref[0:rows, 0:inner] = half_of(gate_pre_ref, 1 - core_ref[0])
-    sent_ref[0:rows, lanes : lanes + inner] = half_of(up_pre_ref, 1 - core_ref[0])
-    sent_ref[rows:, :] = pieces_of(sums)
-    tile = jnp.concatenate(sums + [jnp.zeros((5, 2 * lanes), jnp.float32)], axis=0)
-    sums_ref[...] = tile[:, :LANES]
-
-
-def first(core, gate_pre, up_pre, gate_t, up_t, down):
-    rows, inner = gate_pre.shape
-    lanes = -(-inner // LANES) * LANES
-    return pl.pallas_call(
-        first_kernel,
-        out_shape=(
-            jax.ShapeDtypeStruct((rows // 2 + EXTRA, 2 * lanes), jnp.bfloat16),
-            jax.ShapeDtypeStruct((8, LANES), jnp.float32),
-        ),
-        in_specs=[SMEM] + [VMEM] * 5,
-        out_specs=(VMEM, VMEM),
-        compiler_params=WIDE,
-        cost_estimate=cost(1 << 20, 3 << 19),
-    )(core, gate_pre, up_pre, gate_t, up_t, down)
-
-
-def second_kernel(core_ref, gate_pre_ref, up_pre_ref, other_ref, sums_ref, out_ref, pre_ref, sent_ref):
-    rows, inner = gate_pre_ref.shape[0] // 2, gate_pre_ref.shape[1]
-    lanes = other_ref.shape[1] // 2
-    pre_ref[...] = jnp.concatenate(
-        [
-            half_of(gate_pre_ref, core_ref[0]),
-            other_ref[0:rows, 0:inner],
-            half_of(up_pre_ref, core_ref[0]),
-            other_ref[0:rows, lanes : lanes + inner],
-        ],
-        axis=1,
-    )
-    others = totals_of(other_ref[rows:, :LANES].astype(jnp.float32))
-    extra = pieces_of([sums_ref[n : n + 1, :] + others[n] for n in range(3)])
+        sums.append(jnp.broadcast_to(jnp.sum(total, axis=1, keepdims=True), (1, LANES)))
     blocks = [out_ref[:, j * LANES : (j + 1) * LANES] for j in range(out_ref.shape[1] // LANES)]
-    block = jnp.concatenate(blocks + [extra], axis=0)
+    block = jnp.concatenate(blocks + [pieces_of(sums)], axis=0)
     for k in range(N_CHIP):
         sent_ref[k] = block
 
 
-def second(core, gate_pre, up_pre, other, sums, grad_out):
+def first(grad_out, gate_t, up_t, down):
     rows, width = grad_out.shape
-    inner = gate_pre.shape[1]
-    return pl.pallas_call(
-        second_kernel,
-        out_shape=(
-            jax.ShapeDtypeStruct((rows, 4 * inner), jnp.bfloat16),
-            jax.ShapeDtypeStruct((N_CHIP, rows * width // LANES + EXTRA, LANES), jnp.bfloat16),
-        ),
-        in_specs=[SMEM] + [VMEM] * 5,
-        out_specs=(VMEM, VMEM),
+    return pl.pallas_call(
+        first_kernel,
+        out_shape=jax.ShapeDtypeStruct((N_CHIP, rows * width // LANES + EXTRA, LANES), jnp.bfloat16),
+        in_specs=[VMEM] * 4,
+        out_specs=VMEM,
         compiler_params=WIDE,
-        cost_estimate=cost(1 << 16, 1 << 20),
-    )(core, gate_pre, up_pre, other, sums, grad_out)
+        cost_estimate=cost(1 << 20, 5 << 19),
+    )(grad_out, gate_t, up_t, down)
 
 
 def tile_kernel(extra_ref, after_ref, tile_ref):
@@ -156,12 +107,12 @@
     return pl.pallas_call(
         tile_kernel,
         grid=(1,),
-        out_shape=jax.ShapeDtypeStruct((N_ROW, 8, LANES), jnp.float32),
+        out_shape=jax.ShapeDtypeStruct((2 * N_ROW, 8, LANES), jnp.float32),
         in_specs=[
             pl.BlockSpec((N_CHIP, EXTRA, LANES), lambda i: (0, rows // EXTRA, 0)),
             pl.BlockSpec(after.shape, lambda i: (0, 0)),
         ],
-        out_specs=pl.BlockSpec((N_ROW, 8, LANES), lambda i: (0, 0, 0)),
+        out_specs=pl.BlockSpec((2 * N_ROW, 8, LANES), lambda i: (0, 0, 0)),
         compiler_params=PARAMS,
         cost_estimate=cost(1 << 16, 1 << 18),
     )(received, after)
@@ -176,7 +127,7 @@
     return jnp.clip(values.astype(jnp.float32), -scale, scale).astype(jnp.bfloat16)
 
 
-def partial_kernel(tile_ref, received_ref, down_ref, other_ref, partial_ref, out_ref, done_ref, quant_ref):
+def partial_kernel(tile_ref, received_ref, down_ref, other_ref, partial_ref, out_ref, quant_ref):
     rows = partial_ref.shape[1]
     inner, width = down_ref.shape
 
@@ -189,7 +140,6 @@
     blocks = [received_ref[:, j * rows : (j + 1) * rows, :] for j in range(width // LANES)]
     out_rows = jnp.concatenate([block.reshape((-1, LANES)) for block in blocks], axis=1)
     out_ref[...] = out_rows
-    done_ref[...] = jnp.zeros(done_ref.shape, jnp.float32)
     partial = contract_last(out_rows, quant_ref[...])
     partial_ref[...] = partial.astype(jnp.bfloat16).reshape(partial_ref.shape)
 
@@ -205,7 +155,6 @@
         out_shape=(
             jax.ShapeDtypeStruct((N_ROW, rows, 2 * inner), jnp.bfloat16),
             jax.ShapeDtypeStruct((N_CHIP * rows, width), jnp.bfloat16),
-            jax.ShapeDtypeStruct((8, LANES), jnp.float32),
         ),
         in_specs=[
             pl.BlockSpec(tile.shape, lambda i: (0, 0, 0)),
@@ -216,7 +165,6 @@
         out_specs=(
             pl.BlockSpec((blocks, rows, 2 * inner), lambda i: (i, 0, 0)),
             pl.BlockSpec((blocks * rows, width), lambda i: (i, 0)),
-            pl.BlockSpec((8, LANES), lambda i: (0, 0)),
         ),
         scratch_shapes=[pltpu.VMEM((2 * inner, width), jnp.bfloat16)],
         compiler_params=PARAMS,
@@ -264,7 +212,8 @@
 def act_kernel(hid_ref, pre_ref, quant_ref, partial_ref, acts_ref):
     both = hid_ref.shape[2]
     grad_hidden = hid_ref[...].reshape((-1, both)).astype(jnp.float32)
-    acts = swiglu_grads(grad_hidden, pre_ref[:, :both], pre_ref[:, both:])
+    pre = pre_ref[...].reshape((-1, 2 * both))
+    acts = swiglu_grads(grad_hidden, pre[:, :both], pre[:, both:])
     partial = matmul(acts[0], quant_ref[0]) + matmul(acts[1], quant_ref[1])
     partial_ref[...] = partial.astype(jnp.bfloat16).reshape(partial_ref.shape)
     for n, act in enumerate(acts):
@@ -284,7 +233,7 @@
         ),
         in_specs=[
             pl.BlockSpec((blocks, rows, both), lambda i: (i, 0, 0)),
-            pl.BlockSpec((blocks * rows, 2 * both), lambda i: (i, 0)),
+            pl.BlockSpec((blocks, 1, rows, 2 * both), lambda i: (i % 2, i // 2, 0, 0)),
             pl.BlockSpec(quant.shape, lambda i: (0, 0, 0)),
         ],
         out_specs=(
@@ -293,14 +242,14 @@
         ),
         compiler_params=WIDE,
         cost_estimate=cost(4 * 512 * 896 * 512, 8 << 20),
-    )(grad_hidden, pre_half, quant)
+    )(grad_hidden, pre_half.reshape((N_ROW // 2, 2, rows, 2 * both)), quant)
 
 
 def latent_grads_kernel(place_ref, acts_ref, out_ref, tokens_ref, own_ref, sent_ref, rows_ref):
     rows = tokens_ref.shape[1]
     for block in range(2 * N_Y):
-        flip, bits = block & 1, block >> 1
-        offset = 2 * (bits & 3) + bits // 4
+        flip = (block >> 2) & 1
+        offset = 2 * (block & 3) + (block >> 3)
         chip = (place_ref[0] ^ flip) * N_Y + (place_ref[1] ^ offset)
         rows_ref[pl.ds(pl.multiple_of(chip * rows, rows), rows), :] = tokens_ref[block]
     inner = own_ref.shape[1]
@@ -380,14 +329,24 @@
     return jnp.concatenate([blocks] + others, axis=0)
 
 
-def token_pair(tokens):
-    blocks = exchanged(tokens[None], "xl", 1)
+def far_tokens(tokens, done):
+    blocks = exchanged(copy_after(tokens, done)[None], "y", 2, 4, 6)
     return blocks, blocks[-1, :EXTRA, :LANES]
 
 
-def far_tokens(blocks, done):
-    blocks = exchanged(copy_after(blocks, done), "y", 2, 4, 6)
-    return blocks, blocks[-1, :EXTRA, :LANES]
+def own_half(core, gate_pre, up_pre):
+    inner = gate_pre.shape[1]
+    pre = jnp.concatenate([gate_pre, up_pre], axis=1).reshape((2, -1, 2 * inner))
+    own = lax.dynamic_index_in_dim(pre, core, 0, keepdims=False)
+    other = swapped(lax.dynamic_index_in_dim(pre, 1 - core, 0, keepdims=False))
+    rows = jnp.concatenate(
+        [own[:, :inner], other[:, :inner], own[:, inner:], other[:, inner:]], axis=1
+    )
+    other = lax.ppermute(rows, "xh", [(0, 1), (1, 0)])
+    pair = jnp.where(
+        lax.axis_index("xh") == 0, jnp.stack([rows, other]), jnp.stack([other, rows])
+    )
+    return pair.reshape((-1, 4 * inner)), pair[0, :EXTRA, :LANES]
 
 
 def in_branch(work, *operands):
@@ -402,30 +361,35 @@
 
 
 def shards(tokens, grad_out, gate_pre, up_pre, gate_latent, up_latent, down_latent):
-    core = lax.axis_index("core").astype(jnp.int32).reshape((1,))
+    core = lax.axis_index("core")
     place = jnp.stack([lax.axis_index("xl"), lax.axis_index("y")]).astype(jnp.int32)
-
     gate_t, up_t = gate_latent.T, up_latent.T
-    sent, sums = first(core, gate_pre, up_pre, gate_t, up_t, down_latent)
-    pre_rows, sent = second(core, gate_pre, up_pre, swapped(sent), sums, grad_out)
-    pre_half = lax.all_gather(pre_rows, ROW, axis=0, tiled=True)
-
-    def exchanges(sent, tokens, gate_t, up_t, down):
+    sent = first(grad_out, gate_t, up_t, down_latent)
+
+    def gathers(sent, core, gate_pre, up_pre, down):
         received = lax.all_to_all(sent, CHIP, 0, 0)
         down_other = swapped(down)
-        pair, after = in_branch(token_pair, tokens)
-        tile = lax.all_to_all(sums_tile(received, after), ROW, 0, 0)
-        partial, out_half, done = hidden_partial(tile, received, down, down_other)
+        pre_rows, after = in_branch(own_half, core, gate_pre, up_pre)
+        return (received, down_other, pre_rows, sums_tile(received, after))
+
+    received, down_other, pre_rows, tile = in_branch(
+        gathers, sent, core, gate_pre, up_pre, down_latent
+    )
+    pre_half = lax.all_gather(pre_rows, "z", axis=0, tiled=True)
+
+    def exchanges(received, tile, tokens, gate_t, up_t, down, down_other):
+        tile = lax.all_to_all(tile, ROW + ("core",), 0, 0)
+        partial, out_half = hidden_partial(tile, received, down, down_other)
         parts = lax.all_to_all(partial, ROW, 0, 0)
-        most_tokens, after = in_branch(far_tokens, pair, done)
+        far, after = in_branch(far_tokens, tokens, out_half[:EXTRA, :LANES])
         other_latents = swapped(jnp.stack([gate_t, up_t]))
         quant = clipped_latents(tile, gate_t, up_t, other_latents)
-        token_blocks = exchanged(most_tokens, "y", 1)
+        token_blocks = exchanged(exchanged(far, "xl", 1), "y", 1)
         grad_hidden = lax.all_to_all(spread(parts, after), ROW, 0, 0)
         return (out_half, quant, grad_hidden, token_blocks)
 
     out_half, quant, grad_hidden, token_blocks = in_branch(
-        exchanges, sent, tokens, gate_t, up_t, down_latent
+        exchanges, received, tile, tokens, gate_t, up_t, down_latent, down_other
     )
 
     partial, acts = act_partial(grad_hidden, pre_half, quant)

time: 165 us -> 167 us (1.012)
  the two profiles are of different devices: /device:TPU:10 before, /device:TPU:14 now
where the time goes in v9:
time: 167 us; the launch traced here: 166 us
  starting transfers between devices  60.4 us (36%)
  waiting for transfers between devices  42 us (25%)
  blocking collectives  23 us (14%)
  Pallas kernels  21.8 us (13%)
  between operations  14.1 us (8%)
  local copies, waits for them, and re-layouts  2.27 us (1%)
  other arithmetic  1.81 us (1%)
    all_to_all x1, blocking collectives, exchanges(): tile = lax.all_to_all(tile, ROW + ('core',), 0, 0)  23 us
    ppermute x5, waiting for transfers between devices, exchanged(): lax.ppermute(blocks, axis, [(k, k ^ step) for k in range(count)])  18.4 us
    ppermute x5, starting transfers between devices, exchanged(): lax.ppermute(blocks, axis, [(k, k ^ step) for k in range(count)])  17.1 us
    all_to_all x1, waiting for transfers between devices, exchanges(): parts = lax.all_to_all(partial, ROW, 0, 0)  9.08 us
    all_to_all x1, starting transfers between devices, gathers(): received = lax.all_to_all(sent, CHIP, 0, 0)  8.61 us
    ppermute x4, starting transfers between devices, swapped(): return lax.ppermute(values, 'core', [(0, 1), (1, 0)])  8.16 us
    all_to_all x1, starting transfers between devices, shards(): parts = lax.all_to_all(partial, CHIP, 0, 0)  7.95 us
    all_to_all x1, starting transfers between devices, exchanges(): grad_hidden = lax.all_to_all(spread(parts, after), ROW, 0, 0)  7.4 us
  transfers between devices with their start and end apart: 15, of which 10 were waited for; matrix products, arithmetic and copies ran while one was open for 2% of the time, Pallas kernels for 8%

profile of v9, /device:TPU:14, one launch (start us, length us, event | category | flops | bytes accessed | tf_op | source)
XLA Modules:
  0.0 165.6 jit_solution(180971185749939861)
XLA Ops:
  7.2 0.0 copy-start.2
  7.2 0.0 copy-start.3
  7.2 0.0 copy-start.4
  7.2 0.0 all-gather.2.cloned.1.call-start
  7.2 2.6 %shard_map.105 = bf16[16,144,128]{2,1,0:T(8,128)(2,1)} custom-call(bf16[32,512]{1,0:T(8,128)(2,1)} %out_ref.1, bf16[448,512]{1,0:T(8,128)(2,1)} %bitcast.22, bf16[448,512]{1,0:T(8,128)(2,1)} %bitcast.25, bf16[448,512]{1,0:T(8,128)(2,1)} %down_ref.1), custom_call_target="tpu_custom_call" | custom-call | flops 1048576 | bytes 2621440 | tf_op jit(solution)/shard_map/pallas_call | solution.py:89
  9.8 0.0 copy-done.2
  9.8 0.0 copy-done.3
  9.8 0.0 copy-start
  9.8 0.0 copy-start.1
  9.9 26.7 %conditional.5 = (bf16[16,144,128]{2,1,0:T(8,128)(2,1)}, bf16[448,512]{1,0:T(8,128)(2,1)}, bf16[64,1792]{1,0:T(8,128)(2,1)}, f32[32,8,128]{2,1,0:T(8,128)S(1)}) conditional(s32[]{:T(128)} %convert_element_type.11, () %tuple.48, (bf16[16,144,128]{2,1,0:T(8,128)(2,1)}, bf16[448,512]{1,0:T(8,128)(2,1)S(1)}, bf16[64,448]{1,0:T(8,128)(2,1)S(1)}, ...), branch_computations={%region_0.0_spmd, %region_1.4_spmd} | conditional | flops 638992 | bytes 5939600 | solution.py:360
  9.9 8.6 %all-to-all-start.3 = ((bf16[16,144,128]{2,1,0:T(8,128)(2,1)}), bf16[16,144,128]{2,1,0:T(8,128)(2,1)}, u32[]{:S(2)}, u32[]{:S(2)}) async-start(bf16[16,144,128]{2,1,0:T(8,128)(2,1)} %get-tuple-element.46), calls=%async_computation.3 | async-start | bytes 1179648 | tf_op jit(solution)/shard_map/cond/branch_1_fun/all_to_all | solution.py:370
  18.5 1.9 %collective-permute-start.9 = (bf16[448,512]{1,0:T(8,128)(2,1)S(1)}, bf16[448,512]{1,0:T(8,128)(2,1)}, u32[]{:S(2)}, u32[]{:S(2)}) collective-permute-start(bf16[448,512]{1,0:T(8,128)(2,1)S(1)} %get-tuple-element.47), channel_id=1, source_target_pairs={{0,1},{1,0},{2,3},{3,2},{4,5},{5,4},{6,7},{7,6},{8,9},{9,8},{10,11... | collective-permute-start | bytes 1376264 | tf_op jit(solution)/shard_map/cond/branch_1_fun/ppermute | solution.py:58
  20.4 15.3 %conditional = (bf16[64,1792]{1,0:T(8,128)(2,1)}, bf16[16,128]{1,0:T(8,128)(2,1)S(1)}) conditional(s32[]{:T(128)} %convert_element_type.3, () %tuple.29, (bf16[64,448]{1,0:T(8,128)(2,1)S(1)}, bf16[64,448]{1,0:T(8,128)(2,1)S(1)}, s32[]{:T(128)}) %tuple.30), branch_computations={%region_2.0_spmd, %region_3.3_spmd} | conditional | flops 573451 | bytes 2072802 | solution.py:360
  20.4 0.1 pad_maximum_fusion
  20.5 2.4 %collective-permute-start.7 = (bf16[32,896]{1,0:T(8,128)(2,1)S(1)}, bf16[32,896]{1,0:T(8,128)(2,1)S(1)}, u32[]{:S(2)}, u32[]{:S(2)}) collective-permute-start(bf16[32,896]{1,0:T(8,128)(2,1)S(1)} %get-tuple-element.110), channel_id=1, source_target_pairs={{0,1},{1,0},{2,3},{3,2},{4,5},{5,4},{6,7},{7,6},{8,9},{9,8},{10,11... | collective-permute-start | bytes 172040 | tf_op jit(solution)/shard_map/cond/branch_1_fun/cond/branch_1_fun/ppermute | solution.py:58
  22.9 0.1 fusion.1
  23.0 0.8 collective-permute-done.7
  23.8 0.1 fusion
  23.9 0.1 concatenate.12
  24.0 4.7 %collective-permute-start.8 = (bf16[32,1792]{1,0:T(8,128)(2,1)S(1)}, bf16[32,1792]{1,0:T(8,128)(2,1)S(1)}, u32[]{:S(2)}, u32[]{:S(2)}) collective-permute-start(bf16[32,1792]{1,0:T(8,128)(2,1)S(1)} %concatenate.12), channel_id=1, source_target_pairs={{0,256},{256,0},{1,257},{257,1},{2,258},{258,2},{3,259},{259,3},{4... | collective-permute-start | bytes 344072 | tf_op jit(solution)/shard_map/cond/branch_1_fun/cond/branch_1_fun/ppermute | solution.py:345
  28.7 5.6 %collective-permute-done.8 = bf16[32,1792]{1,0:T(8,128)(2,1)S(1)} collective-permute-done((bf16[32,1792]{1,0:T(8,128)(2,1)S(1)}, bf16[32,1792]{1,0:T(8,128)(2,1)S(1)}, u32[]{:S(2)}, u32[]{:S(2)}) %collective-permute-start.8) | collective-permute-done | bytes 114720 | tf_op jit(solution)/shard_map/cond/branch_1_fun/cond/branch_1_fun/ppermute | solution.py:345
  34.2 0.7 maximum_select_fusion
  35.0 0.7 slice_bitcast_fusion
  35.6 0.0 all-to-all-done.3.extra_ref
  35.6 0.9 branch_1_fun.7
  36.5 0.0 collective-permute-done.9
  36.5 0.0 all-gather.2.cloned.1.call-update
  36.6 93.6 %conditional.6 = (bf16[512,512]{1,0:T(8,128)(2,1)}, bf16[2,896,512]{2,1,0:T(8,128)(2,1)S(1)}, bf16[16,32,896]{2,1,0:T(8,128)(2,1)}, bf16[16,32,512]{2,1,0:T(8,128)(2,1)S(1)}) conditional(s32[]{:T(128)} %convert_element_type.11, () %tuple.47, (f32[32,8,128]{2,1,0:T(8,128)S(1)}, bf16[16,144,128]{2,1,0:T(8,128)(2,1)}, bf16[448,512]{1,0:T(8,128)(2,1)S(1)}, ...), branch_computations={%region_4.5_spmd, %region_5.8_spmd} | conditional | flops 472645632 | bytes 25772472 | solution.py:360
  36.6 23.0 %all_to_all.21.tile_ref = f32[32,8,128]{2,1,0:T(8,128)S(1)} all-to-all(f32[32,8,128]{2,1,0:T(8,128)S(1)} %get-tuple-element.55), channel_id=1, replica_groups=mesh['xh'=2,'z'=8,'xl'=2,'y'=8,'core'=2] {'xh','z','core'}, dimensions={0} | all-to-all | bytes 262144 | tf_op jit(solution)/shard_map/cond/branch_1_fun/all_to_all | solution.py:381
  59.6 4.7 %branch_1_fun.9 = (bf16[16,32,896]{2,1,0:T(8,128)(2,1)}, bf16[512,512]{1,0:T(8,128)(2,1)}) custom-call(f32[32,8,128]{2,1,0:T(8,128)S(1)} %all_to_all.21.tile_ref, bf16[16,144,128]{2,1,0:T(8,128)(2,1)} %get-tuple-element.56.received_ref, bf16[448,512]{1,0:T(8,128)(2,1)S(1)} %get-tuple-element.57.down_ref, bf16[448,512]{1,0:T(8,128)(2,1)} %get-tuple-element.58.other_ref), custom_call_target="tpu_custom_call" | custom-call | flops 469762048 | bytes 4194304 | tf_op jit(solution)/shard_map/cond/branch_1_fun/pallas_call | solution.py:152
  64.3 6.5 %all-to-all-start.1 = ((bf16[16,32,896]{2,1,0:T(8,128)(2,1)}), bf16[16,32,896]{2,1,0:T(8,128)(2,1)S(1)}, u32[]{:S(2)}, u32[]{:S(2)}) async-start(bf16[16,32,896]{2,1,0:T(8,128)(2,1)} %get-tuple-element.62), calls=%async_computation.1 | async-start | bytes 1835008 | tf_op jit(solution)/shard_map/cond/branch_1_fun/all_to_all | solution.py:383
  70.8 19.0 %conditional.1 = (bf16[4,32,512]{2,1,0:T(8,128)(2,1)S(1)}, bf16[16,128]{1,0:T(8,128)(2,1)S(1)}) conditional(s32[]{:T(128)} %convert_element_type.6, () %tuple.35, (bf16[512,512]{1,0:T(8,128)(2,1)}, bf16[32,512]{1,0:T(8,128)(2,1)S(1)}) %tuple.77), branch_computations={%region_6.6_spmd, %region_7.7_spmd} | conditional | flops 196609 | bytes 737416 | solution.py:360
  70.8 1.3 slice.20.after_ref
  72.1 1.3 branch_1_fun.8
  73.4 4.5 %collective-permute-start.3 = (bf16[1,32,512]{2,1,0:T(8,128)(2,1)}, bf16[1,32,512]{2,1,0:T(8,128)(2,1)S(1)}, u32[]{:S(2)}, u32[]{:S(2)}) collective-permute-start(bf16[1,32,512]{2,1,0:T(8,128)(2,1)} %bitcast.33), channel_id=1, source_target_pairs={{0,12},{2,14},{4,8},{6,10},{8,4},{10,6},{12,0},{14,2},{1,13},{3,15... | collective-permute-start | bytes 98312 | tf_op jit(solution)/shard_map/cond/branch_1_fun/cond/branch_1_fun/ppermute | solution.py:328
  77.9 4.1 %collective-permute-start.2 = (bf16[1,32,512]{2,1,0:T(8,128)(2,1)}, bf16[1,32,512]{2,1,0:T(8,128)(2,1)S(1)}, u32[]{:S(2)}, u32[]{:S(2)}) collective-permute-start(bf16[1,32,512]{2,1,0:T(8,128)(2,1)} %bitcast.34), channel_id=1, source_target_pairs={{0,8},{2,10},{4,12},{6,14},{8,0},{10,2},{12,4},{14,6},{1,9},{3,11}... | collective-permute-start | bytes 98312 | tf_op jit(solution)/shard_map/cond/branch_1_fun/cond/branch_1_fun/ppermute | solution.py:328
  82.1 3.5 %collective-permute-start.1 = (bf16[1,32,512]{2,1,0:T(8,128)(2,1)}, bf16[1,32,512]{2,1,0:T(8,128)(2,1)S(1)}, u32[]{:S(2)}, u32[]{:S(2)}) collective-permute-start(bf16[1,32,512]{2,1,0:T(8,128)(2,1)} %bitcast.35), channel_id=1, source_target_pairs={{0,4},{2,6},{4,0},{6,2},{8,12},{10,14},{12,8},{14,10},{1,5},{3,7},... | collective-permute-start | bytes 98312 | tf_op jit(solution)/shard_map/cond/branch_1_fun/cond/branch_1_fun/ppermute | solution.py:328
  85.6 0.0 collective-permute-done.3
  85.6 2.2 %collective-permute-done.2 = bf16[1,32,512]{2,1,0:T(8,128)(2,1)S(1)} collective-permute-done((bf16[1,32,512]{2,1,0:T(8,128)(2,1)}, bf16[1,32,512]{2,1,0:T(8,128)(2,1)S(1)}, u32[]{:S(2)}, u32[]{:S(2)}) %collective-permute-start.2) | collective-permute-done | bytes 32800 | tf_op jit(solution)/shard_map/cond/branch_1_fun/cond/branch_1_fun/ppermute | solution.py:328
  87.9 1.1 collective-permute-done.1
  89.0 0.8 pad_maximum_fusion.1
  89.8 9.1 %all-to-all-done.1.parts_ref = bf16[16,32,896]{2,1,0:T(8,128)(2,1)S(1)} async-done(((bf16[16,32,896]{2,1,0:T(8,128)(2,1)}), bf16[16,32,896]{2,1,0:T(8,128)(2,1)S(1)}, u32[]{:S(2)}, u32[]{:S(2)}) %all-to-all-start.1) | async-done | bytes 917536 | tf_op jit(solution)/shard_map/cond/branch_1_fun/all_to_all | solution.py:383
  98.9 1.1 branch_1_fun.11
  99.9 7.4 %all-to-all-start.2 = ((bf16[16,32,896]{2,1,0:T(8,128)(2,1)}), bf16[16,32,896]{2,1,0:T(8,128)(2,1)}, u32[]{:S(2)}, u32[]{:S(2)}) async-start(bf16[16,32,896]{2,1,0:T(8,128)(2,1)} %branch_1_fun.11), calls=%async_computation.2 | async-start | bytes 1835008 | tf_op jit(solution)/shard_map/cond/branch_1_fun/all_to_all | solution.py:388
  107.3 0.1 pad_maximum_fusion.2
  107.4 1.9 %collective-permute-start.4 = (bf16[2,448,512]{2,1,0:T(8,128)(2,1)S(1)}, bf16[2,448,512]{2,1,0:T(8,128)(2,1)S(1)}, u32[]{:S(2)}, u32[]{:S(2)}) collective-permute-start(bf16[2,448,512]{2,1,0:T(8,128)(2,1)S(1)} %pad_maximum_fusion.2), channel_id=1, source_target_pairs={{0,1},{1,0},{2,3},{3,2},{4,5},{5,4},{6,7},{7,6},{8,9},{9,8},{10,11... | collective-permute-start | bytes 2752520 | tf_op jit(solution)/shard_map/cond/branch_1_fun/ppermute | solution.py:58
  109.3 2.6 %collective-permute-start.5 = (bf16[4,32,512]{2,1,0:T(8,128)(2,1)S(1)}, bf16[4,32,512]{2,1,0:T(8,128)(2,1)S(1)}, u32[]{:S(2)}, u32[]{:S(2)}) collective-permute-start(bf16[4,32,512]{2,1,0:T(8,128)(2,1)S(1)} %get-tuple-element.65), channel_id=1, source_target_pairs={{0,16},{16,0},{1,17},{17,1},{2,18},{18,2},{3,19},{19,3},{4,20},{20... | collective-permute-start | bytes 393224 | tf_op jit(solution)/shard_map/cond/branch_1_fun/ppermute | solution.py:328
  111.9 7.4 %collective-permute-done.5 = bf16[4,32,512]{2,1,0:T(8,128)(2,1)S(1)} collective-permute-done((bf16[4,32,512]{2,1,0:T(8,128)(2,1)S(1)}, bf16[4,32,512]{2,1,0:T(8,128)(2,1)S(1)}, u32[]{:S(2)}, u32[]{:S(2)}) %collective-permute-start.5) | collective-permute-done | bytes 131104 | tf_op jit(solution)/shard_map/cond/branch_1_fun/ppermute | solution.py:328
  119.3 2.3 %collective-permute-start.6 = (bf16[8,32,512]{2,1,0:T(8,128)(2,1)S(1)}, bf16[8,32,512]{2,1,0:T(8,128)(2,1)S(1)}, u32[]{:S(2)}, u32[]{:S(2)}) collective-permute-start(bf16[8,32,512]{2,1,0:T(8,128)(2,1)S(1)} %pad_maximum_fusion.4), channel_id=1, source_target_pairs={{0,2},{2,0},{4,6},{6,4},{8,10},{10,8},{12,14},{14,12},{1,3},{3,1},... | collective-permute-start | bytes 786440 | tf_op jit(solution)/shard_map/cond/branch_1_fun/ppermute | solution.py:328
  121.6 7.6 %collective-permute-done.6 = bf16[8,32,512]{2,1,0:T(8,128)(2,1)S(1)} collective-permute-done((bf16[8,32,512]{2,1,0:T(8,128)(2,1)S(1)}, bf16[8,32,512]{2,1,0:T(8,128)(2,1)S(1)}, u32[]{:S(2)}, u32[]{:S(2)}) %collective-permute-start.6) | collective-permute-done | bytes 262176 | tf_op jit(solution)/shard_map/cond/branch_1_fun/ppermute | solution.py:328
  129.3 0.1 pad_maximum_fusion.3
  129.3 0.0 collective-permute-done.4.other_ref
  129.3 0.7 branch_1_fun.10
  130.0 0.1 all-to-all-done.2
  130.2 5.2 %shard_map.106 = (bf16[16,32,512]{2,1,0:T(8,128)(2,1)}, bf16[3,512,896]{2,1,0:T(8,128)(2,1)}) custom-call(bf16[16,32,896]{2,1,0:T(8,128)(2,1)} %get-tuple-element.93.hid_ref, bf16[8,2,32,1792]{3,2,1,0:T(8,128)(2,1)} %bitcast.28, bf16[2,896,512]{2,1,0:T(8,128)(2,1)S(1)} %get-tuple-element.95.quant_ref), custom_call_target="tpu_custom_call" | custom-call | flops 939524096 | bytes 8388608 | tf_op jit(solution)/shard_map/pallas_call | solution.py:227
  135.3 8.0 %all-to-all-start.4 = ((bf16[16,32,512]{2,1,0:T(8,128)(2,1)}), bf16[16,32,512]{2,1,0:T(8,128)(2,1)S(1)}, u32[]{:S(2)}, u32[]{:S(2)}) async-start(bf16[16,32,512]{2,1,0:T(8,128)(2,1)} %get-tuple-element.96), calls=%async_computation.4 | async-start | bytes 1048576 | tf_op jit(solution)/shard_map/all_to_all | solution.py:396
  143.3 0.1 pad_add_fusion
  143.4 9.8 %conditional.7 = ((bf16[448,512]{1,0:T(8,128)(2,1)}, bf16[448,512]{1,0:T(8,128)(2,1)}, bf16[448,512]{1,0:T(8,128)(2,1)}, f32[8,128]{1,0:T(8,128)S(1)})) conditional(s32[]{:T(128)} %convert_element_type.11, () %tuple.51, (s32[2]{0:T(128)S(1)}, bf16[3,512,896]{2,1,0:T(8,128)(2,1)}, bf16[512,512]{1,0:T(8,128)(2,1)}, ...), branch_computations={%region_8.9_spmd, %region_9.10_spmd} | conditional | flops 1410334720 | bytes 19136560 | solution.py:360
  143.4 3.5 %branch_1_fun.12 = (f32[3,448,512]{2,1,0:T(8,128)S(1)}, bf16[3,448,512]{2,1,0:T(8,128)(2,1)S(1)}) custom-call(s32[2]{0:T(128)S(1)} %get-tuple-element.66.place_ref, bf16[3,512,896]{2,1,0:T(8,128)(2,1)} %get-tuple-element.67.acts_ref, bf16[512,512]{1,0:T(8,128)(2,1)} %get-tuple-element.68.out_ref, bf16[16,32,512]{2,1,0:T(8,128)(2,1)S(1)} %get-tuple-element.69.tokens_ref), custom_call_target="tpu_custom_call" | custom-call | flops 1409286144 | bytes 8388608 | tf_op jit(solution)/shard_map/cond/branch_1_fun/pallas_call | solution.py:265
  146.9 1.9 %collective-permute-start = (bf16[3,448,512]{2,1,0:T(8,128)(2,1)S(1)}, bf16[3,448,512]{2,1,0:T(8,128)(2,1)S(1)}, u32[]{:S(2)}, u32[]{:S(2)}) collective-permute-start(bf16[3,448,512]{2,1,0:T(8,128)(2,1)S(1)} %get-tuple-element.71), channel_id=1, source_target_pairs={{0,1},{1,0},{2,3},{3,2},{4,5},{5,4},{6,7},{7,6},{8,9},{9,8},{10,11... | collective-permute-start | bytes 4128776 | tf_op jit(solution)/shard_map/cond/branch_1_fun/ppermute | solution.py:58
  148.8 3.1 %collective-permute-done.other_ref = bf16[3,448,512]{2,1,0:T(8,128)(2,1)S(1)} collective-permute-done((bf16[3,448,512]{2,1,0:T(8,128)(2,1)S(1)}, bf16[3,448,512]{2,1,0:T(8,128)(2,1)S(1)}, u32[]{:S(2)}, u32[]{:S(2)}) %collective-permute-start) | collective-permute-done | bytes 1376288 | tf_op jit(solution)/shard_map/cond/branch_1_fun/ppermute | solution.py:58
  151.9 1.2 branch_1_fun.13
  153.1 5.0 %all-to-all-done.4.parts_ref = bf16[16,32,512]{2,1,0:T(8,128)(2,1)S(1)} async-done(((bf16[16,32,512]{2,1,0:T(8,128)(2,1)}), bf16[16,32,512]{2,1,0:T(8,128)(2,1)S(1)}, u32[]{:S(2)}, u32[]{:S(2)}) %all-to-all-start.4) | async-done | bytes 524320 | tf_op jit(solution)/shard_map/all_to_all | solution.py:396
  158.1 0.7 shard_map.107
  (9 shorter events, 0.1 us)
Async XLA Ops:
  7.2 2.7 %copy-start.2 = (bf16[448,512]{1,0:T(8,128)(2,1)S(1)}, bf16[448,512]{1,0:T(8,128)(2,1)}, u32[]{:S(2)}) copy-start(bf16[448,512]{1,0:T(8,128)(2,1)} %down_ref.1) | copy-start | bytes 1376260
  7.2 2.6 %copy-start.3 = (bf16[64,448]{1,0:T(8,128)(2,1)S(1)}, bf16[64,448]{1,0:T(8,128)(2,1)}, u32[]{:S(2)}) copy-start(bf16[64,448]{1,0:T(8,128)(2,1)} %param.19) | copy-start | bytes 172036
  7.2 2.6 %copy-start.4 = (bf16[64,448]{1,0:T(8,128)(2,1)S(1)}, bf16[64,448]{1,0:T(8,128)(2,1)}, u32[]{:S(2)}) copy-start(bf16[64,448]{1,0:T(8,128)(2,1)} %param.20) | copy-start | bytes 172036
  7.2 123.0 %all-gather.2.cloned.1.call-start = ((), (), s32[]{:S(2)}) async-start(), calls=%async_computation.5 | async-start | bytes 2064384 | tf_op jit(solution)/shard_map/all_gather | solution.py:378
  9.8 26.7 %copy-start = (bf16[512,448]{0,1:T(8,128)(2,1)S(1)}, bf16[512,448]{0,1:T(8,128)(2,1)}, u32[]{:S(2)}) copy-start(bf16[512,448]{0,1:T(8,128)(2,1)} %param.21) | copy-start | bytes 1376260
  9.8 26.7 %copy-start.1 = (bf16[512,448]{0,1:T(8,128)(2,1)S(1)}, bf16[512,448]{0,1:T(8,128)(2,1)}, u32[]{:S(2)}) copy-start(bf16[512,448]{0,1:T(8,128)(2,1)} %param.22) | copy-start | bytes 1376260
  9.9 25.8 %all-to-all-start.3 = ((bf16[16,144,128]{2,1,0:T(8,128)(2,1)}), bf16[16,144,128]{2,1,0:T(8,128)(2,1)}, u32[]{:S(2)}, u32[]{:S(2)}) async-start(bf16[16,144,128]{2,1,0:T(8,128)(2,1)} %get-tuple-element.46), calls=%async_computation.3 | async-start | bytes 1179648 | tf_op jit(solution)/shard_map/cond/branch_1_fun/all_to_all | solution.py:370
  18.5 18.1 %collective-permute-start.9 = (bf16[448,512]{1,0:T(8,128)(2,1)S(1)}, bf16[448,512]{1,0:T(8,128)(2,1)}, u32[]{:S(2)}, u32[]{:S(2)}) collective-permute-start(bf16[448,512]{1,0:T(8,128)(2,1)S(1)} %get-tuple-element.47), channel_id=1, source_target_pairs={{0,1},{1,0},{2,3},{3,2},{4,5},{5,4},{6,7},{7,6},{8,9},{9,8},{10,11... | collective-permute-start | bytes 1376264 | tf_op jit(solution)/shard_map/cond/branch_1_fun/ppermute | solution.py:58
  20.5 3.3 %collective-permute-start.7 = (bf16[32,896]{1,0:T(8,128)(2,1)S(1)}, bf16[32,896]{1,0:T(8,128)(2,1)S(1)}, u32[]{:S(2)}, u32[]{:S(2)}) collective-permute-start(bf16[32,896]{1,0:T(8,128)(2,1)S(1)} %get-tuple-element.110), channel_id=1, source_target_pairs={{0,1},{1,0},{2,3},{3,2},{4,5},{5,4},{6,7},{7,6},{8,9},{9,8},{10,11... | collective-permute-start | bytes 172040 | tf_op jit(solution)/shard_map/cond/branch_1_fun/cond/branch_1_fun/ppermute | solution.py:58
  24.0 10.2 %collective-permute-start.8 = (bf16[32,1792]{1,0:T(8,128)(2,1)S(1)}, bf16[32,1792]{1,0:T(8,128)(2,1)S(1)}, u32[]{:S(2)}, u32[]{:S(2)}) collective-permute-start(bf16[32,1792]{1,0:T(8,128)(2,1)S(1)} %concatenate.12), channel_id=1, source_target_pairs={{0,256},{256,0},{1,257},{257,1},{2,258},{258,2},{3,259},{259,3},{4... | collective-permute-start | bytes 344072 | tf_op jit(solution)/shard_map/cond/branch_1_fun/cond/branch_1_fun/ppermute | solution.py:345
  59.6 11.2 %copy-start.5 = (bf16[32,512]{1,0:T(8,128)(2,1)S(1)}, bf16[32,512]{1,0:T(8,128)(2,1)}, u32[]{:S(2)}) copy-start(bf16[32,512]{1,0:T(8,128)(2,1)} %get-tuple-element.109) | copy-start | bytes 98308 | tf_op jit(solution)/shard_map/cond
  64.3 34.6 %all-to-all-start.1 = ((bf16[16,32,896]{2,1,0:T(8,128)(2,1)}), bf16[16,32,896]{2,1,0:T(8,128)(2,1)S(1)}, u32[]{:S(2)}, u32[]{:S(2)}) async-start(bf16[16,32,896]{2,1,0:T(8,128)(2,1)} %get-tuple-element.62), calls=%async_computation.1 | async-start | bytes 1835008 | tf_op jit(solution)/shard_map/cond/branch_1_fun/all_to_all | solution.py:383
  73.4 12.2 %collective-permute-start.3 = (bf16[1,32,512]{2,1,0:T(8,128)(2,1)}, bf16[1,32,512]{2,1,0:T(8,128)(2,1)S(1)}, u32[]{:S(2)}, u32[]{:S(2)}) collective-permute-start(bf16[1,32,512]{2,1,0:T(8,128)(2,1)} %bitcast.33), channel_id=1, source_target_pairs={{0,12},{2,14},{4,8},{6,10},{8,4},{10,6},{12,0},{14,2},{1,13},{3,15... | collective-permute-start | bytes 98312 | tf_op jit(solution)/shard_map/cond/branch_1_fun/cond/branch_1_fun/ppermute | solution.py:328
  77.9 9.9 %collective-permute-start.2 = (bf16[1,32,512]{2,1,0:T(8,128)(2,1)}, bf16[1,32,512]{2,1,0:T(8,128)(2,1)S(1)}, u32[]{:S(2)}, u32[]{:S(2)}) collective-permute-start(bf16[1,32,512]{2,1,0:T(8,128)(2,1)} %bitcast.34), channel_id=1, source_target_pairs={{0,8},{2,10},{4,12},{6,14},{8,0},{10,2},{12,4},{14,6},{1,9},{3,11}... | collective-permute-start | bytes 98312 | tf_op jit(solution)/shard_map/cond/branch_1_fun/cond/branch_1_fun/ppermute | solution.py:328
  82.1 6.9 %collective-permute-start.1 = (bf16[1,32,512]{2,1,0:T(8,128)(2,1)}, bf16[1,32,512]{2,1,0:T(8,128)(2,1)S(1)}, u32[]{:S(2)}, u32[]{:S(2)}) collective-permute-start(bf16[1,32,512]{2,1,0:T(8,128)(2,1)} %bitcast.35), channel_id=1, source_target_pairs={{0,4},{2,6},{4,0},{6,2},{8,12},{10,14},{12,8},{14,10},{1,5},{3,7},... | collective-permute-start | bytes 98312 | tf_op jit(solution)/shard_map/cond/branch_1_fun/cond/branch_1_fun/ppermute | solution.py:328
  99.9 30.2 %all-to-all-start.2 = ((bf16[16,32,896]{2,1,0:T(8,128)(2,1)}), bf16[16,32,896]{2,1,0:T(8,128)(2,1)}, u32[]{:S(2)}, u32[]{:S(2)}) async-start(bf16[16,32,896]{2,1,0:T(8,128)(2,1)} %branch_1_fun.11), calls=%async_computation.2 | async-start | bytes 1835008 | tf_op jit(solution)/shard_map/cond/branch_1_fun/all_to_all | solution.py:388
  107.4 21.9 %collective-permute-start.4 = (bf16[2,448,512]{2,1,0:T(8,128)(2,1)S(1)}, bf16[2,448,512]{2,1,0:T(8,128)(2,1)S(1)}, u32[]{:S(2)}, u32[]{:S(2)}) collective-permute-start(bf16[2,448,512]{2,1,0:T(8,128)(2,1)S(1)} %pad_maximum_fusion.2), channel_id=1, source_target_pairs={{0,1},{1,0},{2,3},{3,2},{4,5},{5,4},{6,7},{7,6},{8,9},{9,8},{10,11... | collective-permute-start | bytes 2752520 | tf_op jit(solution)/shard_map/cond/branch_1_fun/ppermute | solution.py:58
  109.3 10.0 %collective-permute-start.5 = (bf16[4,32,512]{2,1,0:T(8,128)(2,1)S(1)}, bf16[4,32,512]{2,1,0:T(8,128)(2,1)S(1)}, u32[]{:S(2)}, u32[]{:S(2)}) collective-permute-start(bf16[4,32,512]{2,1,0:T(8,128)(2,1)S(1)} %get-tuple-element.65), channel_id=1, source_target_pairs={{0,16},{16,0},{1,17},{17,1},{2,18},{18,2},{3,19},{19,3},{4,20},{20... | collective-permute-start | bytes 393224 | tf_op jit(solution)/shard_map/cond/branch_1_fun/ppermute | solution.py:328
  119.3 10.0 %collective-permute-start.6 = (bf16[8,32,512]{2,1,0:T(8,128)(2,1)S(1)}, bf16[8,32,512]{2,1,0:T(8,128)(2,1)S(1)}, u32[]{:S(2)}, u32[]{:S(2)}) collective-permute-start(bf16[8,32,512]{2,1,0:T(8,128)(2,1)S(1)} %pad_maximum_fusion.4), channel_id=1, source_target_pairs={{0,2},{2,0},{4,6},{6,4},{8,10},{10,8},{12,14},{14,12},{1,3},{3,1},... | collective-permute-start | bytes 786440 | tf_op jit(solution)/shard_map/cond/branch_1_fun/ppermute | solution.py:328
  135.3 22.8 %all-to-all-start.4 = ((bf16[16,32,512]{2,1,0:T(8,128)(2,1)}), bf16[16,32,512]{2,1,0:T(8,128)(2,1)S(1)}, u32[]{:S(2)}, u32[]{:S(2)}) async-start(bf16[16,32,512]{2,1,0:T(8,128)(2,1)} %get-tuple-element.96), calls=%async_computation.4 | async-start | bytes 1048576 | tf_op jit(solution)/shard_map/all_to_all | solution.py:396
  146.9 5.0 %collective-permute-start = (bf16[3,448,512]{2,1,0:T(8,128)(2,1)S(1)}, bf16[3,448,512]{2,1,0:T(8,128)(2,1)S(1)}, u32[]{:S(2)}, u32[]{:S(2)}) collective-permute-start(bf16[3,448,512]{2,1,0:T(8,128)(2,1)S(1)} %get-tuple-element.71), channel_id=1, source_target_pairs={{0,1},{1,0},{2,3},{3,2},{4,5},{5,4},{6,7},{7,6},{8,9},{9,8},{10,11... | collective-permute-start | bytes 4128776 | tf_op jit(solution)/shard_map/cond/branch_1_fun/ppermute | solution.py:58
Sparse Core Ops, SparseCore 0:
  36.7 61.5 all-gather.1

commit v10 on v9

--- a/solution.py
+++ b/solution.py
@@ -16,6 +16,7 @@
 LANES = 128
 VMEM = pl.BlockSpec(memory_space=pltpu.VMEM)
 SMEM = pl.BlockSpec(memory_space=pltpu.SMEM)
+ANY = pl.BlockSpec(memory_space=pl.ANY)
 WIDE = pltpu.CompilerParams(vmem_limit_bytes=58 * 1024 * 1024)
 PARAMS = pltpu.CompilerParams(vmem_limit_bytes=40 * 1024 * 1024)
 
@@ -110,7 +111,7 @@
         out_shape=jax.ShapeDtypeStruct((2 * N_ROW, 8, LANES), jnp.float32),
         in_specs=[
             pl.BlockSpec((N_CHIP, EXTRA, LANES), lambda i: (0, rows // EXTRA, 0)),
-            pl.BlockSpec(after.shape, lambda i: (0, 0)),
+            ANY,
         ],
         out_specs=pl.BlockSpec((2 * N_ROW, 8, LANES), lambda i: (0, 0, 0)),
         compiler_params=PARAMS,
@@ -127,49 +128,53 @@
     return jnp.clip(values.astype(jnp.float32), -scale, scale).astype(jnp.bfloat16)
 
 
-def partial_kernel(tile_ref, received_ref, down_ref, other_ref, partial_ref, out_ref, quant_ref):
-    rows = partial_ref.shape[1]
-    inner, width = down_ref.shape
-
-    @pl.when(pl.program_id(0) == 0)
-    def _():
-        scale = scale_of(tile_ref, 2)
-        quant_ref[0:inner, :] = clipped(down_ref[...], scale)
-        quant_ref[inner:, :] = clipped(other_ref[...], scale)
-
-    blocks = [received_ref[:, j * rows : (j + 1) * rows, :] for j in range(width // LANES)]
-    out_rows = jnp.concatenate([block.reshape((-1, LANES)) for block in blocks], axis=1)
-    out_ref[...] = out_rows
-    partial = contract_last(out_rows, quant_ref[...])
-    partial_ref[...] = partial.astype(jnp.bfloat16).reshape(partial_ref.shape)
-
-
-def hidden_partial(tile, received, down, other):
-    blocks, steps = 4, N_CHIP // 4
+def laid_out_kernel(received_ref, down_ref, other_ref, out_ref, both_ref):
+    width = out_ref.shape[1]
+    rows = (received_ref.shape[1] - EXTRA) * LANES // width
+    for j in range(width // LANES):
+        block = received_ref[:, j * rows : (j + 1) * rows, :].reshape((-1, LANES))
+        out_ref[:, j * LANES : (j + 1) * LANES] = block
+    both_ref[0] = down_ref[...]
+    both_ref[1] = other_ref[...]
+
+
+def laid_out(received, down, other):
     inner, width = down.shape
     rows = (received.shape[1] - EXTRA) * LANES // width
-    whole = pl.BlockSpec((inner, width), lambda i: (0, 0))
+    return pl.pallas_call(
+        laid_out_kernel,
+        out_shape=(
+            jax.ShapeDtypeStruct((N_CHIP * rows, width), jnp.bfloat16),
+            jax.ShapeDtypeStruct((2, inner, width), jnp.bfloat16),
+        ),
+        in_specs=[VMEM] * 3,
+        out_specs=(VMEM, VMEM),
+        compiler_params=PARAMS,
+        cost_estimate=cost(1 << 10, 3 << 20),
+    )(received, down, other)
+
+
+def partial_kernel(tile_ref, out_ref, both_ref, partial_ref):
+    inner, width = both_ref.shape[1:]
+    quant = clipped(both_ref[...].reshape((2 * inner, width)), scale_of(tile_ref, 2))
+    rows = out_ref.shape[0] // 4
+    blocks = partial_ref.shape[0] // 4
+    for n in range(4):
+        partial = contract_last(out_ref[n * rows : (n + 1) * rows, :], quant).astype(jnp.bfloat16)
+        partial_ref[n * blocks : (n + 1) * blocks] = partial.reshape((blocks, -1, 2 * inner))
+
+
+def hidden_partial(tile, out_half, both):
+    inner = both.shape[1]
+    rows = out_half.shape[0] // N_CHIP
     return pl.pallas_call(
         partial_kernel,
-        grid=(steps,),
-        out_shape=(
-            jax.ShapeDtypeStruct((N_ROW, rows, 2 * inner), jnp.bfloat16),
-            jax.ShapeDtypeStruct((N_CHIP * rows, width), jnp.bfloat16),
-        ),
-        in_specs=[
-            pl.BlockSpec(tile.shape, lambda i: (0, 0, 0)),
-            pl.BlockSpec((blocks,) + received.shape[1:], lambda i: (i, 0, 0)),
-            whole,
-            whole,
-        ],
-        out_specs=(
-            pl.BlockSpec((blocks, rows, 2 * inner), lambda i: (i, 0, 0)),
-            pl.BlockSpec((blocks * rows, width), lambda i: (i, 0)),
-        ),
-        scratch_shapes=[pltpu.VMEM((2 * inner, width), jnp.bfloat16)],
+        out_shape=jax.ShapeDtypeStruct((N_ROW, rows, 2 * inner), jnp.bfloat16),
+        in_specs=[VMEM] * 3,
+        out_specs=VMEM,
         compiler_params=PARAMS,
         cost_estimate=cost(2 * 512 * 896 * 512, 4 << 20),
-    )(tile, received, down, other)
+    )(tile, out_half, both)
 
 
 def spread_kernel(parts_ref, after_ref, sent_ref):
@@ -182,7 +187,7 @@
     return pl.pallas_call(
         spread_kernel,
         out_shape=jax.ShapeDtypeStruct(parts.shape, jnp.bfloat16),
-        in_specs=[VMEM] * 2,
+        in_specs=[VMEM, ANY],
         out_specs=VMEM,
         compiler_params=PARAMS,
         cost_estimate=cost(1 << 19, 2 << 20),
@@ -317,21 +322,22 @@
     return pl.pallas_call(
         copy_kernel,
         out_shape=jax.ShapeDtypeStruct(values.shape, values.dtype),
-        in_specs=[VMEM] * 2,
+        in_specs=[VMEM, ANY],
         out_specs=VMEM,
         cost_estimate=cost(1, 1 << 16),
     )(values, after)
 
 
 def exchanged(blocks, axis, *steps):
-    count = 2 if axis == "xl" else N_Y
+    count = N_CHIP if axis == CHIP else N_Y
     others = [lax.ppermute(blocks, axis, [(k, k ^ step) for k in range(count)]) for step in steps]
     return jnp.concatenate([blocks] + others, axis=0)
 
 
-def far_tokens(tokens, done):
+def far_work(tokens, done, tile, gate_t, up_t):
+    other_latents = swapped(jnp.stack([gate_t, up_t]))
     blocks = exchanged(copy_after(tokens, done)[None], "y", 2, 4, 6)
-    return blocks, blocks[-1, :EXTRA, :LANES]
+    return blocks, clipped_latents(tile, gate_t, up_t, other_latents)
 
 
 def own_half(core, gate_pre, up_pre):
@@ -346,7 +352,7 @@
     pair = jnp.where(
         lax.axis_index("xh") == 0, jnp.stack([rows, other]), jnp.stack([other, rows])
     )
-    return pair.reshape((-1, 4 * inner)), pair[0, :EXTRA, :LANES]
+    return (pair.reshape((-1, 4 * inner)),)
 
 
 def in_branch(work, *operands):
@@ -369,8 +375,8 @@
     def gathers(sent, core, gate_pre, up_pre, down):
         received = lax.all_to_all(sent, CHIP, 0, 0)
         down_other = swapped(down)
-        pre_rows, after = in_branch(own_half, core, gate_pre, up_pre)
-        return (received, down_other, pre_rows, sums_tile(received, after))
+        (pre_rows,) = in_branch(own_half, core, gate_pre, up_pre)
+        return (received, down_other, pre_rows, sums_tile(received, pre_rows))
 
     received, down_other, pre_rows, tile = in_branch(
         gathers, sent, core, gate_pre, up_pre, down_latent
@@ -379,13 +385,12 @@
 
     def exchanges(received, tile, tokens, gate_t, up_t, down, down_other):
         tile = lax.all_to_all(tile, ROW + ("core",), 0, 0)
-        partial, out_half = hidden_partial(tile, received, down, down_other)
+        out_half, both = laid_out(received, down, down_other)
+        partial = hidden_partial(tile, out_half, both)
         parts = lax.all_to_all(partial, ROW, 0, 0)
-        far, after = in_branch(far_tokens, tokens, out_half[:EXTRA, :LANES])
-        other_latents = swapped(jnp.stack([gate_t, up_t]))
-        quant = clipped_latents(tile, gate_t, up_t, other_latents)
-        token_blocks = exchanged(exchanged(far, "xl", 1), "y", 1)
-        grad_hidden = lax.all_to_all(spread(parts, after), ROW, 0, 0)
+        far, quant = in_branch(far_work, tokens, partial, tile, gate_t, up_t)
+        token_blocks = exchanged(far, CHIP, N_Y, 1, N_Y + 1)
+        grad_hidden = lax.all_to_all(spread(parts, far), ROW, 0, 0)
         return (out_half, quant, grad_hidden, token_blocks)
 
     out_half, quant, grad_hidden, token_blocks = in_branch(

time: 167 us -> 166 us (level)
  the two profiles are of different devices: /device:TPU:14 before, /device:TPU:10 now
where the time goes in v10:
time: 166 us; the launch traced here: 165 us
  starting transfers between devices  70.7 us (43%)
  waiting for transfers between devices  53.6 us (32%)
  Pallas kernels  22.7 us (14%)
  between operations  14.1 us (8%)
  other arithmetic  3.56 us (2%)
    ppermute x6, starting transfers between devices, exchanged(): lax.ppermute(blocks, axis, [(k, k ^ step) for k in range(count)])  21.4 us
    all_to_all x1, starting transfers between devices, exchanges(): tile = lax.all_to_all(tile, ROW + ('core',), 0, 0)  11.3 us
    all_to_all x1, waiting for transfers between devices, exchanges(): tile = lax.all_to_all(tile, ROW + ('core',), 0, 0)  10.6 us
    all_to_all x1, waiting for transfers between devices, exchanges(): parts = lax.all_to_all(partial, ROW, 0, 0)  10.3 us
    all_to_all x1, starting transfers between devices, gathers(): received = lax.all_to_all(sent, CHIP, 0, 0)  9.97 us
    ppermute x6, waiting for transfers between devices, exchanged(): lax.ppermute(blocks, axis, [(k, k ^ step) for k in range(count)])  8.97 us
    all_to_all x1, waiting for transfers between devices, exchanges(): grad_hidden = lax.all_to_all(spread(parts, far), ROW, 0, 0)  8.66 us
    all_to_all x1, starting transfers between devices, shards(): parts = lax.all_to_all(partial, CHIP, 0, 0)  8.65 us
  transfers between devices with their start and end apart: 17, of which 12 were waited for; matrix products, arithmetic and copies ran while one was open for 2% of the time, Pallas kernels for 8%

profile of v10, /device:TPU:10, one launch (start us, length us, event | category | flops | bytes accessed | tf_op | source)
XLA Modules:
  0.0 165.1 jit_solution(9762742690121848657)
XLA Ops:
  7.2 0.0 copy-start.4
  7.2 0.0 copy-start.5
  7.2 0.0 all-gather.2.cloned.1.call-start
  7.2 2.6 %shard_map.105 = bf16[16,144,128]{2,1,0:T(8,128)(2,1)} custom-call(bf16[32,512]{1,0:T(8,128)(2,1)} %out_ref.1, bf16[448,512]{1,0:T(8,128)(2,1)} %bitcast.18, bf16[448,512]{1,0:T(8,128)(2,1)} %bitcast.21, bf16[448,512]{1,0:T(8,128)(2,1)} %down_ref.1), custom_call_target="tpu_custom_call" | custom-call | flops 1048576 | bytes 2621440 | tf_op jit(solution)/shard_map/pallas_call | solution.py:90
  9.8 0.0 copy-start
  9.8 0.0 copy-start.1
  9.8 0.0 copy-start.7
  9.9 28.2 %conditional.5 = (bf16[16,144,128]{2,1,0:T(8,128)(2,1)}, bf16[448,512]{1,0:T(8,128)(2,1)}, bf16[64,1792]{1,0:T(8,128)(2,1)}, f32[32,8,128]{2,1,0:T(8,128)}) conditional(s32[]{:T(128)} %convert_element_type.11, () %tuple.46, (bf16[16,144,128]{2,1,0:T(8,128)(2,1)}, bf16[448,512]{1,0:T(8,128)(2,1)S(1)}, bf16[64,448]{1,0:T(8,128)(2,1)S(1)}, ...), branch_computations={%region_0.0_spmd, %region_1.4_spmd} | conditional | flops 638992 | bytes 5931400 | solution.py:366
  9.9 10.0 %all-to-all-start.3 = ((bf16[16,144,128]{2,1,0:T(8,128)(2,1)}), bf16[16,144,128]{2,1,0:T(8,128)(2,1)}, u32[]{:S(2)}, u32[]{:S(2)}) async-start(bf16[16,144,128]{2,1,0:T(8,128)(2,1)} %get-tuple-element.54), calls=%async_computation.3 | async-start | bytes 1179648 | tf_op jit(solution)/shard_map/cond/branch_1_fun/all_to_all | solution.py:376
  19.8 1.9 %collective-permute-start.10 = (bf16[448,512]{1,0:T(8,128)(2,1)S(1)}, bf16[448,512]{1,0:T(8,128)(2,1)}, u32[]{:S(2)}, u32[]{:S(2)}) collective-permute-start(bf16[448,512]{1,0:T(8,128)(2,1)S(1)} %get-tuple-element.55), channel_id=1, source_target_pairs={{0,1},{1,0},{2,3},{3,2},{4,5},{5,4},{6,7},{7,6},{8,9},{9,8},{10,11... | collective-permute-start | bytes 1376264 | tf_op jit(solution)/shard_map/cond/branch_1_fun/ppermute | solution.py:59
  21.8 14.8 %conditional = (bf16[64,1792]{1,0:T(8,128)(2,1)}) conditional(s32[]{:T(128)} %convert_element_type.3, () %tuple.27, (bf16[64,448]{1,0:T(8,128)(2,1)S(1)}, bf16[64,448]{1,0:T(8,128)(2,1)S(1)}, s32[]{:T(128)}) %tuple.28), branch_computations={%region_2.0_spmd, %region_3.3_spmd} | conditional | flops 573451 | bytes 2064602 | solution.py:366
  21.8 0.1 pad_maximum_fusion
  21.9 2.4 %collective-permute-start.8 = (bf16[32,896]{1,0:T(8,128)(2,1)S(1)}, bf16[32,896]{1,0:T(8,128)(2,1)S(1)}, u32[]{:S(2)}, u32[]{:S(2)}) collective-permute-start(bf16[32,896]{1,0:T(8,128)(2,1)S(1)} %get-tuple-element.119), channel_id=1, source_target_pairs={{0,1},{1,0},{2,3},{3,2},{4,5},{5,4},{6,7},{7,6},{8,9},{9,8},{10,11... | collective-permute-start | bytes 172040 | tf_op jit(solution)/shard_map/cond/branch_1_fun/cond/branch_1_fun/ppermute | solution.py:59
  24.3 0.1 fusion.1
  24.4 0.8 collective-permute-done.8
  25.2 0.1 fusion
  25.3 0.1 concatenate.9
  25.4 2.7 %collective-permute-start.9 = (bf16[32,1792]{1,0:T(8,128)(2,1)S(1)}, bf16[32,1792]{1,0:T(8,128)(2,1)S(1)}, u32[]{:S(2)}, u32[]{:S(2)}) collective-permute-start(bf16[32,1792]{1,0:T(8,128)(2,1)S(1)} %concatenate.9), channel_id=1, source_target_pairs={{0,256},{256,0},{1,257},{257,1},{2,258},{258,2},{3,259},{259,3},{4... | collective-permute-start | bytes 344072 | tf_op jit(solution)/shard_map/cond/branch_1_fun/cond/branch_1_fun/ppermute | solution.py:351
  28.1 7.8 %collective-permute-done.9 = bf16[32,1792]{1,0:T(8,128)(2,1)S(1)} collective-permute-done((bf16[32,1792]{1,0:T(8,128)(2,1)S(1)}, bf16[32,1792]{1,0:T(8,128)(2,1)S(1)}, u32[]{:S(2)}, u32[]{:S(2)}) %collective-permute-start.9) | collective-permute-done | bytes 114720 | tf_op jit(solution)/shard_map/cond/branch_1_fun/cond/branch_1_fun/ppermute | solution.py:351
  35.8 0.7 maximum_select_fusion
  36.5 0.0 all-to-all-done.3.extra_ref
  36.5 1.5 branch_1_fun.8
  38.1 0.0 collective-permute-done.10
  38.1 0.0 all-gather.2.cloned.1.call-update
  38.1 91.7 %conditional.6 = (bf16[512,512]{1,0:T(8,128)(2,1)S(1)}, bf16[2,896,512]{2,1,0:T(8,128)(2,1)}, bf16[16,32,896]{2,1,0:T(8,128)(2,1)}, bf16[16,32,512]{2,1,0:T(8,128)(2,1)}) conditional(s32[]{:T(128)} %convert_element_type.11, () %tuple.45, (bf16[16,144,128]{2,1,0:T(8,128)(2,1)}, bf16[448,512]{1,0:T(8,128)(2,1)S(1)}, bf16[448,512]{1,0:T(8,128)(2,1)}, ...), branch_computations={%region_4.5_spmd, %region_5.8_spmd} | conditional | flops 472777728 | bytes 32571958 | solution.py:366
  38.1 11.3 %all-to-all-start = ((f32[32,8,128]{2,1,0:T(8,128)}), f32[32,8,128]{2,1,0:T(8,128)S(1)}, u32[]{:S(2)}, u32[]{:S(2)}) async-start(f32[32,8,128]{2,1,0:T(8,128)} %get-tuple-element.69), calls=%async_computation | async-start | bytes 262144 | tf_op jit(solution)/shard_map/cond/branch_1_fun/all_to_all | solution.py:387
  49.5 1.3 branch_1_fun.11
  50.8 10.6 %all-to-all-done.tile_ref = f32[32,8,128]{2,1,0:T(8,128)S(1)} async-done(((f32[32,8,128]{2,1,0:T(8,128)}), f32[32,8,128]{2,1,0:T(8,128)S(1)}, u32[]{:S(2)}, u32[]{:S(2)}) %all-to-all-start) | async-done | bytes 131104 | tf_op jit(solution)/shard_map/cond/branch_1_fun/all_to_all | solution.py:387
  61.4 2.3 %branch_1_fun.12 = bf16[16,32,896]{2,1,0:T(8,128)(2,1)} custom-call(f32[32,8,128]{2,1,0:T(8,128)S(1)} %all-to-all-done.tile_ref, bf16[512,512]{1,0:T(8,128)(2,1)S(1)} %get-tuple-element.141.out_ref, bf16[2,448,512]{2,1,0:T(8,128)(2,1)S(1)} %get-tuple-element.70.both_ref), custom_call_target="tpu_custom_call" | custom-call | flops 469762048 | bytes 4194304 | tf_op jit(solution)/shard_map/cond/branch_1_fun/pallas_call | solution.py:170
  63.7 3.6 %all-to-all-start.1 = ((bf16[16,32,896]{2,1,0:T(8,128)(2,1)}), bf16[16,32,896]{2,1,0:T(8,128)(2,1)S(1)}, u32[]{:S(2)}, u32[]{:S(2)}) async-start(bf16[16,32,896]{2,1,0:T(8,128)(2,1)} %branch_1_fun.12), calls=%async_computation.1 | async-start | bytes 1835008 | tf_op jit(solution)/shard_map/cond/branch_1_fun/all_to_all | solution.py:390
  67.3 21.9 %conditional.1 = (bf16[4,32,512]{2,1,0:T(8,128)(2,1)S(1)}, bf16[2,896,512]{2,1,0:T(8,128)(2,1)}) conditional(s32[]{:T(128)} %convert_element_type.6, () %tuple.33, (bf16[32,512]{1,0:T(8,128)(2,1)S(1)}, bf16[16,32,896]{2,1,0:T(8,128)(2,1)}, bf16[448,512]{1,0:T(8,128)(2,1)S(1)}, bf16[448,512]{1,0:T(8,128)(2,1)S(1)}, f32[32,8,128]{2,1,0:T(8,128)S(1)}) %tuple.34), branch_computations={%region_6.6_spmd, %region_7.7_spmd} | conditional | flops 1703937 | bytes 10420400 | solution.py:366
  67.4 1.0 pad_maximum_fusion.1
  68.4 1.9 %collective-permute-start.4 = (bf16[2,448,512]{2,1,0:T(8,128)(2,1)}, bf16[2,448,512]{2,1,0:T(8,128)(2,1)S(1)}, u32[]{:S(2)}, u32[]{:S(2)}) collective-permute-start(bf16[2,448,512]{2,1,0:T(8,128)(2,1)} %pad_maximum_fusion.1), channel_id=1, source_target_pairs={{0,1},{1,0},{2,3},{3,2},{4,5},{5,4},{6,7},{7,6},{8,9},{9,8},{10,11... | collective-permute-start | bytes 2752520 | tf_op jit(solution)/shard_map/cond/branch_1_fun/cond/branch_1_fun/ppermute | solution.py:59
  70.3 0.6 branch_1_fun.9
  70.9 4.5 %collective-permute-start.3 = (bf16[1,32,512]{2,1,0:T(8,128)(2,1)}, bf16[1,32,512]{2,1,0:T(8,128)(2,1)S(1)}, u32[]{:S(2)}, u32[]{:S(2)}) collective-permute-start(bf16[1,32,512]{2,1,0:T(8,128)(2,1)} %bitcast.29), channel_id=1, source_target_pairs={{0,12},{2,14},{4,8},{6,10},{8,4},{10,6},{12,0},{14,2},{1,13},{3,15... | collective-permute-start | bytes 98312 | tf_op jit(solution)/shard_map/cond/branch_1_fun/cond/branch_1_fun/ppermute | solution.py:333
  75.5 4.1 %collective-permute-start.2 = (bf16[1,32,512]{2,1,0:T(8,128)(2,1)}, bf16[1,32,512]{2,1,0:T(8,128)(2,1)S(1)}, u32[]{:S(2)}, u32[]{:S(2)}) collective-permute-start(bf16[1,32,512]{2,1,0:T(8,128)(2,1)} %bitcast.30), channel_id=1, source_target_pairs={{0,8},{2,10},{4,12},{6,14},{8,0},{10,2},{12,4},{14,6},{1,9},{3,11}... | collective-permute-start | bytes 98312 | tf_op jit(solution)/shard_map/cond/branch_1_fun/cond/branch_1_fun/ppermute | solution.py:333
  79.6 3.5 %collective-permute-start.1 = (bf16[1,32,512]{2,1,0:T(8,128)(2,1)}, bf16[1,32,512]{2,1,0:T(8,128)(2,1)S(1)}, u32[]{:S(2)}, u32[]{:S(2)}) collective-permute-start(bf16[1,32,512]{2,1,0:T(8,128)(2,1)} %bitcast.31), channel_id=1, source_target_pairs={{0,4},{2,6},{4,0},{6,2},{8,12},{10,14},{12,8},{14,10},{1,5},{3,7},... | collective-permute-start | bytes 98312 | tf_op jit(solution)/shard_map/cond/branch_1_fun/cond/branch_1_fun/ppermute | solution.py:333
  83.1 0.0 collective-permute-done.3
  83.1 2.3 %collective-permute-done.2 = bf16[1,32,512]{2,1,0:T(8,128)(2,1)S(1)} collective-permute-done((bf16[1,32,512]{2,1,0:T(8,128)(2,1)}, bf16[1,32,512]{2,1,0:T(8,128)(2,1)S(1)}, u32[]{:S(2)}, u32[]{:S(2)}) %collective-permute-start.2) | collective-permute-done | bytes 32800 | tf_op jit(solution)/shard_map/cond/branch_1_fun/cond/branch_1_fun/ppermute | solution.py:333
  85.4 1.1 collective-permute-done.1
  86.5 0.8 pad_maximum_fusion.2
  87.3 0.0 collective-permute-done.4.other_ref
  87.3 1.9 %branch_1_fun.10 = bf16[2,896,512]{2,1,0:T(8,128)(2,1)} custom-call(f32[32,8,128]{2,1,0:T(8,128)S(1)} %get-tuple-element.61.tile_ref, bf16[448,512]{1,0:T(8,128)(2,1)S(1)} %get-tuple-element.62.gate_ref, bf16[448,512]{1,0:T(8,128)(2,1)S(1)} %get-tuple-element.63.up_ref, bf16[2,448,512]{2,1,0:T(8,128)(2,1)S(1)} %collective-permute-done.4.other_ref), custom_call_target="tpu_custom_call" | custom-call | flops 1048576 | bytes 4194304 | tf_op jit(solution)/shard_map/cond/branch_1_fun/cond/branch_1_fun/pallas_call | solution.py:207
  89.2 10.3 %all-to-all-done.1.parts_ref = bf16[16,32,896]{2,1,0:T(8,128)(2,1)S(1)} async-done(((bf16[16,32,896]{2,1,0:T(8,128)(2,1)}), bf16[16,32,896]{2,1,0:T(8,128)(2,1)S(1)}, u32[]{:S(2)}, u32[]{:S(2)}) %all-to-all-start.1) | async-done | bytes 917536 | tf_op jit(solution)/shard_map/cond/branch_1_fun/all_to_all | solution.py:390
  99.5 1.1 branch_1_fun.13
  100.6 4.8 %all-to-all-start.2 = ((bf16[16,32,896]{2,1,0:T(8,128)(2,1)}), bf16[16,32,896]{2,1,0:T(8,128)(2,1)}, u32[]{:S(2)}, u32[]{:S(2)}) async-start(bf16[16,32,896]{2,1,0:T(8,128)(2,1)} %branch_1_fun.13), calls=%async_computation.2 | async-start | bytes 1835008 | tf_op jit(solution)/shard_map/cond/branch_1_fun/all_to_all | solution.py:393
  105.4 3.0 %collective-permute-start.7 = (bf16[4,32,512]{2,1,0:T(8,128)(2,1)S(1)}, bf16[4,32,512]{2,1,0:T(8,128)(2,1)S(1)}, u32[]{:S(2)}, u32[]{:S(2)}) collective-permute-start(bf16[4,32,512]{2,1,0:T(8,128)(2,1)S(1)} %get-tuple-element.74.after_ref), channel_id=1, source_target_pairs={{0,18},{2,16},{4,22},{6,20},{8,26},{10,24},{12,30},{14,28},{16,2},... | collective-permute-start | bytes 393224 | tf_op jit(solution)/shard_map/cond/branch_1_fun/ppermute | solution.py:333
  108.4 3.3 %collective-permute-start.6 = (bf16[4,32,512]{2,1,0:T(8,128)(2,1)S(1)}, bf16[4,32,512]{2,1,0:T(8,128)(2,1)S(1)}, u32[]{:S(2)}, u32[]{:S(2)}) collective-permute-start(bf16[4,32,512]{2,1,0:T(8,128)(2,1)S(1)} %get-tuple-element.74.after_ref), channel_id=1, source_target_pairs={{0,2},{2,0},{4,6},{6,4},{8,10},{10,8},{12,14},{14,12},{16,18},{18,... | collective-permute-start | bytes 393224 | tf_op jit(solution)/shard_map/cond/branch_1_fun/ppermute | solution.py:333
  111.7 2.9 %collective-permute-start.5 = (bf16[4,32,512]{2,1,0:T(8,128)(2,1)S(1)}, bf16[4,32,512]{2,1,0:T(8,128)(2,1)S(1)}, u32[]{:S(2)}, u32[]{:S(2)}) collective-permute-start(bf16[4,32,512]{2,1,0:T(8,128)(2,1)S(1)} %get-tuple-element.74.after_ref), channel_id=1, source_target_pairs={{0,16},{2,18},{4,20},{6,22},{8,24},{10,26},{12,28},{14,30},{16,0},... | collective-permute-start | bytes 393224 | tf_op jit(solution)/shard_map/cond/branch_1_fun/ppermute | solution.py:333
  114.6 0.1 collective-permute-done.7
  114.7 0.9 collective-permute-done.6
  115.6 4.7 %collective-permute-done.5 = bf16[4,32,512]{2,1,0:T(8,128)(2,1)S(1)} collective-permute-done((bf16[4,32,512]{2,1,0:T(8,128)(2,1)S(1)}, bf16[4,32,512]{2,1,0:T(8,128)(2,1)S(1)}, u32[]{:S(2)}, u32[]{:S(2)}) %collective-permute-start.5) | collective-permute-done | bytes 131104 | tf_op jit(solution)/shard_map/cond/branch_1_fun/ppermute | solution.py:333
  120.3 0.9 pad_maximum_fusion.3
  121.2 8.7 %all-to-all-done.2 = bf16[16,32,896]{2,1,0:T(8,128)(2,1)} async-done(((bf16[16,32,896]{2,1,0:T(8,128)(2,1)}), bf16[16,32,896]{2,1,0:T(8,128)(2,1)}, u32[]{:S(2)}, u32[]{:S(2)}) %all-to-all-start.2) | async-done | bytes 917536 | tf_op jit(solution)/shard_map/cond/branch_1_fun/all_to_all | solution.py:393
  129.8 5.8 %shard_map.106 = (bf16[16,32,512]{2,1,0:T(8,128)(2,1)}, bf16[3,512,896]{2,1,0:T(8,128)(2,1)}) custom-call(bf16[16,32,896]{2,1,0:T(8,128)(2,1)} %get-tuple-element.102.hid_ref, bf16[8,2,32,1792]{3,2,1,0:T(8,128)(2,1)} %bitcast.24, bf16[2,896,512]{2,1,0:T(8,128)(2,1)} %get-tuple-element.104.quant_ref), custom_call_target="tpu_custom_call" | custom-call | flops 939524096 | bytes 8388608 | tf_op jit(solution)/shard_map/pallas_call | solution.py:232
  135.7 8.6 %all-to-all-start.4 = ((bf16[16,32,512]{2,1,0:T(8,128)(2,1)}), bf16[16,32,512]{2,1,0:T(8,128)(2,1)S(1)}, u32[]{:S(2)}, u32[]{:S(2)}) async-start(bf16[16,32,512]{2,1,0:T(8,128)(2,1)} %get-tuple-element.105), calls=%async_computation.4 | async-start | bytes 1048576 | tf_op jit(solution)/shard_map/all_to_all | solution.py:401
  144.3 0.1 pad_add_fusion
  144.4 9.8 %conditional.7 = ((bf16[448,512]{1,0:T(8,128)(2,1)}, bf16[448,512]{1,0:T(8,128)(2,1)}, bf16[448,512]{1,0:T(8,128)(2,1)}, f32[8,128]{1,0:T(8,128)S(1)})) conditional(s32[]{:T(128)} %convert_element_type.11, () %tuple.49, (s32[2]{0:T(128)S(1)}, bf16[3,512,896]{2,1,0:T(8,128)(2,1)}, bf16[512,512]{1,0:T(8,128)(2,1)S(1)}, ...), branch_computations={%region_8.9_spmd, %region_9.10_spmd} | conditional | flops 1410334720 | bytes 19136560 | solution.py:366
  144.4 3.5 %branch_1_fun.14 = (f32[3,448,512]{2,1,0:T(8,128)S(1)}, bf16[3,448,512]{2,1,0:T(8,128)(2,1)S(1)}) custom-call(s32[2]{0:T(128)S(1)} %get-tuple-element.75.place_ref, bf16[3,512,896]{2,1,0:T(8,128)(2,1)} %get-tuple-element.76.acts_ref, bf16[512,512]{1,0:T(8,128)(2,1)S(1)} %get-tuple-element.77.out_ref, bf16[16,32,512]{2,1,0:T(8,128)(2,1)} %get-tuple-element.78.tokens_ref), custom_call_target="tpu_custom_call" | custom-call | flops 1409286144 | bytes 8388608 | tf_op jit(solution)/shard_map/cond/branch_1_fun/pallas_call | solution.py:270
  147.9 1.9 %collective-permute-start = (bf16[3,448,512]{2,1,0:T(8,128)(2,1)S(1)}, bf16[3,448,512]{2,1,0:T(8,128)(2,1)S(1)}, u32[]{:S(2)}, u32[]{:S(2)}) collective-permute-start(bf16[3,448,512]{2,1,0:T(8,128)(2,1)S(1)} %get-tuple-element.80), channel_id=1, source_target_pairs={{0,1},{1,0},{2,3},{3,2},{4,5},{5,4},{6,7},{7,6},{8,9},{9,8},{10,11... | collective-permute-start | bytes 4128776 | tf_op jit(solution)/shard_map/cond/branch_1_fun/ppermute | solution.py:59
  149.8 3.1 %collective-permute-done.other_ref = bf16[3,448,512]{2,1,0:T(8,128)(2,1)S(1)} collective-permute-done((bf16[3,448,512]{2,1,0:T(8,128)(2,1)S(1)}, bf16[3,448,512]{2,1,0:T(8,128)(2,1)S(1)}, u32[]{:S(2)}, u32[]{:S(2)}) %collective-permute-start) | collective-permute-done | bytes 1376288 | tf_op jit(solution)/shard_map/cond/branch_1_fun/ppermute | solution.py:59
  152.9 1.2 branch_1_fun.15
  154.2 3.4 %all-to-all-done.4.parts_ref = bf16[16,32,512]{2,1,0:T(8,128)(2,1)S(1)} async-done(((bf16[16,32,512]{2,1,0:T(8,128)(2,1)}), bf16[16,32,512]{2,1,0:T(8,128)(2,1)S(1)}, u32[]{:S(2)}, u32[]{:S(2)}) %all-to-all-start.4) | async-done | bytes 524320 | tf_op jit(solution)/shard_map/all_to_all | solution.py:401
  157.6 0.7 shard_map.107
  (13 shorter events, 0.0 us)
Async XLA Ops:
  7.2 2.6 %copy-start.4 = (bf16[448,512]{1,0:T(8,128)(2,1)S(1)}, bf16[448,512]{1,0:T(8,128)(2,1)}, u32[]{:S(2)}) copy-start(bf16[448,512]{1,0:T(8,128)(2,1)} %down_ref.1) | copy-start | bytes 1376260
  7.2 2.6 %copy-start.5 = (bf16[64,448]{1,0:T(8,128)(2,1)S(1)}, bf16[64,448]{1,0:T(8,128)(2,1)}, u32[]{:S(2)}) copy-start(bf16[64,448]{1,0:T(8,128)(2,1)} %param.19) | copy-start | bytes 172036
  7.2 2.6 %copy-start.6 = (bf16[64,448]{1,0:T(8,128)(2,1)S(1)}, bf16[64,448]{1,0:T(8,128)(2,1)}, u32[]{:S(2)}) copy-start(bf16[64,448]{1,0:T(8,128)(2,1)} %param.20) | copy-start | bytes 172036
  7.2 122.6 %all-gather.2.cloned.1.call-start = ((), (), s32[]{:S(2)}) async-start(), calls=%async_computation.5 | async-start | bytes 2064384 | tf_op jit(solution)/shard_map/all_gather | solution.py:384
  9.8 28.3 %copy-start = (bf16[512,448]{0,1:T(8,128)(2,1)S(1)}, bf16[512,448]{0,1:T(8,128)(2,1)}, u32[]{:S(2)}) copy-start(bf16[512,448]{0,1:T(8,128)(2,1)} %param.21) | copy-start | bytes 1376260
  9.8 28.3 %copy-start.1 = (bf16[512,448]{0,1:T(8,128)(2,1)S(1)}, bf16[512,448]{0,1:T(8,128)(2,1)}, u32[]{:S(2)}) copy-start(bf16[512,448]{0,1:T(8,128)(2,1)} %param.22) | copy-start | bytes 1376260
  9.8 28.3 %copy-start.7 = (bf16[32,512]{1,0:T(8,128)(2,1)S(1)}, bf16[32,512]{1,0:T(8,128)(2,1)}, u32[]{:S(2)}) copy-start(bf16[32,512]{1,0:T(8,128)(2,1)} %param.17) | copy-start | bytes 98308
  9.9 26.7 %all-to-all-start.3 = ((bf16[16,144,128]{2,1,0:T(8,128)(2,1)}), bf16[16,144,128]{2,1,0:T(8,128)(2,1)}, u32[]{:S(2)}, u32[]{:S(2)}) async-start(bf16[16,144,128]{2,1,0:T(8,128)(2,1)} %get-tuple-element.54), calls=%async_computation.3 | async-start | bytes 1179648 | tf_op jit(solution)/shard_map/cond/branch_1_fun/all_to_all | solution.py:376
  19.8 18.2 %collective-permute-start.10 = (bf16[448,512]{1,0:T(8,128)(2,1)S(1)}, bf16[448,512]{1,0:T(8,128)(2,1)}, u32[]{:S(2)}, u32[]{:S(2)}) collective-permute-start(bf16[448,512]{1,0:T(8,128)(2,1)S(1)} %get-tuple-element.55), channel_id=1, source_target_pairs={{0,1},{1,0},{2,3},{3,2},{4,5},{5,4},{6,7},{7,6},{8,9},{9,8},{10,11... | collective-permute-start | bytes 1376264 | tf_op jit(solution)/shard_map/cond/branch_1_fun/ppermute | solution.py:59
  21.9 3.3 %collective-permute-start.8 = (bf16[32,896]{1,0:T(8,128)(2,1)S(1)}, bf16[32,896]{1,0:T(8,128)(2,1)S(1)}, u32[]{:S(2)}, u32[]{:S(2)}) collective-permute-start(bf16[32,896]{1,0:T(8,128)(2,1)S(1)} %get-tuple-element.119), channel_id=1, source_target_pairs={{0,1},{1,0},{2,3},{3,2},{4,5},{5,4},{6,7},{7,6},{8,9},{9,8},{10,11... | collective-permute-start | bytes 172040 | tf_op jit(solution)/shard_map/cond/branch_1_fun/cond/branch_1_fun/ppermute | solution.py:59
  25.4 10.4 %collective-permute-start.9 = (bf16[32,1792]{1,0:T(8,128)(2,1)S(1)}, bf16[32,1792]{1,0:T(8,128)(2,1)S(1)}, u32[]{:S(2)}, u32[]{:S(2)}) collective-permute-start(bf16[32,1792]{1,0:T(8,128)(2,1)S(1)} %concatenate.9), channel_id=1, source_target_pairs={{0,256},{256,0},{1,257},{257,1},{2,258},{258,2},{3,259},{259,3},{4... | collective-permute-start | bytes 344072 | tf_op jit(solution)/shard_map/cond/branch_1_fun/cond/branch_1_fun/ppermute | solution.py:351
  38.1 23.3 %all-to-all-start = ((f32[32,8,128]{2,1,0:T(8,128)}), f32[32,8,128]{2,1,0:T(8,128)S(1)}, u32[]{:S(2)}, u32[]{:S(2)}) async-start(f32[32,8,128]{2,1,0:T(8,128)} %get-tuple-element.69), calls=%async_computation | async-start | bytes 262144 | tf_op jit(solution)/shard_map/cond/branch_1_fun/all_to_all | solution.py:387
  50.8 12.9 %copy-start.2 = (bf16[512,512]{1,0:T(8,128)(2,1)}, bf16[512,512]{1,0:T(8,128)(2,1)S(1)}, u32[]{:S(2)}) copy-start(bf16[512,512]{1,0:T(8,128)(2,1)S(1)} %get-tuple-element.141.out_ref) | copy-start | bytes 1572868 | tf_op jit(solution)/shard_map/cond
  63.7 35.8 %all-to-all-start.1 = ((bf16[16,32,896]{2,1,0:T(8,128)(2,1)}), bf16[16,32,896]{2,1,0:T(8,128)(2,1)S(1)}, u32[]{:S(2)}, u32[]{:S(2)}) async-start(bf16[16,32,896]{2,1,0:T(8,128)(2,1)} %branch_1_fun.12), calls=%async_computation.1 | async-start | bytes 1835008 | tf_op jit(solution)/shard_map/cond/branch_1_fun/all_to_all | solution.py:390
  68.4 18.9 %collective-permute-start.4 = (bf16[2,448,512]{2,1,0:T(8,128)(2,1)}, bf16[2,448,512]{2,1,0:T(8,128)(2,1)S(1)}, u32[]{:S(2)}, u32[]{:S(2)}) collective-permute-start(bf16[2,448,512]{2,1,0:T(8,128)(2,1)} %pad_maximum_fusion.1), channel_id=1, source_target_pairs={{0,1},{1,0},{2,3},{3,2},{4,5},{5,4},{6,7},{7,6},{8,9},{9,8},{10,11... | collective-permute-start | bytes 2752520 | tf_op jit(solution)/shard_map/cond/branch_1_fun/cond/branch_1_fun/ppermute | solution.py:59
  70.9 12.2 %collective-permute-start.3 = (bf16[1,32,512]{2,1,0:T(8,128)(2,1)}, bf16[1,32,512]{2,1,0:T(8,128)(2,1)S(1)}, u32[]{:S(2)}, u32[]{:S(2)}) collective-permute-start(bf16[1,32,512]{2,1,0:T(8,128)(2,1)} %bitcast.29), channel_id=1, source_target_pairs={{0,12},{2,14},{4,8},{6,10},{8,4},{10,6},{12,0},{14,2},{1,13},{3,15... | collective-permute-start | bytes 98312 | tf_op jit(solution)/shard_map/cond/branch_1_fun/cond/branch_1_fun/ppermute | solution.py:333
  75.5 10.0 %collective-permute-start.2 = (bf16[1,32,512]{2,1,0:T(8,128)(2,1)}, bf16[1,32,512]{2,1,0:T(8,128)(2,1)S(1)}, u32[]{:S(2)}, u32[]{:S(2)}) collective-permute-start(bf16[1,32,512]{2,1,0:T(8,128)(2,1)} %bitcast.30), channel_id=1, source_target_pairs={{0,8},{2,10},{4,12},{6,14},{8,0},{10,2},{12,4},{14,6},{1,9},{3,11}... | collective-permute-start | bytes 98312 | tf_op jit(solution)/shard_map/cond/branch_1_fun/cond/branch_1_fun/ppermute | solution.py:333
  79.6 6.9 %collective-permute-start.1 = (bf16[1,32,512]{2,1,0:T(8,128)(2,1)}, bf16[1,32,512]{2,1,0:T(8,128)(2,1)S(1)}, u32[]{:S(2)}, u32[]{:S(2)}) collective-permute-start(bf16[1,32,512]{2,1,0:T(8,128)(2,1)} %bitcast.31), channel_id=1, source_target_pairs={{0,4},{2,6},{4,0},{6,2},{8,12},{10,14},{12,8},{14,10},{1,5},{3,7},... | collective-permute-start | bytes 98312 | tf_op jit(solution)/shard_map/cond/branch_1_fun/cond/branch_1_fun/ppermute | solution.py:333
  100.6 29.2 %copy-start.3 = (bf16[512,512]{1,0:T(8,128)(2,1)S(1)}, bf16[512,512]{1,0:T(8,128)(2,1)}, u32[]{:S(2)}) copy-start(bf16[512,512]{1,0:T(8,128)(2,1)} %copy-done.2) | copy-start | bytes 1572868 | tf_op jit(solution)/shard_map/cond
  100.6 29.2 %all-to-all-start.2 = ((bf16[16,32,896]{2,1,0:T(8,128)(2,1)}), bf16[16,32,896]{2,1,0:T(8,128)(2,1)}, u32[]{:S(2)}, u32[]{:S(2)}) async-start(bf16[16,32,896]{2,1,0:T(8,128)(2,1)} %branch_1_fun.13), calls=%async_computation.2 | async-start | bytes 1835008 | tf_op jit(solution)/shard_map/cond/branch_1_fun/all_to_all | solution.py:393
  105.4 9.3 %collective-permute-start.7 = (bf16[4,32,512]{2,1,0:T(8,128)(2,1)S(1)}, bf16[4,32,512]{2,1,0:T(8,128)(2,1)S(1)}, u32[]{:S(2)}, u32[]{:S(2)}) collective-permute-start(bf16[4,32,512]{2,1,0:T(8,128)(2,1)S(1)} %get-tuple-element.74.after_ref), channel_id=1, source_target_pairs={{0,18},{2,16},{4,22},{6,20},{8,26},{10,24},{12,30},{14,28},{16,2},... | collective-permute-start | bytes 393224 | tf_op jit(solution)/shard_map/cond/branch_1_fun/ppermute | solution.py:333
  108.4 7.2 %collective-permute-start.6 = (bf16[4,32,512]{2,1,0:T(8,128)(2,1)S(1)}, bf16[4,32,512]{2,1,0:T(8,128)(2,1)S(1)}, u32[]{:S(2)}, u32[]{:S(2)}) collective-permute-start(bf16[4,32,512]{2,1,0:T(8,128)(2,1)S(1)} %get-tuple-element.74.after_ref), channel_id=1, source_target_pairs={{0,2},{2,0},{4,6},{6,4},{8,10},{10,8},{12,14},{14,12},{16,18},{18,... | collective-permute-start | bytes 393224 | tf_op jit(solution)/shard_map/cond/branch_1_fun/ppermute | solution.py:333
  111.7 8.5 %collective-permute-start.5 = (bf16[4,32,512]{2,1,0:T(8,128)(2,1)S(1)}, bf16[4,32,512]{2,1,0:T(8,128)(2,1)S(1)}, u32[]{:S(2)}, u32[]{:S(2)}) collective-permute-start(bf16[4,32,512]{2,1,0:T(8,128)(2,1)S(1)} %get-tuple-element.74.after_ref), channel_id=1, source_target_pairs={{0,16},{2,18},{4,20},{6,22},{8,24},{10,26},{12,28},{14,30},{16,0},... | collective-permute-start | bytes 393224 | tf_op jit(solution)/shard_map/cond/branch_1_fun/ppermute | solution.py:333
  135.7 21.9 %all-to-all-start.4 = ((bf16[16,32,512]{2,1,0:T(8,128)(2,1)}), bf16[16,32,512]{2,1,0:T(8,128)(2,1)S(1)}, u32[]{:S(2)}, u32[]{:S(2)}) async-start(bf16[16,32,512]{2,1,0:T(8,128)(2,1)} %get-tuple-element.105), calls=%async_computation.4 | async-start | bytes 1048576 | tf_op jit(solution)/shard_map/all_to_all | solution.py:401
  147.9 5.0 %collective-permute-start = (bf16[3,448,512]{2,1,0:T(8,128)(2,1)S(1)}, bf16[3,448,512]{2,1,0:T(8,128)(2,1)S(1)}, u32[]{:S(2)}, u32[]{:S(2)}) collective-permute-start(bf16[3,448,512]{2,1,0:T(8,128)(2,1)S(1)} %get-tuple-element.80), channel_id=1, source_target_pairs={{0,1},{1,0},{2,3},{3,2},{4,5},{5,4},{6,7},{7,6},{8,9},{9,8},{10,11... | collective-permute-start | bytes 4128776 | tf_op jit(solution)/shard_map/cond/branch_1_fun/ppermute | solution.py:59
Sparse Core Ops, SparseCore 0:
  38.2 60.3 all-gather.1

commit v11 on v10

--- a/solution.py
+++ b/solution.py
@@ -97,13 +97,13 @@
     )(grad_out, gate_t, up_t, down)
 
 
-def tile_kernel(extra_ref, after_ref, tile_ref):
+def tile_kernel(extra_ref, tile_ref):
     sums = totals_of(jnp.sum(extra_ref[...].astype(jnp.float32), axis=0))
     tile = jnp.concatenate(sums + [jnp.zeros((5, LANES), jnp.float32)], axis=0)
     tile_ref[...] = jnp.broadcast_to(tile[None], tile_ref.shape)
 
 
-def sums_tile(received, after):
+def sums_tile(received):
     rows = received.shape[1] - EXTRA
     return pl.pallas_call(
         tile_kernel,
@@ -111,12 +111,11 @@
         out_shape=jax.ShapeDtypeStruct((2 * N_ROW, 8, LANES), jnp.float32),
         in_specs=[
             pl.BlockSpec((N_CHIP, EXTRA, LANES), lambda i: (0, rows // EXTRA, 0)),
-            ANY,
         ],
         out_specs=pl.BlockSpec((2 * N_ROW, 8, LANES), lambda i: (0, 0, 0)),
         compiler_params=PARAMS,
         cost_estimate=cost(1 << 16, 1 << 18),
-    )(received, after)
+    )(received)
 
 
 def scale_of(tile_ref, which):
@@ -340,19 +339,37 @@
     return blocks, clipped_latents(tile, gate_t, up_t, other_latents)
 
 
-def own_half(core, gate_pre, up_pre):
-    inner = gate_pre.shape[1]
+def half_of(ref, core):
+    rows = ref.shape[0] // 2
+    return ref[pl.ds(pl.multiple_of(core * rows, rows), rows), :]
+
+
+def pre_rows_kernel(mine_ref, gate_pre_ref, up_pre_ref, near_ref, far_ref, both_ref, after_ref, rows_ref):
+    rows, inner = gate_pre_ref.shape[0] // 2, gate_pre_ref.shape[1]
+    core, xh = mine_ref[0], mine_ref[1]
+    near, far, both = near_ref[...], far_ref[...], both_ref[...]
+    own = [half_of(gate_pre_ref, core), near[:, :inner], half_of(up_pre_ref, core), near[:, inner:]]
+    other = [far[:, :inner], both[:, :inner], far[:, inner:], both[:, inner:]]
+    for at, parts in ((xh, own), (1 - xh, other)):
+        rows_ref[pl.ds(pl.multiple_of(at * rows, rows), rows), :] = jnp.concatenate(parts, axis=1)
+
+
+def own_half(mine, gate_pre, up_pre, after):
+    rows, inner = gate_pre.shape
     pre = jnp.concatenate([gate_pre, up_pre], axis=1).reshape((2, -1, 2 * inner))
-    own = lax.dynamic_index_in_dim(pre, core, 0, keepdims=False)
-    other = swapped(lax.dynamic_index_in_dim(pre, 1 - core, 0, keepdims=False))
-    rows = jnp.concatenate(
-        [own[:, :inner], other[:, :inner], own[:, inner:], other[:, inner:]], axis=1
-    )
-    other = lax.ppermute(rows, "xh", [(0, 1), (1, 0)])
-    pair = jnp.where(
-        lax.axis_index("xh") == 0, jnp.stack([rows, other]), jnp.stack([other, rows])
-    )
-    return (pair.reshape((-1, 4 * inner)),)
+    own = lax.dynamic_index_in_dim(pre, mine[0], 0, keepdims=False)
+    sent = lax.dynamic_index_in_dim(pre, 1 - mine[0], 0, keepdims=False)
+    near = swapped(sent)
+    far = lax.ppermute(own, "xh", [(0, 1), (1, 0)])
+    both = lax.ppermute(sent, ("xh", "core"), [(k, k ^ 3) for k in range(4)])
+    return pl.pallas_call(
+        pre_rows_kernel,
+        out_shape=jax.ShapeDtypeStruct((rows, 4 * inner), jnp.bfloat16),
+        in_specs=[SMEM] + [VMEM] * 5 + [ANY],
+        out_specs=VMEM,
+        compiler_params=PARAMS,
+        cost_estimate=cost(1 << 10, 1 << 19),
+    )(mine, gate_pre, up_pre, near, far, both, after)
 
 
 def in_branch(work, *operands):
@@ -367,24 +384,18 @@
 
 
 def shards(tokens, grad_out, gate_pre, up_pre, gate_latent, up_latent, down_latent):
-    core = lax.axis_index("core")
+    mine = jnp.stack([lax.axis_index("core"), lax.axis_index("xh")]).astype(jnp.int32)
     place = jnp.stack([lax.axis_index("xl"), lax.axis_index("y")]).astype(jnp.int32)
     gate_t, up_t = gate_latent.T, up_latent.T
     sent = first(grad_out, gate_t, up_t, down_latent)
 
-    def gathers(sent, core, gate_pre, up_pre, down):
-        received = lax.all_to_all(sent, CHIP, 0, 0)
-        down_other = swapped(down)
-        (pre_rows,) = in_branch(own_half, core, gate_pre, up_pre)
-        return (received, down_other, pre_rows, sums_tile(received, pre_rows))
-
-    received, down_other, pre_rows, tile = in_branch(
-        gathers, sent, core, gate_pre, up_pre, down_latent
-    )
+    received = lax.all_to_all(sent, CHIP, 0, 0)
+    down_other = swapped(down_latent)
+    pre_rows = own_half(mine, gate_pre, up_pre, sent)
     pre_half = lax.all_gather(pre_rows, "z", axis=0, tiled=True)
 
-    def exchanges(received, tile, tokens, gate_t, up_t, down, down_other):
-        tile = lax.all_to_all(tile, ROW + ("core",), 0, 0)
+    def exchanges(received, tokens, gate_t, up_t, down, down_other):
+        tile = lax.all_to_all(sums_tile(received), ROW + ("core",), 0, 0)
         out_half, both = laid_out(received, down, down_other)
         partial = hidden_partial(tile, out_half, both)
         parts = lax.all_to_all(partial, ROW, 0, 0)
@@ -394,7 +405,7 @@
         return (out_half, quant, grad_hidden, token_blocks)
 
     out_half, quant, grad_hidden, token_blocks = in_branch(
-        exchanges, received, tile, tokens, gate_t, up_t, down_latent, down_other
+        exchanges, received, tokens, gate_t, up_t, down_latent, down_other
     )
 
     partial, acts = act_partial(grad_hidden, pre_half, quant)

time: 166 us -> 172 us (1.036)
  starting transfers between devices: 70.7 us -> 74.5 us
    all_to_all x2, waiting for transfers between devices: 10.6 us -> 23.4 us  [the longest x1 12.4 us: shards(): received = lax.all_to_all(sent, CHIP, 0, 0)]
    all_to_all x1, waiting for transfers between devices: 10.3 us -> 1.78 us  [exchanges(): parts = lax.all_to_all(partial, ROW, 0, 0)]
    ppermute x1 -> x2, waiting for transfers between devices: 7.75 us -> 1.5 us  [the longest x1 1.5 us: own_half(): far = lax.ppermute(own, 'xh', [(0, 1), (1, 0)])]
    ppermute x1 -> x2, starting transfers between devices: 2.67 us -> 7.45 us  [the longest x1 4.14 us: own_half(): both = lax.ppermute(sent, ('xh', 'core'), [(k, k ^ 3) for k in range(4)])]
    all_to_all x1, starting transfers between devices: 4.81 us -> 7.91 us  [exchanges(): grad_hidden = lax.all_to_all(spread(parts, far), ROW, 0, 0)]
    all_to_all x1, starting transfers between devices: 8.65 us -> 6.67 us  [shards(): parts = lax.all_to_all(partial, CHIP, 0, 0)]
  transfers between devices with their start and end apart: 17 -> 18, of which waited for: 12 -> 13; matrix products, arithmetic and copies ran while one was open for 2% -> 2% of each run, Pallas kernels for 8% -> 9%
where the time goes in v11:
time: 172 us; the launch traced here: 170 us
  starting transfers between devices  74.5 us (43%)
  waiting for transfers between devices  53.4 us (31%)
  Pallas kernels  23.2 us (13%)
  between operations  14.2 us (8%)
  other arithmetic  3.78 us (2%)
    ppermute x6, starting transfers between devices, exchanged(): lax.ppermute(blocks, axis, [(k, k ^ step) for k in range(count)])  21.4 us
    all_to_all x1, waiting for transfers between devices, shards(): received = lax.all_to_all(sent, CHIP, 0, 0)  12.4 us
    all_to_all x1, starting transfers between devices, exchanges(): tile = lax.all_to_all(sums_tile(received), ROW + ('core',), 0, 0)  11.3 us
    all_to_all x1, waiting for transfers between devices, exchanges(): tile = lax.all_to_all(sums_tile(received), ROW + ('core',), 0, 0)  11 us
    ppermute x6, waiting for transfers between devices, exchanged(): lax.ppermute(blocks, axis, [(k, k ^ step) for k in range(count)])  9.51 us
    all_to_all x1, waiting for transfers between devices, exchanges(): grad_hidden = lax.all_to_all(spread(parts, far), ROW, 0, 0)  8.82 us
    all_to_all x1, starting transfers between devices, shards(): received = lax.all_to_all(sent, CHIP, 0, 0)  8.48 us
    all_to_all x1, starting transfers between devices, exchanges(): grad_hidden = lax.all_to_all(spread(parts, far), ROW, 0, 0)  7.91 us
  transfers between devices with their start and end apart: 18, of which 13 were waited for; matrix products, arithmetic and copies ran while one was open for 2% of the time, Pallas kernels for 9%

profile of v11, /device:TPU:10, one launch (start us, length us, event | category | flops | bytes accessed | tf_op | source)
XLA Modules:
  0.0 170.4 jit_solution(5873168405491664198)
XLA Ops:
  7.2 0.0 all-gather.2.cloned.1.call-start
  7.2 1.0 pad_maximum_fusion.3
  8.2 1.9 %collective-permute-start.9 = (bf16[32,896]{1,0:T(8,128)(2,1)S(1)}, bf16[32,896]{1,0:T(8,128)(2,1)S(1)}, u32[]{:S(2)}, u32[]{:S(2)}) collective-permute-start(bf16[32,896]{1,0:T(8,128)(2,1)S(1)} %get-tuple-element.78), channel_id=1, source_target_pairs={{0,1},{1,0},{2,3},{3,2},{4,5},{5,4},{6,7},{7,6},{8,9},{9,8},{10,11... | collective-permute-start | bytes 172040 | tf_op jit(solution)/shard_map/ppermute | solution.py:59
  10.2 4.1 %collective-permute-start.11 = (bf16[32,896]{1,0:T(8,128)(2,1)S(1)}, bf16[32,896]{1,0:T(8,128)(2,1)S(1)}, u32[]{:S(2)}, u32[]{:S(2)}) collective-permute-start(bf16[32,896]{1,0:T(8,128)(2,1)S(1)} %get-tuple-element.78), channel_id=1, source_target_pairs={{0,257},{1,256},{256,1},{257,0},{2,259},{3,258},{258,3},{259,2},{4... | collective-permute-start | bytes 172040 | tf_op jit(solution)/shard_map/ppermute | solution.py:364
  14.3 3.3 %collective-permute-start.10 = (bf16[32,896]{1,0:T(8,128)(2,1)S(1)}, bf16[32,896]{1,0:T(8,128)(2,1)S(1)}, u32[]{:S(2)}, u32[]{:S(2)}) collective-permute-start(bf16[32,896]{1,0:T(8,128)(2,1)S(1)} %get-tuple-element.77), channel_id=1, source_target_pairs={{0,256},{256,0},{1,257},{257,1},{2,258},{258,2},{3,259},{259,3},{4... | collective-permute-start | bytes 172040 | tf_op jit(solution)/shard_map/ppermute | solution.py:363
  17.6 0.0 copy-start.7
  17.6 0.0 copy-start.3
  17.7 0.0 copy-start.4
  17.7 0.0 copy-start.10
  17.7 2.6 %shard_map.103.after_ref = bf16[16,144,128]{2,1,0:T(8,128)(2,1)} custom-call(bf16[32,512]{1,0:T(8,128)(2,1)} %out_ref.1, bf16[448,512]{1,0:T(8,128)(2,1)} %bitcast.17, bf16[448,512]{1,0:T(8,128)(2,1)} %bitcast.20, bf16[448,512]{1,0:T(8,128)(2,1)} %down_ref.1), custom_call_target="tpu_custom_call" | custom-call | flops 1048576 | bytes 2621440 | tf_op jit(solution)/shard_map/pallas_call | solution.py:90
  20.3 0.1 pad_add_fusion.mine_ref
  20.4 0.0 collective-permute-done.9.near_ref
  20.4 1.5 collective-permute-done.10.far_ref
  21.9 0.0 collective-permute-done.11.both_ref
  21.9 1.1 copy-done
  23.0 1.3 shard_map.104
  24.3 0.0 all-gather.2.cloned.1.call-update
  24.3 8.5 %all-to-all-start.3 = ((bf16[16,144,128]{2,1,0:T(8,128)(2,1)}), bf16[16,144,128]{2,1,0:T(8,128)(2,1)S(1)}, u32[]{:S(2)}, u32[]{:S(2)}) async-start(bf16[16,144,128]{2,1,0:T(8,128)(2,1)} %shard_map.103.after_ref), calls=%async_computation.3 | async-start | bytes 1179648 | tf_op jit(solution)/shard_map/all_to_all | solution.py:392
  32.8 1.9 %collective-permute-start.8 = (bf16[448,512]{1,0:T(8,128)(2,1)S(1)}, bf16[448,512]{1,0:T(8,128)(2,1)S(1)}, u32[]{:S(2)}, u32[]{:S(2)}) collective-permute-start(bf16[448,512]{1,0:T(8,128)(2,1)S(1)} %copy-done.7), channel_id=1, source_target_pairs={{0,1},{1,0},{2,3},{3,2},{4,5},{5,4},{6,7},{7,6},{8,9},{9,8},{10,11... | collective-permute-start | bytes 1376264 | tf_op jit(solution)/shard_map/ppermute | solution.py:59
  34.7 1.8 %collective-permute-done.8 = bf16[448,512]{1,0:T(8,128)(2,1)S(1)} collective-permute-done((bf16[448,512]{1,0:T(8,128)(2,1)S(1)}, bf16[448,512]{1,0:T(8,128)(2,1)S(1)}, u32[]{:S(2)}, u32[]{:S(2)}) %collective-permute-start.8) | collective-permute-done | bytes 458784 | tf_op jit(solution)/shard_map/ppermute | solution.py:59
  36.5 12.4 %all-to-all-done.3 = bf16[16,144,128]{2,1,0:T(8,128)(2,1)S(1)} async-done(((bf16[16,144,128]{2,1,0:T(8,128)(2,1)}), bf16[16,144,128]{2,1,0:T(8,128)(2,1)S(1)}, u32[]{:S(2)}, u32[]{:S(2)}) %all-to-all-start.3) | async-done | bytes 589856 | tf_op jit(solution)/shard_map/all_to_all | solution.py:392
  48.9 88.0 %conditional.3 = (bf16[512,512]{1,0:T(8,128)(2,1)S(1)}, bf16[2,896,512]{2,1,0:T(8,128)(2,1)}, bf16[16,32,896]{2,1,0:T(8,128)(2,1)}, bf16[16,32,512]{2,1,0:T(8,128)(2,1)}) conditional(s32[]{:T(128)} %convert_element_type.7, () %tuple.31, (bf16[16,144,128]{2,1,0:T(8,128)(2,1)S(1)}, bf16[448,512]{1,0:T(8,128)(2,1)S(1)}, bf16[448,512]{1,0:T(8,128)(2,1)S(1)}, ...), branch_computations={%region_0.1_spmd, %region_1.4_spmd} | conditional | flops 472843264 | bytes 36504176 | solution.py:383
  48.9 0.0 copy-start.8
  48.9 0.0 copy-start.9
  49.0 0.8 branch_1_fun.11
  49.7 11.3 %all-to-all-start = ((f32[32,8,128]{2,1,0:T(8,128)}), f32[32,8,128]{2,1,0:T(8,128)S(1)}, u32[]{:S(2)}, u32[]{:S(2)}) async-start(f32[32,8,128]{2,1,0:T(8,128)} %branch_1_fun.11), calls=%async_computation | async-start | bytes 262144 | tf_op jit(solution)/shard_map/cond/branch_1_fun/all_to_all | solution.py:398
  61.0 1.3 branch_1_fun.10
  62.4 11.0 %all-to-all-done.tile_ref = f32[32,8,128]{2,1,0:T(8,128)S(1)} async-done(((f32[32,8,128]{2,1,0:T(8,128)}), f32[32,8,128]{2,1,0:T(8,128)S(1)}, u32[]{:S(2)}, u32[]{:S(2)}) %all-to-all-start) | async-done | bytes 131104 | tf_op jit(solution)/shard_map/cond/branch_1_fun/all_to_all | solution.py:398
  73.3 2.3 %branch_1_fun.12 = bf16[16,32,896]{2,1,0:T(8,128)(2,1)} custom-call(f32[32,8,128]{2,1,0:T(8,128)S(1)} %all-to-all-done.tile_ref, bf16[512,512]{1,0:T(8,128)(2,1)S(1)} %get-tuple-element.87.out_ref, bf16[2,448,512]{2,1,0:T(8,128)(2,1)S(1)} %get-tuple-element.40.both_ref), custom_call_target="tpu_custom_call" | custom-call | flops 469762048 | bytes 4194304 | tf_op jit(solution)/shard_map/cond/branch_1_fun/pallas_call | solution.py:169
  75.6 3.6 %all-to-all-start.1 = ((bf16[16,32,896]{2,1,0:T(8,128)(2,1)}), bf16[16,32,896]{2,1,0:T(8,128)(2,1)S(1)}, u32[]{:S(2)}, u32[]{:S(2)}) async-start(bf16[16,32,896]{2,1,0:T(8,128)(2,1)} %branch_1_fun.12), calls=%async_computation.1 | async-start | bytes 1835008 | tf_op jit(solution)/shard_map/cond/branch_1_fun/all_to_all | solution.py:401
  79.2 22.8 %conditional = (bf16[4,32,512]{2,1,0:T(8,128)(2,1)S(1)}, bf16[2,896,512]{2,1,0:T(8,128)(2,1)}) conditional(s32[]{:T(128)} %convert_element_type.1, () %tuple.21, (bf16[32,512]{1,0:T(8,128)(2,1)S(1)}, bf16[16,32,896]{2,1,0:T(8,128)(2,1)}, bf16[448,512]{1,0:T(8,128)(2,1)S(1)}, bf16[448,512]{1,0:T(8,128)(2,1)S(1)}, f32[32,8,128]{2,1,0:T(8,128)S(1)}) %tuple.22), branch_computations={%region_2.2_spmd, %region_3.3_spmd} | conditional | flops 1703937 | bytes 10420400 | solution.py:383
  79.2 1.0 pad_maximum_fusion
  80.2 1.9 %collective-permute-start.4 = (bf16[2,448,512]{2,1,0:T(8,128)(2,1)}, bf16[2,448,512]{2,1,0:T(8,128)(2,1)S(1)}, u32[]{:S(2)}, u32[]{:S(2)}) collective-permute-start(bf16[2,448,512]{2,1,0:T(8,128)(2,1)} %pad_maximum_fusion), channel_id=1, source_target_pairs={{0,1},{1,0},{2,3},{3,2},{4,5},{5,4},{6,7},{7,6},{8,9},{9,8},{10,11... | collective-permute-start | bytes 2752520 | tf_op jit(solution)/shard_map/cond/branch_1_fun/cond/branch_1_fun/ppermute | solution.py:59
  82.2 0.6 branch_1_fun.8
  82.8 4.3 %collective-permute-start.3 = (bf16[1,32,512]{2,1,0:T(8,128)(2,1)}, bf16[1,32,512]{2,1,0:T(8,128)(2,1)S(1)}, u32[]{:S(2)}, u32[]{:S(2)}) collective-permute-start(bf16[1,32,512]{2,1,0:T(8,128)(2,1)} %bitcast.27), channel_id=1, source_target_pairs={{0,12},{2,14},{4,8},{6,10},{8,4},{10,6},{12,0},{14,2},{1,13},{3,15... | collective-permute-start | bytes 98312 | tf_op jit(solution)/shard_map/cond/branch_1_fun/cond/branch_1_fun/ppermute | solution.py:332
  87.1 5.2 %collective-permute-start.2 = (bf16[1,32,512]{2,1,0:T(8,128)(2,1)}, bf16[1,32,512]{2,1,0:T(8,128)(2,1)S(1)}, u32[]{:S(2)}, u32[]{:S(2)}) collective-permute-start(bf16[1,32,512]{2,1,0:T(8,128)(2,1)} %bitcast.28), channel_id=1, source_target_pairs={{0,8},{2,10},{4,12},{6,14},{8,0},{10,2},{12,4},{14,6},{1,9},{3,11}... | collective-permute-start | bytes 98312 | tf_op jit(solution)/shard_map/cond/branch_1_fun/cond/branch_1_fun/ppermute | solution.py:332
  92.3 2.7 %collective-permute-start.1 = (bf16[1,32,512]{2,1,0:T(8,128)(2,1)}, bf16[1,32,512]{2,1,0:T(8,128)(2,1)S(1)}, u32[]{:S(2)}, u32[]{:S(2)}) collective-permute-start(bf16[1,32,512]{2,1,0:T(8,128)(2,1)} %bitcast.29), channel_id=1, source_target_pairs={{0,4},{2,6},{4,0},{6,2},{8,12},{10,14},{12,8},{14,10},{1,5},{3,7},... | collective-permute-start | bytes 98312 | tf_op jit(solution)/shard_map/cond/branch_1_fun/cond/branch_1_fun/ppermute | solution.py:332
  95.0 0.0 collective-permute-done.3
  95.0 2.4 %collective-permute-done.2 = bf16[1,32,512]{2,1,0:T(8,128)(2,1)S(1)} collective-permute-done((bf16[1,32,512]{2,1,0:T(8,128)(2,1)}, bf16[1,32,512]{2,1,0:T(8,128)(2,1)S(1)}, u32[]{:S(2)}, u32[]{:S(2)}) %collective-permute-start.2) | collective-permute-done | bytes 32800 | tf_op jit(solution)/shard_map/cond/branch_1_fun/cond/branch_1_fun/ppermute | solution.py:332
  97.5 1.8 %collective-permute-done.1 = bf16[1,32,512]{2,1,0:T(8,128)(2,1)S(1)} collective-permute-done((bf16[1,32,512]{2,1,0:T(8,128)(2,1)}, bf16[1,32,512]{2,1,0:T(8,128)(2,1)S(1)}, u32[]{:S(2)}, u32[]{:S(2)}) %collective-permute-start.1) | collective-permute-done | bytes 32800 | tf_op jit(solution)/shard_map/cond/branch_1_fun/cond/branch_1_fun/ppermute | solution.py:332
  99.2 0.8 pad_maximum_fusion.1
  100.0 0.0 collective-permute-done.4.other_ref
  100.0 1.9 %branch_1_fun.9 = bf16[2,896,512]{2,1,0:T(8,128)(2,1)} custom-call(f32[32,8,128]{2,1,0:T(8,128)S(1)} %get-tuple-element.32.tile_ref, bf16[448,512]{1,0:T(8,128)(2,1)S(1)} %get-tuple-element.33.gate_ref, bf16[448,512]{1,0:T(8,128)(2,1)S(1)} %get-tuple-element.34.up_ref, bf16[2,448,512]{2,1,0:T(8,128)(2,1)S(1)} %collective-permute-done.4.other_ref), custom_call_target="tpu_custom_call" | custom-call | flops 1048576 | bytes 4194304 | tf_op jit(solution)/shard_map/cond/branch_1_fun/cond/branch_1_fun/pallas_call | solution.py:206
  102.0 1.8 %all-to-all-done.1.parts_ref = bf16[16,32,896]{2,1,0:T(8,128)(2,1)S(1)} async-done(((bf16[16,32,896]{2,1,0:T(8,128)(2,1)}), bf16[16,32,896]{2,1,0:T(8,128)(2,1)S(1)}, u32[]{:S(2)}, u32[]{:S(2)}) %all-to-all-start.1) | async-done | bytes 917536 | tf_op jit(solution)/shard_map/cond/branch_1_fun/all_to_all | solution.py:401
  103.7 1.1 branch_1_fun.13
  104.8 7.9 %all-to-all-start.2 = ((bf16[16,32,896]{2,1,0:T(8,128)(2,1)}), bf16[16,32,896]{2,1,0:T(8,128)(2,1)}, u32[]{:S(2)}, u32[]{:S(2)}) async-start(bf16[16,32,896]{2,1,0:T(8,128)(2,1)} %branch_1_fun.13), calls=%async_computation.2 | async-start | bytes 1835008 | tf_op jit(solution)/shard_map/cond/branch_1_fun/all_to_all | solution.py:404
  112.7 3.3 %collective-permute-start.7 = (bf16[4,32,512]{2,1,0:T(8,128)(2,1)S(1)}, bf16[4,32,512]{2,1,0:T(8,128)(2,1)S(1)}, u32[]{:S(2)}, u32[]{:S(2)}) collective-permute-start(bf16[4,32,512]{2,1,0:T(8,128)(2,1)S(1)} %get-tuple-element.44.after_ref), channel_id=1, source_target_pairs={{0,18},{2,16},{4,22},{6,20},{8,26},{10,24},{12,30},{14,28},{16,2},... | collective-permute-start | bytes 393224 | tf_op jit(solution)/shard_map/cond/branch_1_fun/ppermute | solution.py:332
  116.0 3.0 %collective-permute-start.6 = (bf16[4,32,512]{2,1,0:T(8,128)(2,1)S(1)}, bf16[4,32,512]{2,1,0:T(8,128)(2,1)S(1)}, u32[]{:S(2)}, u32[]{:S(2)}) collective-permute-start(bf16[4,32,512]{2,1,0:T(8,128)(2,1)S(1)} %get-tuple-element.44.after_ref), channel_id=1, source_target_pairs={{0,2},{2,0},{4,6},{6,4},{8,10},{10,8},{12,14},{14,12},{16,18},{18,... | collective-permute-start | bytes 393224 | tf_op jit(solution)/shard_map/cond/branch_1_fun/ppermute | solution.py:332
  119.0 2.9 %collective-permute-start.5 = (bf16[4,32,512]{2,1,0:T(8,128)(2,1)S(1)}, bf16[4,32,512]{2,1,0:T(8,128)(2,1)S(1)}, u32[]{:S(2)}, u32[]{:S(2)}) collective-permute-start(bf16[4,32,512]{2,1,0:T(8,128)(2,1)S(1)} %get-tuple-element.44.after_ref), channel_id=1, source_target_pairs={{0,16},{2,18},{4,20},{6,22},{8,24},{10,26},{12,28},{14,30},{16,0},... | collective-permute-start | bytes 393224 | tf_op jit(solution)/shard_map/cond/branch_1_fun/ppermute | solution.py:332
  122.0 0.2 collective-permute-done.7
  122.2 0.7 collective-permute-done.6
  122.9 4.4 %collective-permute-done.5 = bf16[4,32,512]{2,1,0:T(8,128)(2,1)S(1)} collective-permute-done((bf16[4,32,512]{2,1,0:T(8,128)(2,1)S(1)}, bf16[4,32,512]{2,1,0:T(8,128)(2,1)S(1)}, u32[]{:S(2)}, u32[]{:S(2)}) %collective-permute-start.5) | collective-permute-done | bytes 131104 | tf_op jit(solution)/shard_map/cond/branch_1_fun/ppermute | solution.py:332
  127.2 0.9 pad_maximum_fusion.2
  128.1 8.8 %all-to-all-done.2 = bf16[16,32,896]{2,1,0:T(8,128)(2,1)} async-done(((bf16[16,32,896]{2,1,0:T(8,128)(2,1)}), bf16[16,32,896]{2,1,0:T(8,128)(2,1)}, u32[]{:S(2)}, u32[]{:S(2)}) %all-to-all-start.2) | async-done | bytes 917536 | tf_op jit(solution)/shard_map/cond/branch_1_fun/all_to_all | solution.py:404
  136.9 5.8 %shard_map.105 = (bf16[16,32,512]{2,1,0:T(8,128)(2,1)}, bf16[3,512,896]{2,1,0:T(8,128)(2,1)}) custom-call(bf16[16,32,896]{2,1,0:T(8,128)(2,1)} %get-tuple-element.65.hid_ref, bf16[8,2,32,1792]{3,2,1,0:T(8,128)(2,1)} %bitcast.23, bf16[2,896,512]{2,1,0:T(8,128)(2,1)} %get-tuple-element.66.quant_ref), custom_call_target="tpu_custom_call" | custom-call | flops 939524096 | bytes 8388608 | tf_op jit(solution)/shard_map/pallas_call | solution.py:231
  142.8 6.7 %all-to-all-start.4 = ((bf16[16,32,512]{2,1,0:T(8,128)(2,1)}), bf16[16,32,512]{2,1,0:T(8,128)(2,1)S(1)}, u32[]{:S(2)}, u32[]{:S(2)}) async-start(bf16[16,32,512]{2,1,0:T(8,128)(2,1)} %get-tuple-element.67), calls=%async_computation.4 | async-start | bytes 1048576 | tf_op jit(solution)/shard_map/all_to_all | solution.py:412
  149.5 0.1 pad_add_fusion.1
  149.5 9.8 %conditional.4 = ((bf16[448,512]{1,0:T(8,128)(2,1)}, bf16[448,512]{1,0:T(8,128)(2,1)}, bf16[448,512]{1,0:T(8,128)(2,1)}, f32[8,128]{1,0:T(8,128)S(1)})) conditional(s32[]{:T(128)} %convert_element_type.7, () %tuple.33, (s32[2]{0:T(128)S(1)}, bf16[3,512,896]{2,1,0:T(8,128)(2,1)}, bf16[512,512]{1,0:T(8,128)(2,1)S(1)}, ...), branch_computations={%region_4.5_spmd, %region_5.6_spmd} | conditional | flops 1410334720 | bytes 19136560 | solution.py:383
  149.5 3.5 %branch_1_fun.14 = (f32[3,448,512]{2,1,0:T(8,128)S(1)}, bf16[3,448,512]{2,1,0:T(8,128)(2,1)S(1)}) custom-call(s32[2]{0:T(128)S(1)} %get-tuple-element.45.place_ref, bf16[3,512,896]{2,1,0:T(8,128)(2,1)} %get-tuple-element.46.acts_ref, bf16[512,512]{1,0:T(8,128)(2,1)S(1)} %get-tuple-element.47.out_ref, bf16[16,32,512]{2,1,0:T(8,128)(2,1)} %get-tuple-element.48.tokens_ref), custom_call_target="tpu_custom_call" | custom-call | flops 1409286144 | bytes 8388608 | tf_op jit(solution)/shard_map/cond/branch_1_fun/pallas_call | solution.py:269
  153.1 1.9 %collective-permute-start = (bf16[3,448,512]{2,1,0:T(8,128)(2,1)S(1)}, bf16[3,448,512]{2,1,0:T(8,128)(2,1)S(1)}, u32[]{:S(2)}, u32[]{:S(2)}) collective-permute-start(bf16[3,448,512]{2,1,0:T(8,128)(2,1)S(1)} %get-tuple-element.50), channel_id=1, source_target_pairs={{0,1},{1,0},{2,3},{3,2},{4,5},{5,4},{6,7},{7,6},{8,9},{9,8},{10,11... | collective-permute-start | bytes 4128776 | tf_op jit(solution)/shard_map/cond/branch_1_fun/ppermute | solution.py:59
  155.0 3.1 %collective-permute-done.other_ref = bf16[3,448,512]{2,1,0:T(8,128)(2,1)S(1)} collective-permute-done((bf16[3,448,512]{2,1,0:T(8,128)(2,1)S(1)}, bf16[3,448,512]{2,1,0:T(8,128)(2,1)S(1)}, u32[]{:S(2)}, u32[]{:S(2)}) %collective-permute-start) | collective-permute-done | bytes 1376288 | tf_op jit(solution)/shard_map/cond/branch_1_fun/ppermute | solution.py:59
  158.1 1.2 branch_1_fun.15
  159.3 3.5 %all-to-all-done.4.parts_ref = bf16[16,32,512]{2,1,0:T(8,128)(2,1)S(1)} async-done(((bf16[16,32,512]{2,1,0:T(8,128)(2,1)}), bf16[16,32,512]{2,1,0:T(8,128)(2,1)S(1)}, u32[]{:S(2)}, u32[]{:S(2)}) %all-to-all-start.4) | async-done | bytes 524320 | tf_op jit(solution)/shard_map/all_to_all | solution.py:412
  162.9 0.7 shard_map.106
  (17 shorter events, 0.1 us)
Async XLA Ops:
  7.2 14.7 %copy-start.1 = (bf16[64,448]{1,0:T(8,128)(2,1)S(1)}, bf16[64,448]{1,0:T(8,128)(2,1)}, u32[]{:S(2)}) copy-start(bf16[64,448]{1,0:T(8,128)(2,1)} %gate_pre_ref.1) | copy-start | bytes 172036
  7.2 14.7 %copy-start.2 = (bf16[64,448]{1,0:T(8,128)(2,1)S(1)}, bf16[64,448]{1,0:T(8,128)(2,1)}, u32[]{:S(2)}) copy-start(bf16[64,448]{1,0:T(8,128)(2,1)} %up_pre_ref.1) | copy-start | bytes 172036
  7.2 129.8 %all-gather.2.cloned.1.call-start = ((), (), s32[]{:S(2)}) async-start(), calls=%async_computation.5 | async-start | bytes 2064384 | tf_op jit(solution)/shard_map/all_gather | solution.py:395
  8.2 12.2 %collective-permute-start.9 = (bf16[32,896]{1,0:T(8,128)(2,1)S(1)}, bf16[32,896]{1,0:T(8,128)(2,1)S(1)}, u32[]{:S(2)}, u32[]{:S(2)}) collective-permute-start(bf16[32,896]{1,0:T(8,128)(2,1)S(1)} %get-tuple-element.78), channel_id=1, source_target_pairs={{0,1},{1,0},{2,3},{3,2},{4,5},{5,4},{6,7},{7,6},{8,9},{9,8},{10,11... | collective-permute-start | bytes 172040 | tf_op jit(solution)/shard_map/ppermute | solution.py:59
  10.2 11.7 %collective-permute-start.11 = (bf16[32,896]{1,0:T(8,128)(2,1)S(1)}, bf16[32,896]{1,0:T(8,128)(2,1)S(1)}, u32[]{:S(2)}, u32[]{:S(2)}) collective-permute-start(bf16[32,896]{1,0:T(8,128)(2,1)S(1)} %get-tuple-element.78), channel_id=1, source_target_pairs={{0,257},{1,256},{256,1},{257,0},{2,259},{3,258},{258,3},{259,2},{4... | collective-permute-start | bytes 172040 | tf_op jit(solution)/shard_map/ppermute | solution.py:364
  14.3 7.6 %collective-permute-start.10 = (bf16[32,896]{1,0:T(8,128)(2,1)S(1)}, bf16[32,896]{1,0:T(8,128)(2,1)S(1)}, u32[]{:S(2)}, u32[]{:S(2)}) collective-permute-start(bf16[32,896]{1,0:T(8,128)(2,1)S(1)} %get-tuple-element.77), channel_id=1, source_target_pairs={{0,256},{256,0},{1,257},{257,1},{2,258},{258,2},{3,259},{259,3},{4... | collective-permute-start | bytes 172040 | tf_op jit(solution)/shard_map/ppermute | solution.py:363
  17.6 15.2 %copy-start.7 = (bf16[448,512]{1,0:T(8,128)(2,1)S(1)}, bf16[448,512]{1,0:T(8,128)(2,1)}, u32[]{:S(2)}) copy-start(bf16[448,512]{1,0:T(8,128)(2,1)} %down_ref.1) | copy-start | bytes 1376260
  17.6 31.3 %copy-start.3 = (bf16[512,448]{0,1:T(8,128)(2,1)S(1)}, bf16[512,448]{0,1:T(8,128)(2,1)}, u32[]{:S(2)}) copy-start(bf16[512,448]{0,1:T(8,128)(2,1)} %param.17) | copy-start | bytes 1376260
  17.7 31.3 %copy-start.4 = (bf16[512,448]{0,1:T(8,128)(2,1)S(1)}, bf16[512,448]{0,1:T(8,128)(2,1)}, u32[]{:S(2)}) copy-start(bf16[512,448]{0,1:T(8,128)(2,1)} %param.18) | copy-start | bytes 1376260
  17.7 31.3 %copy-start.10 = (bf16[32,512]{1,0:T(8,128)(2,1)S(1)}, bf16[32,512]{1,0:T(8,128)(2,1)}, u32[]{:S(2)}) copy-start(bf16[32,512]{1,0:T(8,128)(2,1)} %param.13) | copy-start | bytes 98308
  21.9 1.1 copy-start
  24.3 24.6 %all-to-all-start.3 = ((bf16[16,144,128]{2,1,0:T(8,128)(2,1)}), bf16[16,144,128]{2,1,0:T(8,128)(2,1)S(1)}, u32[]{:S(2)}, u32[]{:S(2)}) async-start(bf16[16,144,128]{2,1,0:T(8,128)(2,1)} %shard_map.103.after_ref), calls=%async_computation.3 | async-start | bytes 1179648 | tf_op jit(solution)/shard_map/all_to_all | solution.py:392
  32.8 3.7 %collective-permute-start.8 = (bf16[448,512]{1,0:T(8,128)(2,1)S(1)}, bf16[448,512]{1,0:T(8,128)(2,1)S(1)}, u32[]{:S(2)}, u32[]{:S(2)}) collective-permute-start(bf16[448,512]{1,0:T(8,128)(2,1)S(1)} %copy-done.7), channel_id=1, source_target_pairs={{0,1},{1,0},{2,3},{3,2},{4,5},{5,4},{6,7},{7,6},{8,9},{9,8},{10,11... | collective-permute-start | bytes 1376264 | tf_op jit(solution)/shard_map/ppermute | solution.py:59
  48.9 12.1 %copy-start.8 = (bf16[448,512]{1,0:T(8,128)(2,1)}, bf16[448,512]{1,0:T(8,128)(2,1)S(1)}, u32[]{:S(2)}) copy-start(bf16[448,512]{1,0:T(8,128)(2,1)S(1)} %get-tuple-element.36.down_ref) | copy-start | bytes 1376260 | tf_op jit(solution)/shard_map/cond
  48.9 12.1 %copy-start.9 = (bf16[448,512]{1,0:T(8,128)(2,1)}, bf16[448,512]{1,0:T(8,128)(2,1)S(1)}, u32[]{:S(2)}) copy-start(bf16[448,512]{1,0:T(8,128)(2,1)S(1)} %get-tuple-element.37.other_ref) | copy-start | bytes 1376260 | tf_op jit(solution)/shard_map/cond
  49.7 23.6 %all-to-all-start = ((f32[32,8,128]{2,1,0:T(8,128)}), f32[32,8,128]{2,1,0:T(8,128)S(1)}, u32[]{:S(2)}, u32[]{:S(2)}) async-start(f32[32,8,128]{2,1,0:T(8,128)} %branch_1_fun.11), calls=%async_computation | async-start | bytes 262144 | tf_op jit(solution)/shard_map/cond/branch_1_fun/all_to_all | solution.py:398
  62.3 13.2 %copy-start.5 = (bf16[512,512]{1,0:T(8,128)(2,1)}, bf16[512,512]{1,0:T(8,128)(2,1)S(1)}, u32[]{:S(2)}) copy-start(bf16[512,512]{1,0:T(8,128)(2,1)S(1)} %get-tuple-element.87.out_ref) | copy-start | bytes 1572868 | tf_op jit(solution)/shard_map/cond
  75.6 28.2 %all-to-all-start.1 = ((bf16[16,32,896]{2,1,0:T(8,128)(2,1)}), bf16[16,32,896]{2,1,0:T(8,128)(2,1)S(1)}, u32[]{:S(2)}, u32[]{:S(2)}) async-start(bf16[16,32,896]{2,1,0:T(8,128)(2,1)} %branch_1_fun.12), calls=%async_computation.1 | async-start | bytes 1835008 | tf_op jit(solution)/shard_map/cond/branch_1_fun/all_to_all | solution.py:401
  80.2 19.8 %collective-permute-start.4 = (bf16[2,448,512]{2,1,0:T(8,128)(2,1)}, bf16[2,448,512]{2,1,0:T(8,128)(2,1)S(1)}, u32[]{:S(2)}, u32[]{:S(2)}) collective-permute-start(bf16[2,448,512]{2,1,0:T(8,128)(2,1)} %pad_maximum_fusion), channel_id=1, source_target_pairs={{0,1},{1,0},{2,3},{3,2},{4,5},{5,4},{6,7},{7,6},{8,9},{9,8},{10,11... | collective-permute-start | bytes 2752520 | tf_op jit(solution)/shard_map/cond/branch_1_fun/cond/branch_1_fun/ppermute | solution.py:59
  82.8 12.2 %collective-permute-start.3 = (bf16[1,32,512]{2,1,0:T(8,128)(2,1)}, bf16[1,32,512]{2,1,0:T(8,128)(2,1)S(1)}, u32[]{:S(2)}, u32[]{:S(2)}) collective-permute-start(bf16[1,32,512]{2,1,0:T(8,128)(2,1)} %bitcast.27), channel_id=1, source_target_pairs={{0,12},{2,14},{4,8},{6,10},{8,4},{10,6},{12,0},{14,2},{1,13},{3,15... | collective-permute-start | bytes 98312 | tf_op jit(solution)/shard_map/cond/branch_1_fun/cond/branch_1_fun/ppermute | solution.py:332
  87.1 10.4 %collective-permute-start.2 = (bf16[1,32,512]{2,1,0:T(8,128)(2,1)}, bf16[1,32,512]{2,1,0:T(8,128)(2,1)S(1)}, u32[]{:S(2)}, u32[]{:S(2)}) collective-permute-start(bf16[1,32,512]{2,1,0:T(8,128)(2,1)} %bitcast.28), channel_id=1, source_target_pairs={{0,8},{2,10},{4,12},{6,14},{8,0},{10,2},{12,4},{14,6},{1,9},{3,11}... | collective-permute-start | bytes 98312 | tf_op jit(solution)/shard_map/cond/branch_1_fun/cond/branch_1_fun/ppermute | solution.py:332
  92.3 6.9 %collective-permute-start.1 = (bf16[1,32,512]{2,1,0:T(8,128)(2,1)}, bf16[1,32,512]{2,1,0:T(8,128)(2,1)S(1)}, u32[]{:S(2)}, u32[]{:S(2)}) collective-permute-start(bf16[1,32,512]{2,1,0:T(8,128)(2,1)} %bitcast.29), channel_id=1, source_target_pairs={{0,4},{2,6},{4,0},{6,2},{8,12},{10,14},{12,8},{14,10},{1,5},{3,7},... | collective-permute-start | bytes 98312 | tf_op jit(solution)/shard_map/cond/branch_1_fun/cond/branch_1_fun/ppermute | solution.py:332
  104.8 32.1 %copy-start.6 = (bf16[512,512]{1,0:T(8,128)(2,1)S(1)}, bf16[512,512]{1,0:T(8,128)(2,1)}, u32[]{:S(2)}) copy-start(bf16[512,512]{1,0:T(8,128)(2,1)} %copy-done.5) | copy-start | bytes 1572868 | tf_op jit(solution)/shard_map/cond
  104.8 32.1 %all-to-all-start.2 = ((bf16[16,32,896]{2,1,0:T(8,128)(2,1)}), bf16[16,32,896]{2,1,0:T(8,128)(2,1)}, u32[]{:S(2)}, u32[]{:S(2)}) async-start(bf16[16,32,896]{2,1,0:T(8,128)(2,1)} %branch_1_fun.13), calls=%async_computation.2 | async-start | bytes 1835008 | tf_op jit(solution)/shard_map/cond/branch_1_fun/all_to_all | solution.py:404
  112.7 9.5 %collective-permute-start.7 = (bf16[4,32,512]{2,1,0:T(8,128)(2,1)S(1)}, bf16[4,32,512]{2,1,0:T(8,128)(2,1)S(1)}, u32[]{:S(2)}, u32[]{:S(2)}) collective-permute-start(bf16[4,32,512]{2,1,0:T(8,128)(2,1)S(1)} %get-tuple-element.44.after_ref), channel_id=1, source_target_pairs={{0,18},{2,16},{4,22},{6,20},{8,26},{10,24},{12,30},{14,28},{16,2},... | collective-permute-start | bytes 393224 | tf_op jit(solution)/shard_map/cond/branch_1_fun/ppermute | solution.py:332
  116.0 6.9 %collective-permute-start.6 = (bf16[4,32,512]{2,1,0:T(8,128)(2,1)S(1)}, bf16[4,32,512]{2,1,0:T(8,128)(2,1)S(1)}, u32[]{:S(2)}, u32[]{:S(2)}) collective-permute-start(bf16[4,32,512]{2,1,0:T(8,128)(2,1)S(1)} %get-tuple-element.44.after_ref), channel_id=1, source_target_pairs={{0,2},{2,0},{4,6},{6,4},{8,10},{10,8},{12,14},{14,12},{16,18},{18,... | collective-permute-start | bytes 393224 | tf_op jit(solution)/shard_map/cond/branch_1_fun/ppermute | solution.py:332
  119.0 8.2 %collective-permute-start.5 = (bf16[4,32,512]{2,1,0:T(8,128)(2,1)S(1)}, bf16[4,32,512]{2,1,0:T(8,128)(2,1)S(1)}, u32[]{:S(2)}, u32[]{:S(2)}) collective-permute-start(bf16[4,32,512]{2,1,0:T(8,128)(2,1)S(1)} %get-tuple-element.44.after_ref), channel_id=1, source_target_pairs={{0,16},{2,18},{4,20},{6,22},{8,24},{10,26},{12,28},{14,30},{16,0},... | collective-permute-start | bytes 393224 | tf_op jit(solution)/shard_map/cond/branch_1_fun/ppermute | solution.py:332
  142.8 20.1 %all-to-all-start.4 = ((bf16[16,32,512]{2,1,0:T(8,128)(2,1)}), bf16[16,32,512]{2,1,0:T(8,128)(2,1)S(1)}, u32[]{:S(2)}, u32[]{:S(2)}) async-start(bf16[16,32,512]{2,1,0:T(8,128)(2,1)} %get-tuple-element.67), calls=%async_computation.4 | async-start | bytes 1048576 | tf_op jit(solution)/shard_map/all_to_all | solution.py:412
  153.1 5.0 %collective-permute-start = (bf16[3,448,512]{2,1,0:T(8,128)(2,1)S(1)}, bf16[3,448,512]{2,1,0:T(8,128)(2,1)S(1)}, u32[]{:S(2)}, u32[]{:S(2)}) collective-permute-start(bf16[3,448,512]{2,1,0:T(8,128)(2,1)S(1)} %get-tuple-element.50), channel_id=1, source_target_pairs={{0,1},{1,0},{2,3},{3,2},{4,5},{5,4},{6,7},{7,6},{8,9},{9,8},{10,11... | collective-permute-start | bytes 4128776 | tf_op jit(solution)/shard_map/cond/branch_1_fun/ppermute | solution.py:59
Sparse Core Ops, SparseCore 0:
  24.4 49.0 all-gather.1

commit v12 on v10

--- a/solution.py
+++ b/solution.py
@@ -217,8 +217,7 @@
 def act_kernel(hid_ref, pre_ref, quant_ref, partial_ref, acts_ref):
     both = hid_ref.shape[2]
     grad_hidden = hid_ref[...].reshape((-1, both)).astype(jnp.float32)
-    pre = pre_ref[...].reshape((-1, 2 * both))
-    acts = swiglu_grads(grad_hidden, pre[:, :both], pre[:, both:])
+    acts = swiglu_grads(grad_hidden, pre_ref[:, :both], pre_ref[:, both:])
     partial = matmul(acts[0], quant_ref[0]) + matmul(acts[1], quant_ref[1])
     partial_ref[...] = partial.astype(jnp.bfloat16).reshape(partial_ref.shape)
     for n, act in enumerate(acts):
@@ -238,7 +237,7 @@
         ),
         in_specs=[
             pl.BlockSpec((blocks, rows, both), lambda i: (i, 0, 0)),
-            pl.BlockSpec((blocks, 1, rows, 2 * both), lambda i: (i % 2, i // 2, 0, 0)),
+            pl.BlockSpec((blocks * rows, 2 * both), lambda i: (i, 0)),
             pl.BlockSpec(quant.shape, lambda i: (0, 0, 0)),
         ],
         out_specs=(
@@ -247,14 +246,14 @@
         ),
         compiler_params=WIDE,
         cost_estimate=cost(4 * 512 * 896 * 512, 8 << 20),
-    )(grad_hidden, pre_half.reshape((N_ROW // 2, 2, rows, 2 * both)), quant)
+    )(grad_hidden, pre_half, quant)
 
 
 def latent_grads_kernel(place_ref, acts_ref, out_ref, tokens_ref, own_ref, sent_ref, rows_ref):
     rows = tokens_ref.shape[1]
     for block in range(2 * N_Y):
-        flip = (block >> 2) & 1
-        offset = 2 * (block & 3) + (block >> 3)
+        flip, bits = block & 1, block >> 1
+        offset = 2 * (bits & 3) + bits // 4
         chip = (place_ref[0] ^ flip) * N_Y + (place_ref[1] ^ offset)
         rows_ref[pl.ds(pl.multiple_of(chip * rows, rows), rows), :] = tokens_ref[block]
     inner = own_ref.shape[1]
@@ -329,14 +328,18 @@
 
 
 def exchanged(blocks, axis, *steps):
-    count = N_CHIP if axis == CHIP else N_Y
+    count = 2 if axis == "xl" else N_Y
     others = [lax.ppermute(blocks, axis, [(k, k ^ step) for k in range(count)]) for step in steps]
     return jnp.concatenate([blocks] + others, axis=0)
 
 
-def far_work(tokens, done, tile, gate_t, up_t):
+def near_work(tokens):
+    return (exchanged(tokens[None], "xl", 1),)
+
+
+def far_work(pair, done, tile, gate_t, up_t):
     other_latents = swapped(jnp.stack([gate_t, up_t]))
-    blocks = exchanged(copy_after(tokens, done)[None], "y", 2, 4, 6)
+    blocks = exchanged(copy_after(pair, done), "y", 2, 4, 6)
     return blocks, clipped_latents(tile, gate_t, up_t, other_latents)
 
 
@@ -348,11 +351,7 @@
     rows = jnp.concatenate(
         [own[:, :inner], other[:, :inner], own[:, inner:], other[:, inner:]], axis=1
     )
-    other = lax.ppermute(rows, "xh", [(0, 1), (1, 0)])
-    pair = jnp.where(
-        lax.axis_index("xh") == 0, jnp.stack([rows, other]), jnp.stack([other, rows])
-    )
-    return (pair.reshape((-1, 4 * inner)),)
+    return rows
 
 
 def in_branch(work, *operands):
@@ -370,31 +369,24 @@
     core = lax.axis_index("core")
     place = jnp.stack([lax.axis_index("xl"), lax.axis_index("y")]).astype(jnp.int32)
     gate_t, up_t = gate_latent.T, up_latent.T
+    pre_half = lax.all_gather(own_half(core, gate_pre, up_pre), ROW, axis=0, tiled=True)
     sent = first(grad_out, gate_t, up_t, down_latent)
 
-    def gathers(sent, core, gate_pre, up_pre, down):
+    def exchanges(sent, tokens, gate_t, up_t, down):
         received = lax.all_to_all(sent, CHIP, 0, 0)
         down_other = swapped(down)
-        (pre_rows,) = in_branch(own_half, core, gate_pre, up_pre)
-        return (received, down_other, pre_rows, sums_tile(received, pre_rows))
-
-    received, down_other, pre_rows, tile = in_branch(
-        gathers, sent, core, gate_pre, up_pre, down_latent
-    )
-    pre_half = lax.all_gather(pre_rows, "z", axis=0, tiled=True)
-
-    def exchanges(received, tile, tokens, gate_t, up_t, down, down_other):
-        tile = lax.all_to_all(tile, ROW + ("core",), 0, 0)
+        (pair,) = in_branch(near_work, tokens)
+        tile = lax.all_to_all(sums_tile(received, pair), ROW + ("core",), 0, 0)
         out_half, both = laid_out(received, down, down_other)
         partial = hidden_partial(tile, out_half, both)
         parts = lax.all_to_all(partial, ROW, 0, 0)
-        far, quant = in_branch(far_work, tokens, partial, tile, gate_t, up_t)
-        token_blocks = exchanged(far, CHIP, N_Y, 1, N_Y + 1)
+        far, quant = in_branch(far_work, pair, partial, tile, gate_t, up_t)
+        token_blocks = exchanged(far, "y", 1)
         grad_hidden = lax.all_to_all(spread(parts, far), ROW, 0, 0)
         return (out_half, quant, grad_hidden, token_blocks)
 
     out_half, quant, grad_hidden, token_blocks = in_branch(
-        exchanges, received, tile, tokens, gate_t, up_t, down_latent, down_other
+        exchanges, sent, tokens, gate_t, up_t, down_latent
     )
 
     partial, acts = act_partial(grad_hidden, pre_half, quant)

time: 166 us -> 170 us (1.024)
  waiting for transfers between devices: 53.6 us -> 64.1 us
  starting transfers between devices: 70.7 us -> 63.5 us
    all_to_all x2, waiting for transfers between devices: 10.6 us -> 19.1 us  [the longest x1 11.1 us: exchanges(): tile = lax.all_to_all(sums_tile(received, pair), ROW + ('core',), 0, 0)]
    ppermute x1 -> x0, waiting for transfers between devices: 7.75 us -> none  [own_half(): other = lax.ppermute(rows, 'xh', [(0, 1), (1, 0)])]
    all_to_all x1, waiting for transfers between devices: 8.66 us -> 16.2 us  [exchanges(): grad_hidden = lax.all_to_all(spread(parts, far), ROW, 0, 0)]
    ppermute x6 -> x5, waiting for transfers between devices: 8.97 us -> 15.5 us  [exchanged(): lax.ppermute(blocks, axis, [(k, k ^ step) for k in range(count)])]
    all_to_all x1, waiting for transfers between devices: 10.3 us -> 3.89 us  [exchanges(): parts = lax.all_to_all(partial, ROW, 0, 0)]
    ppermute x6 -> x5, starting transfers between devices: 21.4 us -> 18.5 us  [exchanged(): lax.ppermute(blocks, axis, [(k, k ^ step) for k in range(count)])]
    ppermute x1 -> x0, starting transfers between devices: 2.67 us -> none  [own_half(): other = lax.ppermute(rows, 'xh', [(0, 1), (1, 0)])]
  transfers between devices with their start and end apart: 17 -> 15, of which waited for: 12 -> 11; matrix products, arithmetic and copies ran while one was open for 2% -> 2% of each run, Pallas kernels for 8% -> 10%
where the time goes in v12:
time: 170 us; the launch traced here: 169 us
  waiting for transfers between devices  64.1 us (38%)
  starting transfers between devices  63.5 us (37%)
  Pallas kernels  22.6 us (13%)
  between operations  14.1 us (8%)
  other arithmetic  3.89 us (2%)
    ppermute x5, starting transfers between devices, exchanged(): lax.ppermute(blocks, axis, [(k, k ^ step) for k in range(count)])  18.5 us
    all_to_all x1, waiting for transfers between devices, exchanges(): grad_hidden = lax.all_to_all(spread(parts, far), ROW, 0, 0)  16.2 us
    ppermute x5, waiting for transfers between devices, exchanged(): lax.ppermute(blocks, axis, [(k, k ^ step) for k in range(count)])  15.5 us
    all_to_all x1, starting transfers between devices, exchanges(): tile = lax.all_to_all(sums_tile(received, pair), ROW + ('core',), 0, 0)  11.2 us
    all_to_all x1, waiting for transfers between devices, exchanges(): tile = lax.all_to_all(sums_tile(received, pair), ROW + ('core',), 0, 0)  11.1 us
    all_to_all x1, starting transfers between devices, exchanges(): received = lax.all_to_all(sent, CHIP, 0, 0)  9.23 us
    all_to_all x1, waiting for transfers between devices, exchanges(): received = lax.all_to_all(sent, CHIP, 0, 0)  8 us
    ppermute x4, starting transfers between devices, swapped(): return lax.ppermute(values, 'core', [(0, 1), (1, 0)])  7.66 us
  transfers between devices with their start and end apart: 15, of which 11 were waited for; matrix products, arithmetic and copies ran while one was open for 2% of the time, Pallas kernels for 10%

profile of v12, /device:TPU:10, one launch (start us, length us, event | category | flops | bytes accessed | tf_op | source)
XLA Modules:
  0.0 169.3 jit_solution(4557698500271625710)
XLA Ops:
  7.2 0.0 copy-start
  7.2 0.0 copy-start.1
  7.2 0.0 copy-start.2
  7.2 0.0 copy-start.3
  7.2 0.0 all-gather.2.cloned.1.call-start
  7.3 1.1 pad_maximum_fusion.4
  8.3 1.9 %collective-permute-start.8 = (bf16[32,896]{1,0:T(8,128)(2,1)S(1)}, bf16[32,896]{1,0:T(8,128)(2,1)S(1)}, u32[]{:S(2)}, u32[]{:S(2)}) collective-permute-start(bf16[32,896]{1,0:T(8,128)(2,1)S(1)} %get-tuple-element.78), channel_id=1, source_target_pairs={{0,1},{1,0},{2,3},{3,2},{4,5},{5,4},{6,7},{7,6},{8,9},{9,8},{10,11... | collective-permute-start | bytes 172040 | tf_op jit(solution)/shard_map/ppermute | solution.py:59
  10.3 0.1 fusion.1
  10.4 1.1 collective-permute-done.8
  11.5 0.1 fusion
  11.6 0.8 concatenate.16
  12.3 0.0 all-gather.2.cloned.1.call-update
  12.3 2.5 %shard_map.106 = bf16[16,144,128]{2,1,0:T(8,128)(2,1)} custom-call(bf16[32,512]{1,0:T(8,128)(2,1)} %out_ref.1, bf16[448,512]{1,0:T(8,128)(2,1)} %bitcast.14, bf16[448,512]{1,0:T(8,128)(2,1)} %bitcast.17, bf16[448,512]{1,0:T(8,128)(2,1)} %down_ref.1), custom_call_target="tpu_custom_call" | custom-call | flops 1048576 | bytes 2621440 | tf_op jit(solution)/shard_map/pallas_call | solution.py:90
  14.9 0.0 copy-done
  14.9 0.0 copy-done.1
  14.9 0.0 copy-done.2
  14.9 0.0 copy-done.3
  14.9 118.4 %conditional.4 = (bf16[512,512]{1,0:T(8,128)(2,1)}, bf16[2,896,512]{2,1,0:T(8,128)(2,1)}, bf16[16,32,896]{2,1,0:T(8,128)(2,1)}, bf16[16,32,512]{2,1,0:T(8,128)(2,1)}) conditional(s32[]{:T(128)} %convert_element_type.8, () %tuple.37, (bf16[16,144,128]{2,1,0:T(8,128)(2,1)}, bf16[448,512]{1,0:T(8,128)(2,1)S(1)}, bf16[32,512]{1,0:T(8,128)(2,1)S(1)}, ...), branch_computations={%region_0.1_spmd, %region_1.6_spmd} | conditional | flops 472548352 | bytes 32637478 | solution.py:365
  14.9 9.2 %all-to-all-start = ((bf16[16,144,128]{2,1,0:T(8,128)(2,1)}), bf16[16,144,128]{2,1,0:T(8,128)(2,1)S(1)}, u32[]{:S(2)}, u32[]{:S(2)}) async-start(bf16[16,144,128]{2,1,0:T(8,128)(2,1)} %get-tuple-element.37), calls=%async_computation | async-start | bytes 1179648 | tf_op jit(solution)/shard_map/cond/branch_1_fun/all_to_all | solution.py:376
  24.1 1.9 %collective-permute-start.6 = (bf16[448,512]{1,0:T(8,128)(2,1)S(1)}, bf16[448,512]{1,0:T(8,128)(2,1)S(1)}, u32[]{:S(2)}, u32[]{:S(2)}) collective-permute-start(bf16[448,512]{1,0:T(8,128)(2,1)S(1)} %get-tuple-element.38.down_ref), channel_id=1, source_target_pairs={{0,1},{1,0},{2,3},{3,2},{4,5},{5,4},{6,7},{7,6},{8,9},{9,8},{10,11... | collective-permute-start | bytes 1376264 | tf_op jit(solution)/shard_map/cond/branch_1_fun/ppermute | solution.py:59
  26.0 7.4 %conditional = (bf16[2,32,512]{2,1,0:T(8,128)(2,1)S(1)}) conditional(s32[]{:T(128)} %convert_element_type.1, () %tuple.27, bf16[32,512]{1,0:T(8,128)(2,1)S(1)} %get-tuple-element.77), branch_computations={%region_2.2_spmd, %region_3.3_spmd} | conditional | flops 32768 | bytes 262192 | solution.py:365
  26.1 2.4 %collective-permute-start.1 = (bf16[1,32,512]{2,1,0:T(8,128)(2,1)S(1)}, bf16[1,32,512]{2,1,0:T(8,128)(2,1)S(1)}, u32[]{:S(2)}, u32[]{:S(2)}) collective-permute-start(bf16[1,32,512]{2,1,0:T(8,128)(2,1)S(1)} %bitcast.23), channel_id=1, source_target_pairs={{0,16},{16,0},{1,17},{17,1},{2,18},{18,2},{3,19},{19,3},{4,20},{20... | collective-permute-start | bytes 98312 | tf_op jit(solution)/shard_map/cond/branch_1_fun/cond/branch_1_fun/ppermute | solution.py:332
  28.5 5.0 %collective-permute-done.1 = bf16[1,32,512]{2,1,0:T(8,128)(2,1)S(1)} collective-permute-done((bf16[1,32,512]{2,1,0:T(8,128)(2,1)S(1)}, bf16[1,32,512]{2,1,0:T(8,128)(2,1)S(1)}, u32[]{:S(2)}, u32[]{:S(2)}) %collective-permute-start.1) | collective-permute-done | bytes 32800 | tf_op jit(solution)/shard_map/cond/branch_1_fun/cond/branch_1_fun/ppermute | solution.py:332
  33.5 8.0 %all-to-all-done.received_ref.extra_ref = bf16[16,144,128]{2,1,0:T(8,128)(2,1)S(1)} async-done(((bf16[16,144,128]{2,1,0:T(8,128)(2,1)}), bf16[16,144,128]{2,1,0:T(8,128)(2,1)S(1)}, u32[]{:S(2)}, u32[]{:S(2)}) %all-to-all-start) | async-done | bytes 589856 | tf_op jit(solution)/shard_map/cond/branch_1_fun/all_to_all | solution.py:376
  41.5 0.7 branch_1_fun.11
  42.2 11.2 %all-to-all-start.1 = ((f32[32,8,128]{2,1,0:T(8,128)}), f32[32,8,128]{2,1,0:T(8,128)S(1)}, u32[]{:S(2)}, u32[]{:S(2)}) async-start(f32[32,8,128]{2,1,0:T(8,128)} %branch_1_fun.11), calls=%async_computation.1 | async-start | bytes 262144 | tf_op jit(solution)/shard_map/cond/branch_1_fun/all_to_all | solution.py:379
  53.3 0.0 collective-permute-done.6.other_ref
  53.3 1.0 branch_1_fun.10
  54.3 11.1 %all-to-all-done.1.tile_ref = f32[32,8,128]{2,1,0:T(8,128)S(1)} async-done(((f32[32,8,128]{2,1,0:T(8,128)}), f32[32,8,128]{2,1,0:T(8,128)S(1)}, u32[]{:S(2)}, u32[]{:S(2)}) %all-to-all-start.1) | async-done | bytes 131104 | tf_op jit(solution)/shard_map/cond/branch_1_fun/all_to_all | solution.py:379
  65.5 3.3 %branch_1_fun.12 = bf16[16,32,896]{2,1,0:T(8,128)(2,1)} custom-call(f32[32,8,128]{2,1,0:T(8,128)S(1)} %all-to-all-done.1.tile_ref, bf16[512,512]{1,0:T(8,128)(2,1)} %get-tuple-element.92.out_ref, bf16[2,448,512]{2,1,0:T(8,128)(2,1)S(1)} %get-tuple-element.41.both_ref), custom_call_target="tpu_custom_call" | custom-call | flops 469762048 | bytes 4194304 | tf_op jit(solution)/shard_map/cond/branch_1_fun/pallas_call | solution.py:170
  68.8 3.6 %all-to-all-start.2 = ((bf16[16,32,896]{2,1,0:T(8,128)(2,1)}), bf16[16,32,896]{2,1,0:T(8,128)(2,1)S(1)}, u32[]{:S(2)}, u32[]{:S(2)}) async-start(bf16[16,32,896]{2,1,0:T(8,128)(2,1)} %branch_1_fun.12), calls=%async_computation.2 | async-start | bytes 1835008 | tf_op jit(solution)/shard_map/cond/branch_1_fun/all_to_all | solution.py:382
  72.4 23.2 %conditional.1 = (bf16[8,32,512]{2,1,0:T(8,128)(2,1)S(1)}, bf16[2,896,512]{2,1,0:T(8,128)(2,1)}) conditional(s32[]{:T(128)} %convert_element_type.1, () %tuple.26, (bf16[2,32,512]{2,1,0:T(8,128)(2,1)S(1)}, bf16[16,32,896]{2,1,0:T(8,128)(2,1)}, bf16[448,512]{1,0:T(8,128)(2,1)S(1)}, bf16[448,512]{1,0:T(8,128)(2,1)S(1)}, ...), branch_computations={%region_4.4_spmd, %region_5.5_spmd} | conditional | flops 1900545 | bytes 11075760 | solution.py:365
  72.4 1.0 pad_maximum_fusion.1
  73.5 1.9 %collective-permute-start.5 = (bf16[2,448,512]{2,1,0:T(8,128)(2,1)}, bf16[2,448,512]{2,1,0:T(8,128)(2,1)S(1)}, u32[]{:S(2)}, u32[]{:S(2)}) collective-permute-start(bf16[2,448,512]{2,1,0:T(8,128)(2,1)} %pad_maximum_fusion.1), channel_id=1, source_target_pairs={{0,1},{1,0},{2,3},{3,2},{4,5},{5,4},{6,7},{7,6},{8,9},{9,8},{10,11... | collective-permute-start | bytes 2752520 | tf_op jit(solution)/shard_map/cond/branch_1_fun/cond/branch_1_fun/ppermute | solution.py:59
  75.4 0.6 branch_1_fun.8
  76.0 3.7 %collective-permute-start.4 = (bf16[2,32,512]{2,1,0:T(8,128)(2,1)}, bf16[2,32,512]{2,1,0:T(8,128)(2,1)S(1)}, u32[]{:S(2)}, u32[]{:S(2)}) collective-permute-start(bf16[2,32,512]{2,1,0:T(8,128)(2,1)} %branch_1_fun.8), channel_id=1, source_target_pairs={{0,12},{2,14},{4,8},{6,10},{8,4},{10,6},{12,0},{14,2},{1,13},{3,15... | collective-permute-start | bytes 196616 | tf_op jit(solution)/shard_map/cond/branch_1_fun/cond/branch_1_fun/ppermute | solution.py:332
  79.7 5.0 %collective-permute-start.3 = (bf16[2,32,512]{2,1,0:T(8,128)(2,1)}, bf16[2,32,512]{2,1,0:T(8,128)(2,1)S(1)}, u32[]{:S(2)}, u32[]{:S(2)}) collective-permute-start(bf16[2,32,512]{2,1,0:T(8,128)(2,1)} %branch_1_fun.8), channel_id=1, source_target_pairs={{0,8},{2,10},{4,12},{6,14},{8,0},{10,2},{12,4},{14,6},{1,9},{3,11}... | collective-permute-start | bytes 196616 | tf_op jit(solution)/shard_map/cond/branch_1_fun/cond/branch_1_fun/ppermute | solution.py:332
  84.7 3.5 %collective-permute-start.2 = (bf16[2,32,512]{2,1,0:T(8,128)(2,1)}, bf16[2,32,512]{2,1,0:T(8,128)(2,1)S(1)}, u32[]{:S(2)}, u32[]{:S(2)}) collective-permute-start(bf16[2,32,512]{2,1,0:T(8,128)(2,1)} %branch_1_fun.8), channel_id=1, source_target_pairs={{0,4},{2,6},{4,0},{6,2},{8,12},{10,14},{12,8},{14,10},{1,5},{3,7},... | collective-permute-start | bytes 196616 | tf_op jit(solution)/shard_map/cond/branch_1_fun/cond/branch_1_fun/ppermute | solution.py:332
  88.2 0.0 collective-permute-done.4
  88.2 3.3 %collective-permute-done.3 = bf16[2,32,512]{2,1,0:T(8,128)(2,1)S(1)} collective-permute-done((bf16[2,32,512]{2,1,0:T(8,128)(2,1)}, bf16[2,32,512]{2,1,0:T(8,128)(2,1)S(1)}, u32[]{:S(2)}, u32[]{:S(2)}) %collective-permute-start.3) | collective-permute-done | bytes 65568 | tf_op jit(solution)/shard_map/cond/branch_1_fun/cond/branch_1_fun/ppermute | solution.py:332
  91.5 1.3 collective-permute-done.2
  92.8 0.9 pad_maximum_fusion.2
  93.7 0.0 collective-permute-done.5.other_ref
  93.7 2.0 %branch_1_fun.9 = bf16[2,896,512]{2,1,0:T(8,128)(2,1)} custom-call(f32[32,8,128]{2,1,0:T(8,128)S(1)} %get-tuple-element.34.tile_ref, bf16[448,512]{1,0:T(8,128)(2,1)S(1)} %get-tuple-element.35.gate_ref, bf16[448,512]{1,0:T(8,128)(2,1)S(1)} %get-tuple-element.36.up_ref, bf16[2,448,512]{2,1,0:T(8,128)(2,1)S(1)} %collective-permute-done.5.other_ref), custom_call_target="tpu_custom_call" | custom-call | flops 1048576 | bytes 4194304 | tf_op jit(solution)/shard_map/cond/branch_1_fun/cond/branch_1_fun/pallas_call | solution.py:207
  95.7 3.9 %all-to-all-done.2.parts_ref = bf16[16,32,896]{2,1,0:T(8,128)(2,1)S(1)} async-done(((bf16[16,32,896]{2,1,0:T(8,128)(2,1)}), bf16[16,32,896]{2,1,0:T(8,128)(2,1)S(1)}, u32[]{:S(2)}, u32[]{:S(2)}) %all-to-all-start.2) | async-done | bytes 917536 | tf_op jit(solution)/shard_map/cond/branch_1_fun/all_to_all | solution.py:382
  99.6 1.1 branch_1_fun.13
  100.6 5.7 %all-to-all-start.3 = ((bf16[16,32,896]{2,1,0:T(8,128)(2,1)}), bf16[16,32,896]{2,1,0:T(8,128)(2,1)}, u32[]{:S(2)}, u32[]{:S(2)}) async-start(bf16[16,32,896]{2,1,0:T(8,128)(2,1)} %branch_1_fun.13), calls=%async_computation.3 | async-start | bytes 1835008 | tf_op jit(solution)/shard_map/cond/branch_1_fun/all_to_all | solution.py:385
  106.4 3.9 %collective-permute-start.7 = (bf16[8,32,512]{2,1,0:T(8,128)(2,1)S(1)}, bf16[8,32,512]{2,1,0:T(8,128)(2,1)S(1)}, u32[]{:S(2)}, u32[]{:S(2)}) collective-permute-start(bf16[8,32,512]{2,1,0:T(8,128)(2,1)S(1)} %get-tuple-element.45.after_ref), channel_id=1, source_target_pairs={{0,2},{2,0},{4,6},{6,4},{8,10},{10,8},{12,14},{14,12},{1,3},{3,1},... | collective-permute-start | bytes 786440 | tf_op jit(solution)/shard_map/cond/branch_1_fun/ppermute | solution.py:332
  110.3 6.0 %collective-permute-done.7 = bf16[8,32,512]{2,1,0:T(8,128)(2,1)S(1)} collective-permute-done((bf16[8,32,512]{2,1,0:T(8,128)(2,1)S(1)}, bf16[8,32,512]{2,1,0:T(8,128)(2,1)S(1)}, u32[]{:S(2)}, u32[]{:S(2)}) %collective-permute-start.7) | collective-permute-done | bytes 262176 | tf_op jit(solution)/shard_map/cond/branch_1_fun/ppermute | solution.py:332
  116.3 0.9 pad_maximum_fusion.3
  117.1 16.2 %all-to-all-done.3 = bf16[16,32,896]{2,1,0:T(8,128)(2,1)} async-done(((bf16[16,32,896]{2,1,0:T(8,128)(2,1)}), bf16[16,32,896]{2,1,0:T(8,128)(2,1)}, u32[]{:S(2)}, u32[]{:S(2)}) %all-to-all-start.3) | async-done | bytes 917536 | tf_op jit(solution)/shard_map/cond/branch_1_fun/all_to_all | solution.py:385
  133.3 0.0 all-gather.2.cloned.1.call-done.pre_ref
  133.3 5.8 %shard_map.107 = (bf16[16,32,512]{2,1,0:T(8,128)(2,1)}, bf16[3,512,896]{2,1,0:T(8,128)(2,1)}) custom-call(bf16[16,32,896]{2,1,0:T(8,128)(2,1)} %get-tuple-element.66.hid_ref, bf16[512,1792]{1,0:T(8,128)(2,1)} %all-gather.2.cloned.1.call-done.pre_ref, bf16[2,896,512]{2,1,0:T(8,128)(2,1)} %get-tuple-element.67.quant_ref), custom_call_target="tpu_custom_call" | custom-call | flops 939524096 | bytes 8388608 | tf_op jit(solution)/shard_map/pallas_call | solution.py:231
  139.2 7.5 %all-to-all-start.4 = ((bf16[16,32,512]{2,1,0:T(8,128)(2,1)}), bf16[16,32,512]{2,1,0:T(8,128)(2,1)S(1)}, u32[]{:S(2)}, u32[]{:S(2)}) async-start(bf16[16,32,512]{2,1,0:T(8,128)(2,1)} %get-tuple-element.68), calls=%async_computation.4 | async-start | bytes 1048576 | tf_op jit(solution)/shard_map/all_to_all | solution.py:393
  146.7 0.1 pad_add_fusion
  146.8 10.0 %conditional.5 = ((bf16[448,512]{1,0:T(8,128)(2,1)}, bf16[448,512]{1,0:T(8,128)(2,1)}, bf16[448,512]{1,0:T(8,128)(2,1)}, f32[8,128]{1,0:T(8,128)S(1)})) conditional(s32[]{:T(128)} %convert_element_type.8, () %tuple.39, (s32[2]{0:T(128)S(1)}, bf16[3,512,896]{2,1,0:T(8,128)(2,1)}, bf16[512,512]{1,0:T(8,128)(2,1)}, bf16[16,32,512]{2,1,0:T(8,128)(2,1)}) %tuple.40), branch_computations={%region_6.7_spmd, %region_7.8_spmd} | conditional | flops 1410334720 | bytes 19136560 | solution.py:365
  146.8 3.7 %branch_1_fun.14 = (f32[3,448,512]{2,1,0:T(8,128)S(1)}, bf16[3,448,512]{2,1,0:T(8,128)(2,1)S(1)}) custom-call(s32[2]{0:T(128)S(1)} %get-tuple-element.46.place_ref, bf16[3,512,896]{2,1,0:T(8,128)(2,1)} %get-tuple-element.47.acts_ref, bf16[512,512]{1,0:T(8,128)(2,1)} %get-tuple-element.48.out_ref, bf16[16,32,512]{2,1,0:T(8,128)(2,1)} %get-tuple-element.49.tokens_ref), custom_call_target="tpu_custom_call" | custom-call | flops 1409286144 | bytes 8388608 | tf_op jit(solution)/shard_map/cond/branch_1_fun/pallas_call | solution.py:269
  150.5 1.9 %collective-permute-start = (bf16[3,448,512]{2,1,0:T(8,128)(2,1)S(1)}, bf16[3,448,512]{2,1,0:T(8,128)(2,1)S(1)}, u32[]{:S(2)}, u32[]{:S(2)}) collective-permute-start(bf16[3,448,512]{2,1,0:T(8,128)(2,1)S(1)} %get-tuple-element.51), channel_id=1, source_target_pairs={{0,1},{1,0},{2,3},{3,2},{4,5},{5,4},{6,7},{7,6},{8,9},{9,8},{10,11... | collective-permute-start | bytes 4128776 | tf_op jit(solution)/shard_map/cond/branch_1_fun/ppermute | solution.py:59
  152.4 3.1 %collective-permute-done.other_ref = bf16[3,448,512]{2,1,0:T(8,128)(2,1)S(1)} collective-permute-done((bf16[3,448,512]{2,1,0:T(8,128)(2,1)S(1)}, bf16[3,448,512]{2,1,0:T(8,128)(2,1)S(1)}, u32[]{:S(2)}, u32[]{:S(2)}) %collective-permute-start) | collective-permute-done | bytes 1376288 | tf_op jit(solution)/shard_map/cond/branch_1_fun/ppermute | solution.py:59
  155.5 1.2 branch_1_fun.15
  156.7 5.1 %all-to-all-done.4.parts_ref = bf16[16,32,512]{2,1,0:T(8,128)(2,1)S(1)} async-done(((bf16[16,32,512]{2,1,0:T(8,128)(2,1)}), bf16[16,32,512]{2,1,0:T(8,128)(2,1)S(1)}, u32[]{:S(2)}, u32[]{:S(2)}) %all-to-all-start.4) | async-done | bytes 524320 | tf_op jit(solution)/shard_map/all_to_all | solution.py:393
  161.8 0.7 shard_map.108
  (2 shorter events, 0.0 us)
Async XLA Ops:
  7.2 7.7 %copy-start = (bf16[512,448]{0,1:T(8,128)(2,1)S(1)}, bf16[512,448]{0,1:T(8,128)(2,1)}, u32[]{:S(2)}) copy-start(bf16[512,448]{0,1:T(8,128)(2,1)} %param.19) | copy-start | bytes 1376260
  7.2 7.7 %copy-start.1 = (bf16[512,448]{0,1:T(8,128)(2,1)S(1)}, bf16[512,448]{0,1:T(8,128)(2,1)}, u32[]{:S(2)}) copy-start(bf16[512,448]{0,1:T(8,128)(2,1)} %param.20) | copy-start | bytes 1376260
  7.2 7.7 %copy-start.2 = (bf16[448,512]{1,0:T(8,128)(2,1)S(1)}, bf16[448,512]{1,0:T(8,128)(2,1)}, u32[]{:S(2)}) copy-start(bf16[448,512]{1,0:T(8,128)(2,1)} %down_ref.1) | copy-start | bytes 1376260
  7.2 7.7 %copy-start.3 = (bf16[32,512]{1,0:T(8,128)(2,1)S(1)}, bf16[32,512]{1,0:T(8,128)(2,1)}, u32[]{:S(2)}) copy-start(bf16[32,512]{1,0:T(8,128)(2,1)} %param.15) | copy-start | bytes 98308
  7.2 126.1 %all-gather.2.cloned.1.call-start = ((), (), s32[]{:S(2)}) async-start(), calls=%async_computation.5 | async-start | bytes 1949696 | tf_op jit(solution)/shard_map/all_gather | solution.py:372
  8.3 3.1 %collective-permute-start.8 = (bf16[32,896]{1,0:T(8,128)(2,1)S(1)}, bf16[32,896]{1,0:T(8,128)(2,1)S(1)}, u32[]{:S(2)}, u32[]{:S(2)}) collective-permute-start(bf16[32,896]{1,0:T(8,128)(2,1)S(1)} %get-tuple-element.78), channel_id=1, source_target_pairs={{0,1},{1,0},{2,3},{3,2},{4,5},{5,4},{6,7},{7,6},{8,9},{9,8},{10,11... | collective-permute-start | bytes 172040 | tf_op jit(solution)/shard_map/ppermute | solution.py:59
  14.9 26.6 %all-to-all-start = ((bf16[16,144,128]{2,1,0:T(8,128)(2,1)}), bf16[16,144,128]{2,1,0:T(8,128)(2,1)S(1)}, u32[]{:S(2)}, u32[]{:S(2)}) async-start(bf16[16,144,128]{2,1,0:T(8,128)(2,1)} %get-tuple-element.37), calls=%async_computation | async-start | bytes 1179648 | tf_op jit(solution)/shard_map/cond/branch_1_fun/all_to_all | solution.py:376
  24.1 29.2 %collective-permute-start.6 = (bf16[448,512]{1,0:T(8,128)(2,1)S(1)}, bf16[448,512]{1,0:T(8,128)(2,1)S(1)}, u32[]{:S(2)}, u32[]{:S(2)}) collective-permute-start(bf16[448,512]{1,0:T(8,128)(2,1)S(1)} %get-tuple-element.38.down_ref), channel_id=1, source_target_pairs={{0,1},{1,0},{2,3},{3,2},{4,5},{5,4},{6,7},{7,6},{8,9},{9,8},{10,11... | collective-permute-start | bytes 1376264 | tf_op jit(solution)/shard_map/cond/branch_1_fun/ppermute | solution.py:59
  26.1 7.4 %collective-permute-start.1 = (bf16[1,32,512]{2,1,0:T(8,128)(2,1)S(1)}, bf16[1,32,512]{2,1,0:T(8,128)(2,1)S(1)}, u32[]{:S(2)}, u32[]{:S(2)}) collective-permute-start(bf16[1,32,512]{2,1,0:T(8,128)(2,1)S(1)} %bitcast.23), channel_id=1, source_target_pairs={{0,16},{16,0},{1,17},{17,1},{2,18},{18,2},{3,19},{19,3},{4,20},{20... | collective-permute-start | bytes 98312 | tf_op jit(solution)/shard_map/cond/branch_1_fun/cond/branch_1_fun/ppermute | solution.py:332
  42.2 23.3 %all-to-all-start.1 = ((f32[32,8,128]{2,1,0:T(8,128)}), f32[32,8,128]{2,1,0:T(8,128)S(1)}, u32[]{:S(2)}, u32[]{:S(2)}) async-start(f32[32,8,128]{2,1,0:T(8,128)} %branch_1_fun.11), calls=%async_computation.1 | async-start | bytes 262144 | tf_op jit(solution)/shard_map/cond/branch_1_fun/all_to_all | solution.py:379
  68.8 30.8 %all-to-all-start.2 = ((bf16[16,32,896]{2,1,0:T(8,128)(2,1)}), bf16[16,32,896]{2,1,0:T(8,128)(2,1)S(1)}, u32[]{:S(2)}, u32[]{:S(2)}) async-start(bf16[16,32,896]{2,1,0:T(8,128)(2,1)} %branch_1_fun.12), calls=%async_computation.2 | async-start | bytes 1835008 | tf_op jit(solution)/shard_map/cond/branch_1_fun/all_to_all | solution.py:382
  73.5 20.2 %collective-permute-start.5 = (bf16[2,448,512]{2,1,0:T(8,128)(2,1)}, bf16[2,448,512]{2,1,0:T(8,128)(2,1)S(1)}, u32[]{:S(2)}, u32[]{:S(2)}) collective-permute-start(bf16[2,448,512]{2,1,0:T(8,128)(2,1)} %pad_maximum_fusion.1), channel_id=1, source_target_pairs={{0,1},{1,0},{2,3},{3,2},{4,5},{5,4},{6,7},{7,6},{8,9},{9,8},{10,11... | collective-permute-start | bytes 2752520 | tf_op jit(solution)/shard_map/cond/branch_1_fun/cond/branch_1_fun/ppermute | solution.py:59
  76.0 12.2 %collective-permute-start.4 = (bf16[2,32,512]{2,1,0:T(8,128)(2,1)}, bf16[2,32,512]{2,1,0:T(8,128)(2,1)S(1)}, u32[]{:S(2)}, u32[]{:S(2)}) collective-permute-start(bf16[2,32,512]{2,1,0:T(8,128)(2,1)} %branch_1_fun.8), channel_id=1, source_target_pairs={{0,12},{2,14},{4,8},{6,10},{8,4},{10,6},{12,0},{14,2},{1,13},{3,15... | collective-permute-start | bytes 196616 | tf_op jit(solution)/shard_map/cond/branch_1_fun/cond/branch_1_fun/ppermute | solution.py:332
  79.7 11.8 %collective-permute-start.3 = (bf16[2,32,512]{2,1,0:T(8,128)(2,1)}, bf16[2,32,512]{2,1,0:T(8,128)(2,1)S(1)}, u32[]{:S(2)}, u32[]{:S(2)}) collective-permute-start(bf16[2,32,512]{2,1,0:T(8,128)(2,1)} %branch_1_fun.8), channel_id=1, source_target_pairs={{0,8},{2,10},{4,12},{6,14},{8,0},{10,2},{12,4},{14,6},{1,9},{3,11}... | collective-permute-start | bytes 196616 | tf_op jit(solution)/shard_map/cond/branch_1_fun/cond/branch_1_fun/ppermute | solution.py:332
  84.7 8.1 %collective-permute-start.2 = (bf16[2,32,512]{2,1,0:T(8,128)(2,1)}, bf16[2,32,512]{2,1,0:T(8,128)(2,1)S(1)}, u32[]{:S(2)}, u32[]{:S(2)}) collective-permute-start(bf16[2,32,512]{2,1,0:T(8,128)(2,1)} %branch_1_fun.8), channel_id=1, source_target_pairs={{0,4},{2,6},{4,0},{6,2},{8,12},{10,14},{12,8},{14,10},{1,5},{3,7},... | collective-permute-start | bytes 196616 | tf_op jit(solution)/shard_map/cond/branch_1_fun/cond/branch_1_fun/ppermute | solution.py:332
  100.6 32.7 %all-to-all-start.3 = ((bf16[16,32,896]{2,1,0:T(8,128)(2,1)}), bf16[16,32,896]{2,1,0:T(8,128)(2,1)}, u32[]{:S(2)}, u32[]{:S(2)}) async-start(bf16[16,32,896]{2,1,0:T(8,128)(2,1)} %branch_1_fun.13), calls=%async_computation.3 | async-start | bytes 1835008 | tf_op jit(solution)/shard_map/cond/branch_1_fun/all_to_all | solution.py:385
  106.4 9.9 %collective-permute-start.7 = (bf16[8,32,512]{2,1,0:T(8,128)(2,1)S(1)}, bf16[8,32,512]{2,1,0:T(8,128)(2,1)S(1)}, u32[]{:S(2)}, u32[]{:S(2)}) collective-permute-start(bf16[8,32,512]{2,1,0:T(8,128)(2,1)S(1)} %get-tuple-element.45.after_ref), channel_id=1, source_target_pairs={{0,2},{2,0},{4,6},{6,4},{8,10},{10,8},{12,14},{14,12},{1,3},{3,1},... | collective-permute-start | bytes 786440 | tf_op jit(solution)/shard_map/cond/branch_1_fun/ppermute | solution.py:332
  139.2 22.6 %all-to-all-start.4 = ((bf16[16,32,512]{2,1,0:T(8,128)(2,1)}), bf16[16,32,512]{2,1,0:T(8,128)(2,1)S(1)}, u32[]{:S(2)}, u32[]{:S(2)}) async-start(bf16[16,32,512]{2,1,0:T(8,128)(2,1)} %get-tuple-element.68), calls=%async_computation.4 | async-start | bytes 1048576 | tf_op jit(solution)/shard_map/all_to_all | solution.py:393
  150.5 5.0 %collective-permute-start = (bf16[3,448,512]{2,1,0:T(8,128)(2,1)S(1)}, bf16[3,448,512]{2,1,0:T(8,128)(2,1)S(1)}, u32[]{:S(2)}, u32[]{:S(2)}) collective-permute-start(bf16[3,448,512]{2,1,0:T(8,128)(2,1)S(1)} %get-tuple-element.51), channel_id=1, source_target_pairs={{0,1},{1,0},{2,3},{3,2},{4,5},{5,4},{6,7},{7,6},{8,9},{9,8},{10,11... | collective-permute-start | bytes 4128776 | tf_op jit(solution)/shard_map/cond/branch_1_fun/ppermute | solution.py:59
Sparse Core Ops, SparseCore 0:
  12.5 109.6 all-gather.1

commit v13 on v12

--- a/solution.py
+++ b/solution.py
@@ -74,27 +74,76 @@
     return [jnp.sum(pieces[3 * k : 3 * k + 3], axis=0, keepdims=True) for k in range(3)]
 
 
-def first_kernel(out_ref, gate_ref, up_ref, down_ref, sent_ref):
+def half_of(ref, core):
+    rows = ref.shape[0] // 2
+    return ref[pl.ds(pl.multiple_of(core * rows, rows), rows), :]
+
+
+def first_kernel(core_ref, gate_pre_ref, up_pre_ref, gate_ref, up_ref, down_ref, sent_ref, sums_ref):
+    rows, inner = gate_pre_ref.shape[0] // 2, gate_pre_ref.shape[1]
+    lanes = sent_ref.shape[1] // 2
     sums = []
     for ref in (gate_ref, up_ref, down_ref):
         total = jnp.sum(jnp.abs(ref[...].astype(jnp.float32)), axis=0, keepdims=True)
-        sums.append(jnp.broadcast_to(jnp.sum(total, axis=1, keepdims=True), (1, LANES)))
+        sums.append(jnp.broadcast_to(jnp.sum(total, axis=1, keepdims=True), (1, 2 * lanes)))
+    sent_ref[...] = jnp.zeros(sent_ref.shape, sent_ref.dtype)
+    sent_ref[0:rows, 0:inner] = half_of(gate_pre_ref, 1 - core_ref[0])
+    sent_ref[0:rows, lanes : lanes + inner] = half_of(up_pre_ref, 1 - core_ref[0])
+    sent_ref[rows:, :] = pieces_of(sums)
+    tile = jnp.concatenate(sums + [jnp.zeros((5, 2 * lanes), jnp.float32)], axis=0)
+    sums_ref[...] = tile[:, :LANES]
+
+
+def first(core, gate_pre, up_pre, gate_t, up_t, down):
+    rows, inner = gate_pre.shape
+    lanes = -(-inner // LANES) * LANES
+    return pl.pallas_call(
+        first_kernel,
+        out_shape=(
+            jax.ShapeDtypeStruct((rows // 2 + EXTRA, 2 * lanes), jnp.bfloat16),
+            jax.ShapeDtypeStruct((8, LANES), jnp.float32),
+        ),
+        in_specs=[SMEM] + [VMEM] * 5,
+        out_specs=(VMEM, VMEM),
+        compiler_params=WIDE,
+        cost_estimate=cost(1 << 20, 3 << 19),
+    )(core, gate_pre, up_pre, gate_t, up_t, down)
+
+
+def second_kernel(core_ref, gate_pre_ref, up_pre_ref, other_ref, sums_ref, out_ref, pre_ref, sent_ref):
+    rows, inner = gate_pre_ref.shape[0] // 2, gate_pre_ref.shape[1]
+    lanes = other_ref.shape[1] // 2
+    pre_ref[...] = jnp.concatenate(
+        [
+            half_of(gate_pre_ref, core_ref[0]),
+            other_ref[0:rows, 0:inner],
+            half_of(up_pre_ref, core_ref[0]),
+            other_ref[0:rows, lanes : lanes + inner],
+        ],
+        axis=1,
+    )
+    others = totals_of(other_ref[rows:, :LANES].astype(jnp.float32))
+    extra = pieces_of([sums_ref[n : n + 1, :] + others[n] for n in range(3)])
     blocks = [out_ref[:, j * LANES : (j + 1) * LANES] for j in range(out_ref.shape[1] // LANES)]
-    block = jnp.concatenate(blocks + [pieces_of(sums)], axis=0)
+    block = jnp.concatenate(blocks + [extra], axis=0)
     for k in range(N_CHIP):
         sent_ref[k] = block
 
 
-def first(grad_out, gate_t, up_t, down):
+def second(core, gate_pre, up_pre, other, sums, grad_out):
     rows, width = grad_out.shape
-    return pl.pallas_call(
-        first_kernel,
-        out_shape=jax.ShapeDtypeStruct((N_CHIP, rows * width // LANES + EXTRA, LANES), jnp.bfloat16),
-        in_specs=[VMEM] * 4,
-        out_specs=VMEM,
+    inner = gate_pre.shape[1]
+    return pl.pallas_call(
+        second_kernel,
+        out_shape=(
+            jax.ShapeDtypeStruct((rows, 4 * inner), jnp.bfloat16),
+            jax.ShapeDtypeStruct((N_CHIP, rows * width // LANES + EXTRA, LANES), jnp.bfloat16),
+        ),
+        in_specs=[SMEM] + [VMEM] * 5,
+        out_specs=(VMEM, VMEM),
         compiler_params=WIDE,
-        cost_estimate=cost(1 << 20, 5 << 19),
-    )(grad_out, gate_t, up_t, down)
+        cost_estimate=cost(1 << 16, 1 << 20),
+    )(core, gate_pre, up_pre, other, sums, grad_out)
 
 
 def tile_kernel(extra_ref, after_ref, tile_ref):
@@ -108,12 +157,12 @@
     return pl.pallas_call(
         tile_kernel,
         grid=(1,),
-        out_shape=jax.ShapeDtypeStruct((2 * N_ROW, 8, LANES), jnp.float32),
+        out_shape=jax.ShapeDtypeStruct((N_ROW, 8, LANES), jnp.float32),
         in_specs=[
             pl.BlockSpec((N_CHIP, EXTRA, LANES), lambda i: (0, rows // EXTRA, 0)),
             ANY,
         ],
-        out_specs=pl.BlockSpec((2 * N_ROW, 8, LANES), lambda i: (0, 0, 0)),
+        out_specs=pl.BlockSpec((N_ROW, 8, LANES), lambda i: (0, 0, 0)),
         compiler_params=PARAMS,
         cost_estimate=cost(1 << 16, 1 << 18),
     )(received, after)
@@ -343,17 +392,6 @@
     return blocks, clipped_latents(tile, gate_t, up_t, other_latents)
 
 
-def own_half(core, gate_pre, up_pre):
-    inner = gate_pre.shape[1]
-    pre = jnp.concatenate([gate_pre, up_pre], axis=1).reshape((2, -1, 2 * inner))
-    own = lax.dynamic_index_in_dim(pre, core, 0, keepdims=False)
-    other = swapped(lax.dynamic_index_in_dim(pre, 1 - core, 0, keepdims=False))
-    rows = jnp.concatenate(
-        [own[:, :inner], other[:, :inner], own[:, inner:], other[:, inner:]], axis=1
-    )
-    return rows
-
-
 def in_branch(work, *operands):
     def nothing(*operands):
         shapes = jax.eval_shape(work, *operands)
@@ -366,17 +404,18 @@
 
 
 def shards(tokens, grad_out, gate_pre, up_pre, gate_latent, up_latent, down_latent):
-    core = lax.axis_index("core")
+    core = lax.axis_index("core").astype(jnp.int32).reshape((1,))
     place = jnp.stack([lax.axis_index("xl"), lax.axis_index("y")]).astype(jnp.int32)
     gate_t, up_t = gate_latent.T, up_latent.T
-    pre_half = lax.all_gather(own_half(core, gate_pre, up_pre), ROW, axis=0, tiled=True)
-    sent = first(grad_out, gate_t, up_t, down_latent)
+    sent, sums = first(core, gate_pre, up_pre, gate_t, up_t, down_latent)
+    pre_rows, sent = second(core, gate_pre, up_pre, swapped(sent), sums, grad_out)
+    pre_half = lax.all_gather(pre_rows, ROW, axis=0, tiled=True)
 
     def exchanges(sent, tokens, gate_t, up_t, down):
         received = lax.all_to_all(sent, CHIP, 0, 0)
         down_other = swapped(down)
         (pair,) = in_branch(near_work, tokens)
-        tile = lax.all_to_all(sums_tile(received, pair), ROW + ("core",), 0, 0)
+        tile = lax.all_to_all(sums_tile(received, pair), ROW, 0, 0)
         out_half, both = laid_out(received, down, down_other)
         partial = hidden_partial(tile, out_half, both)
         parts = lax.all_to_all(partial, ROW, 0, 0)

time: 170 us -> 167 us (0.982)
  the two profiles are of different devices: /device:TPU:10 before, /device:TPU:14 now
where the time goes in v13:
time: 167 us; the launch traced here: 166 us
  starting transfers between devices  71.1 us (43%)
  waiting for transfers between devices  54.1 us (32%)
  Pallas kernels  23 us (14%)
  between operations  14.1 us (8%)
  other arithmetic  2.8 us (2%)
    ppermute x5, starting transfers between devices, exchanged(): lax.ppermute(blocks, axis, [(k, k ^ step) for k in range(count)])  18.6 us
    all_to_all x1, waiting for transfers between devices, exchanges(): grad_hidden = lax.all_to_all(spread(parts, far), ROW, 0, 0)  15.1 us
    ppermute x5, waiting for transfers between devices, exchanged(): lax.ppermute(blocks, axis, [(k, k ^ step) for k in range(count)])  14.7 us
    all_to_all x1, starting transfers between devices, exchanges(): tile = lax.all_to_all(sums_tile(received, pair), ROW, 0, 0)  13.3 us
    all_to_all x1, starting transfers between devices, exchanges(): grad_hidden = lax.all_to_all(spread(parts, far), ROW, 0, 0)  9.66 us
    all_to_all x1, starting transfers between devices, exchanges(): received = lax.all_to_all(sent, CHIP, 0, 0)  8.48 us
    all_to_all x1, waiting for transfers between devices, exchanges(): received = lax.all_to_all(sent, CHIP, 0, 0)  8.22 us
    ppermute x4, starting transfers between devices, swapped(): return lax.ppermute(values, 'core', [(0, 1), (1, 0)])  7.65 us
  transfers between devices with their start and end apart: 15, of which 10 were waited for; matrix products, arithmetic and copies ran while one was open for 2% of the time, Pallas kernels for 8%

profile of v13, /device:TPU:14, one launch (start us, length us, event | category | flops | bytes accessed | tf_op | source)
XLA Modules:
  0.0 165.9 jit_solution(11915695006127471180)
XLA Ops:
  7.2 0.0 copy-start
  7.2 0.0 copy-start.1
  7.2 0.0 copy-start.2
  7.2 0.0 copy-start.4
  7.2 0.0 all-gather.2.cloned.1.call-start
  7.3 2.5 %shard_map.106 = (bf16[48,1024]{1,0:T(8,128)(2,1)}, f32[8,128]{1,0:T(8,128)}) custom-call(s32[1]{0:T(128)} %bitcast.3.core_ref, bf16[64,448]{1,0:T(8,128)(2,1)} %gate_pre_ref.3, bf16[64,448]{1,0:T(8,128)(2,1)} %up_pre_ref.3, bf16[448,512]{1,0:T(8,128)(2,1)} %bitcast.10, bf16[448,512]{1,0:T(8,128)(2,1)} %bitcast.13, bf16[448,512]{1,0:T(8,128)(2,1)} %down_ref.1), custom_call_target="tpu_custom_call" | custom-call | flops 1048576 | bytes 1572864 | tf_op jit(solution)/shard_map/pallas_call | solution.py:100
  9.7 1.9 %collective-permute-start.8 = (bf16[48,1024]{1,0:T(8,128)(2,1)}, bf16[48,1024]{1,0:T(8,128)(2,1)S(1)}, u32[]{:S(2)}, u32[]{:S(2)}) collective-permute-start(bf16[48,1024]{1,0:T(8,128)(2,1)} %get-tuple-element.70), channel_id=1, source_target_pairs={{0,1},{1,0},{2,3},{3,2},{4,5},{5,4},{6,7},{7,6},{8,9},{9,8},{10,11... | collective-permute-start | bytes 294920 | tf_op jit(solution)/shard_map/ppermute | solution.py:59
  11.6 1.5 collective-permute-done.8.other_ref
  13.1 0.0 copy-start.3
  13.1 0.6 copy-done.3
  13.8 1.9 %shard_map.107 = (bf16[32,1792]{1,0:T(8,128)(2,1)}, bf16[16,144,128]{2,1,0:T(8,128)(2,1)}) custom-call(s32[1]{0:T(128)} %bitcast.3.core_ref, bf16[64,448]{1,0:T(8,128)(2,1)} %gate_pre_ref.3, bf16[64,448]{1,0:T(8,128)(2,1)} %up_pre_ref.3, bf16[48,1024]{1,0:T(8,128)(2,1)} %copy-done.3, f32[8,128]{1,0:T(8,128)} %get-tuple-element.71.sums_ref, ...), custom_call_target="tpu_custom_call" | custom-call | flops 65536 | bytes 1048576 | tf_op jit(solution)/shard_map/pallas_call | solution.py:136
  15.7 0.0 all-gather.2.cloned.1.call-update
  15.7 0.0 copy-done
  15.7 0.0 copy-done.1
  15.7 0.0 copy-done.2
  15.7 0.0 copy-done.4
  15.7 115.9 %conditional.4 = (bf16[512,512]{1,0:T(8,128)(2,1)}, bf16[2,896,512]{2,1,0:T(8,128)(2,1)}, bf16[16,32,896]{2,1,0:T(8,128)(2,1)}, bf16[16,32,512]{2,1,0:T(8,128)(2,1)}) conditional(s32[]{:T(128)} %convert_element_type.8, () %tuple.37, (bf16[16,144,128]{2,1,0:T(8,128)(2,1)}, bf16[448,512]{1,0:T(8,128)(2,1)S(1)}, bf16[32,512]{1,0:T(8,128)(2,1)S(1)}, ...), branch_computations={%region_0.0_spmd, %region_1.0_spmd} | conditional | flops 472548352 | bytes 32440870 | solution.py:403
  15.7 8.5 %all-to-all-start = ((bf16[16,144,128]{2,1,0:T(8,128)(2,1)}), bf16[16,144,128]{2,1,0:T(8,128)(2,1)S(1)}, u32[]{:S(2)}, u32[]{:S(2)}) async-start(bf16[16,144,128]{2,1,0:T(8,128)(2,1)} %get-tuple-element.37), calls=%async_computation | async-start | bytes 1179648 | tf_op jit(solution)/shard_map/cond/branch_1_fun/all_to_all | solution.py:415
  24.2 1.9 %collective-permute-start.6 = (bf16[448,512]{1,0:T(8,128)(2,1)S(1)}, bf16[448,512]{1,0:T(8,128)(2,1)S(1)}, u32[]{:S(2)}, u32[]{:S(2)}) collective-permute-start(bf16[448,512]{1,0:T(8,128)(2,1)S(1)} %get-tuple-element.38.down_ref), channel_id=1, source_target_pairs={{0,1},{1,0},{2,3},{3,2},{4,5},{5,4},{6,7},{7,6},{8,9},{9,8},{10,11... | collective-permute-start | bytes 1376264 | tf_op jit(solution)/shard_map/cond/branch_1_fun/ppermute | solution.py:59
  26.1 6.8 %conditional = (bf16[2,32,512]{2,1,0:T(8,128)(2,1)S(1)}) conditional(s32[]{:T(128)} %convert_element_type.1, () %tuple.27, bf16[32,512]{1,0:T(8,128)(2,1)S(1)} %get-tuple-element.85), branch_computations={%region_2.0_spmd, %region_3.0_spmd} | conditional | flops 32768 | bytes 262192 | solution.py:403
  26.1 2.5 %collective-permute-start.1 = (bf16[1,32,512]{2,1,0:T(8,128)(2,1)S(1)}, bf16[1,32,512]{2,1,0:T(8,128)(2,1)S(1)}, u32[]{:S(2)}, u32[]{:S(2)}) collective-permute-start(bf16[1,32,512]{2,1,0:T(8,128)(2,1)S(1)} %bitcast.18), channel_id=1, source_target_pairs={{0,16},{16,0},{1,17},{17,1},{2,18},{18,2},{3,19},{19,3},{4,20},{20... | collective-permute-start | bytes 98312 | tf_op jit(solution)/shard_map/cond/branch_1_fun/cond/branch_1_fun/ppermute | solution.py:381
  28.6 4.3 %collective-permute-done.1 = bf16[1,32,512]{2,1,0:T(8,128)(2,1)S(1)} collective-permute-done((bf16[1,32,512]{2,1,0:T(8,128)(2,1)S(1)}, bf16[1,32,512]{2,1,0:T(8,128)(2,1)S(1)}, u32[]{:S(2)}, u32[]{:S(2)}) %collective-permute-start.1) | collective-permute-done | bytes 32800 | tf_op jit(solution)/shard_map/cond/branch_1_fun/cond/branch_1_fun/ppermute | solution.py:381
  33.0 8.2 %all-to-all-done.received_ref.extra_ref = bf16[16,144,128]{2,1,0:T(8,128)(2,1)S(1)} async-done(((bf16[16,144,128]{2,1,0:T(8,128)(2,1)}), bf16[16,144,128]{2,1,0:T(8,128)(2,1)S(1)}, u32[]{:S(2)}, u32[]{:S(2)}) %all-to-all-start) | async-done | bytes 589856 | tf_op jit(solution)/shard_map/cond/branch_1_fun/all_to_all | solution.py:415
  41.2 0.7 branch_1_fun.11
  41.8 13.3 %all-to-all-start.1 = ((f32[16,8,128]{2,1,0:T(8,128)}), f32[16,8,128]{2,1,0:T(8,128)S(1)}, u32[]{:S(2)}, u32[]{:S(2)}) async-start(f32[16,8,128]{2,1,0:T(8,128)} %branch_1_fun.11), calls=%async_computation.1 | async-start | bytes 131072 | tf_op jit(solution)/shard_map/cond/branch_1_fun/all_to_all | solution.py:418
  55.1 0.0 collective-permute-done.6.other_ref
  55.2 1.0 branch_1_fun.10
  56.1 6.4 %all-to-all-done.1.tile_ref = f32[16,8,128]{2,1,0:T(8,128)S(1)} async-done(((f32[16,8,128]{2,1,0:T(8,128)}), f32[16,8,128]{2,1,0:T(8,128)S(1)}, u32[]{:S(2)}, u32[]{:S(2)}) %all-to-all-start.1) | async-done | bytes 65568 | tf_op jit(solution)/shard_map/cond/branch_1_fun/all_to_all | solution.py:418
  62.5 3.3 %branch_1_fun.12 = bf16[16,32,896]{2,1,0:T(8,128)(2,1)} custom-call(f32[16,8,128]{2,1,0:T(8,128)S(1)} %all-to-all-done.1.tile_ref, bf16[512,512]{1,0:T(8,128)(2,1)} %get-tuple-element.94.out_ref, bf16[2,448,512]{2,1,0:T(8,128)(2,1)S(1)} %get-tuple-element.41.both_ref), custom_call_target="tpu_custom_call" | custom-call | flops 469762048 | bytes 4194304 | tf_op jit(solution)/shard_map/cond/branch_1_fun/pallas_call | solution.py:219
  65.8 6.3 %all-to-all-start.2 = ((bf16[16,32,896]{2,1,0:T(8,128)(2,1)}), bf16[16,32,896]{2,1,0:T(8,128)(2,1)S(1)}, u32[]{:S(2)}, u32[]{:S(2)}) async-start(bf16[16,32,896]{2,1,0:T(8,128)(2,1)} %branch_1_fun.12), calls=%async_computation.2 | async-start | bytes 1835008 | tf_op jit(solution)/shard_map/cond/branch_1_fun/all_to_all | solution.py:421
  72.1 23.3 %conditional.1 = (bf16[8,32,512]{2,1,0:T(8,128)(2,1)S(1)}, bf16[2,896,512]{2,1,0:T(8,128)(2,1)}) conditional(s32[]{:T(128)} %convert_element_type.1, () %tuple.26, (bf16[2,32,512]{2,1,0:T(8,128)(2,1)S(1)}, bf16[16,32,896]{2,1,0:T(8,128)(2,1)}, bf16[448,512]{1,0:T(8,128)(2,1)S(1)}, bf16[448,512]{1,0:T(8,128)(2,1)S(1)}, ...), branch_computations={%region_4.0_spmd, %region_5.0_spmd} | conditional | flops 1900545 | bytes 11075760 | solution.py:403
  72.1 1.0 pad_maximum_fusion.1
  73.1 1.9 %collective-permute-start.5 = (bf16[2,448,512]{2,1,0:T(8,128)(2,1)}, bf16[2,448,512]{2,1,0:T(8,128)(2,1)S(1)}, u32[]{:S(2)}, u32[]{:S(2)}) collective-permute-start(bf16[2,448,512]{2,1,0:T(8,128)(2,1)} %pad_maximum_fusion.1), channel_id=1, source_target_pairs={{0,1},{1,0},{2,3},{3,2},{4,5},{5,4},{6,7},{7,6},{8,9},{9,8},{10,11... | collective-permute-start | bytes 2752520 | tf_op jit(solution)/shard_map/cond/branch_1_fun/cond/branch_1_fun/ppermute | solution.py:59
  75.0 0.6 branch_1_fun.8
  75.6 3.8 %collective-permute-start.4 = (bf16[2,32,512]{2,1,0:T(8,128)(2,1)}, bf16[2,32,512]{2,1,0:T(8,128)(2,1)S(1)}, u32[]{:S(2)}, u32[]{:S(2)}) collective-permute-start(bf16[2,32,512]{2,1,0:T(8,128)(2,1)} %branch_1_fun.8), channel_id=1, source_target_pairs={{0,12},{2,14},{4,8},{6,10},{8,4},{10,6},{12,0},{14,2},{1,13},{3,15... | collective-permute-start | bytes 196616 | tf_op jit(solution)/shard_map/cond/branch_1_fun/cond/branch_1_fun/ppermute | solution.py:381
  79.5 4.9 %collective-permute-start.3 = (bf16[2,32,512]{2,1,0:T(8,128)(2,1)}, bf16[2,32,512]{2,1,0:T(8,128)(2,1)S(1)}, u32[]{:S(2)}, u32[]{:S(2)}) collective-permute-start(bf16[2,32,512]{2,1,0:T(8,128)(2,1)} %branch_1_fun.8), channel_id=1, source_target_pairs={{0,8},{2,10},{4,12},{6,14},{8,0},{10,2},{12,4},{14,6},{1,9},{3,11}... | collective-permute-start | bytes 196616 | tf_op jit(solution)/shard_map/cond/branch_1_fun/cond/branch_1_fun/ppermute | solution.py:381
  84.4 3.5 %collective-permute-start.2 = (bf16[2,32,512]{2,1,0:T(8,128)(2,1)}, bf16[2,32,512]{2,1,0:T(8,128)(2,1)S(1)}, u32[]{:S(2)}, u32[]{:S(2)}) collective-permute-start(bf16[2,32,512]{2,1,0:T(8,128)(2,1)} %branch_1_fun.8), channel_id=1, source_target_pairs={{0,4},{2,6},{4,0},{6,2},{8,12},{10,14},{12,8},{14,10},{1,5},{3,7},... | collective-permute-start | bytes 196616 | tf_op jit(solution)/shard_map/cond/branch_1_fun/cond/branch_1_fun/ppermute | solution.py:381
  87.9 0.0 collective-permute-done.4
  87.9 3.4 %collective-permute-done.3 = bf16[2,32,512]{2,1,0:T(8,128)(2,1)S(1)} collective-permute-done((bf16[2,32,512]{2,1,0:T(8,128)(2,1)}, bf16[2,32,512]{2,1,0:T(8,128)(2,1)S(1)}, u32[]{:S(2)}, u32[]{:S(2)}) %collective-permute-start.3) | collective-permute-done | bytes 65568 | tf_op jit(solution)/shard_map/cond/branch_1_fun/cond/branch_1_fun/ppermute | solution.py:381
  91.3 1.3 collective-permute-done.2
  92.6 0.9 pad_maximum_fusion.2
  93.5 0.0 collective-permute-done.5.other_ref
  93.5 1.9 %branch_1_fun.9 = bf16[2,896,512]{2,1,0:T(8,128)(2,1)} custom-call(f32[16,8,128]{2,1,0:T(8,128)S(1)} %get-tuple-element.34.tile_ref, bf16[448,512]{1,0:T(8,128)(2,1)S(1)} %get-tuple-element.35.gate_ref, bf16[448,512]{1,0:T(8,128)(2,1)S(1)} %get-tuple-element.36.up_ref, bf16[2,448,512]{2,1,0:T(8,128)(2,1)S(1)} %collective-permute-done.5.other_ref), custom_call_target="tpu_custom_call" | custom-call | flops 1048576 | bytes 4194304 | tf_op jit(solution)/shard_map/cond/branch_1_fun/cond/branch_1_fun/pallas_call | solution.py:256
  95.4 0.0 all-to-all-done.2.parts_ref
  95.4 1.1 branch_1_fun.13
  96.5 9.7 %all-to-all-start.3 = ((bf16[16,32,896]{2,1,0:T(8,128)(2,1)}), bf16[16,32,896]{2,1,0:T(8,128)(2,1)}, u32[]{:S(2)}, u32[]{:S(2)}) async-start(bf16[16,32,896]{2,1,0:T(8,128)(2,1)} %branch_1_fun.13), calls=%async_computation.3 | async-start | bytes 1835008 | tf_op jit(solution)/shard_map/cond/branch_1_fun/all_to_all | solution.py:424
  106.1 4.0 %collective-permute-start.7 = (bf16[8,32,512]{2,1,0:T(8,128)(2,1)S(1)}, bf16[8,32,512]{2,1,0:T(8,128)(2,1)S(1)}, u32[]{:S(2)}, u32[]{:S(2)}) collective-permute-start(bf16[8,32,512]{2,1,0:T(8,128)(2,1)S(1)} %get-tuple-element.45.after_ref), channel_id=1, source_target_pairs={{0,2},{2,0},{4,6},{6,4},{8,10},{10,8},{12,14},{14,12},{1,3},{3,1},... | collective-permute-start | bytes 786440 | tf_op jit(solution)/shard_map/cond/branch_1_fun/ppermute | solution.py:381
  110.1 5.6 %collective-permute-done.7 = bf16[8,32,512]{2,1,0:T(8,128)(2,1)S(1)} collective-permute-done((bf16[8,32,512]{2,1,0:T(8,128)(2,1)S(1)}, bf16[8,32,512]{2,1,0:T(8,128)(2,1)S(1)}, u32[]{:S(2)}, u32[]{:S(2)}) %collective-permute-start.7) | collective-permute-done | bytes 262176 | tf_op jit(solution)/shard_map/cond/branch_1_fun/ppermute | solution.py:381
  115.7 0.8 pad_maximum_fusion.3
  116.6 15.1 %all-to-all-done.3 = bf16[16,32,896]{2,1,0:T(8,128)(2,1)} async-done(((bf16[16,32,896]{2,1,0:T(8,128)(2,1)}), bf16[16,32,896]{2,1,0:T(8,128)(2,1)}, u32[]{:S(2)}, u32[]{:S(2)}) %all-to-all-start.3) | async-done | bytes 917536 | tf_op jit(solution)/shard_map/cond/branch_1_fun/all_to_all | solution.py:424
  131.6 0.0 all-gather.2.cloned.1.call-done.pre_ref
  131.6 5.3 %shard_map.108 = (bf16[16,32,512]{2,1,0:T(8,128)(2,1)}, bf16[3,512,896]{2,1,0:T(8,128)(2,1)S(1)}) custom-call(bf16[16,32,896]{2,1,0:T(8,128)(2,1)} %get-tuple-element.73.hid_ref, bf16[512,1792]{1,0:T(8,128)(2,1)} %all-gather.2.cloned.1.call-done.pre_ref, bf16[2,896,512]{2,1,0:T(8,128)(2,1)} %get-tuple-element.75.quant_ref), custom_call_target="tpu_custom_call" | custom-call | flops 939524096 | bytes 8388608 | tf_op jit(solution)/shard_map/pallas_call | solution.py:280
  137.0 7.1 %all-to-all-start.4 = ((bf16[16,32,512]{2,1,0:T(8,128)(2,1)}), bf16[16,32,512]{2,1,0:T(8,128)(2,1)S(1)}, u32[]{:S(2)}, u32[]{:S(2)}) async-start(bf16[16,32,512]{2,1,0:T(8,128)(2,1)} %get-tuple-element.76), calls=%async_computation.4 | async-start | bytes 1048576 | tf_op jit(solution)/shard_map/all_to_all | solution.py:432
  144.0 0.1 pad_add_fusion
  144.1 9.2 %conditional.5 = ((bf16[448,512]{1,0:T(8,128)(2,1)}, bf16[448,512]{1,0:T(8,128)(2,1)}, bf16[448,512]{1,0:T(8,128)(2,1)}, f32[8,128]{1,0:T(8,128)S(1)})) conditional(s32[]{:T(128)} %convert_element_type.8, () %tuple.39, (s32[2]{0:T(128)S(1)}, bf16[3,512,896]{2,1,0:T(8,128)(2,1)S(1)}, bf16[512,512]{1,0:T(8,128)(2,1)}, ...), branch_computations={%region_6.0_spmd, %region_7.0_spmd} | conditional | flops 1410334720 | bytes 19136560 | solution.py:403
  144.1 2.9 %branch_1_fun.14 = (f32[3,448,512]{2,1,0:T(8,128)S(1)}, bf16[3,448,512]{2,1,0:T(8,128)(2,1)S(1)}) custom-call(s32[2]{0:T(128)S(1)} %get-tuple-element.46.place_ref, bf16[3,512,896]{2,1,0:T(8,128)(2,1)S(1)} %get-tuple-element.47.acts_ref, bf16[512,512]{1,0:T(8,128)(2,1)} %get-tuple-element.48.out_ref, bf16[16,32,512]{2,1,0:T(8,128)(2,1)} %get-tuple-element.49.tokens_ref), custom_call_target="tpu_custom_call" | custom-call | flops 1409286144 | bytes 8388608 | tf_op jit(solution)/shard_map/cond/branch_1_fun/pallas_call | solution.py:318
  147.0 1.9 %collective-permute-start = (bf16[3,448,512]{2,1,0:T(8,128)(2,1)S(1)}, bf16[3,448,512]{2,1,0:T(8,128)(2,1)S(1)}, u32[]{:S(2)}, u32[]{:S(2)}) collective-permute-start(bf16[3,448,512]{2,1,0:T(8,128)(2,1)S(1)} %get-tuple-element.51), channel_id=1, source_target_pairs={{0,1},{1,0},{2,3},{3,2},{4,5},{5,4},{6,7},{7,6},{8,9},{9,8},{10,11... | collective-permute-start | bytes 4128776 | tf_op jit(solution)/shard_map/cond/branch_1_fun/ppermute | solution.py:59
  148.9 3.1 %collective-permute-done.other_ref = bf16[3,448,512]{2,1,0:T(8,128)(2,1)S(1)} collective-permute-done((bf16[3,448,512]{2,1,0:T(8,128)(2,1)S(1)}, bf16[3,448,512]{2,1,0:T(8,128)(2,1)S(1)}, u32[]{:S(2)}, u32[]{:S(2)}) %collective-permute-start) | collective-permute-done | bytes 1376288 | tf_op jit(solution)/shard_map/cond/branch_1_fun/ppermute | solution.py:59
  152.0 1.2 branch_1_fun.15
  153.2 5.1 %all-to-all-done.4.parts_ref = bf16[16,32,512]{2,1,0:T(8,128)(2,1)S(1)} async-done(((bf16[16,32,512]{2,1,0:T(8,128)(2,1)}), bf16[16,32,512]{2,1,0:T(8,128)(2,1)S(1)}, u32[]{:S(2)}, u32[]{:S(2)}) %all-to-all-start.4) | async-done | bytes 524320 | tf_op jit(solution)/shard_map/all_to_all | solution.py:432
  158.4 0.7 shard_map.109
  (1 shorter events, 0.0 us)
Async XLA Ops:
  7.2 8.5 %copy-start = (bf16[512,448]{0,1:T(8,128)(2,1)S(1)}, bf16[512,448]{0,1:T(8,128)(2,1)}, u32[]{:S(2)}) copy-start(bf16[512,448]{0,1:T(8,128)(2,1)} %param.19) | copy-start | bytes 1376260
  7.2 8.5 %copy-start.1 = (bf16[512,448]{0,1:T(8,128)(2,1)S(1)}, bf16[512,448]{0,1:T(8,128)(2,1)}, u32[]{:S(2)}) copy-start(bf16[512,448]{0,1:T(8,128)(2,1)} %param.20) | copy-start | bytes 1376260
  7.2 8.5 %copy-start.2 = (bf16[448,512]{1,0:T(8,128)(2,1)S(1)}, bf16[448,512]{1,0:T(8,128)(2,1)}, u32[]{:S(2)}) copy-start(bf16[448,512]{1,0:T(8,128)(2,1)} %down_ref.1) | copy-start | bytes 1376260
  7.2 8.5 %copy-start.4 = (bf16[32,512]{1,0:T(8,128)(2,1)S(1)}, bf16[32,512]{1,0:T(8,128)(2,1)}, u32[]{:S(2)}) copy-start(bf16[32,512]{1,0:T(8,128)(2,1)} %param.15) | copy-start | bytes 98308
  7.2 124.4 %all-gather.2.cloned.1.call-start = ((), (), s32[]{:S(2)}) async-start(), calls=%async_computation.5 | async-start | bytes 1949696 | tf_op jit(solution)/shard_map/all_gather | solution.py:412
  9.7 3.4 %collective-permute-start.8 = (bf16[48,1024]{1,0:T(8,128)(2,1)}, bf16[48,1024]{1,0:T(8,128)(2,1)S(1)}, u32[]{:S(2)}, u32[]{:S(2)}) collective-permute-start(bf16[48,1024]{1,0:T(8,128)(2,1)} %get-tuple-element.70), channel_id=1, source_target_pairs={{0,1},{1,0},{2,3},{3,2},{4,5},{5,4},{6,7},{7,6},{8,9},{9,8},{10,11... | collective-permute-start | bytes 294920 | tf_op jit(solution)/shard_map/ppermute | solution.py:59
  13.1 0.6 copy-start.3
  15.7 25.4 %all-to-all-start = ((bf16[16,144,128]{2,1,0:T(8,128)(2,1)}), bf16[16,144,128]{2,1,0:T(8,128)(2,1)S(1)}, u32[]{:S(2)}, u32[]{:S(2)}) async-start(bf16[16,144,128]{2,1,0:T(8,128)(2,1)} %get-tuple-element.37), calls=%async_computation | async-start | bytes 1179648 | tf_op jit(solution)/shard_map/cond/branch_1_fun/all_to_all | solution.py:415
  24.2 30.9 %collective-permute-start.6 = (bf16[448,512]{1,0:T(8,128)(2,1)S(1)}, bf16[448,512]{1,0:T(8,128)(2,1)S(1)}, u32[]{:S(2)}, u32[]{:S(2)}) collective-permute-start(bf16[448,512]{1,0:T(8,128)(2,1)S(1)} %get-tuple-element.38.down_ref), channel_id=1, source_target_pairs={{0,1},{1,0},{2,3},{3,2},{4,5},{5,4},{6,7},{7,6},{8,9},{9,8},{10,11... | collective-permute-start | bytes 1376264 | tf_op jit(solution)/shard_map/cond/branch_1_fun/ppermute | solution.py:59
  26.1 6.8 %collective-permute-start.1 = (bf16[1,32,512]{2,1,0:T(8,128)(2,1)S(1)}, bf16[1,32,512]{2,1,0:T(8,128)(2,1)S(1)}, u32[]{:S(2)}, u32[]{:S(2)}) collective-permute-start(bf16[1,32,512]{2,1,0:T(8,128)(2,1)S(1)} %bitcast.18), channel_id=1, source_target_pairs={{0,16},{16,0},{1,17},{17,1},{2,18},{18,2},{3,19},{19,3},{4,20},{20... | collective-permute-start | bytes 98312 | tf_op jit(solution)/shard_map/cond/branch_1_fun/cond/branch_1_fun/ppermute | solution.py:381
  41.8 20.6 %all-to-all-start.1 = ((f32[16,8,128]{2,1,0:T(8,128)}), f32[16,8,128]{2,1,0:T(8,128)S(1)}, u32[]{:S(2)}, u32[]{:S(2)}) async-start(f32[16,8,128]{2,1,0:T(8,128)} %branch_1_fun.11), calls=%async_computation.1 | async-start | bytes 131072 | tf_op jit(solution)/shard_map/cond/branch_1_fun/all_to_all | solution.py:418
  65.8 29.6 %all-to-all-start.2 = ((bf16[16,32,896]{2,1,0:T(8,128)(2,1)}), bf16[16,32,896]{2,1,0:T(8,128)(2,1)S(1)}, u32[]{:S(2)}, u32[]{:S(2)}) async-start(bf16[16,32,896]{2,1,0:T(8,128)(2,1)} %branch_1_fun.12), calls=%async_computation.2 | async-start | bytes 1835008 | tf_op jit(solution)/shard_map/cond/branch_1_fun/all_to_all | solution.py:421
  73.1 20.4 %collective-permute-start.5 = (bf16[2,448,512]{2,1,0:T(8,128)(2,1)}, bf16[2,448,512]{2,1,0:T(8,128)(2,1)S(1)}, u32[]{:S(2)}, u32[]{:S(2)}) collective-permute-start(bf16[2,448,512]{2,1,0:T(8,128)(2,1)} %pad_maximum_fusion.1), channel_id=1, source_target_pairs={{0,1},{1,0},{2,3},{3,2},{4,5},{5,4},{6,7},{7,6},{8,9},{9,8},{10,11... | collective-permute-start | bytes 2752520 | tf_op jit(solution)/shard_map/cond/branch_1_fun/cond/branch_1_fun/ppermute | solution.py:59
  75.6 12.2 %collective-permute-start.4 = (bf16[2,32,512]{2,1,0:T(8,128)(2,1)}, bf16[2,32,512]{2,1,0:T(8,128)(2,1)S(1)}, u32[]{:S(2)}, u32[]{:S(2)}) collective-permute-start(bf16[2,32,512]{2,1,0:T(8,128)(2,1)} %branch_1_fun.8), channel_id=1, source_target_pairs={{0,12},{2,14},{4,8},{6,10},{8,4},{10,6},{12,0},{14,2},{1,13},{3,15... | collective-permute-start | bytes 196616 | tf_op jit(solution)/shard_map/cond/branch_1_fun/cond/branch_1_fun/ppermute | solution.py:381
  79.5 11.8 %collective-permute-start.3 = (bf16[2,32,512]{2,1,0:T(8,128)(2,1)}, bf16[2,32,512]{2,1,0:T(8,128)(2,1)S(1)}, u32[]{:S(2)}, u32[]{:S(2)}) collective-permute-start(bf16[2,32,512]{2,1,0:T(8,128)(2,1)} %branch_1_fun.8), channel_id=1, source_target_pairs={{0,8},{2,10},{4,12},{6,14},{8,0},{10,2},{12,4},{14,6},{1,9},{3,11}... | collective-permute-start | bytes 196616 | tf_op jit(solution)/shard_map/cond/branch_1_fun/cond/branch_1_fun/ppermute | solution.py:381
  84.4 8.2 %collective-permute-start.2 = (bf16[2,32,512]{2,1,0:T(8,128)(2,1)}, bf16[2,32,512]{2,1,0:T(8,128)(2,1)S(1)}, u32[]{:S(2)}, u32[]{:S(2)}) collective-permute-start(bf16[2,32,512]{2,1,0:T(8,128)(2,1)} %branch_1_fun.8), channel_id=1, source_target_pairs={{0,4},{2,6},{4,0},{6,2},{8,12},{10,14},{12,8},{14,10},{1,5},{3,7},... | collective-permute-start | bytes 196616 | tf_op jit(solution)/shard_map/cond/branch_1_fun/cond/branch_1_fun/ppermute | solution.py:381
  96.5 35.2 %all-to-all-start.3 = ((bf16[16,32,896]{2,1,0:T(8,128)(2,1)}), bf16[16,32,896]{2,1,0:T(8,128)(2,1)}, u32[]{:S(2)}, u32[]{:S(2)}) async-start(bf16[16,32,896]{2,1,0:T(8,128)(2,1)} %branch_1_fun.13), calls=%async_computation.3 | async-start | bytes 1835008 | tf_op jit(solution)/shard_map/cond/branch_1_fun/all_to_all | solution.py:424
  106.1 9.6 %collective-permute-start.7 = (bf16[8,32,512]{2,1,0:T(8,128)(2,1)S(1)}, bf16[8,32,512]{2,1,0:T(8,128)(2,1)S(1)}, u32[]{:S(2)}, u32[]{:S(2)}) collective-permute-start(bf16[8,32,512]{2,1,0:T(8,128)(2,1)S(1)} %get-tuple-element.45.after_ref), channel_id=1, source_target_pairs={{0,2},{2,0},{4,6},{6,4},{8,10},{10,8},{12,14},{14,12},{1,3},{3,1},... | collective-permute-start | bytes 786440 | tf_op jit(solution)/shard_map/cond/branch_1_fun/ppermute | solution.py:381
  137.0 21.4 %all-to-all-start.4 = ((bf16[16,32,512]{2,1,0:T(8,128)(2,1)}), bf16[16,32,512]{2,1,0:T(8,128)(2,1)S(1)}, u32[]{:S(2)}, u32[]{:S(2)}) async-start(bf16[16,32,512]{2,1,0:T(8,128)(2,1)} %get-tuple-element.76), calls=%async_computation.4 | async-start | bytes 1048576 | tf_op jit(solution)/shard_map/all_to_all | solution.py:432
  147.0 5.0 %collective-permute-start = (bf16[3,448,512]{2,1,0:T(8,128)(2,1)S(1)}, bf16[3,448,512]{2,1,0:T(8,128)(2,1)S(1)}, u32[]{:S(2)}, u32[]{:S(2)}) collective-permute-start(bf16[3,448,512]{2,1,0:T(8,128)(2,1)S(1)} %get-tuple-element.51), channel_id=1, source_target_pairs={{0,1},{1,0},{2,3},{3,2},{4,5},{5,4},{6,7},{7,6},{8,9},{9,8},{10,11... | collective-permute-start | bytes 4128776 | tf_op jit(solution)/shard_map/cond/branch_1_fun/ppermute | solution.py:59
Sparse Core Ops, SparseCore 0:
  15.8 105.0 all-gather.1

commit v14 on v11

--- a/solution.py
+++ b/solution.py
@@ -97,13 +97,13 @@
     )(grad_out, gate_t, up_t, down)
 
 
-def tile_kernel(extra_ref, tile_ref):
+def tile_kernel(extra_ref, after_ref, tile_ref):
     sums = totals_of(jnp.sum(extra_ref[...].astype(jnp.float32), axis=0))
     tile = jnp.concatenate(sums + [jnp.zeros((5, LANES), jnp.float32)], axis=0)
     tile_ref[...] = jnp.broadcast_to(tile[None], tile_ref.shape)
 
 
-def sums_tile(received):
+def sums_tile(received, after):
     rows = received.shape[1] - EXTRA
     return pl.pallas_call(
         tile_kernel,
@@ -111,11 +111,12 @@
         out_shape=jax.ShapeDtypeStruct((2 * N_ROW, 8, LANES), jnp.float32),
         in_specs=[
             pl.BlockSpec((N_CHIP, EXTRA, LANES), lambda i: (0, rows // EXTRA, 0)),
+            ANY,
         ],
         out_specs=pl.BlockSpec((2 * N_ROW, 8, LANES), lambda i: (0, 0, 0)),
         compiler_params=PARAMS,
         cost_estimate=cost(1 << 16, 1 << 18),
-    )(received)
+    )(received, after)
 
 
 def scale_of(tile_ref, which):
@@ -344,7 +345,7 @@
     return ref[pl.ds(pl.multiple_of(core * rows, rows), rows), :]
 
 
-def pre_rows_kernel(mine_ref, gate_pre_ref, up_pre_ref, near_ref, far_ref, both_ref, after_ref, rows_ref):
+def pre_rows_kernel(mine_ref, gate_pre_ref, up_pre_ref, near_ref, far_ref, both_ref, rows_ref):
     rows, inner = gate_pre_ref.shape[0] // 2, gate_pre_ref.shape[1]
     core, xh = mine_ref[0], mine_ref[1]
     near, far, both = near_ref[...], far_ref[...], both_ref[...]
@@ -354,7 +355,7 @@
         rows_ref[pl.ds(pl.multiple_of(at * rows, rows), rows), :] = jnp.concatenate(parts, axis=1)
 
 
-def own_half(mine, gate_pre, up_pre, after):
+def own_half(mine, gate_pre, up_pre):
     rows, inner = gate_pre.shape
     pre = jnp.concatenate([gate_pre, up_pre], axis=1).reshape((2, -1, 2 * inner))
     own = lax.dynamic_index_in_dim(pre, mine[0], 0, keepdims=False)
@@ -362,14 +363,15 @@
     near = swapped(sent)
     far = lax.ppermute(own, "xh", [(0, 1), (1, 0)])
     both = lax.ppermute(sent, ("xh", "core"), [(k, k ^ 3) for k in range(4)])
-    return pl.pallas_call(
+    rows_pair = pl.pallas_call(
         pre_rows_kernel,
         out_shape=jax.ShapeDtypeStruct((rows, 4 * inner), jnp.bfloat16),
-        in_specs=[SMEM] + [VMEM] * 5 + [ANY],
+        in_specs=[SMEM] + [VMEM] * 5,
         out_specs=VMEM,
         compiler_params=PARAMS,
         cost_estimate=cost(1 << 10, 1 << 19),
-    )(mine, gate_pre, up_pre, near, far, both, after)
+    )(mine, gate_pre, up_pre, near, far, both)
+    return (rows_pair,)
 
 
 def in_branch(work, *operands):
@@ -389,13 +391,19 @@
     gate_t, up_t = gate_latent.T, up_latent.T
     sent = first(grad_out, gate_t, up_t, down_latent)
 
-    received = lax.all_to_all(sent, CHIP, 0, 0)
-    down_other = swapped(down_latent)
-    pre_rows = own_half(mine, gate_pre, up_pre, sent)
+    def gathers(sent, mine, gate_pre, up_pre, down):
+        received = lax.all_to_all(sent, CHIP, 0, 0)
+        down_other = swapped(down)
+        (pre_rows,) = in_branch(own_half, mine, gate_pre, up_pre)
+        return (received, down_other, pre_rows, sums_tile(received, pre_rows))
+
+    received, down_other, pre_rows, tile = in_branch(
+        gathers, sent, mine, gate_pre, up_pre, down_latent
+    )
     pre_half = lax.all_gather(pre_rows, "z", axis=0, tiled=True)
 
-    def exchanges(received, tokens, gate_t, up_t, down, down_other):
-        tile = lax.all_to_all(sums_tile(received), ROW + ("core",), 0, 0)
+    def exchanges(received, tile, tokens, gate_t, up_t, down, down_other):
+        tile = lax.all_to_all(tile, ROW + ("core",), 0, 0)
         out_half, both = laid_out(received, down, down_other)
         partial = hidden_partial(tile, out_half, both)
         parts = lax.all_to_all(partial, ROW, 0, 0)
@@ -405,7 +413,7 @@
         return (out_half, quant, grad_hidden, token_blocks)
 
     out_half, quant, grad_hidden, token_blocks = in_branch(
-        exchanges, received, tokens, gate_t, up_t, down_latent, down_other
+        exchanges, received, tile, tokens, gate_t, up_t, down_latent, down_other
     )
 
     partial, acts = act_partial(grad_hidden, pre_half, quant)

time: 172 us -> 167 us (0.971)
  waiting for transfers between devices: 53.4 us -> 50.6 us
    all_to_all x2, waiting for transfers between devices: 23.4 us -> 10.6 us  [the longest x1 10.6 us: exchanges(): tile = lax.all_to_all(tile, ROW + ('core',), 0, 0)]
    all_to_all x1, waiting for transfers between devices: 1.78 us -> 10.3 us  [exchanges(): parts = lax.all_to_all(partial, ROW, 0, 0)]
    all_to_all x1, starting transfers between devices: 7.91 us -> 4.84 us  [exchanges(): grad_hidden = lax.all_to_all(spread(parts, far), ROW, 0, 0)]
    ppermute x1, waiting for transfers between devices: 0.01 us -> 2.46 us  [own_half(): both = lax.ppermute(sent, ('xh', 'core'), [(k, k ^ 3) for k in range(4)])]
    all_to_all x2, starting transfers between devices: 19.7 us -> 21.5 us  [the longest x1 11.6 us: exchanges(): tile = lax.all_to_all(tile, ROW + ('core',), 0, 0)]
    ppermute x4, waiting for transfers between devices: 4.88 us -> 3.1 us  [swapped(): return lax.ppermute(values, 'core', [(0, 1), (1, 0)])]
  transfers between devices with their start and end apart: 18 -> 18, of which waited for: 13 -> 12; matrix products, arithmetic and copies ran while one was open for 2% -> 2% of each run, Pallas kernels for 9% -> 9%
where the time goes in v14:
time: 167 us; the launch traced here: 166 us
  starting transfers between devices  73.9 us (44%)
  waiting for transfers between devices  50.6 us (30%)
  Pallas kernels  23.9 us (14%)
  between operations  14.1 us (8%)
  other arithmetic  2.92 us (2%)
    ppermute x6, starting transfers between devices, exchanged(): lax.ppermute(blocks, axis, [(k, k ^ step) for k in range(count)])  21.4 us
    all_to_all x1, starting transfers between devices, exchanges(): tile = lax.all_to_all(tile, ROW + ('core',), 0, 0)  11.6 us
    all_to_all x1, waiting for transfers between devices, exchanges(): tile = lax.all_to_all(tile, ROW + ('core',), 0, 0)  10.6 us
    all_to_all x1, waiting for transfers between devices, exchanges(): parts = lax.all_to_all(partial, ROW, 0, 0)  10.3 us
    all_to_all x1, starting transfers between devices, gathers(): received = lax.all_to_all(sent, CHIP, 0, 0)  9.97 us
    ppermute x6, waiting for transfers between devices, exchanged(): lax.ppermute(blocks, axis, [(k, k ^ step) for k in range(count)])  9.55 us
    all_to_all x1, waiting for transfers between devices, exchanges(): grad_hidden = lax.all_to_all(spread(parts, far), ROW, 0, 0)  9.09 us
    ppermute x4, starting transfers between devices, swapped(): return lax.ppermute(values, 'core', [(0, 1), (1, 0)])  8.14 us
  transfers between devices with their start and end apart: 18, of which 12 were waited for; matrix products, arithmetic and copies ran while one was open for 2% of the time, Pallas kernels for 9%

profile of v14, /device:TPU:10, one launch (start us, length us, event | category | flops | bytes accessed | tf_op | source)
XLA Modules:
  0.0 165.7 jit_solution(1208039709219235734)
XLA Ops:
  7.2 0.0 copy-start.4
  7.2 0.0 all-gather.2.cloned.1.call-start
  7.2 0.1 pad_add_fusion
  7.3 2.6 %shard_map.105 = bf16[16,144,128]{2,1,0:T(8,128)(2,1)} custom-call(bf16[32,512]{1,0:T(8,128)(2,1)} %out_ref.1, bf16[448,512]{1,0:T(8,128)(2,1)} %bitcast.17, bf16[448,512]{1,0:T(8,128)(2,1)} %bitcast.20, bf16[448,512]{1,0:T(8,128)(2,1)} %down_ref.1), custom_call_target="tpu_custom_call" | custom-call | flops 1048576 | bytes 2621440 | tf_op jit(solution)/shard_map/pallas_call | solution.py:90
  9.9 0.0 copy-done.6
  9.9 0.0 copy-start
  9.9 0.0 copy-start.1
  9.9 0.0 copy-start.7
  9.9 28.3 %conditional.5 = (bf16[16,144,128]{2,1,0:T(8,128)(2,1)}, bf16[448,512]{1,0:T(8,128)(2,1)}, bf16[64,1792]{1,0:T(8,128)(2,1)}, f32[32,8,128]{2,1,0:T(8,128)}) conditional(s32[]{:T(128)} %convert_element_type.11, () %tuple.46, (bf16[16,144,128]{2,1,0:T(8,128)(2,1)}, bf16[448,512]{1,0:T(8,128)(2,1)S(1)}, bf16[64,448]{1,0:T(8,128)(2,1)S(1)}, ...), branch_computations={%region_0.0_spmd, %region_1.4_spmd} | conditional | flops 295948 | bytes 5538190 | solution.py:385
  9.9 10.0 %all-to-all-start = ((bf16[16,144,128]{2,1,0:T(8,128)(2,1)}), bf16[16,144,128]{2,1,0:T(8,128)(2,1)}, u32[]{:S(2)}, u32[]{:S(2)}) async-start(bf16[16,144,128]{2,1,0:T(8,128)(2,1)} %get-tuple-element.59), calls=%async_computation | async-start | bytes 1179648 | tf_op jit(solution)/shard_map/cond/branch_1_fun/all_to_all | solution.py:395
  19.9 1.9 %collective-permute-start.4 = (bf16[448,512]{1,0:T(8,128)(2,1)S(1)}, bf16[448,512]{1,0:T(8,128)(2,1)}, u32[]{:S(2)}, u32[]{:S(2)}) collective-permute-start(bf16[448,512]{1,0:T(8,128)(2,1)S(1)} %get-tuple-element.60), channel_id=1, source_target_pairs={{0,1},{1,0},{2,3},{3,2},{4,5},{5,4},{6,7},{7,6},{8,9},{9,8},{10,11... | collective-permute-start | bytes 1376264 | tf_op jit(solution)/shard_map/cond/branch_1_fun/ppermute | solution.py:59
  21.8 14.9 %conditional = (bf16[64,1792]{1,0:T(8,128)(2,1)}) conditional(s32[]{:T(128)} %convert_element_type.3, () %tuple.27, (bf16[64,448]{1,0:T(8,128)(2,1)S(1)}, bf16[64,448]{1,0:T(8,128)(2,1)S(1)}, s32[]{:T(128)}, s32[2]{0:T(128)S(1)}) %tuple.28), branch_computations={%region_2.0_spmd, %region_3.3_spmd} | conditional | flops 230407 | bytes 1671384 | solution.py:385
  21.8 0.1 pad_maximum_fusion
  21.9 2.4 %collective-permute-start.1 = (bf16[32,896]{1,0:T(8,128)(2,1)S(1)}, bf16[32,896]{1,0:T(8,128)(2,1)S(1)}, u32[]{:S(2)}, u32[]{:S(2)}) collective-permute-start(bf16[32,896]{1,0:T(8,128)(2,1)S(1)} %get-tuple-element.126), channel_id=1, source_target_pairs={{0,1},{1,0},{2,3},{3,2},{4,5},{5,4},{6,7},{7,6},{8,9},{9,8},{10,11... | collective-permute-start | bytes 172040 | tf_op jit(solution)/shard_map/cond/branch_1_fun/cond/branch_1_fun/ppermute | solution.py:59
  24.4 2.7 %collective-permute-start.2 = (bf16[32,896]{1,0:T(8,128)(2,1)S(1)}, bf16[32,896]{1,0:T(8,128)(2,1)S(1)}, u32[]{:S(2)}, u32[]{:S(2)}) collective-permute-start(bf16[32,896]{1,0:T(8,128)(2,1)S(1)} %get-tuple-element.125), channel_id=1, source_target_pairs={{0,256},{256,0},{1,257},{257,1},{2,258},{258,2},{3,259},{259,3},{4... | collective-permute-start | bytes 172040 | tf_op jit(solution)/shard_map/cond/branch_1_fun/cond/branch_1_fun/ppermute | solution.py:364
  27.0 4.0 %collective-permute-start.3 = (bf16[32,896]{1,0:T(8,128)(2,1)S(1)}, bf16[32,896]{1,0:T(8,128)(2,1)S(1)}, u32[]{:S(2)}, u32[]{:S(2)}) collective-permute-start(bf16[32,896]{1,0:T(8,128)(2,1)S(1)} %get-tuple-element.126), channel_id=1, source_target_pairs={{0,257},{1,256},{256,1},{257,0},{2,259},{3,258},{258,3},{259,2},{4... | collective-permute-start | bytes 172040 | tf_op jit(solution)/shard_map/cond/branch_1_fun/cond/branch_1_fun/ppermute | solution.py:365
  31.1 0.0 collective-permute-done.1.near_ref
  31.1 1.9 %collective-permute-done.2.far_ref = bf16[32,896]{1,0:T(8,128)(2,1)S(1)} collective-permute-done((bf16[32,896]{1,0:T(8,128)(2,1)S(1)}, bf16[32,896]{1,0:T(8,128)(2,1)S(1)}, u32[]{:S(2)}, u32[]{:S(2)}) %collective-permute-start.2) | collective-permute-done | bytes 57376 | tf_op jit(solution)/shard_map/cond/branch_1_fun/cond/branch_1_fun/ppermute | solution.py:364
  32.9 2.5 %collective-permute-done.3.both_ref = bf16[32,896]{1,0:T(8,128)(2,1)S(1)} collective-permute-done((bf16[32,896]{1,0:T(8,128)(2,1)S(1)}, bf16[32,896]{1,0:T(8,128)(2,1)S(1)}, u32[]{:S(2)}, u32[]{:S(2)}) %collective-permute-start.3) | collective-permute-done | bytes 57376 | tf_op jit(solution)/shard_map/cond/branch_1_fun/cond/branch_1_fun/ppermute | solution.py:365
  35.4 1.3 branch_1_fun.9
  36.7 0.0 all-to-all-done.extra_ref
  36.7 1.5 branch_1_fun.10
  38.3 0.0 collective-permute-done.4
  38.3 0.0 all-gather.2.cloned.1.call-update
  38.3 93.0 %conditional.6 = (bf16[512,512]{1,0:T(8,128)(2,1)S(1)}, bf16[2,896,512]{2,1,0:T(8,128)(2,1)}, bf16[16,32,896]{2,1,0:T(8,128)(2,1)}, bf16[16,32,512]{2,1,0:T(8,128)(2,1)}) conditional(s32[]{:T(128)} %convert_element_type.11, () %tuple.45, (bf16[16,144,128]{2,1,0:T(8,128)(2,1)}, bf16[448,512]{1,0:T(8,128)(2,1)S(1)}, bf16[448,512]{1,0:T(8,128)(2,1)}, ...), branch_computations={%region_4.5_spmd, %region_5.8_spmd} | conditional | flops 472777728 | bytes 32571958 | solution.py:385
  38.3 11.6 %all-to-all-start.1 = ((f32[32,8,128]{2,1,0:T(8,128)}), f32[32,8,128]{2,1,0:T(8,128)S(1)}, u32[]{:S(2)}, u32[]{:S(2)}) async-start(f32[32,8,128]{2,1,0:T(8,128)} %get-tuple-element.75), calls=%async_computation.1 | async-start | bytes 262144 | tf_op jit(solution)/shard_map/cond/branch_1_fun/all_to_all | solution.py:406
  49.9 1.3 branch_1_fun.13
  51.3 10.6 %all-to-all-done.1.tile_ref = f32[32,8,128]{2,1,0:T(8,128)S(1)} async-done(((f32[32,8,128]{2,1,0:T(8,128)}), f32[32,8,128]{2,1,0:T(8,128)S(1)}, u32[]{:S(2)}, u32[]{:S(2)}) %all-to-all-start.1) | async-done | bytes 131104 | tf_op jit(solution)/shard_map/cond/branch_1_fun/all_to_all | solution.py:406
  61.9 2.3 %branch_1_fun.14 = bf16[16,32,896]{2,1,0:T(8,128)(2,1)} custom-call(f32[32,8,128]{2,1,0:T(8,128)S(1)} %all-to-all-done.1.tile_ref, bf16[512,512]{1,0:T(8,128)(2,1)S(1)} %get-tuple-element.143.out_ref, bf16[2,448,512]{2,1,0:T(8,128)(2,1)S(1)} %get-tuple-element.76.both_ref), custom_call_target="tpu_custom_call" | custom-call | flops 469762048 | bytes 4194304 | tf_op jit(solution)/shard_map/cond/branch_1_fun/pallas_call | solution.py:170
  64.2 3.6 %all-to-all-start.2 = ((bf16[16,32,896]{2,1,0:T(8,128)(2,1)}), bf16[16,32,896]{2,1,0:T(8,128)(2,1)S(1)}, u32[]{:S(2)}, u32[]{:S(2)}) async-start(bf16[16,32,896]{2,1,0:T(8,128)(2,1)} %branch_1_fun.14), calls=%async_computation.2 | async-start | bytes 1835008 | tf_op jit(solution)/shard_map/cond/branch_1_fun/all_to_all | solution.py:409
  67.8 22.5 %conditional.1 = (bf16[4,32,512]{2,1,0:T(8,128)(2,1)S(1)}, bf16[2,896,512]{2,1,0:T(8,128)(2,1)}) conditional(s32[]{:T(128)} %convert_element_type.6, () %tuple.33, (bf16[32,512]{1,0:T(8,128)(2,1)S(1)}, bf16[16,32,896]{2,1,0:T(8,128)(2,1)}, bf16[448,512]{1,0:T(8,128)(2,1)S(1)}, bf16[448,512]{1,0:T(8,128)(2,1)S(1)}, f32[32,8,128]{2,1,0:T(8,128)S(1)}) %tuple.34), branch_computations={%region_6.6_spmd, %region_7.7_spmd} | conditional | flops 1703937 | bytes 10420400 | solution.py:385
  67.8 1.0 pad_maximum_fusion.1
  68.8 1.9 %collective-permute-start.8 = (bf16[2,448,512]{2,1,0:T(8,128)(2,1)}, bf16[2,448,512]{2,1,0:T(8,128)(2,1)S(1)}, u32[]{:S(2)}, u32[]{:S(2)}) collective-permute-start(bf16[2,448,512]{2,1,0:T(8,128)(2,1)} %pad_maximum_fusion.1), channel_id=1, source_target_pairs={{0,1},{1,0},{2,3},{3,2},{4,5},{5,4},{6,7},{7,6},{8,9},{9,8},{10,11... | collective-permute-start | bytes 2752520 | tf_op jit(solution)/shard_map/cond/branch_1_fun/cond/branch_1_fun/ppermute | solution.py:59
  70.7 0.6 branch_1_fun.11
  71.3 4.4 %collective-permute-start.7 = (bf16[1,32,512]{2,1,0:T(8,128)(2,1)}, bf16[1,32,512]{2,1,0:T(8,128)(2,1)S(1)}, u32[]{:S(2)}, u32[]{:S(2)}) collective-permute-start(bf16[1,32,512]{2,1,0:T(8,128)(2,1)} %bitcast.27), channel_id=1, source_target_pairs={{0,12},{2,14},{4,8},{6,10},{8,4},{10,6},{12,0},{14,2},{1,13},{3,15... | collective-permute-start | bytes 98312 | tf_op jit(solution)/shard_map/cond/branch_1_fun/cond/branch_1_fun/ppermute | solution.py:333
  75.7 4.9 %collective-permute-start.6 = (bf16[1,32,512]{2,1,0:T(8,128)(2,1)}, bf16[1,32,512]{2,1,0:T(8,128)(2,1)S(1)}, u32[]{:S(2)}, u32[]{:S(2)}) collective-permute-start(bf16[1,32,512]{2,1,0:T(8,128)(2,1)} %bitcast.28), channel_id=1, source_target_pairs={{0,8},{2,10},{4,12},{6,14},{8,0},{10,2},{12,4},{14,6},{1,9},{3,11}... | collective-permute-start | bytes 98312 | tf_op jit(solution)/shard_map/cond/branch_1_fun/cond/branch_1_fun/ppermute | solution.py:333
  80.7 2.9 %collective-permute-start.5 = (bf16[1,32,512]{2,1,0:T(8,128)(2,1)}, bf16[1,32,512]{2,1,0:T(8,128)(2,1)S(1)}, u32[]{:S(2)}, u32[]{:S(2)}) collective-permute-start(bf16[1,32,512]{2,1,0:T(8,128)(2,1)} %bitcast.29), channel_id=1, source_target_pairs={{0,4},{2,6},{4,0},{6,2},{8,12},{10,14},{12,8},{14,10},{1,5},{3,7},... | collective-permute-start | bytes 98312 | tf_op jit(solution)/shard_map/cond/branch_1_fun/cond/branch_1_fun/ppermute | solution.py:333
  83.6 0.0 collective-permute-done.7
  83.6 2.1 %collective-permute-done.6 = bf16[1,32,512]{2,1,0:T(8,128)(2,1)S(1)} collective-permute-done((bf16[1,32,512]{2,1,0:T(8,128)(2,1)}, bf16[1,32,512]{2,1,0:T(8,128)(2,1)S(1)}, u32[]{:S(2)}, u32[]{:S(2)}) %collective-permute-start.6) | collective-permute-done | bytes 32800 | tf_op jit(solution)/shard_map/cond/branch_1_fun/cond/branch_1_fun/ppermute | solution.py:333
  85.7 1.9 %collective-permute-done.5 = bf16[1,32,512]{2,1,0:T(8,128)(2,1)S(1)} collective-permute-done((bf16[1,32,512]{2,1,0:T(8,128)(2,1)}, bf16[1,32,512]{2,1,0:T(8,128)(2,1)S(1)}, u32[]{:S(2)}, u32[]{:S(2)}) %collective-permute-start.5) | collective-permute-done | bytes 32800 | tf_op jit(solution)/shard_map/cond/branch_1_fun/cond/branch_1_fun/ppermute | solution.py:333
  87.6 0.8 pad_maximum_fusion.2
  88.4 0.0 collective-permute-done.8.other_ref
  88.4 2.0 %branch_1_fun.12 = bf16[2,896,512]{2,1,0:T(8,128)(2,1)} custom-call(f32[32,8,128]{2,1,0:T(8,128)S(1)} %get-tuple-element.67.tile_ref, bf16[448,512]{1,0:T(8,128)(2,1)S(1)} %get-tuple-element.68.gate_ref, bf16[448,512]{1,0:T(8,128)(2,1)S(1)} %get-tuple-element.69.up_ref, bf16[2,448,512]{2,1,0:T(8,128)(2,1)S(1)} %collective-permute-done.8.other_ref), custom_call_target="tpu_custom_call" | custom-call | flops 1048576 | bytes 4194304 | tf_op jit(solution)/shard_map/cond/branch_1_fun/cond/branch_1_fun/pallas_call | solution.py:207
  90.3 10.3 %all-to-all-done.2.parts_ref = bf16[16,32,896]{2,1,0:T(8,128)(2,1)S(1)} async-done(((bf16[16,32,896]{2,1,0:T(8,128)(2,1)}), bf16[16,32,896]{2,1,0:T(8,128)(2,1)S(1)}, u32[]{:S(2)}, u32[]{:S(2)}) %all-to-all-start.2) | async-done | bytes 917536 | tf_op jit(solution)/shard_map/cond/branch_1_fun/all_to_all | solution.py:409
  100.6 1.1 branch_1_fun.15
  101.7 4.8 %all-to-all-start.3 = ((bf16[16,32,896]{2,1,0:T(8,128)(2,1)}), bf16[16,32,896]{2,1,0:T(8,128)(2,1)}, u32[]{:S(2)}, u32[]{:S(2)}) async-start(bf16[16,32,896]{2,1,0:T(8,128)(2,1)} %branch_1_fun.15), calls=%async_computation.3 | async-start | bytes 1835008 | tf_op jit(solution)/shard_map/cond/branch_1_fun/all_to_all | solution.py:412
  106.5 2.4 %collective-permute-start.11 = (bf16[4,32,512]{2,1,0:T(8,128)(2,1)S(1)}, bf16[4,32,512]{2,1,0:T(8,128)(2,1)S(1)}, u32[]{:S(2)}, u32[]{:S(2)}) collective-permute-start(bf16[4,32,512]{2,1,0:T(8,128)(2,1)S(1)} %get-tuple-element.80.after_ref), channel_id=1, source_target_pairs={{0,18},{2,16},{4,22},{6,20},{8,26},{10,24},{12,30},{14,28},{16,2},... | collective-permute-start | bytes 393224 | tf_op jit(solution)/shard_map/cond/branch_1_fun/ppermute | solution.py:333
  109.0 3.3 %collective-permute-start.10 = (bf16[4,32,512]{2,1,0:T(8,128)(2,1)S(1)}, bf16[4,32,512]{2,1,0:T(8,128)(2,1)S(1)}, u32[]{:S(2)}, u32[]{:S(2)}) collective-permute-start(bf16[4,32,512]{2,1,0:T(8,128)(2,1)S(1)} %get-tuple-element.80.after_ref), channel_id=1, source_target_pairs={{0,2},{2,0},{4,6},{6,4},{8,10},{10,8},{12,14},{14,12},{16,18},{18,... | collective-permute-start | bytes 393224 | tf_op jit(solution)/shard_map/cond/branch_1_fun/ppermute | solution.py:333
  112.3 3.5 %collective-permute-start.9 = (bf16[4,32,512]{2,1,0:T(8,128)(2,1)S(1)}, bf16[4,32,512]{2,1,0:T(8,128)(2,1)S(1)}, u32[]{:S(2)}, u32[]{:S(2)}) collective-permute-start(bf16[4,32,512]{2,1,0:T(8,128)(2,1)S(1)} %get-tuple-element.80.after_ref), channel_id=1, source_target_pairs={{0,16},{2,18},{4,20},{6,22},{8,24},{10,26},{12,28},{14,30},{16,0},... | collective-permute-start | bytes 393224 | tf_op jit(solution)/shard_map/cond/branch_1_fun/ppermute | solution.py:333
  115.8 0.2 collective-permute-done.11
  116.0 0.1 collective-permute-done.10
  116.1 5.2 %collective-permute-done.9 = bf16[4,32,512]{2,1,0:T(8,128)(2,1)S(1)} collective-permute-done((bf16[4,32,512]{2,1,0:T(8,128)(2,1)S(1)}, bf16[4,32,512]{2,1,0:T(8,128)(2,1)S(1)}, u32[]{:S(2)}, u32[]{:S(2)}) %collective-permute-start.9) | collective-permute-done | bytes 131104 | tf_op jit(solution)/shard_map/cond/branch_1_fun/ppermute | solution.py:333
  121.3 0.9 pad_maximum_fusion.3
  122.2 9.1 %all-to-all-done.3 = bf16[16,32,896]{2,1,0:T(8,128)(2,1)} async-done(((bf16[16,32,896]{2,1,0:T(8,128)(2,1)}), bf16[16,32,896]{2,1,0:T(8,128)(2,1)}, u32[]{:S(2)}, u32[]{:S(2)}) %all-to-all-start.3) | async-done | bytes 917536 | tf_op jit(solution)/shard_map/cond/branch_1_fun/all_to_all | solution.py:412
  131.3 5.8 %shard_map.106 = (bf16[16,32,512]{2,1,0:T(8,128)(2,1)}, bf16[3,512,896]{2,1,0:T(8,128)(2,1)}) custom-call(bf16[16,32,896]{2,1,0:T(8,128)(2,1)} %get-tuple-element.108.hid_ref, bf16[8,2,32,1792]{3,2,1,0:T(8,128)(2,1)} %bitcast.23, bf16[2,896,512]{2,1,0:T(8,128)(2,1)} %get-tuple-element.110.quant_ref), custom_call_target="tpu_custom_call" | custom-call | flops 939524096 | bytes 8388608 | tf_op jit(solution)/shard_map/pallas_call | solution.py:232
  137.1 7.6 %all-to-all-start.4 = ((bf16[16,32,512]{2,1,0:T(8,128)(2,1)}), bf16[16,32,512]{2,1,0:T(8,128)(2,1)S(1)}, u32[]{:S(2)}, u32[]{:S(2)}) async-start(bf16[16,32,512]{2,1,0:T(8,128)(2,1)} %get-tuple-element.111), calls=%async_computation.4 | async-start | bytes 1048576 | tf_op jit(solution)/shard_map/all_to_all | solution.py:420
  144.7 0.1 pad_add_fusion.1
  144.8 9.8 %conditional.7 = ((bf16[448,512]{1,0:T(8,128)(2,1)}, bf16[448,512]{1,0:T(8,128)(2,1)}, bf16[448,512]{1,0:T(8,128)(2,1)}, f32[8,128]{1,0:T(8,128)S(1)})) conditional(s32[]{:T(128)} %convert_element_type.11, () %tuple.49, (s32[2]{0:T(128)S(1)}, bf16[3,512,896]{2,1,0:T(8,128)(2,1)}, bf16[512,512]{1,0:T(8,128)(2,1)S(1)}, ...), branch_computations={%region_8.9_spmd, %region_9.10_spmd} | conditional | flops 1410334720 | bytes 19136560 | solution.py:385
  144.8 3.5 %branch_1_fun.16 = (f32[3,448,512]{2,1,0:T(8,128)S(1)}, bf16[3,448,512]{2,1,0:T(8,128)(2,1)S(1)}) custom-call(s32[2]{0:T(128)S(1)} %get-tuple-element.81.place_ref, bf16[3,512,896]{2,1,0:T(8,128)(2,1)} %get-tuple-element.82.acts_ref, bf16[512,512]{1,0:T(8,128)(2,1)S(1)} %get-tuple-element.83.out_ref, bf16[16,32,512]{2,1,0:T(8,128)(2,1)} %get-tuple-element.84.tokens_ref), custom_call_target="tpu_custom_call" | custom-call | flops 1409286144 | bytes 8388608 | tf_op jit(solution)/shard_map/cond/branch_1_fun/pallas_call | solution.py:270
  148.3 1.9 %collective-permute-start = (bf16[3,448,512]{2,1,0:T(8,128)(2,1)S(1)}, bf16[3,448,512]{2,1,0:T(8,128)(2,1)S(1)}, u32[]{:S(2)}, u32[]{:S(2)}) collective-permute-start(bf16[3,448,512]{2,1,0:T(8,128)(2,1)S(1)} %get-tuple-element.86), channel_id=1, source_target_pairs={{0,1},{1,0},{2,3},{3,2},{4,5},{5,4},{6,7},{7,6},{8,9},{9,8},{10,11... | collective-permute-start | bytes 4128776 | tf_op jit(solution)/shard_map/cond/branch_1_fun/ppermute | solution.py:59
  150.3 3.1 %collective-permute-done.other_ref = bf16[3,448,512]{2,1,0:T(8,128)(2,1)S(1)} collective-permute-done((bf16[3,448,512]{2,1,0:T(8,128)(2,1)S(1)}, bf16[3,448,512]{2,1,0:T(8,128)(2,1)S(1)}, u32[]{:S(2)}, u32[]{:S(2)}) %collective-permute-start) | collective-permute-done | bytes 1376288 | tf_op jit(solution)/shard_map/cond/branch_1_fun/ppermute | solution.py:59
  153.3 1.2 branch_1_fun.17
  154.6 3.6 %all-to-all-done.4.parts_ref = bf16[16,32,512]{2,1,0:T(8,128)(2,1)S(1)} async-done(((bf16[16,32,512]{2,1,0:T(8,128)(2,1)}), bf16[16,32,512]{2,1,0:T(8,128)(2,1)S(1)}, u32[]{:S(2)}, u32[]{:S(2)}) %all-to-all-start.4) | async-done | bytes 524320 | tf_op jit(solution)/shard_map/all_to_all | solution.py:420
  158.2 0.7 shard_map.107
  (13 shorter events, 0.0 us)
Async XLA Ops:
  7.2 2.7 %copy-start.4 = (bf16[448,512]{1,0:T(8,128)(2,1)S(1)}, bf16[448,512]{1,0:T(8,128)(2,1)}, u32[]{:S(2)}) copy-start(bf16[448,512]{1,0:T(8,128)(2,1)} %down_ref.1) | copy-start | bytes 1376260
  7.2 2.7 %copy-start.5 = (bf16[64,448]{1,0:T(8,128)(2,1)S(1)}, bf16[64,448]{1,0:T(8,128)(2,1)}, u32[]{:S(2)}) copy-start(bf16[64,448]{1,0:T(8,128)(2,1)} %param.19) | copy-start | bytes 172036
  7.2 2.7 %copy-start.6 = (bf16[64,448]{1,0:T(8,128)(2,1)S(1)}, bf16[64,448]{1,0:T(8,128)(2,1)}, u32[]{:S(2)}) copy-start(bf16[64,448]{1,0:T(8,128)(2,1)} %param.20) | copy-start | bytes 172036
  7.2 124.1 %all-gather.2.cloned.1.call-start = ((), (), s32[]{:S(2)}) async-start(), calls=%async_computation.5 | async-start | bytes 2064384 | tf_op jit(solution)/shard_map/all_gather | solution.py:403
  9.9 28.4 %copy-start = (bf16[512,448]{0,1:T(8,128)(2,1)S(1)}, bf16[512,448]{0,1:T(8,128)(2,1)}, u32[]{:S(2)}) copy-start(bf16[512,448]{0,1:T(8,128)(2,1)} %param.21) | copy-start | bytes 1376260
  9.9 28.4 %copy-start.1 = (bf16[512,448]{0,1:T(8,128)(2,1)S(1)}, bf16[512,448]{0,1:T(8,128)(2,1)}, u32[]{:S(2)}) copy-start(bf16[512,448]{0,1:T(8,128)(2,1)} %param.22) | copy-start | bytes 1376260
  9.9 28.4 %copy-start.7 = (bf16[32,512]{1,0:T(8,128)(2,1)S(1)}, bf16[32,512]{1,0:T(8,128)(2,1)}, u32[]{:S(2)}) copy-start(bf16[32,512]{1,0:T(8,128)(2,1)} %param.17) | copy-start | bytes 98308
  9.9 26.8 %all-to-all-start = ((bf16[16,144,128]{2,1,0:T(8,128)(2,1)}), bf16[16,144,128]{2,1,0:T(8,128)(2,1)}, u32[]{:S(2)}, u32[]{:S(2)}) async-start(bf16[16,144,128]{2,1,0:T(8,128)(2,1)} %get-tuple-element.59), calls=%async_computation | async-start | bytes 1179648 | tf_op jit(solution)/shard_map/cond/branch_1_fun/all_to_all | solution.py:395
  19.9 18.4 %collective-permute-start.4 = (bf16[448,512]{1,0:T(8,128)(2,1)S(1)}, bf16[448,512]{1,0:T(8,128)(2,1)}, u32[]{:S(2)}, u32[]{:S(2)}) collective-permute-start(bf16[448,512]{1,0:T(8,128)(2,1)S(1)} %get-tuple-element.60), channel_id=1, source_target_pairs={{0,1},{1,0},{2,3},{3,2},{4,5},{5,4},{6,7},{7,6},{8,9},{9,8},{10,11... | collective-permute-start | bytes 1376264 | tf_op jit(solution)/shard_map/cond/branch_1_fun/ppermute | solution.py:59
  21.9 9.1 %collective-permute-start.1 = (bf16[32,896]{1,0:T(8,128)(2,1)S(1)}, bf16[32,896]{1,0:T(8,128)(2,1)S(1)}, u32[]{:S(2)}, u32[]{:S(2)}) collective-permute-start(bf16[32,896]{1,0:T(8,128)(2,1)S(1)} %get-tuple-element.126), channel_id=1, source_target_pairs={{0,1},{1,0},{2,3},{3,2},{4,5},{5,4},{6,7},{7,6},{8,9},{9,8},{10,11... | collective-permute-start | bytes 172040 | tf_op jit(solution)/shard_map/cond/branch_1_fun/cond/branch_1_fun/ppermute | solution.py:59
  24.4 8.6 %collective-permute-start.2 = (bf16[32,896]{1,0:T(8,128)(2,1)S(1)}, bf16[32,896]{1,0:T(8,128)(2,1)S(1)}, u32[]{:S(2)}, u32[]{:S(2)}) collective-permute-start(bf16[32,896]{1,0:T(8,128)(2,1)S(1)} %get-tuple-element.125), channel_id=1, source_target_pairs={{0,256},{256,0},{1,257},{257,1},{2,258},{258,2},{3,259},{259,3},{4... | collective-permute-start | bytes 172040 | tf_op jit(solution)/shard_map/cond/branch_1_fun/cond/branch_1_fun/ppermute | solution.py:364
  27.0 8.4 %collective-permute-start.3 = (bf16[32,896]{1,0:T(8,128)(2,1)S(1)}, bf16[32,896]{1,0:T(8,128)(2,1)S(1)}, u32[]{:S(2)}, u32[]{:S(2)}) collective-permute-start(bf16[32,896]{1,0:T(8,128)(2,1)S(1)} %get-tuple-element.126), channel_id=1, source_target_pairs={{0,257},{1,256},{256,1},{257,0},{2,259},{3,258},{258,3},{259,2},{4... | collective-permute-start | bytes 172040 | tf_op jit(solution)/shard_map/cond/branch_1_fun/cond/branch_1_fun/ppermute | solution.py:365
  38.3 23.5 %all-to-all-start.1 = ((f32[32,8,128]{2,1,0:T(8,128)}), f32[32,8,128]{2,1,0:T(8,128)S(1)}, u32[]{:S(2)}, u32[]{:S(2)}) async-start(f32[32,8,128]{2,1,0:T(8,128)} %get-tuple-element.75), calls=%async_computation.1 | async-start | bytes 262144 | tf_op jit(solution)/shard_map/cond/branch_1_fun/all_to_all | solution.py:406
  51.3 12.9 %copy-start.2 = (bf16[512,512]{1,0:T(8,128)(2,1)}, bf16[512,512]{1,0:T(8,128)(2,1)S(1)}, u32[]{:S(2)}) copy-start(bf16[512,512]{1,0:T(8,128)(2,1)S(1)} %get-tuple-element.143.out_ref) | copy-start | bytes 1572868 | tf_op jit(solution)/shard_map/cond
  64.2 36.5 %all-to-all-start.2 = ((bf16[16,32,896]{2,1,0:T(8,128)(2,1)}), bf16[16,32,896]{2,1,0:T(8,128)(2,1)S(1)}, u32[]{:S(2)}, u32[]{:S(2)}) async-start(bf16[16,32,896]{2,1,0:T(8,128)(2,1)} %branch_1_fun.14), calls=%async_computation.2 | async-start | bytes 1835008 | tf_op jit(solution)/shard_map/cond/branch_1_fun/all_to_all | solution.py:409
  68.8 19.5 %collective-permute-start.8 = (bf16[2,448,512]{2,1,0:T(8,128)(2,1)}, bf16[2,448,512]{2,1,0:T(8,128)(2,1)S(1)}, u32[]{:S(2)}, u32[]{:S(2)}) collective-permute-start(bf16[2,448,512]{2,1,0:T(8,128)(2,1)} %pad_maximum_fusion.1), channel_id=1, source_target_pairs={{0,1},{1,0},{2,3},{3,2},{4,5},{5,4},{6,7},{7,6},{8,9},{9,8},{10,11... | collective-permute-start | bytes 2752520 | tf_op jit(solution)/shard_map/cond/branch_1_fun/cond/branch_1_fun/ppermute | solution.py:59
  71.3 12.2 %collective-permute-start.7 = (bf16[1,32,512]{2,1,0:T(8,128)(2,1)}, bf16[1,32,512]{2,1,0:T(8,128)(2,1)S(1)}, u32[]{:S(2)}, u32[]{:S(2)}) collective-permute-start(bf16[1,32,512]{2,1,0:T(8,128)(2,1)} %bitcast.27), channel_id=1, source_target_pairs={{0,12},{2,14},{4,8},{6,10},{8,4},{10,6},{12,0},{14,2},{1,13},{3,15... | collective-permute-start | bytes 98312 | tf_op jit(solution)/shard_map/cond/branch_1_fun/cond/branch_1_fun/ppermute | solution.py:333
  75.7 9.9 %collective-permute-start.6 = (bf16[1,32,512]{2,1,0:T(8,128)(2,1)}, bf16[1,32,512]{2,1,0:T(8,128)(2,1)S(1)}, u32[]{:S(2)}, u32[]{:S(2)}) collective-permute-start(bf16[1,32,512]{2,1,0:T(8,128)(2,1)} %bitcast.28), channel_id=1, source_target_pairs={{0,8},{2,10},{4,12},{6,14},{8,0},{10,2},{12,4},{14,6},{1,9},{3,11}... | collective-permute-start | bytes 98312 | tf_op jit(solution)/shard_map/cond/branch_1_fun/cond/branch_1_fun/ppermute | solution.py:333
  80.7 6.9 %collective-permute-start.5 = (bf16[1,32,512]{2,1,0:T(8,128)(2,1)}, bf16[1,32,512]{2,1,0:T(8,128)(2,1)S(1)}, u32[]{:S(2)}, u32[]{:S(2)}) collective-permute-start(bf16[1,32,512]{2,1,0:T(8,128)(2,1)} %bitcast.29), channel_id=1, source_target_pairs={{0,4},{2,6},{4,0},{6,2},{8,12},{10,14},{12,8},{14,10},{1,5},{3,7},... | collective-permute-start | bytes 98312 | tf_op jit(solution)/shard_map/cond/branch_1_fun/cond/branch_1_fun/ppermute | solution.py:333
  101.7 29.7 %copy-start.3 = (bf16[512,512]{1,0:T(8,128)(2,1)S(1)}, bf16[512,512]{1,0:T(8,128)(2,1)}, u32[]{:S(2)}) copy-start(bf16[512,512]{1,0:T(8,128)(2,1)} %copy-done.2) | copy-start | bytes 1572868 | tf_op jit(solution)/shard_map/cond
  101.7 29.6 %all-to-all-start.3 = ((bf16[16,32,896]{2,1,0:T(8,128)(2,1)}), bf16[16,32,896]{2,1,0:T(8,128)(2,1)}, u32[]{:S(2)}, u32[]{:S(2)}) async-start(bf16[16,32,896]{2,1,0:T(8,128)(2,1)} %branch_1_fun.15), calls=%async_computation.3 | async-start | bytes 1835008 | tf_op jit(solution)/shard_map/cond/branch_1_fun/all_to_all | solution.py:412
  106.5 9.5 %collective-permute-start.11 = (bf16[4,32,512]{2,1,0:T(8,128)(2,1)S(1)}, bf16[4,32,512]{2,1,0:T(8,128)(2,1)S(1)}, u32[]{:S(2)}, u32[]{:S(2)}) collective-permute-start(bf16[4,32,512]{2,1,0:T(8,128)(2,1)S(1)} %get-tuple-element.80.after_ref), channel_id=1, source_target_pairs={{0,18},{2,16},{4,22},{6,20},{8,26},{10,24},{12,30},{14,28},{16,2},... | collective-permute-start | bytes 393224 | tf_op jit(solution)/shard_map/cond/branch_1_fun/ppermute | solution.py:333
  109.0 7.2 %collective-permute-start.10 = (bf16[4,32,512]{2,1,0:T(8,128)(2,1)S(1)}, bf16[4,32,512]{2,1,0:T(8,128)(2,1)S(1)}, u32[]{:S(2)}, u32[]{:S(2)}) collective-permute-start(bf16[4,32,512]{2,1,0:T(8,128)(2,1)S(1)} %get-tuple-element.80.after_ref), channel_id=1, source_target_pairs={{0,2},{2,0},{4,6},{6,4},{8,10},{10,8},{12,14},{14,12},{16,18},{18,... | collective-permute-start | bytes 393224 | tf_op jit(solution)/shard_map/cond/branch_1_fun/ppermute | solution.py:333
  112.3 9.0 %collective-permute-start.9 = (bf16[4,32,512]{2,1,0:T(8,128)(2,1)S(1)}, bf16[4,32,512]{2,1,0:T(8,128)(2,1)S(1)}, u32[]{:S(2)}, u32[]{:S(2)}) collective-permute-start(bf16[4,32,512]{2,1,0:T(8,128)(2,1)S(1)} %get-tuple-element.80.after_ref), channel_id=1, source_target_pairs={{0,16},{2,18},{4,20},{6,22},{8,24},{10,26},{12,28},{14,30},{16,0},... | collective-permute-start | bytes 393224 | tf_op jit(solution)/shard_map/cond/branch_1_fun/ppermute | solution.py:333
  137.1 21.0 %all-to-all-start.4 = ((bf16[16,32,512]{2,1,0:T(8,128)(2,1)}), bf16[16,32,512]{2,1,0:T(8,128)(2,1)S(1)}, u32[]{:S(2)}, u32[]{:S(2)}) async-start(bf16[16,32,512]{2,1,0:T(8,128)(2,1)} %get-tuple-element.111), calls=%async_computation.4 | async-start | bytes 1048576 | tf_op jit(solution)/shard_map/all_to_all | solution.py:420
  148.3 5.0 %collective-permute-start = (bf16[3,448,512]{2,1,0:T(8,128)(2,1)S(1)}, bf16[3,448,512]{2,1,0:T(8,128)(2,1)S(1)}, u32[]{:S(2)}, u32[]{:S(2)}) collective-permute-start(bf16[3,448,512]{2,1,0:T(8,128)(2,1)S(1)} %get-tuple-element.86), channel_id=1, source_target_pairs={{0,1},{1,0},{2,3},{3,2},{4,5},{5,4},{6,7},{7,6},{8,9},{9,8},{10,11... | collective-permute-start | bytes 4128776 | tf_op jit(solution)/shard_map/cond/branch_1_fun/ppermute | solution.py:59
Sparse Core Ops, SparseCore 0:
  38.4 61.1 all-gather.1
